TPU v7x, 32 devices: a whole 2x2x4 slice. The times are simulated.
32 devices in a mesh: blk: 16 (over z, y, core), ij: 2 (over x).
Axes of the slice: x: 2, y: 2, z: 4, core: 2. Of those that a mesh axis runs over, the one named last changes fastest.
Arguments:
- density: float32 [16, 6, 256, 128], P('blk', None, 'ij'), may hold values from 0.8 to 1.2
- momentum: float32 [16, 3, 6, 256, 128], P('blk', None, None, 'ij'), may hold values from -2.5 to 2.5
- energy: float32 [16, 6, 256, 128], P('blk', None, 'ij'), may hold values from 2.5 to 4
- metrics: float32 [16, 4, 256, 128], P('blk', None, 'ij'), may hold values from -1 to 1
- volume: float32 [16, 256, 128], P('blk', 'ij'), may hold values from 0.5 to 2
- placed: int32 [16], replicated, may hold values from 0 to 15, each once
- neighbour: int32 [16, 2], replicated, may hold values from 0 to 15, as said below
- face: int32 [16, 2], replicated, may hold values from 0 to 1, as said below
- orient: int32 [16, 2], replicated, may hold values from 0 to 1, as said below
Outputs:
- next_density: float32 [16, 6, 256, 128], P('blk', None, 'ij')
- next_momentum: float32 [16, 3, 6, 256, 128], P('blk', None, None, 'ij')
- next_energy: float32 [16, 6, 256, 128], P('blk', None, 'ij')
Inputs may be any that keep to these rules, and one draw needn't show every extreme that they name: If face f of block b meets face g of block c with orientation o, then face g of c meets face f of b with orientation o; every block id appears as a neighbour. `face`: consistent with neighbour as stated there. `orient`: consistent with neighbour as stated there.
All inputs are finite; a program needn't handle non-finite values.
Results may differ from a plain program's by a relative error of at most 0.00002.
Values sent between devices are 32-bit elements; how exact they have to be, the bound alone decides.
No kernel may reach another device: no remote copies, remote signals or barrier semaphores. Data moves between devices by JAX's collectives and lax.ppermute only.
A program may use at most 128 MiB of HBM per device.

v0:
```python
import functools

import jax
import jax.numpy as jnp
from jax import lax
from jax.experimental import pallas as pl
from jax.experimental.pallas import tpu as pltpu
from jax.sharding import PartitionSpec as P

pressure_factor = 0.4
viscosity = 0.05
time_step = 0.03
unit = time_step / 12.0

LANES = 128
PAD = 8
DEPTH = 4
CH = 5
VMEM_LIMIT = 48 * 1024 * 1024


def turn(x, shift, axis):
    shift = shift % x.shape[axis]
    return x if shift == 0 else pltpu.roll(x, shift, axis)


def lanes_of(shape):
    return lax.broadcasted_iota(jnp.int32, shape, len(shape) - 1)


def rows_of(shape):
    return lax.broadcasted_iota(jnp.int32, shape, len(shape) - 2)


def plane_at(refs, c, k, rows):
    dens, mom, en, met, vol = refs
    if k == dens.shape[1]:
        return met[0, c, rows] if c < 4 else vol[0, rows]
    if c == 0:
        return dens[0, k, rows]
    if c == 4:
        return en[0, k, rows]
    return mom[0, c - 1, k, rows]


def point(f):
    rho, m1, m2, m3, e = f
    r = 1.0 / rho
    u1, u2, u3 = m1 * r, m2 * r, m3 * r
    kin = 0.5 * (m1 * u1 + m2 * u2 + m3 * u3)
    p = pressure_factor * (e - kin)
    return (u1, u2, u3, (kin + 2.0 * p) * r), p, e + p


def metric_terms(m):
    ax, ay, bx, by, v = m
    kv = viscosity * unit
    rw = kv * (ax * ax + ay * ay)
    cw = kv * (bx * bx + by * by)
    return v * ax, v * ay, v * bx, v * by, -unit / v, rw, cw, 30.0 * (rw + cw + kv)


def flux(f, w, p, h, gx, gy):
    rho, m1, m2, m3, _ = f
    u = gx * w[0] + gy * w[1]
    return (rho * u, m1 * u + gx * p, m2 * u + gy * p, m3 * u, h * u)


def flux_planes(f, w, p, h):
    u3 = w[2]
    return (f[3], f[1] * u3, f[2] * u3, f[3] * u3 + p, h * u3)


def slope(x, at):
    return 8.0 * (at(x, 1) - at(x, -1)) - (at(x, 2) - at(x, -2))


def curve(x, at):
    return 16.0 * (at(x, 1) + at(x, -1)) - (at(x, 2) + at(x, -2))


def along(axis):
    return lambda x, o: turn(x, -o, axis)


def plane_shift(x, o):
    o = o % x.shape[0]
    return jnp.concatenate([x[o:], x[:o]], axis=0)


def tile_rate(f, m, at_i, at_j):
    vax, vay, vbx, vby, niv, rw, cw, tw = metric_terms(m)
    kv = viscosity * unit
    w, p, h = point(f)
    fi = flux(f, w, p, h, vax, vay)
    fj = flux(f, w, p, h, vbx, vby)
    fk = flux_planes(f, w, p, h)
    out = []
    for c in range(CH):
        val = niv * (slope(fi[c], at_i) + slope(fj[c], at_j)) - unit * slope(fk[c], plane_shift)
        if c > 0:
            x = w[c - 1]
            val = val + (
                rw * curve(x, at_i) + cw * curve(x, at_j) + kv * curve(x, plane_shift) - tw * x
            )
        out.append(val)
    return out, fj, w, niv, cw


def edge_terms(fn, w, niv, cw):
    out = []
    for face in range(2):
        rows = rows_of(fn[face][0].shape)
        terms = []
        for c in range(CH):
            a, b = fn[face][c], fn[1 - face][c]
            first = 8.0 * (turn(a, -1, 1) + b) - (turn(a, -2, 1) + turn(b, 1, 1))
            second = -(turn(a, -2, 1) + turn(b, -1, 1))
            val = niv[face] * jnp.where(rows == 1, first, second)
            if c > 0:
                a, b = w[face][c - 1], w[1 - face][c - 1]
                first = 16.0 * (turn(a, -1, 1) - b) - (turn(a, -2, 1) - turn(b, 1, 1))
                second = -(turn(a, -2, 1) - turn(b, -1, 1))
                val = val + cw[face] * jnp.where(rows == 1, first, second)
            terms.append(val)
        out.append(terms)
    return out


def put_edges(ref, terms, planes, wide):
    for c in range(CH):
        for k in range(planes):
            at = (c * planes + k) * 4
            ref[at : at + 2, 0:wide] = terms[1][c][k, 0:2]
            ref[at + 2 : at + 3, 0:wide] = terms[0][c][k, 1:2]
            ref[at + 3 : at + 4, 0:wide] = terms[0][c][k, 0:1]


def edge_lanes(tile, index):
    lane = lanes_of(tile.shape)
    moved = turn(tile, LANES - 2 - 4 * index, 1)
    return jnp.where((lane < 2) | (lane >= LANES - 2), moved, 0.0)


def cut_kernel(halves, dens, mom, en, met, vol, placed, orient, send, own, *rest):
    edges, scratch = rest[:-1], rest[-1]
    refs = (dens, mom, en, met, vol)
    planes, rows = dens.shape[1], dens.shape[2]
    block = placed[lax.axis_index("blk")]
    half = lax.axis_index("ij")
    twist = [orient[block, 0] == 1, orient[block, 1] == 1]
    lane = lanes_of((rows, LANES))
    mirror = jnp.where(
        rows_of((LANES, LANES)) + lanes_of((LANES, LANES)) == rows - 1, 1.0, 0.0
    )
    row = rows_of((64, LANES))
    twisted = jnp.where(
        row % 8 < 4, jnp.where(twist[1], 1, 0), jnp.where(twist[0], 1, 0)
    ) == 1
    scratch[CH * 64 :] = jnp.zeros((3 * 64, LANES), jnp.float32)
    for c in range(CH):
        packed = jnp.zeros((rows, LANES), jnp.float32)
        for k in range(planes + 1):
            x = plane_at(refs, c, k, slice(None))
            packed = jnp.where(lane // 8 == k, turn(x, 8 * k + 4, 1), packed)
        if rows < LANES:
            packed = jnp.concatenate(
                [packed, jnp.zeros((LANES - rows, LANES), jnp.float32)], axis=0
            )
        strip = packed.T[0:64]
        if c in (2, 3):
            strip = jnp.where((row >= planes * 8) & (row % 8 >= 4), -strip, strip)
        own[c] = strip
        back = jnp.dot(
            strip,
            mirror,
            precision=lax.Precision.HIGHEST,
            preferred_element_type=jnp.float32,
        )
        if c < 2:
            back = jnp.where(row >= planes * 8, -back, back)
        scratch[c * 64 : c * 64 + 64] = jnp.where(twisted, back, strip)
    for k in range(planes + 1):
        for d in range(DEPTH):
            at = (k * DEPTH + d) * 16
            send[at : at + 8] = scratch[pl.ds(k * 8 + 4 + d, 8, stride=64)]
            send[at + 8 : at + 16] = scratch[pl.ds(k * 8 + 3 - d, 8, stride=64)]
    for c in range(CH):
        for k in range(planes + 1):
            low = plane_at(refs, c, k, slice(0, 4))
            high = plane_at(refs, c, k, slice(rows - 4, rows))
            if len(edges) == 1:
                edges[0][c, k * 4 : k * 4 + 4] = jnp.where(half == 0, high, low)
            else:
                edges[0][c, k * 4 : k * 4 + 4] = low
                edges[1][c, k * 4 : k * 4 + 4] = high


def relay_kernel(halves, rows, placed, neighbour, face, orient, got, send, ext, where_is):
    blocks = placed.shape[0]

    def note(slot, _):
        where_is[placed[slot]] = slot
        return 0

    lax.fori_loop(0, blocks, note, 0)
    lane = lanes_of((8, LANES))

    def pass_on(n, _):
        slot, f = n // 2, n % 2
        block = placed[slot]
        partner = where_is[neighbour[block, f]]
        side, turned = face[block, f], orient[block, f]
        for half in range(halves):

            def piece(h):
                h = jnp.where(turned == 1, halves - 1 - h, h)
                at = ((partner * halves + h) * 2 + side) * 8
                return got[pl.ds(pl.multiple_of(at, 8), 8)]

            at = pl.multiple_of(((slot * halves + half) * 2 + f) * 8, 8)
            send[pl.ds(at, 8)] = piece(half)
            low, high = piece(max(half - 1, 0)), piece(min(half + 1, halves - 1))
            ends = jnp.where(lane < 2, turn(low, 2 - rows, 1), turn(high, 2, 1))
            ext[pl.ds(at, 8)] = jnp.where(lane < 4, ends, 0.0)
        return 0

    lax.fori_loop(0, 2 * blocks, pass_on, 0)
    count = 2 * blocks * halves
    ends = ext[pl.ds(0, count, stride=8)]
    for c in range(1, CH):
        ends = ends + turn(ext[pl.ds(c, count, stride=8)], 4 * c, 1)
    send[pl.ds(5, count, stride=8)] = ends


def flux_chunk(get, mets, fi, w, r, rest=None):
    rows = pl.ds(r, 8)
    vax, vay, vbx, vby, niv, rw, cw, tw = [mets[j, rows] for j in range(8)]
    at_j = along(1)
    for k in range(fi.shape[1]):
        f = [get(c, k, r) for c in range(CH)]
        wk, p, h = point(f)
        for c, x in enumerate(flux(f, wk, p, h, vax, vay)):
            fi[c, k, rows] = x
        for c in range(4):
            w[c, k, rows] = wk[c]
        if rest is None:
            continue
        fk, acc = rest
        fj = flux(f, wk, p, h, vbx, vby)
        for c in range(CH):
            val = niv * slope(fj[c], at_j)
            if c > 0:
                val = val + (cw * curve(wk[c - 1], at_j) - tw * wk[c - 1])
            acc[c, k, rows] = val
        for c, x in enumerate(flux_planes(f, wk, p, h)):
            fk[c, k, rows] = x


def sum_chunk(mets, fi, w, fk, acc, r, emit):
    planes = fi.shape[1]
    kv = viscosity * unit
    rows = pl.ds(r, 8)
    niv, rw = mets[4, rows], mets[5, rows]
    for c in range(CH):
        t = [fk[c, k, rows] for k in range(planes)]
        x = [w[c - 1, k, rows] for k in range(planes)] if c > 0 else None
        for k in range(planes):

            def near(v, o):
                return v[(k + o) % planes]

            def at_i(v, o):
                return v[pl.ds(r + o, 8)]

            val = acc[c, k, rows] + niv * slope(fi.at[c, k], at_i) - unit * slope(t, near)
            if c > 0:
                val = val + (rw * curve(w.at[c - 1, k], at_i) + kv * curve(x, near))
            emit(c, k, r, val)


def chunks(count, body):
    def step(n, _):
        body(pl.multiple_of(n * 8, 8))
        return 0

    lax.fori_loop(0, count, step, 0)


def first_kernel(dens, mom, en, met, vol, part, mets, fi, w, fk, acc):
    refs = (dens, mom, en, met, vol)
    planes, rows = dens.shape[1], dens.shape[2]

    def terms(r):
        m = [plane_at(refs, c, planes, pl.ds(r, 8)) for c in range(CH)]
        for j, x in enumerate(metric_terms(m)):
            mets[j, pl.ds(r + PAD, 8)] = x

    def get(c, k, r):
        return plane_at(refs, c, k, pl.ds(r - PAD, 8))

    def fluxes(r):
        terms(r)
        flux_chunk(get, mets, fi, w, r + PAD, (fk, acc))

    def emit(c, k, r, val):
        part[c, k, pl.ds(r - PAD, 8)] = get(c, k, r) + val

    def sums(r):
        sum_chunk(mets, fi, w, fk, acc, r + PAD, emit)

    empty = jnp.zeros((PAD, LANES), jnp.float32)
    for k in range(planes):
        for c in range(CH):
            fi[c, k, 0:PAD] = empty
            fi[c, k, rows + PAD :] = empty
        for c in range(4):
            w[c, k, 0:PAD] = empty
            w[c, k, rows + PAD :] = empty
    chunks(rows // 8, fluxes)
    chunks(rows // 8, sums)


def last_kernel(
    halves, dens, mom, en, met, vol, placed, orient, own, below, above, got, part,
    next_dens, next_mom, next_en,
    tall, strips, turned, back, sec, mets, fi, w, fk, acc,
):
    refs = (dens, mom, en, met, vol)
    planes, rows = dens.shape[1], dens.shape[2]
    every = planes + 1
    half = lax.axis_index("ij")
    block = placed[lax.axis_index("blk")]
    low_wall, high_wall = half == 0, half == halves - 1
    low_flag, high_flag = jnp.where(low_wall, 1, 0), jnp.where(high_wall, 1, 0)

    for c in range(CH):
        for k in range(every):
            tall[0, c, k, 4:8] = plane_at(refs, c, k, slice(0, 4))
            tall[1, c, k, 0:4] = plane_at(refs, c, k, slice(rows - 4, rows))

    @pl.when(low_wall)
    def _():
        for c in range(CH):
            for k in range(every):
                sign = -1.0 if 1 <= c <= 3 and k < planes else 1.0
                for d in range(4):
                    tall[0, c, k, 3 - d : 4 - d] = sign * plane_at(refs, c, k, slice(d, d + 1))

    @pl.when(jnp.logical_not(low_wall))
    def _():
        for c in range(CH):
            for k in range(every):
                tall[0, c, k, 0:4] = below[c, k * 4 : k * 4 + 4]

    @pl.when(high_wall)
    def _():
        for c in range(CH):
            for k in range(every):
                for d in range(4):
                    tall[1, c, k, 4 + d : 5 + d] = plane_at(
                        refs, c, k, slice(rows - 1 - d, rows - d)
                    )

    @pl.when(jnp.logical_not(high_wall))
    def _():
        for c in range(CH):
            for k in range(every):
                tall[1, c, k, 4:8] = above[c, k * 4 : k * 4 + 4]

    lane8, row8 = lanes_of((8, LANES)), rows_of((8, LANES))
    stacked = []
    for c in range(CH):
        packed = jnp.zeros((8, LANES), jnp.float32)
        for k in range(every):
            x = jnp.where(row8 < 4, tall[0, c, k], tall[1, c, k])
            packed = jnp.where(lane8 // 8 == k, turn(x, 8 * k + 4, 1), packed)
        stacked.append(packed)
    stacked.append(jnp.zeros((LANES - 8 * CH, LANES), jnp.float32))
    ends = jnp.concatenate(stacked, axis=0).T[0:64]

    count = DEPTH * every
    lane = lanes_of((count, LANES))
    row = rows_of((count, LANES))
    is_field = row < planes * DEPTH
    lane64 = lanes_of((64, LANES))

    def set_strip(c, f, first, second, rows_at):
        for k in range(every):
            for at, start, size in rows_at(k):
                strips[c, f, k, at : at + size, 0:LANES] = first[start : start + size]
                strips[c, f, k, at : at + size, LANES:] = second[start : start + size]

    def spread(main, outer, lane):
        if rows == LANES:
            return main, outer
        return jnp.where((lane == rows) | (lane == rows + 1), turn(outer, rows, 1), main), outer

    for c in range(CH):
        outer = turn(ends, -(8 * c + 4), 1)
        if c in (2, 3):
            r64 = rows_of((64, LANES))
            outer = jnp.where((r64 >= planes * 8) & (r64 % 8 >= 4), -outer, outer)
        first, second = spread(own[c], outer, lane64)
        set_strip(c, 1, first, second, lambda k: ((0, k * 8 + 2, 2),))
        set_strip(c, 0, first, second, lambda k: ((0, k * 8 + 5, 1), (1, k * 8 + 4, 1)))
        for f in range(2):
            twist = jnp.where(orient[block, f] == 1, 1, 0)
            main = got[pl.ds(f * 8 + c, count, stride=16)]
            outer = turn(got[pl.ds(f * 8 + 5, count, stride=16)], LANES - 2 - 4 * c, 1)
            if c in (2, 3):
                main = jnp.where(is_field, main, -main)
                outer = jnp.where(is_field, outer, -outer)
            low = jnp.where(lane == LANES - 2, turn(main, LANES - 3, 1), turn(main, LANES - 1, 1))
            high = jnp.where(lane == 0, turn(main, 1 - rows, 1), turn(main, 3 - rows, 1))
            if 1 <= c <= 3:
                low = jnp.where(is_field & (twist == 0), -low, low)
                high = jnp.where(is_field & (twist == 1), -high, high)
            outer = jnp.where((lane >= LANES // 2) & (low_flag == 1), low, outer)
            outer = jnp.where((lane < LANES // 2) & (high_flag == 1), high, outer)
            first, second = spread(main, outer, lane)
            set_strip(c, f, first, second, lambda k: ((2, k * DEPTH, DEPTH),))
            for k in range(every):
                strips[c, f, k, 6:8] = jnp.ones((2, 2 * LANES), jnp.float32)

    fn, ws, nivs, cws = [], [], [], []
    for f in range(2):
        fields = [strips[c, f, 0:planes] for c in range(CH)]
        m = [strips[c, f, planes] for c in range(CH)]
        rate, flux_n, wn, niv, cw = tile_rate(fields, m, along(2), along(1))
        for c in range(CH):
            strips[c, f, 0:planes] = fields[c] + rate[c]
        fn.append(flux_n)
        ws.append(wn)
        nivs.append(niv)
        cws.append(cw)
    turned[...] = jnp.zeros((LANES, 2 * LANES), jnp.float32)
    put_edges(turned, edge_terms(fn, ws, nivs, cws), planes, 2 * LANES)
    back[PAD : PAD + LANES] = turned[:, 0:LANES].T
    back[PAD + LANES : PAD + 2 * LANES] = turned[:, LANES:].T
    back[0:PAD] = back[2 * LANES : 2 * LANES + PAD]

    def finish(r):
        tile = back[pl.ds(r + PAD, 8)]
        for c in range(CH):
            for k in range(planes):
                sec[c, k, pl.ds(r + PAD, 8)] = part[c, k, pl.ds(r, 8)] + edge_lanes(
                    tile, c * planes + k
                )

    chunks(rows // 8, finish)
    sub = rows_of((planes, 8, LANES))
    for end in range(2):
        start = -4 if end == 0 else rows - 4
        fields = [tall[end, c, 0:planes] for c in range(CH)]
        m = [tall[end, c, planes] for c in range(CH)]
        rate = tile_rate(fields, m, along(1), along(2))[0]
        tile = back[PAD + start : PAD + start + 8]
        for c in range(CH):
            extra = jnp.stack([edge_lanes(tile, c * planes + k) for k in range(planes)])
            x = fields[c] + rate[c] + extra
            if end == 0:
                sign = -1.0 if 1 <= c <= 3 else 1.0
                wall = sign * jnp.where(sub == 2, turn(x, -3, 1), turn(x, -1, 1))
                x = jnp.where((sub < 4) & (low_flag == 1), wall, x)
            else:
                wall = jnp.where(sub == 4, turn(x, 1, 1), turn(x, 3, 1))
                x = jnp.where((sub >= 4) & (high_flag == 1), wall, x)
            for k in range(planes):
                sec[c, k, PAD + start + 2 : PAD + start + 6] = x[k, 2:6]

    if rows < LANES:
        back[...] = jnp.zeros(back.shape, jnp.float32)

    def pack(r):
        packed = jnp.zeros((8, LANES), jnp.float32)
        for c in range(CH):
            for k in range(planes):
                index = c * planes + k
                x = turn(sec[c, k, pl.ds(r + PAD, 8)], 4 * index + 2, 1)
                packed = jnp.where(lane8 // 4 == index, x, packed)
        back[pl.ds(r, 8)] = packed

    chunks(rows // 8, pack)
    columns = back[0:LANES].T
    fn, ws = [], []
    for c in range(CH):
        for k in range(planes):
            at = (c * planes + k) * 4
            strips[c, 1, k, 0:2, 0:LANES] = columns[at : at + 2]
            strips[c, 0, k, 0:1, 0:LANES] = columns[at + 3 : at + 4]
            strips[c, 0, k, 1:2, 0:LANES] = columns[at + 2 : at + 3]
    for f in range(2):
        fields = [strips[c, f, 0:planes, :, 0:LANES] for c in range(CH)]
        m = [strips[c, f, planes, :, 0:LANES] for c in range(CH)]
        _, _, vbx, vby, _, _, _, _ = metric_terms(m)
        wn, p, h = point(fields)
        fn.append(flux(fields, wn, p, h, vbx, vby))
        ws.append(wn)
    nivs = [x[:, 0:LANES] for x in nivs]
    cws = [x[:, 0:LANES] for x in cws]
    put_edges(turned, edge_terms(fn, ws, nivs, cws), planes, LANES)
    back[0:LANES] = turned[:, 0:LANES].T

    def terms(r):
        m = [plane_at(refs, c, planes, pl.ds(r, 8)) for c in range(CH)]
        for j, x in enumerate(metric_terms(m)):
            mets[j, pl.ds(r + PAD, 8)] = x

    for end, at in ((0, PAD - 4), (1, PAD + rows - 4)):
        m = [tall[end, c, planes] for c in range(CH)]
        for j, x in enumerate(metric_terms(m)):
            mets[j, at : at + 8] = x

    def get(c, k, r):
        return sec[c, k, pl.ds(r, 8)]

    def fluxes(r):
        terms(r)
        flux_chunk(get, mets, fi, w, r + PAD, (fk, acc))

    def emit(c, k, r, val):
        at = pl.ds(r - PAD, 8)
        extra = edge_lanes(back[at], c * planes + k)
        x = 0.5 * (plane_at(refs, c, k, at) + (get(c, k, r) + (val + extra)))
        if c == 0:
            next_dens[0, k, at] = x
        elif c == 4:
            next_en[0, k, at] = x
        else:
            next_mom[0, c - 1, k, at] = x

    def sums(r):
        sum_chunk(mets, fi, w, fk, acc, r + PAD, emit)

    flux_chunk(get, mets, fi, w, 0)
    flux_chunk(get, mets, fi, w, rows + PAD)
    chunks(rows // 8, fluxes)
    chunks(rows // 8, sums)


def local(mesh_shape, density, momentum, energy, metrics, volume, placed, neighbour, face, orient):
    halves = mesh_shape["ij"]
    devices = mesh_shape["blk"] * halves
    planes, rows = density.shape[1], density.shape[2]
    fields = (density, momentum, energy, metrics, volume)
    f32 = jnp.float32
    vmem = pl.BlockSpec(memory_space=pltpu.VMEM)
    smem = pl.BlockSpec(memory_space=pltpu.SMEM)
    params = pltpu.CompilerParams(vmem_limit_bytes=VMEM_LIMIT)
    piece = jax.ShapeDtypeStruct((devices * 16, LANES), f32)
    edge = jax.ShapeDtypeStruct((CH, 4 * (planes + 1), LANES), f32)
    edges = 1 if halves == 2 else 2

    sent, own, *halo = pl.pallas_call(
        functools.partial(cut_kernel, halves),
        out_shape=[piece, jax.ShapeDtypeStruct((CH, 64, LANES), f32)] + [edge] * edges,
        in_specs=[vmem] * 5 + [smem] * 2,
        out_specs=[vmem] * (2 + edges),
        scratch_shapes=[pltpu.VMEM((8 * 64, LANES), f32)],
        compiler_params=params,
        name="cut",
    )(*fields, placed, orient)

    def swap(x):
        x = x.reshape(devices, 16, LANES)
        x = lax.all_to_all(x, ("blk", "ij"), 0, 0, tiled=True)
        return x.reshape(devices * 16, LANES)

    if edges == 1:
        below = above = lax.ppermute(halo[0], "ij", [(0, 1), (1, 0)])
    else:
        below = lax.ppermute(halo[1], "ij", [(i, i + 1) for i in range(halves - 1)])
        above = lax.ppermute(halo[0], "ij", [(i + 1, i) for i in range(halves - 1)])
    got = swap(sent)
    relayed = pl.pallas_call(
        functools.partial(relay_kernel, halves, rows),
        out_shape=piece,
        in_specs=[smem] * 4 + [vmem],
        out_specs=vmem,
        scratch_shapes=[
            pltpu.VMEM((devices * 16, LANES), f32),
            pltpu.SMEM((placed.shape[0],), jnp.int32),
        ],
        compiler_params=params,
        name="relay",
    )(placed, neighbour, face, orient, got)
    ghosts = swap(relayed)

    tall = rows + 2 * PAD
    stage = [
        pltpu.VMEM((8, tall, LANES), f32),
        pltpu.VMEM((CH, planes, tall, LANES), f32),
        pltpu.VMEM((4, planes, tall, LANES), f32),
        pltpu.VMEM((CH, planes, tall, LANES), f32),
        pltpu.VMEM((CH, planes, tall, LANES), f32),
    ]
    part = pl.pallas_call(
        first_kernel,
        out_shape=jax.ShapeDtypeStruct((CH, planes, rows, LANES), f32),
        in_specs=[vmem] * 5,
        out_specs=vmem,
        scratch_shapes=stage,
        compiler_params=params,
        name="first_section",
    )(*fields)

    return pl.pallas_call(
        functools.partial(last_kernel, halves),
        out_shape=[
            jax.ShapeDtypeStruct(density.shape, f32),
            jax.ShapeDtypeStruct(momentum.shape, f32),
            jax.ShapeDtypeStruct(energy.shape, f32),
        ],
        in_specs=[vmem] * 5 + [smem] * 2 + [vmem] * 5,
        out_specs=[vmem] * 3,
        scratch_shapes=[
            pltpu.VMEM((2, CH, planes + 1, 8, LANES), f32),
            pltpu.VMEM((CH, 2, planes + 1, 8, 2 * LANES), f32),
            pltpu.VMEM((LANES, 2 * LANES), f32),
            pltpu.VMEM((2 * LANES + PAD, LANES), f32),
            pltpu.VMEM((CH, planes, tall, LANES), f32),
        ]
        + stage,
        compiler_params=params,
        name="second_section",
    )(*fields, placed, orient, own, below, above, ghosts, part)


def solution(mesh):
    return jax.shard_map(
        functools.partial(local, dict(mesh.shape)),
        mesh=mesh,
        in_specs=(
            P("blk", None, "ij", None),
            P("blk", None, None, "ij", None),
            P("blk", None, "ij", None),
            P("blk", None, "ij", None),
            P("blk", "ij", None),
            P(),
            P(),
            P(),
            P(),
        ),
        out_specs=(
            P("blk", None, "ij", None),
            P("blk", None, None, "ij", None),
            P("blk", None, "ij", None),
        ),
        check_vma=False,
    )
```

profile of v0, /device:TPU:0, one launch (start us, length us, event | category | flops | bytes accessed | tf_op | source)
XLA Modules:
  0.0 67.3 jit_solution(7056548563429222948)
XLA Ops:
  0.6 0.8 %copy.16.orient = s32[16,2]{1,0:T(8,128)S(1)} copy(s32[16,2]{0,1:T(2,128)} %param.17) | data formatting | bytes 256 | tf_op args[8]
  1.4 0.0 copy-start
  1.4 1.3 %copy-done = f32[1,3,6,128,128]{4,3,2,1,0:T(8,128)S(1)} copy-done((f32[1,3,6,128,128]{4,3,2,1,0:T(8,128)S(1)}, f32[1,3,6,128,128]{4,3,2,1,0:T(8,128)}, u32[]{:S(2)}) %copy-start) | copy-done | bytes 1179672
  2.7 0.0 copy-start.2
  2.7 1.0 %copy-done.2 = f32[1,6,128,128]{3,2,1,0:T(8,128)S(1)} copy-done((f32[1,6,128,128]{3,2,1,0:T(8,128)S(1)}, f32[1,6,128,128]{3,2,1,0:T(8,128)}, u32[]{:S(2)}) %copy-start.2) | copy-done | bytes 393240
  3.7 0.0 copy-start.4
  3.7 1.0 %copy-done.4 = f32[1,6,128,128]{3,2,1,0:T(8,128)S(1)} copy-done((f32[1,6,128,128]{3,2,1,0:T(8,128)S(1)}, f32[1,6,128,128]{3,2,1,0:T(8,128)}, u32[]{:S(2)}) %copy-start.4) | copy-done | bytes 393240
  4.7 0.0 copy-start.7
  4.7 0.9 %copy-done.7 = f32[1,4,128,128]{3,2,1,0:T(8,128)S(1)} copy-done((f32[1,4,128,128]{3,2,1,0:T(8,128)S(1)}, f32[1,4,128,128]{3,2,1,0:T(8,128)}, u32[]{:S(2)}) %copy-start.7) | copy-done | bytes 262168
  5.6 0.0 copy-start.10
  5.6 0.8 %copy-done.10 = f32[1,128,128]{2,1,0:T(8,128)S(1)} copy-done((f32[1,128,128]{2,1,0:T(8,128)S(1)}, f32[1,128,128]{2,1,0:T(8,128)}, u32[]{:S(2)}) %copy-start.10) | copy-done | bytes 65560
  6.4 0.0 copy-start.17
  6.4 0.7 copy-done.17
  7.1 0.0 copy-start.19
  7.1 0.0 copy-start.20
  7.1 0.0 copy-start.18
  7.1 2.5 %cut.1 = (f32[512,128]{1,0:T(8,128)}, f32[5,64,128]{2,1,0:T(8,128)S(1)}, f32[5,28,128]{2,1,0:T(8,128)}) custom-call(f32[1,6,128,128]{3,2,1,0:T(8,128)S(1)} %copy-done.2, f32[1,3,6,128,128]{4,3,2,1,0:T(8,128)S(1)} %copy-done, f32[1,6,128,128]{3,2,1,0:T(8,128)S(1)} %copy-done.4, f32[1,4,128,128]{3,2,1,0:T(8,128)S(1)} %copy-done.7, ...), custom_call_target="tpu_custom_call" | custom-call | tf_op jit(solution)/shard_map/cut/pallas_call | solution.py:555
  9.7 0.0 copy-start.15
  9.7 0.7 copy-done.15
  10.3 0.0 copy-start.1
  10.3 0.0 copy-start.3
  10.3 7.3 %all-to-all-start = ((f32[32,16,128]{2,1,0:T(8,128)}), f32[32,16,128]{2,1,0:T(8,128)S(1)}, u32[]{:S(2)}, u32[]{:S(2)}) async-start(f32[32,16,128]{2,1,0:T(8,128)} %bitcast), calls=%async_computation | async-start | bytes 524288 | tf_op jit(solution)/shard_map/all_to_all | solution.py:567
  17.6 0.0 copy-done.19
  17.6 0.1 copy.13.neighbour
  17.7 0.0 copy-done.20
  17.7 0.1 copy.14.face
  17.8 10.5 %all-to-all-done = f32[32,16,128]{2,1,0:T(8,128)S(1)} async-done(((f32[32,16,128]{2,1,0:T(8,128)}), f32[32,16,128]{2,1,0:T(8,128)S(1)}, u32[]{:S(2)}, u32[]{:S(2)}) %all-to-all-start) | async-done | bytes 262176 | tf_op jit(solution)/shard_map/all_to_all | solution.py:567
  28.3 0.0 copy-done.18
  28.3 4.2 %relay.1 = f32[512,128]{1,0:T(8,128)} custom-call(s32[16]{0:T(128)S(1)} %copy-done.18, s32[16,2]{1,0:T(8,128)S(1)} %copy.13.neighbour, s32[16,2]{1,0:T(8,128)S(1)} %copy.14.face, s32[16,2]{1,0:T(8,128)S(1)} %copy.16.orient, f32[512,128]{1,0:T(8,128)S(1)} %bitcast.4), custom_call_target="tpu_custom_call" | custom-call | tf_op jit(solution)/shard_map/relay/pallas_call | solution.py:576
  32.5 3.3 %all-to-all-start.1 = ((f32[32,16,128]{2,1,0:T(8,128)}), f32[32,16,128]{2,1,0:T(8,128)}, u32[]{:S(2)}, u32[]{:S(2)}) async-start(f32[32,16,128]{2,1,0:T(8,128)} %bitcast.2), calls=%async_computation.1 | async-start | bytes 524288 | tf_op jit(solution)/shard_map/all_to_all | solution.py:567
  35.9 1.6 %collective-permute-start = (f32[5,28,128]{2,1,0:T(8,128)}, f32[5,28,128]{2,1,0:T(8,128)S(1)}, u32[]{:S(2)}, u32[]{:S(2)}) collective-permute-start(f32[5,28,128]{2,1,0:T(8,128)} %get-tuple-element.7), channel_id=1, source_target_pairs={{0,1},{1,0},{2,3},{3,2},{4,5},{5,4},{6,7},{7,6},{8,9},{9,8},{10,11... | collective-permute-start | bytes 215048 | tf_op jit(solution)/shard_map/ppermute | solution.py:571
  37.5 0.0 copy-done.1
  37.5 0.0 copy-done.3
  37.5 0.0 copy-start.5
  37.5 1.0 %copy-done.5 = f32[1,6,128,128]{3,2,1,0:T(8,128)S(1)} copy-done((f32[1,6,128,128]{3,2,1,0:T(8,128)S(1)}, f32[1,6,128,128]{3,2,1,0:T(8,128)}, u32[]{:S(2)}) %copy-start.5) | copy-done | bytes 393240
  38.5 0.9 %copy-done.8 = f32[1,4,128,128]{3,2,1,0:T(8,128)S(1)} copy-done((f32[1,4,128,128]{3,2,1,0:T(8,128)S(1)}, f32[1,4,128,128]{3,2,1,0:T(8,128)}, u32[]{:S(2)}) %copy-start.8) | copy-done | bytes 262168
  39.4 0.8 %copy-done.11 = f32[1,128,128]{2,1,0:T(8,128)S(1)} copy-done((f32[1,128,128]{2,1,0:T(8,128)S(1)}, f32[1,128,128]{2,1,0:T(8,128)}, u32[]{:S(2)}) %copy-start.11) | copy-done | bytes 65560
  40.3 6.4 %first_section.1.part = f32[5,6,128,128]{3,2,1,0:T(8,128)S(1)} custom-call(f32[1,6,128,128]{3,2,1,0:T(8,128)S(1)} %copy-done.3, f32[1,3,6,128,128]{4,3,2,1,0:T(8,128)S(1)} %copy-done.1, f32[1,6,128,128]{3,2,1,0:T(8,128)S(1)} %copy-done.5, f32[1,4,128,128]{3,2,1,0:T(8,128)S(1)} %copy-done.8, f32[1,128,128]{2,1,0:T(8,128)S(1)} %copy-done.11), custom_call_target="tpu_custom_call" | custom-call | tf_op jit(solution)/shard_map/first_section/pallas_call | solution.py:598
  46.7 0.0 collective-permute-done.below.above
  46.7 0.0 copy-start.13
  46.7 0.6 copy-done.13
  47.3 0.0 all-to-all-done.1
  47.4 1.0 %copy-done.6 = f32[1,6,128,128]{3,2,1,0:T(8,128)S(1)} copy-done((f32[1,6,128,128]{3,2,1,0:T(8,128)S(1)}, f32[1,6,128,128]{3,2,1,0:T(8,128)}, u32[]{:S(2)}) %copy-start.6) | copy-done | bytes 393240
  48.4 0.9 %copy-done.9 = f32[1,4,128,128]{3,2,1,0:T(8,128)S(1)} copy-done((f32[1,4,128,128]{3,2,1,0:T(8,128)S(1)}, f32[1,4,128,128]{3,2,1,0:T(8,128)}, u32[]{:S(2)}) %copy-start.9) | copy-done | bytes 262168
  49.3 0.8 %copy-done.12 = f32[1,128,128]{2,1,0:T(8,128)S(1)} copy-done((f32[1,128,128]{2,1,0:T(8,128)S(1)}, f32[1,128,128]{2,1,0:T(8,128)}, u32[]{:S(2)}) %copy-start.12) | copy-done | bytes 65560
  50.1 0.9 %copy-done.14 = f32[5,28,128]{2,1,0:T(8,128)S(1)} copy-done((f32[5,28,128]{2,1,0:T(8,128)S(1)}, f32[5,28,128]{2,1,0:T(8,128)}, u32[]{:S(2)}) %copy-start.14) | copy-done | bytes 71704
  51.0 0.9 %copy-done.16 = f32[5,64,128]{2,1,0:T(8,128)S(1)} copy-done((f32[5,64,128]{2,1,0:T(8,128)S(1)}, f32[5,64,128]{2,1,0:T(8,128)}, u32[]{:S(2)}) %copy-start.16) | copy-done | bytes 163864
  51.9 15.3 %second_section.1 = (f32[1,6,128,128]{3,2,1,0:T(8,128)}, f32[1,3,6,128,128]{4,3,2,1,0:T(8,128)}, f32[1,6,128,128]{3,2,1,0:T(8,128)}) custom-call(f32[1,6,128,128]{3,2,1,0:T(8,128)S(1)} %copy-done.3, f32[1,3,6,128,128]{4,3,2,1,0:T(8,128)S(1)} %copy-done.1, f32[1,6,128,128]{3,2,1,0:T(8,128)S(1)} %copy-done.6, f32[1,4,128,128]{3,2,1,0:T(8,128)S(1)} %copy-done.9, ...), custom_call_target="tpu_custom_call" | custom-call | tf_op jit(solution)/shard_map/second_section/pallas_call | solution.py:608
  (7 shorter events, 0.0 us)
Async XLA Ops:
  1.4 1.3 %copy-start = (f32[1,3,6,128,128]{4,3,2,1,0:T(8,128)S(1)}, f32[1,3,6,128,128]{4,3,2,1,0:T(8,128)}, u32[]{:S(2)}) copy-start(f32[1,3,6,128,128]{4,3,2,1,0:T(8,128)} %mom.5) | copy-start | bytes 3538948
  2.7 1.0 %copy-start.2 = (f32[1,6,128,128]{3,2,1,0:T(8,128)S(1)}, f32[1,6,128,128]{3,2,1,0:T(8,128)}, u32[]{:S(2)}) copy-start(f32[1,6,128,128]{3,2,1,0:T(8,128)} %dens.5) | copy-start | bytes 1179652
  3.7 1.0 %copy-start.4 = (f32[1,6,128,128]{3,2,1,0:T(8,128)S(1)}, f32[1,6,128,128]{3,2,1,0:T(8,128)}, u32[]{:S(2)}) copy-start(f32[1,6,128,128]{3,2,1,0:T(8,128)} %en.5) | copy-start | bytes 1179652
  4.7 0.9 %copy-start.7 = (f32[1,4,128,128]{3,2,1,0:T(8,128)S(1)}, f32[1,4,128,128]{3,2,1,0:T(8,128)}, u32[]{:S(2)}) copy-start(f32[1,4,128,128]{3,2,1,0:T(8,128)} %met.5) | copy-start | bytes 786436
  5.6 0.8 %copy-start.10 = (f32[1,128,128]{2,1,0:T(8,128)S(1)}, f32[1,128,128]{2,1,0:T(8,128)}, u32[]{:S(2)}) copy-start(f32[1,128,128]{2,1,0:T(8,128)} %vol.5) | copy-start | bytes 196612
  6.4 0.7 copy-start.17
  7.1 10.5 %copy-start.19 = (s32[16,2]{0,1:T(2,128)S(1)}, s32[16,2]{0,1:T(2,128)}, u32[]{:S(2)}) copy-start(s32[16,2]{0,1:T(2,128)} %param.15) | copy-start | bytes 388
  7.1 10.6 %copy-start.20 = (s32[16,2]{0,1:T(2,128)S(1)}, s32[16,2]{0,1:T(2,128)}, u32[]{:S(2)}) copy-start(s32[16,2]{0,1:T(2,128)} %param.16) | copy-start | bytes 388
  7.1 21.2 %copy-start.18 = (s32[16]{0:T(128)S(1)}, s32[16]{0:T(128)}, u32[]{:S(2)}) copy-start(s32[16]{0:T(128)} %placed.5) | copy-start | bytes 196
  9.7 0.7 copy-start.15
  10.3 27.2 %copy-start.1 = (f32[1,3,6,128,128]{4,3,2,1,0:T(8,128)S(1)}, f32[1,3,6,128,128]{4,3,2,1,0:T(8,128)}, u32[]{:S(2)}) copy-start(f32[1,3,6,128,128]{4,3,2,1,0:T(8,128)} %mom.5) | copy-start | bytes 3538948
  10.3 27.2 %copy-start.3 = (f32[1,6,128,128]{3,2,1,0:T(8,128)S(1)}, f32[1,6,128,128]{3,2,1,0:T(8,128)}, u32[]{:S(2)}) copy-start(f32[1,6,128,128]{3,2,1,0:T(8,128)} %dens.5) | copy-start | bytes 1179652
  10.3 18.0 %all-to-all-start = ((f32[32,16,128]{2,1,0:T(8,128)}), f32[32,16,128]{2,1,0:T(8,128)S(1)}, u32[]{:S(2)}, u32[]{:S(2)}) async-start(f32[32,16,128]{2,1,0:T(8,128)} %bitcast), calls=%async_computation | async-start | bytes 524288 | tf_op jit(solution)/shard_map/all_to_all | solution.py:567
  32.5 14.8 %all-to-all-start.1 = ((f32[32,16,128]{2,1,0:T(8,128)}), f32[32,16,128]{2,1,0:T(8,128)}, u32[]{:S(2)}, u32[]{:S(2)}) async-start(f32[32,16,128]{2,1,0:T(8,128)} %bitcast.2), calls=%async_computation.1 | async-start | bytes 524288 | tf_op jit(solution)/shard_map/all_to_all | solution.py:567
  35.9 10.8 %collective-permute-start = (f32[5,28,128]{2,1,0:T(8,128)}, f32[5,28,128]{2,1,0:T(8,128)S(1)}, u32[]{:S(2)}, u32[]{:S(2)}) collective-permute-start(f32[5,28,128]{2,1,0:T(8,128)} %get-tuple-element.7), channel_id=1, source_target_pairs={{0,1},{1,0},{2,3},{3,2},{4,5},{5,4},{6,7},{7,6},{8,9},{9,8},{10,11... | collective-permute-start | bytes 215048 | tf_op jit(solution)/shard_map/ppermute | solution.py:571
  37.5 1.0 %copy-start.5 = (f32[1,6,128,128]{3,2,1,0:T(8,128)S(1)}, f32[1,6,128,128]{3,2,1,0:T(8,128)}, u32[]{:S(2)}) copy-start(f32[1,6,128,128]{3,2,1,0:T(8,128)} %en.5) | copy-start | bytes 1179652
  38.5 0.9 %copy-start.8 = (f32[1,4,128,128]{3,2,1,0:T(8,128)S(1)}, f32[1,4,128,128]{3,2,1,0:T(8,128)}, u32[]{:S(2)}) copy-start(f32[1,4,128,128]{3,2,1,0:T(8,128)} %met.5) | copy-start | bytes 786436
  39.4 0.8 %copy-start.11 = (f32[1,128,128]{2,1,0:T(8,128)S(1)}, f32[1,128,128]{2,1,0:T(8,128)}, u32[]{:S(2)}) copy-start(f32[1,128,128]{2,1,0:T(8,128)} %vol.5) | copy-start | bytes 196612
  46.7 0.6 copy-start.13
  47.4 1.0 %copy-start.6 = (f32[1,6,128,128]{3,2,1,0:T(8,128)S(1)}, f32[1,6,128,128]{3,2,1,0:T(8,128)}, u32[]{:S(2)}) copy-start(f32[1,6,128,128]{3,2,1,0:T(8,128)} %en.5) | copy-start | bytes 1179652
  48.3 0.9 %copy-start.9 = (f32[1,4,128,128]{3,2,1,0:T(8,128)S(1)}, f32[1,4,128,128]{3,2,1,0:T(8,128)}, u32[]{:S(2)}) copy-start(f32[1,4,128,128]{3,2,1,0:T(8,128)} %met.5) | copy-start | bytes 786436
  49.3 0.8 %copy-start.12 = (f32[1,128,128]{2,1,0:T(8,128)S(1)}, f32[1,128,128]{2,1,0:T(8,128)}, u32[]{:S(2)}) copy-start(f32[1,128,128]{2,1,0:T(8,128)} %vol.5) | copy-start | bytes 196612
  50.1 0.9 %copy-start.14 = (f32[5,28,128]{2,1,0:T(8,128)S(1)}, f32[5,28,128]{2,1,0:T(8,128)}, u32[]{:S(2)}) copy-start(f32[5,28,128]{2,1,0:T(8,128)} %copy-done.13) | copy-start | bytes 215044
  51.0 0.9 %copy-start.16 = (f32[5,64,128]{2,1,0:T(8,128)S(1)}, f32[5,64,128]{2,1,0:T(8,128)}, u32[]{:S(2)}) copy-start(f32[5,64,128]{2,1,0:T(8,128)} %copy-done.15) | copy-start | bytes 491524
where the time goes:
time: 68 us; the launch traced here: 67.3 us
  Pallas kernels  28.5 us (42%)
  local copies, waits for them, and re-layouts  15.3 us (22%)
  starting transfers between devices  12.2 us (18%)
  waiting for transfers between devices  10.5 us (15%)
  between operations  0.7 us (1%)
    pallas_call x1, Pallas kernels, local(): pl.pallas_call(functools.partial(last_kernel, halves), out_shape=[jax.Sha...  15.3 us
    unnamed x45, local copies, waits for them, and re-layouts  15.3 us
    all_to_all x2, starting transfers between devices, swap(): x = lax.all_to_all(x, ('blk', 'ij'), 0, 0, tiled=True)  10.6 us
    all_to_all x2, waiting for transfers between devices, swap(): x = lax.all_to_all(x, ('blk', 'ij'), 0, 0, tiled=True)  10.5 us
    pallas_call x1, Pallas kernels, local(): pl.pallas_call(first_kernel, out_shape=jax.ShapeDtypeStruct((CH, planes,...  6.41 us
    pallas_call x1, Pallas kernels, local(): pl.pallas_call(functools.partial(relay_kernel, halves, rows), out_shape=p...  4.22 us
    pallas_call x1, Pallas kernels, local(): pl.pallas_call(functools.partial(cut_kernel, halves), out_shape=[piece, j...  2.55 us
    ppermute x1, starting transfers between devices, local(): below = above = lax.ppermute(halo[0], 'ij', [(0, 1), (1, 0)])  1.63 us
  transfers between devices with their start and end apart: 3, of which 1 were waited for; matrix products, arithmetic and copies ran while one was open for 0% of the time, Pallas kernels for 10%

commit v1 on v0

v1 whole, which is shorter than its diff:
```python
import functools

import jax
import jax.numpy as jnp
from jax import lax
from jax.experimental import pallas as pl
from jax.experimental.pallas import tpu as pltpu
from jax.sharding import PartitionSpec as P

pressure_factor = 0.4
viscosity = 0.05
time_step = 0.03
unit = time_step / 12.0

LANES = 128
PAD = 8
DEPTH = 4
CH = 5
SENT = 2 * CH
PASSED = 2 * CH + 1
FIRST = 4


def turn(x, shift, axis):
    shift = shift % x.shape[axis]
    return x if shift == 0 else pltpu.roll(x, shift, axis)


def lanes_of(shape):
    return lax.broadcasted_iota(jnp.int32, shape, len(shape) - 1)


def rows_of(shape):
    return lax.broadcasted_iota(jnp.int32, shape, len(shape) - 2)


def plane_at(refs, c, k, rows):
    dens, mom, en, met, vol = refs
    if k == dens.shape[1]:
        return met[0, c, rows] if c < 4 else vol[0, rows]
    if c == 0:
        return dens[0, k, rows]
    if c == 4:
        return en[0, k, rows]
    return mom[0, c - 1, k, rows]


def point(f):
    rho, m1, m2, m3, e = f
    r = 1.0 / rho
    u1, u2, u3 = m1 * r, m2 * r, m3 * r
    kin = 0.5 * (m1 * u1 + m2 * u2 + m3 * u3)
    p = pressure_factor * (e - kin)
    return (u1, u2, u3, (kin + 2.0 * p) * r), p, e + p


def metric_terms(m):
    ax, ay, bx, by, v = m
    kv = viscosity * unit
    rw = kv * (ax * ax + ay * ay)
    cw = kv * (bx * bx + by * by)
    return v * ax, v * ay, v * bx, v * by, -unit / v, rw, cw, 30.0 * (rw + cw + kv)


def flux(f, w, p, h, gx, gy):
    rho, m1, m2, m3, _ = f
    u = gx * w[0] + gy * w[1]
    return (rho * u, m1 * u + gx * p, m2 * u + gy * p, m3 * u, h * u)


def flux_planes(f, w, p, h):
    u3 = w[2]
    return (f[3], f[1] * u3, f[2] * u3, f[3] * u3 + p, h * u3)


def slope(x, at):
    return 8.0 * (at(x, 1) - at(x, -1)) - (at(x, 2) - at(x, -2))


def curve(x, at):
    return 16.0 * (at(x, 1) + at(x, -1)) - (at(x, 2) + at(x, -2))


def along(axis):
    return lambda x, o: turn(x, -o, axis)


def plane_shift(x, o):
    o = o % x.shape[0]
    return jnp.concatenate([x[o:], x[:o]], axis=0)


def tile_rate(f, m, at_i, at_j):
    vax, vay, vbx, vby, niv, rw, cw, tw = metric_terms(m)
    kv = viscosity * unit
    w, p, h = point(f)
    fi = flux(f, w, p, h, vax, vay)
    fj = flux(f, w, p, h, vbx, vby)
    fk = flux_planes(f, w, p, h)
    out = []
    for c in range(CH):
        val = niv * (slope(fi[c], at_i) + slope(fj[c], at_j)) - unit * slope(fk[c], plane_shift)
        if c > 0:
            x = w[c - 1]
            val = val + (
                rw * curve(x, at_i) + cw * curve(x, at_j) + kv * curve(x, plane_shift) - tw * x
            )
        out.append(val)
    return out, fj, w, niv, cw


def pack_columns(x, k, low_from, high_from, packed):
    lane = lanes_of(x.shape)
    if (high_from - low_from) % LANES == 4:
        return jnp.where(lane // 8 == k, turn(x, 8 * k - low_from, 1), packed)
    packed = jnp.where(lane // 4 == 2 * k, turn(x, 8 * k - low_from, 1), packed)
    return jnp.where(lane // 4 == 2 * k + 1, turn(x, 8 * k + 4 - high_from, 1), packed)


def across(x):
    if x.shape[0] < LANES:
        x = jnp.concatenate([x, jnp.zeros((LANES - x.shape[0], LANES), jnp.float32)], axis=0)
    return x.T


def cut_kernel(halves, dens, mom, en, met, vol, placed, face, orient, send, own, *rest):
    edges, (scratch, *held, sems) = rest[:-7], rest[-7:]
    planes, rows = dens.shape[1], dens.shape[2]
    copies = [
        pltpu.make_async_copy(src, dst, sems.at[n])
        for n, (src, dst) in enumerate(zip((dens, mom, en, met, vol), held))
    ]
    for n in (3, 4, 0, 1, 2):
        copies[n].start()
    block = placed[lax.axis_index("blk")]
    half = lax.axis_index("ij")
    row = rows_of((64, LANES))
    high_side = row % 8 < 4
    mirror = jnp.where(
        rows_of((LANES, LANES)) + lanes_of((LANES, LANES)) == rows - 1, 1.0, 0.0
    )
    flip = [jnp.where(orient[block, f] == 1, -1.0, 1.0) for f in range(2)]
    same = [jnp.where(face[block, f] == f, -1.0, 1.0) for f in range(2)]
    rising = [face[block, f] == 1 for f in range(2)]
    turned = jnp.where(high_side, flip[1], flip[0])
    facing = jnp.where(high_side, same[1], same[0])
    for n in (3, 4):
        copies[n].wait()
    for c in range(CH):
        if c == 0:
            copies[0].wait()
        elif c == 1:
            copies[1].wait()
        elif c == 4:
            copies[2].wait()
        packed = jnp.zeros((rows, LANES), jnp.float32)
        for k in range(planes + 1):
            x = plane_at(held, c, k, slice(None))
            packed = pack_columns(x, k, LANES - 4, 0, packed)
        strip = across(packed)[0:64]
        own[c] = strip
        back = jnp.dot(
            strip,
            mirror,
            precision=lax.Precision.HIGHEST,
            preferred_element_type=jnp.float32,
        )
        moved = jnp.where(turned < 0.0, back, strip)
        if c < 4:
            moved = jnp.where(row >= planes * 8, moved * (turned if c < 2 else facing), moved)
        scratch[c * 64 : c * 64 + 64] = moved
    for k in range(planes + 1):
        for e in range(DEPTH):
            at = (FIRST + k * DEPTH + e) * SENT
            low = k * 8 + 4 + jnp.where(rising[0], e, 3 - e)
            high = k * 8 + jnp.where(rising[1], 3 - e, e)
            send[at : at + CH] = scratch[pl.ds(low, CH, stride=64)]
            send[at + CH : at + SENT] = scratch[pl.ds(high, CH, stride=64)]
    for c in range(CH):
        for k in range(planes + 1):
            low = plane_at(held, c, k, slice(0, 4))
            high = plane_at(held, c, k, slice(rows - 4, rows))
            if len(edges) == 1:
                edges[0][c, k * 4 : k * 4 + 4] = jnp.where(half == 0, high, low)
            else:
                edges[0][c, k * 4 : k * 4 + 4] = low
                edges[1][c, k * 4 : k * 4 + 4] = high


def relay_kernel(
    halves, rows, planes, placed, neighbour, face, orient, got, part,
    send, below, above, signs, where_is,
):
    del part
    blocks = placed.shape[0]
    devices = blocks * halves
    me = lax.axis_index("blk") * halves + lax.axis_index("ij")
    is_field = (me >= FIRST) & (me < FIRST + DEPTH * planes)

    def note(slot, _):
        where_is[placed[slot]] = slot
        return 0

    lax.fori_loop(0, blocks, note, 0, unroll=True)

    def pass_on(slot, _):
        block = placed[slot]
        for f in range(2):
            partner = where_is[neighbour[block, f]]
            side, turned = face[block, f], orient[block, f]
            sign = jnp.where(turned == 1, -1.0, 1.0)

            def piece(h):
                h = jnp.where(turned == 1, halves - 1 - h, h)
                return got[pl.ds((partner * halves + h) * SENT + side * CH, CH)]

            pieces = [piece(h) for h in range(halves)]
            for half in range(halves):
                at = slot * halves + half
                send[pl.ds(at * PASSED + f * CH, CH)] = pieces[half]
                below[pl.ds((f * devices + at) * 8, CH)] = pieces[max(half - 1, 0)]
                above[pl.ds((f * devices + at) * 8, CH)] = pieces[min(half + 1, halves - 1)]
                signs[pl.ds(f * devices + at, 1)] = jnp.full((1, LANES), sign, jnp.float32)
        return 0

    lax.fori_loop(0, blocks, pass_on, 0, unroll=4)
    count = 2 * devices
    lane = lanes_of((count, LANES))
    half = rows_of((count, LANES)) % halves
    sign = signs[...]
    ends = jnp.zeros((count, LANES), jnp.float32)
    for c in range(CH):
        low, high = below[pl.ds(c, count, stride=8)], above[pl.ds(c, count, stride=8)]
        at = 4 * c
        low_wall = jnp.where(lane == at, turn(low, at - 1, 1), turn(low, at + 1, 1))
        high_wall = jnp.where(
            lane == at + 2, turn(high, at + 3 - rows, 1), turn(high, at + 5 - rows, 1)
        )
        if 1 <= c <= 3:
            low_wall = jnp.where(is_field, -sign * low_wall, low_wall)
            high_wall = jnp.where(is_field, sign * high_wall, high_wall)
        low = jnp.where(half == 0, low_wall, turn(low, at + 2 - rows, 1))
        high = jnp.where(half == halves - 1, high_wall, turn(high, at + 2, 1))
        ends = jnp.where(lane // 2 == 2 * c, low, jnp.where(lane // 2 == 2 * c + 1, high, ends))
    send[pl.ds(2 * CH, devices, stride=PASSED)] = ends[0:devices] + turn(
        ends[devices:], 4 * CH, 1
    )


def flux_chunk(get, mets, fi, w, r, rest=None):
    rows = pl.ds(r, 8)
    vax, vay, vbx, vby, niv, rw, cw, tw = [mets[j, rows] for j in range(8)]
    at_j = along(1)
    for k in range(fi.shape[1]):
        f = [get(c, k, r) for c in range(CH)]
        wk, p, h = point(f)
        for c, x in enumerate(flux(f, wk, p, h, vax, vay)):
            fi[c, k, rows] = x
        for c in range(4):
            w[c, k, rows] = wk[c]
        if rest is None:
            continue
        fk, acc = rest
        fj = flux(f, wk, p, h, vbx, vby)
        for c in range(CH):
            val = niv * slope(fj[c], at_j)
            if c > 0:
                val = val + (cw * curve(wk[c - 1], at_j) - tw * wk[c - 1])
            acc[c, k, rows] = val
        for c, x in enumerate(flux_planes(f, wk, p, h)):
            fk[c, k, rows] = x


def sum_chunk(mets, fi, w, fk, acc, r, emit):
    planes = fi.shape[1]
    kv = viscosity * unit
    rows = pl.ds(r, 8)
    niv, rw = mets[4, rows], mets[5, rows]
    for c in range(CH):
        t = [fk[c, k, rows] for k in range(planes)]
        x = [w[c - 1, k, rows] for k in range(planes)] if c > 0 else None
        for k in range(planes):

            def near(v, o):
                return v[(k + o) % planes]

            def at_i(v, o):
                return v[pl.ds(r + o, 8)]

            val = acc[c, k, rows] + niv * slope(fi.at[c, k], at_i) - unit * slope(t, near)
            if c > 0:
                val = val + (rw * curve(w.at[c - 1, k], at_i) + kv * curve(x, near))
            emit(c, k, r, val)


def chunks(count, body):
    def step(n, _):
        body(pl.multiple_of(n * 8, 8))
        return 0

    lax.fori_loop(0, count, step, 0)


def first_kernel(dens, mom, en, met, vol, part, mets, fi, w, fk, acc):
    refs = (dens, mom, en, met, vol)
    planes, rows = dens.shape[1], dens.shape[2]

    def terms(r):
        m = [plane_at(refs, c, planes, pl.ds(r, 8)) for c in range(CH)]
        for j, x in enumerate(metric_terms(m)):
            mets[j, pl.ds(r + PAD, 8)] = x

    def get(c, k, r):
        return plane_at(refs, c, k, pl.ds(r - PAD, 8))

    def fluxes(r):
        terms(r)
        flux_chunk(get, mets, fi, w, r + PAD, (fk, acc))

    def emit(c, k, r, val):
        part[c, k, pl.ds(r - PAD, 8)] = get(c, k, r) + val

    def sums(r):
        sum_chunk(mets, fi, w, fk, acc, r + PAD, emit)

    empty = jnp.zeros((PAD, LANES), jnp.float32)
    for k in range(planes):
        for c in range(CH):
            fi[c, k, 0:PAD] = empty
            fi[c, k, rows + PAD :] = empty
        for c in range(4):
            w[c, k, 0:PAD] = empty
            w[c, k, rows + PAD :] = empty
    chunks(rows // 8, fluxes)
    chunks(rows // 8, sums)


def pack_ends(tall, count):
    row8, lane8 = rows_of((8, LANES)), lanes_of((8, LANES))
    stacked = []
    for c in range(CH):
        packed = jnp.zeros((8, LANES), jnp.float32)
        for k in range(count):
            x = jnp.where(row8 < 4, tall[0, c, k], tall[1, c, k])
            packed = pack_columns(x, k, LANES - 4, 0, packed)
        stacked.append(packed)
    ends = across(jnp.concatenate(stacked, axis=0))
    out = []
    for c in range(CH):
        x = jnp.zeros((8, LANES), jnp.float32)
        for k in range(count):
            moved = turn(ends[k * 8 : k * 8 + 8], 4 * k - (8 * c + 2), 1)
            x = jnp.where(lane8 // 4 == k, moved, x)
        out.append(x)
    return out


def second_kernel(
    halves, dens, mom, en, met, vol, below, above, part,
    out, ends_base, ends_sec, inner,
    tall, sec, mets, fi, w, fk, acc,
):
    refs = (dens, mom, en, met, vol)
    planes, rows = dens.shape[1], dens.shape[2]
    every = planes + 1
    half = lax.axis_index("ij")
    low_wall, high_wall = half == 0, half == halves - 1
    low_flag, high_flag = jnp.where(low_wall, 1, 0), jnp.where(high_wall, 1, 0)

    for c in range(CH):
        for k in range(every):
            tall[0, c, k, 4:8] = plane_at(refs, c, k, slice(0, 4))
            tall[1, c, k, 0:4] = plane_at(refs, c, k, slice(rows - 4, rows))

    @pl.when(low_wall)
    def _():
        for c in range(CH):
            for k in range(every):
                sign = -1.0 if 1 <= c <= 3 and k < planes else 1.0
                for d in range(4):
                    tall[0, c, k, 3 - d : 4 - d] = sign * plane_at(refs, c, k, slice(d, d + 1))

    @pl.when(jnp.logical_not(low_wall))
    def _():
        for c in range(CH):
            for k in range(every):
                tall[0, c, k, 0:4] = below[c, k * 4 : k * 4 + 4]

    @pl.when(high_wall)
    def _():
        for c in range(CH):
            for k in range(every):
                for d in range(4):
                    tall[1, c, k, 4 + d : 5 + d] = plane_at(
                        refs, c, k, slice(rows - 1 - d, rows - d)
                    )

    @pl.when(jnp.logical_not(high_wall))
    def _():
        for c in range(CH):
            for k in range(every):
                tall[1, c, k, 4:8] = above[c, k * 4 : k * 4 + 4]

    for c, x in enumerate(pack_ends(tall, every)):
        ends_base[c] = x

    def terms(r):
        m = [plane_at(refs, c, planes, pl.ds(r, 8)) for c in range(CH)]
        for j, x in enumerate(metric_terms(m)):
            mets[j, pl.ds(r + PAD, 8)] = x

    for end, at in ((0, PAD - 4), (1, PAD + rows - 4)):
        m = [tall[end, c, planes] for c in range(CH)]
        for j, x in enumerate(metric_terms(m)):
            mets[j, at : at + 8] = x

    def finish(r):
        for c in range(CH):
            for k in range(planes):
                sec[c, k, pl.ds(r + PAD, 8)] = part[c, k, pl.ds(r, 8)]

    chunks(rows // 8, finish)
    sub = rows_of((planes, 8, LANES))
    for end in range(2):
        start = -4 if end == 0 else rows - 4
        fields = [tall[end, c, 0:planes] for c in range(CH)]
        m = [tall[end, c, planes] for c in range(CH)]
        rate = tile_rate(fields, m, along(1), along(2))[0]
        for c in range(CH):
            x = fields[c] + rate[c]
            tall[end, c, 0:planes] = x
            if end == 0:
                sign = -1.0 if 1 <= c <= 3 else 1.0
                wall = sign * jnp.where(sub == 2, turn(x, -3, 1), turn(x, -1, 1))
                x = jnp.where((sub < 4) & (low_flag == 1), wall, x)
            else:
                wall = jnp.where(sub == 4, turn(x, 1, 1), turn(x, 3, 1))
                x = jnp.where((sub >= 4) & (high_flag == 1), wall, x)
            for k in range(planes):
                sec[c, k, PAD + start + 2 : PAD + start + 6] = x[k, 2:6]
    for c, x in enumerate(pack_ends(tall, planes)):
        ends_sec[c] = x
    for c in range(CH):
        packed = jnp.zeros((rows, LANES), jnp.float32)
        for k in range(every):
            x = sec[c, k, PAD : PAD + rows] if k < planes else plane_at(refs, c, k, slice(None))
            packed = pack_columns(x, k, LANES - 6, 2, packed)
        inner[c] = across(packed)[0:64]

    def get(c, k, r):
        return sec[c, k, pl.ds(r, 8)]

    def fluxes(r):
        terms(r)
        flux_chunk(get, mets, fi, w, r + PAD, (fk, acc))

    def emit(c, k, r, val):
        at = pl.ds(r - PAD, 8)
        out[c, k, at] = 0.5 * (plane_at(refs, c, k, at) + (get(c, k, r) + val))

    def sums(r):
        sum_chunk(mets, fi, w, fk, acc, r + PAD, emit)

    flux_chunk(get, mets, fi, w, 0)
    flux_chunk(get, mets, fi, w, rows + PAD)
    chunks(rows // 8, fluxes)
    chunks(rows // 8, sums)


def beyond(packed, f, k, rows):
    base = 4 * (7 * f + k)
    low = turn(packed, LANES - 2 - base, 1)
    top = rows % LANES
    high = low if top == 0 else turn(packed, top - 2 - base, 1)
    lane = lanes_of(packed.shape)

    def at(x, o):
        if o < 0:
            x = jnp.where(lane >= LANES + o, low, x)
        else:
            x = jnp.where((lane >= top) & (lane < top + o), high, x)
        return turn(x, -o, 1)

    return at


def strip_stage(rows, planes, fields, mets, ends, ends_gx, ends_gy, hold, done):
    kv = viscosity * unit
    fk, ws, acc = hold
    at_j = along(0)
    wx, px, hx = point(ends)
    fx = flux(ends, wx, px, hx, ends_gx, ends_gy)
    for f in range(2):
        vax, vay, vbx, vby, niv, rw, cw, tw = mets[f]
        for k in range(planes):
            x = [fields(c, f, k) for c in range(CH)]
            w, p, h = point(x)
            fi, fj = flux(x, w, p, h, vax, vay), flux(x, w, p, h, vbx, vby)
            for c in range(CH):
                val = niv * (slope(fi[c], beyond(fx[c], f, k, rows)) + slope(fj[c], at_j))
                if c > 0:
                    v = w[c - 1]
                    ext = beyond(wx[c - 1], f, k, rows)
                    val = val + (rw * curve(v, ext) + cw * curve(v, at_j) - tw * v)
                    ws[c - 1, f, k] = v
                acc[c, f, k] = x[c] + val
            for c, v in enumerate(flux_planes(x, w, p, h)):
                fk[c, f, k] = v
        for c in range(CH):
            t = [fk[c, f, k] for k in range(planes)]
            v = [ws[c - 1, f, k] for k in range(planes)] if c > 0 else None
            for k in range(planes):

                def near(y, o):
                    return y[(k + o) % planes]

                val = acc[c, f, k] - unit * slope(t, near)
                if c > 0:
                    val = val + kv * curve(v, near)
                done(c, f, k, val)


def last_kernel(
    halves, rows, planes, own, ends_base, ends_sec, inner, got, out,
    next_dens, next_mom, next_en,
    base, sec, fk, ws, acc, turned, back, full, sems,
):
    half = lax.axis_index("ij")
    low_wall, high_wall = half == 0, half == halves - 1
    sub, lane = rows_of((8, LANES)), lanes_of((8, LANES))

    def ghost(row, f, k):
        if f == 1:
            return got[pl.ds(DEPTH * k * PASSED + row, 8, stride=PASSED)]
        if k < planes:
            return got[pl.ds((FIRST + DEPTH * k) * PASSED + row, 8, stride=PASSED)]
        return turn(got[pl.ds(DEPTH * k * PASSED + row, 8, stride=PASSED)], 4, 0)

    def mix(f, mine, others):
        return jnp.where((sub < 4) == (f == 1), mine, others)

    for c in range(CH):
        for k in range(planes + 1):
            mine = own[c, k * 8 : k * 8 + 8]
            for f in range(2):
                base[c, f, k] = mix(f, mine, ghost(f * CH + c, f, k))
    mets = [metric_terms([base[c, f, planes] for c in range(CH)]) for f in range(2)]

    arrived = [[ghost(2 * CH, f, k) for k in range(planes + 1)] for f in range(2)]
    twice, ends = [], []
    for c in range(CH):
        mine = jnp.where(lane < 28, ends_base[c], turn(ends_base[c], 28, 1))
        others = jnp.zeros((8, LANES), jnp.float32)
        for f in range(2):
            for k in range(planes + 1):
                to = 28 * f + 4 * k
                moved = turn(arrived[f][k], to - 4 * CH * f - 4 * c, 1)
                others = jnp.where(lane // 4 == to // 4, moved, others)
        twice.append(mine)
        ends.append(jnp.where((lane < 28) == (sub >= 4), mine, others))

    def spread(x):
        y = x
        for k in range(planes):
            y = jnp.where((lane % 28) // 4 == k, turn(x, 4 * (k - planes), 1), y)
        return y

    vax, vay, vbx, vby, niv, rw, cw, tw = [spread(x) for x in metric_terms(ends)]
    wrapped = [spread(x) for x in metric_terms(twice)[2:4]]

    def keep(c, f, k, val):
        sec[c, f, k] = val

    strip_stage(
        rows, planes, lambda c, f, k: base[c, f, k], mets, ends, vax, vay, (fk, ws, acc), keep
    )

    for c in range(CH):
        for k in range(planes + 1):
            mine = inner[c, k * 8 : k * 8 + 8]
            for f in range(2):
                x = sec[c, f, k] if k < planes else base[c, f, k]
                sec[c, f, k] = mix(f, mine, turn(x, 2 if f == 1 else -2, 0))

    def shifted(x):
        return jnp.where(lane < 28, turn(x, -2, 0), turn(x, 2, 0))

    w1, p1, h1 = point(ends)
    w0, p0, h0 = point(twice)
    new, old = flux(ends, w1, p1, h1, vbx, vby), flux(twice, w0, p0, h0, *wrapped)
    at_j = along(0)
    touched = jnp.where(lane < 28, (sub - 4) // 2, (sub - 2) // 2) == 0
    second = []
    for c in range(CH):
        add = niv * slope(new[c] - old[c], at_j)
        if c > 0:
            add = add + cw * curve(w1[c - 1] - w0[c - 1], at_j)
        x = jnp.where(lane < 28, ends_sec[c], turn(ends_sec[c], 28, 1))
        x = shifted(x + jnp.where(touched, add, 0.0))
        for f in range(2):
            for k in range(planes):
                to = 28 * f + 4 * k
                first = jnp.where(low_wall, to, to + 2)
                one = pltpu.roll(
                    sec[c, f, k], jnp.where(low_wall, (to - 1) % LANES, (to + 3 - rows) % LANES), 1
                )
                two = pltpu.roll(
                    sec[c, f, k], jnp.where(low_wall, (to + 1) % LANES, (to + 5 - rows) % LANES), 1
                )
                if 1 <= c <= 3:
                    sign = jnp.where(low_wall, -1.0, 1.0)
                    one, two = sign * one, sign * two
                at = jnp.where(low_wall | high_wall, lane - first, -1)
                x = jnp.where(at == 0, one, jnp.where(at == 1, two, x))
        second.append(x)
    mets = [metric_terms([sec[c, f, planes] for c in range(CH)]) for f in range(2)]
    strip_stage(
        rows, planes, lambda c, f, k: sec[c, f, k], mets, second, shifted(vax), shifted(vay),
        (fk, ws, acc), keep,
    )

    per = LANES // 8
    for c in range(CH):
        for k in range(planes):
            x = jnp.where(sub < 4, turn(sec[c, 1, k], -2, 0), turn(sec[c, 0, k], 2, 0))
            at = (c * planes + k) * 8
            turned[at : at + 8] = 0.5 * (own[c, k * 8 : k * 8 + 8] + x)
    blocks = turned.shape[0] // LANES
    for n in range(blocks):
        back[n] = turned[n * LANES : (n + 1) * LANES].T
    copies = []
    for c in range(CH):

        def merge(r, c=c):
            at = pl.ds(r, 8)
            for k in range(planes):
                index = c * planes + k
                moved = turn(back[index // per, at], LANES - 4 - 8 * (index % per), 1)
                inside = (lane >= 4) & (lane < LANES - 4)
                full[c, k, at] = jnp.where(inside, out[c, k, at], moved)

        chunks(rows // 8, merge)
        dst = next_dens.at[0] if c == 0 else next_en.at[0] if c == 4 else next_mom.at[0, c - 1]
        copies.append(pltpu.make_async_copy(full.at[c], dst, sems.at[c]))
        copies[-1].start()
    for copy in copies:
        copy.wait()


def local(mesh_shape, density, momentum, energy, metrics, volume, placed, neighbour, face, orient):
    halves = mesh_shape["ij"]
    devices = mesh_shape["blk"] * halves
    planes, rows = density.shape[1], density.shape[2]
    every = planes + 1
    fields = (density, momentum, energy, metrics, volume)
    f32 = jnp.float32
    vmem = pl.BlockSpec(memory_space=pltpu.VMEM)
    smem = pl.BlockSpec(memory_space=pltpu.SMEM)
    hbm = pl.BlockSpec(memory_space=pltpu.HBM)

    def call(kernel, name, outs, ins, out_specs, scratch, mib, cost=None):
        return pl.pallas_call(
            kernel,
            out_shape=outs,
            in_specs=ins,
            out_specs=out_specs,
            scratch_shapes=scratch,
            compiler_params=pltpu.CompilerParams(vmem_limit_bytes=mib * 1024 * 1024),
            cost_estimate=cost,
            name=name,
        )

    def shape(*dims):
        return jax.ShapeDtypeStruct(dims, f32)

    edge = shape(CH, 4 * every, LANES)
    edges = 1 if halves == 2 else 2
    sent, own, *halo = call(
        functools.partial(cut_kernel, halves),
        "cut",
        [shape(devices * SENT, LANES), shape(CH, 64, LANES)] + [edge] * edges,
        [hbm] * 5 + [smem] * 3,
        [vmem] * (2 + edges),
        [pltpu.VMEM((CH * 64, LANES), f32)]
        + [pltpu.VMEM(x.shape, f32) for x in fields]
        + [pltpu.SemaphoreType.DMA((5,))],
        16,
    )(*fields, placed, face, orient)

    def swap(x):
        x = x.reshape(devices, x.shape[0] // devices, 1, LANES)
        x = lax.all_to_all(x, ("blk", "ij"), 0, 0, tiled=True)
        return x.reshape(x.shape[0] * x.shape[1], LANES)

    got = swap(sent)
    if edges == 1:
        below = above = lax.ppermute(halo[0], "ij", [(0, 1), (1, 0)])
    else:
        below = lax.ppermute(halo[1], "ij", [(i, i + 1) for i in range(halves - 1)])
        above = lax.ppermute(halo[0], "ij", [(i + 1, i) for i in range(halves - 1)])

    tall = rows + 2 * PAD
    block = shape(CH, planes, rows, LANES)
    stage = [
        pltpu.VMEM((8, tall, LANES), f32),
        pltpu.VMEM((CH, planes, tall, LANES), f32),
        pltpu.VMEM((4, planes, tall, LANES), f32),
        pltpu.VMEM((CH, planes, tall, LANES), f32),
        pltpu.VMEM((CH, planes, tall, LANES), f32),
    ]
    work = planes * rows * LANES
    cost = pl.CostEstimate(flops=300 * work, bytes_accessed=150 * work, transcendentals=work)
    part = call(
        first_kernel, "first_section", block, [vmem] * 5, vmem, stage, 24, cost
    )(*fields)
    relayed = call(
        functools.partial(relay_kernel, halves, rows, planes),
        "relay",
        shape(devices * PASSED, LANES),
        [smem] * 4 + [vmem, pl.BlockSpec(memory_space=pl.ANY)],
        vmem,
        [
            pltpu.VMEM((devices * 16, LANES), f32),
            pltpu.VMEM((devices * 16, LANES), f32),
            pltpu.VMEM((devices * 2, LANES), f32),
            pltpu.SMEM((placed.shape[0],), jnp.int32),
        ],
        16,
    )(placed, neighbour, face, orient, got, part)
    ghosts = swap(relayed)
    out, ends_base, ends_sec, inner = call(
        functools.partial(second_kernel, halves),
        "second_section",
        [block, shape(CH, 8, LANES), shape(CH, 8, LANES), shape(CH, 64, LANES)],
        [vmem] * 8,
        [vmem] * 4,
        [
            pltpu.VMEM((2, CH, every, 8, LANES), f32),
            pltpu.VMEM((CH, planes, tall, LANES), f32),
        ]
        + stage,
        32,
        cost,
    )(*fields, below, above, part)
    strip = pltpu.VMEM((CH, 2, every, 8, LANES), f32)
    flat = -(-CH * planes * 8 // LANES)
    return call(
        functools.partial(last_kernel, halves, rows, planes),
        "strips",
        [shape(*density.shape), shape(*momentum.shape), shape(*energy.shape)],
        [vmem] * 6,
        [hbm] * 3,
        [strip] * 5
        + [
            pltpu.VMEM((flat * LANES, LANES), f32),
            pltpu.VMEM((flat, LANES, LANES), f32),
            pltpu.VMEM((CH, planes, rows, LANES), f32),
            pltpu.SemaphoreType.DMA((CH,)),
        ],
        16,
    )(own, ends_base, ends_sec, inner, ghosts, out)


def solution(mesh):
    return jax.shard_map(
        functools.partial(local, dict(mesh.shape)),
        mesh=mesh,
        in_specs=(
            P("blk", None, "ij", None),
            P("blk", None, None, "ij", None),
            P("blk", None, "ij", None),
            P("blk", None, "ij", None),
            P("blk", "ij", None),
            P(),
            P(),
            P(),
            P(),
        ),
        out_specs=(
            P("blk", None, "ij", None),
            P("blk", None, None, "ij", None),
            P("blk", None, "ij", None),
        ),
        check_vma=False,
    )
```

time: 68 us -> 89.2 us (1.31)
  Pallas kernels: 28.5 us -> 42.7 us
  local copies, waits for them, and re-layouts: 15.3 us -> 25.4 us
  waiting for transfers between devices: 10.5 us -> 4.21 us
  starting transfers between devices: 12.2 us -> 15.1 us
    pallas_call x4 -> x5, Pallas kernels: 28.5 us -> 42.7 us  [the longest x1 21.2 us: local(): call(functools.partial(last_kernel, halves, rows, planes), 'strips', [sha...]
    all_to_all x2, waiting for transfers between devices: 10.5 us -> 0.01 us  [swap(): x = lax.all_to_all(x, ('blk', 'ij'), 0, 0, tiled=True)]
    unnamed x45 -> x59, local copies, waits for them, and re-layouts: 15.3 us -> 25.4 us
    ppermute x1, waiting for transfers between devices: 0.01 us -> 4.21 us  [local(): below = above = lax.ppermute(halo[0], 'ij', [(0, 1), (1, 0)])]
    all_to_all x2, starting transfers between devices: 10.6 us -> 13.3 us  [swap(): x = lax.all_to_all(x, ('blk', 'ij'), 0, 0, tiled=True)]
  transfers between devices with their start and end apart: 3 -> 3, of which waited for: 1 -> 1; matrix products, arithmetic and copies ran while one was open for 0% -> 2% of each run, Pallas kernels for 10% -> 18%
where the time goes in v1:
time: 89.2 us; the launch traced here: 88.2 us
  Pallas kernels  42.7 us (48%)
  local copies, waits for them, and re-layouts  25.4 us (28%)
  starting transfers between devices  15.1 us (17%)
  waiting for transfers between devices  4.21 us (5%)
    unnamed x59, local copies, waits for them, and re-layouts  25.4 us
    pallas_call x1, Pallas kernels, local(): call(functools.partial(last_kernel, halves, rows, planes), 'strips', [sha...  21.2 us
    all_to_all x2, starting transfers between devices, swap(): x = lax.all_to_all(x, ('blk', 'ij'), 0, 0, tiled=True)  13.3 us
    pallas_call x1, Pallas kernels, local(): call(functools.partial(second_kernel, halves), 'second_section', [block,...  9.68 us
    pallas_call x1, Pallas kernels, local(): call(first_kernel, 'first_section', block, [vmem] * 5, vmem, stage, 24, c...  6.41 us
    ppermute x1, waiting for transfers between devices, local(): below = above = lax.ppermute(halo[0], 'ij', [(0, 1), (1, 0)])  4.21 us
    pallas_call x1, Pallas kernels, local(): call(functools.partial(cut_kernel, halves), 'cut', [shape(devices * SENT,...  3.88 us
  transfers between devices with their start and end apart: 3, of which 1 were waited for; matrix products, arithmetic and copies ran while one was open for 2% of the time, Pallas kernels for 18%

profile of v1, /device:TPU:0, one launch (start us, length us, event | category | flops | bytes accessed | tf_op | source)
XLA Modules:
  0.0 88.2 jit_solution(3724924398537599187)
XLA Ops:
  0.6 0.8 copy.22.face
  1.4 0.8 copy.23.orient
  2.1 0.0 copy-start
  2.1 1.3 %copy-done = f32[1,3,6,128,128]{4,3,2,1,0:T(8,128)S(1)} copy-done((f32[1,3,6,128,128]{4,3,2,1,0:T(8,128)S(1)}, f32[1,3,6,128,128]{4,3,2,1,0:T(8,128)}, u32[]{:S(2)}) %copy-start) | copy-done | bytes 1179672
  3.4 0.0 copy-start.2
  3.4 1.0 %copy-done.2 = f32[1,6,128,128]{3,2,1,0:T(8,128)S(1)} copy-done((f32[1,6,128,128]{3,2,1,0:T(8,128)S(1)}, f32[1,6,128,128]{3,2,1,0:T(8,128)}, u32[]{:S(2)}) %copy-start.2) | copy-done | bytes 393240
  4.4 0.0 copy-start.4
  4.4 1.0 %copy-done.4 = f32[1,6,128,128]{3,2,1,0:T(8,128)S(1)} copy-done((f32[1,6,128,128]{3,2,1,0:T(8,128)S(1)}, f32[1,6,128,128]{3,2,1,0:T(8,128)}, u32[]{:S(2)}) %copy-start.4) | copy-done | bytes 393240
  5.4 0.9 %copy-done.7 = f32[1,4,128,128]{3,2,1,0:T(8,128)S(1)} copy-done((f32[1,4,128,128]{3,2,1,0:T(8,128)S(1)}, f32[1,4,128,128]{3,2,1,0:T(8,128)}, u32[]{:S(2)}) %copy-start.7) | copy-done | bytes 262168
  6.4 0.8 copy-done.13
  7.2 0.7 copy-done.25
  7.9 3.9 %cut.1 = (f32[320,128]{1,0:T(8,128)}, f32[5,64,128]{2,1,0:T(8,128)S(1)}, f32[5,28,128]{2,1,0:T(8,128)S(1)}) custom-call(f32[1,6,128,128]{3,2,1,0:T(8,128)S(1)} %copy-done.2, f32[1,3,6,128,128]{4,3,2,1,0:T(8,128)S(1)} %copy-done, f32[1,6,128,128]{3,2,1,0:T(8,128)S(1)} %copy-done.4, f32[1,4,128,128]{3,2,1,0:T(8,128)S(1)} %copy-done.7, ...), custom_call_target="tpu_custom_call" | custom-call | tf_op jit(solution)/shard_map/cut/pallas_call | solution.py:678
  11.7 0.0 copy-start.16
  11.8 0.7 copy-done.16
  12.4 0.6 copy-done.27
  13.1 7.4 %all-to-all-start = ((f32[32,10,1,128]{3,2,1,0:T(1,128)}), f32[32,10,1,128]{3,2,1,0:T(1,128)}, u32[]{:S(2)}, u32[]{:S(2)}) async-start(f32[32,10,1,128]{3,2,1,0:T(1,128)} %bitcast), calls=%async_computation | async-start | bytes 327680 | tf_op jit(solution)/shard_map/all_to_all | solution.py:692
  20.5 1.4 %copy.25.neighbour = s32[16,2]{1,0:T(8,128)} copy(s32[16,2]{0,1:T(2,128)} %param.15) | data formatting | bytes 256 | tf_op args[6]
  21.8 0.0 copy-done.1
  21.8 0.0 copy-done.3
  21.8 1.0 %copy-done.5 = f32[1,6,128,128]{3,2,1,0:T(8,128)S(1)} copy-done((f32[1,6,128,128]{3,2,1,0:T(8,128)S(1)}, f32[1,6,128,128]{3,2,1,0:T(8,128)}, u32[]{:S(2)}) %copy-start.5) | copy-done | bytes 393240
  22.8 0.9 %copy-done.8 = f32[1,4,128,128]{3,2,1,0:T(8,128)S(1)} copy-done((f32[1,4,128,128]{3,2,1,0:T(8,128)S(1)}, f32[1,4,128,128]{3,2,1,0:T(8,128)}, u32[]{:S(2)}) %copy-start.8) | copy-done | bytes 262168
  23.8 0.8 copy-done.14
  24.6 6.4 %first_section.1.part = f32[5,6,128,128]{3,2,1,0:T(8,128)S(1)} custom-call(f32[1,6,128,128]{3,2,1,0:T(8,128)S(1)} %copy-done.3, f32[1,3,6,128,128]{4,3,2,1,0:T(8,128)S(1)} %copy-done.1, f32[1,6,128,128]{3,2,1,0:T(8,128)S(1)} %copy-done.5, f32[1,4,128,128]{3,2,1,0:T(8,128)S(1)} %copy-done.8, f32[1,128,128]{2,1,0:T(8,128)S(1)} %copy-done.14), custom_call_target="tpu_custom_call" | custom-call | flops 29491200 | bytes 14745600 | tf_op jit(solution)/shard_map/first_section/pallas_call | solution.py:713
  31.0 0.0 all-to-all-done
  31.0 0.0 copy-start.20
  31.1 0.7 copy-done.20
  31.7 0.7 copy-done.26
  32.4 1.6 %relay.1 = f32[352,128]{1,0:T(8,128)S(1)} custom-call(s32[16]{0:T(128)S(1)} %copy-done.26, s32[16,2]{1,0:T(8,128)S(1)} %copy-done.20, s32[16,2]{1,0:T(8,128)S(1)} %copy.22.face, s32[16,2]{1,0:T(8,128)S(1)} %copy.23.orient, f32[320,128]{1,0:T(8,128)} %bitcast.1.got, f32[5,6,128,128]{3,2,1,0:T(8,128)S(1)} %first_section.1.part), custom_call_target="tpu_custom_call" | custom-call | tf_op jit(solution)/shard_map/relay/pallas_call | solution.py:716
  34.0 0.7 copy-done.12
  34.6 5.9 %all-to-all-start.1 = ((f32[32,11,1,128]{3,2,1,0:T(1,128)}), f32[32,11,1,128]{3,2,1,0:T(1,128)}, u32[]{:S(2)}, u32[]{:S(2)}) async-start(f32[32,11,1,128]{3,2,1,0:T(1,128)} %bitcast.4), calls=%async_computation.1 | async-start | bytes 360448 | tf_op jit(solution)/shard_map/all_to_all | solution.py:692
  40.5 1.8 %collective-permute-start = (f32[5,28,128]{2,1,0:T(8,128)}, f32[5,28,128]{2,1,0:T(8,128)S(1)}, u32[]{:S(2)}, u32[]{:S(2)}) collective-permute-start(f32[5,28,128]{2,1,0:T(8,128)} %copy-done.27), channel_id=1, source_target_pairs={{0,1},{1,0},{2,3},{3,2},{4,5},{5,4},{6,7},{7,6},{8,9},{9,8},{10,11... | collective-permute-start | bytes 215048 | tf_op jit(solution)/shard_map/ppermute | solution.py:697
  42.3 4.2 %collective-permute-done.below.above = f32[5,28,128]{2,1,0:T(8,128)S(1)} collective-permute-done((f32[5,28,128]{2,1,0:T(8,128)}, f32[5,28,128]{2,1,0:T(8,128)S(1)}, u32[]{:S(2)}, u32[]{:S(2)}) %collective-permute-start) | collective-permute-done | bytes 71712 | tf_op jit(solution)/shard_map/ppermute | solution.py:697
  46.5 1.0 %copy-done.6 = f32[1,6,128,128]{3,2,1,0:T(8,128)S(1)} copy-done((f32[1,6,128,128]{3,2,1,0:T(8,128)S(1)}, f32[1,6,128,128]{3,2,1,0:T(8,128)}, u32[]{:S(2)}) %copy-start.6) | copy-done | bytes 393240
  47.5 0.9 %copy-done.9 = f32[1,4,128,128]{3,2,1,0:T(8,128)S(1)} copy-done((f32[1,4,128,128]{3,2,1,0:T(8,128)S(1)}, f32[1,4,128,128]{3,2,1,0:T(8,128)}, u32[]{:S(2)}) %copy-start.9) | copy-done | bytes 262168
  48.5 0.8 copy-done.15
  49.3 9.7 %second_section.1 = (f32[5,6,128,128]{3,2,1,0:T(8,128)S(1)}, f32[5,8,128]{2,1,0:T(8,128)S(1)}, f32[5,8,128]{2,1,0:T(8,128)S(1)}, f32[5,64,128]{2,1,0:T(8,128)S(1)}) custom-call(f32[1,6,128,128]{3,2,1,0:T(8,128)S(1)} %copy-done.3, f32[1,3,6,128,128]{4,3,2,1,0:T(8,128)S(1)} %copy-done.1, f32[1,6,128,128]{3,2,1,0:T(8,128)S(1)} %copy-done.6, ...), custom_call_target="tpu_custom_call" | custom-call | flops 29491200 | bytes 14745600 | tf_op jit(solution)/shard_map/second_section/pallas_call | solution.py:731
  59.0 0.0 copy-start.10
  59.0 1.3 %copy-done.10 = f32[5,6,128,128]{3,2,1,0:T(8,128)} copy-done((f32[5,6,128,128]{3,2,1,0:T(8,128)}, f32[5,6,128,128]{3,2,1,0:T(8,128)S(1)}, u32[]{:S(2)}) %copy-start.10) | copy-done | bytes 1966104
  60.3 0.7 copy-done.18
  61.0 0.6 copy-done.21
  61.6 0.6 copy-done.23
  62.2 0.0 all-to-all-done.1
  62.2 1.5 %copy-done.11 = f32[5,6,128,128]{3,2,1,0:T(8,128)S(1)} copy-done((f32[5,6,128,128]{3,2,1,0:T(8,128)S(1)}, f32[5,6,128,128]{3,2,1,0:T(8,128)}, u32[]{:S(2)}) %copy-start.11) | copy-done | bytes 1966104
  63.7 0.9 %copy-done.17 = f32[5,64,128]{2,1,0:T(8,128)S(1)} copy-done((f32[5,64,128]{2,1,0:T(8,128)S(1)}, f32[5,64,128]{2,1,0:T(8,128)}, u32[]{:S(2)}) %copy-start.17) | copy-done | bytes 163864
  64.6 0.9 %copy-done.19 = f32[5,64,128]{2,1,0:T(8,128)S(1)} copy-done((f32[5,64,128]{2,1,0:T(8,128)S(1)}, f32[5,64,128]{2,1,0:T(8,128)}, u32[]{:S(2)}) %copy-start.19) | copy-done | bytes 163864
  65.5 0.7 copy-done.22
  66.3 0.7 copy-done.24
  67.0 21.2 %strips.1 = (f32[1,6,128,128]{3,2,1,0:T(8,128)}, f32[1,3,6,128,128]{4,3,2,1,0:T(8,128)}, f32[1,6,128,128]{3,2,1,0:T(8,128)}) custom-call(f32[5,64,128]{2,1,0:T(8,128)S(1)} %copy-done.17, f32[5,8,128]{2,1,0:T(8,128)S(1)} %copy-done.22, f32[5,8,128]{2,1,0:T(8,128)S(1)} %copy-done.24, f32[5,64,128]{2,1,0:T(8,128)S(1)} %copy-done.19, f32[352,128]{1,0:T(8,128)} %bitcast.3.got, ...), custom_call_target="tpu_custom_call" | custom-call | tf_op jit(solution)/shard_map/strips/pallas_call | solution.py:747
  (22 shorter events, 0.0 us)
Async XLA Ops:
  2.1 1.3 %copy-start = (f32[1,3,6,128,128]{4,3,2,1,0:T(8,128)S(1)}, f32[1,3,6,128,128]{4,3,2,1,0:T(8,128)}, u32[]{:S(2)}) copy-start(f32[1,3,6,128,128]{4,3,2,1,0:T(8,128)} %mom.5) | copy-start | bytes 3538948
  3.4 1.0 %copy-start.2 = (f32[1,6,128,128]{3,2,1,0:T(8,128)S(1)}, f32[1,6,128,128]{3,2,1,0:T(8,128)}, u32[]{:S(2)}) copy-start(f32[1,6,128,128]{3,2,1,0:T(8,128)} %dens.5) | copy-start | bytes 1179652
  4.4 1.0 %copy-start.4 = (f32[1,6,128,128]{3,2,1,0:T(8,128)S(1)}, f32[1,6,128,128]{3,2,1,0:T(8,128)}, u32[]{:S(2)}) copy-start(f32[1,6,128,128]{3,2,1,0:T(8,128)} %en.5) | copy-start | bytes 1179652
  5.4 0.9 %copy-start.7 = (f32[1,4,128,128]{3,2,1,0:T(8,128)S(1)}, f32[1,4,128,128]{3,2,1,0:T(8,128)}, u32[]{:S(2)}) copy-start(f32[1,4,128,128]{3,2,1,0:T(8,128)} %met.5) | copy-start | bytes 786436
  6.4 0.8 copy-start.13
  7.2 0.7 copy-start.25
  7.9 14.0 %copy-start.1 = (f32[1,3,6,128,128]{4,3,2,1,0:T(8,128)S(1)}, f32[1,3,6,128,128]{4,3,2,1,0:T(8,128)}, u32[]{:S(2)}) copy-start(f32[1,3,6,128,128]{4,3,2,1,0:T(8,128)} %mom.5) | copy-start | bytes 3538948
  7.9 14.0 %copy-start.3 = (f32[1,6,128,128]{3,2,1,0:T(8,128)S(1)}, f32[1,6,128,128]{3,2,1,0:T(8,128)}, u32[]{:S(2)}) copy-start(f32[1,6,128,128]{3,2,1,0:T(8,128)} %dens.5) | copy-start | bytes 1179652
  11.7 0.7 copy-start.16
  12.4 0.6 copy-start.27
  13.1 18.0 %all-to-all-start = ((f32[32,10,1,128]{3,2,1,0:T(1,128)}), f32[32,10,1,128]{3,2,1,0:T(1,128)}, u32[]{:S(2)}, u32[]{:S(2)}) async-start(f32[32,10,1,128]{3,2,1,0:T(1,128)} %bitcast), calls=%async_computation | async-start | bytes 327680 | tf_op jit(solution)/shard_map/all_to_all | solution.py:692
  21.8 1.0 %copy-start.5 = (f32[1,6,128,128]{3,2,1,0:T(8,128)S(1)}, f32[1,6,128,128]{3,2,1,0:T(8,128)}, u32[]{:S(2)}) copy-start(f32[1,6,128,128]{3,2,1,0:T(8,128)} %en.5) | copy-start | bytes 1179652
  22.8 0.9 %copy-start.8 = (f32[1,4,128,128]{3,2,1,0:T(8,128)S(1)}, f32[1,4,128,128]{3,2,1,0:T(8,128)}, u32[]{:S(2)}) copy-start(f32[1,4,128,128]{3,2,1,0:T(8,128)} %met.5) | copy-start | bytes 786436
  23.8 0.8 copy-start.14
  31.0 0.7 copy-start.20
  31.7 0.7 copy-start.26
  34.0 0.7 copy-start.12
  34.6 27.5 %all-to-all-start.1 = ((f32[32,11,1,128]{3,2,1,0:T(1,128)}), f32[32,11,1,128]{3,2,1,0:T(1,128)}, u32[]{:S(2)}, u32[]{:S(2)}) async-start(f32[32,11,1,128]{3,2,1,0:T(1,128)} %bitcast.4), calls=%async_computation.1 | async-start | bytes 360448 | tf_op jit(solution)/shard_map/all_to_all | solution.py:692
  40.5 6.0 %collective-permute-start = (f32[5,28,128]{2,1,0:T(8,128)}, f32[5,28,128]{2,1,0:T(8,128)S(1)}, u32[]{:S(2)}, u32[]{:S(2)}) collective-permute-start(f32[5,28,128]{2,1,0:T(8,128)} %copy-done.27), channel_id=1, source_target_pairs={{0,1},{1,0},{2,3},{3,2},{4,5},{5,4},{6,7},{7,6},{8,9},{9,8},{10,11... | collective-permute-start | bytes 215048 | tf_op jit(solution)/shard_map/ppermute | solution.py:697
  46.5 1.0 %copy-start.6 = (f32[1,6,128,128]{3,2,1,0:T(8,128)S(1)}, f32[1,6,128,128]{3,2,1,0:T(8,128)}, u32[]{:S(2)}) copy-start(f32[1,6,128,128]{3,2,1,0:T(8,128)} %en.5) | copy-start | bytes 1179652
  47.5 0.9 %copy-start.9 = (f32[1,4,128,128]{3,2,1,0:T(8,128)S(1)}, f32[1,4,128,128]{3,2,1,0:T(8,128)}, u32[]{:S(2)}) copy-start(f32[1,4,128,128]{3,2,1,0:T(8,128)} %met.5) | copy-start | bytes 786436
  48.5 0.8 copy-start.15
  59.0 1.3 %copy-start.10 = (f32[5,6,128,128]{3,2,1,0:T(8,128)}, f32[5,6,128,128]{3,2,1,0:T(8,128)S(1)}, u32[]{:S(2)}) copy-start(f32[5,6,128,128]{3,2,1,0:T(8,128)S(1)} %get-tuple-element.16.out) | copy-start | bytes 5898244
  60.3 0.7 copy-start.18
  60.9 0.6 copy-start.21
  61.6 0.6 copy-start.23
  62.2 1.5 %copy-start.11 = (f32[5,6,128,128]{3,2,1,0:T(8,128)S(1)}, f32[5,6,128,128]{3,2,1,0:T(8,128)}, u32[]{:S(2)}) copy-start(f32[5,6,128,128]{3,2,1,0:T(8,128)} %copy-done.10) | copy-start | bytes 5898244
  63.7 0.9 %copy-start.17 = (f32[5,64,128]{2,1,0:T(8,128)S(1)}, f32[5,64,128]{2,1,0:T(8,128)}, u32[]{:S(2)}) copy-start(f32[5,64,128]{2,1,0:T(8,128)} %copy-done.16) | copy-start | bytes 491524
  64.6 0.9 %copy-start.19 = (f32[5,64,128]{2,1,0:T(8,128)S(1)}, f32[5,64,128]{2,1,0:T(8,128)}, u32[]{:S(2)}) copy-start(f32[5,64,128]{2,1,0:T(8,128)} %copy-done.18) | copy-start | bytes 491524
  65.5 0.7 copy-start.22
  66.3 0.7 copy-start.24

commit v2 on v1

v2 whole, which is shorter than its diff:
```python
import functools

import jax
import jax.numpy as jnp
from jax import lax
from jax.experimental import pallas as pl
from jax.experimental.pallas import tpu as pltpu
from jax.sharding import PartitionSpec as P

pressure_factor = 0.4
viscosity = 0.05
time_step = 0.03
unit = time_step / 12.0

LANES = 128
PAD = 8
DEPTH = 4
CH = 5
VMEM_LIMIT = 60 * 1024 * 1024
SENT = 2 * CH
PASSED = 2 * CH + 1
FIRST = 4


def turn(x, shift, axis):
    shift = shift % x.shape[axis]
    return x if shift == 0 else pltpu.roll(x, shift, axis)


def lanes_of(shape):
    return lax.broadcasted_iota(jnp.int32, shape, len(shape) - 1)


def rows_of(shape):
    return lax.broadcasted_iota(jnp.int32, shape, len(shape) - 2)


def metric_at(refs, c, rows):
    return refs[3][0, c, rows] if c < 4 else refs[4][0, rows]


def field_at(refs, c, k, rows):
    dens, mom, en, _, _ = refs
    if c == 0:
        return dens[0, k, rows]
    if c == 4:
        return en[0, k, rows]
    return mom[0, c - 1, k, rows]


def point(f):
    rho, m1, m2, m3, e = f
    r = 1.0 / rho
    u1, u2, u3 = m1 * r, m2 * r, m3 * r
    kin = 0.5 * (m1 * u1 + m2 * u2 + m3 * u3)
    p = pressure_factor * (e - kin)
    return (u1, u2, u3, (kin + 2.0 * p) * r), p, e + p


def metric_terms(m):
    ax, ay, bx, by, v = m
    kv = viscosity * unit
    rw = kv * (ax * ax + ay * ay)
    cw = kv * (bx * bx + by * by)
    return v * ax, v * ay, v * bx, v * by, -unit / v, rw, cw, 30.0 * (rw + cw + kv)


def flux(f, w, p, h, gx, gy):
    rho, m1, m2, m3, _ = f
    u = gx * w[0] + gy * w[1]
    return (rho * u, m1 * u + gx * p, m2 * u + gy * p, m3 * u, h * u)


def flux_planes(f, w, p, h):
    u3 = w[2]
    return (f[3], f[1] * u3, f[2] * u3, f[3] * u3 + p, h * u3)


def slope(x, at):
    return 8.0 * (at(x, 1) - at(x, -1)) - (at(x, 2) - at(x, -2))


def curve(x, at):
    return 16.0 * (at(x, 1) + at(x, -1)) - (at(x, 2) + at(x, -2))


def along(axis):
    return lambda x, o: turn(x, -o, axis)


def within(lane, start, size):
    return (lane >= start) & (lane < start + size)


def roll_by(x, shift, axis=1):
    size = x.shape[axis]
    return pltpu.roll(x, lax.rem(shift + 4 * size, size), axis)


def across(x):
    if x.shape[0] < LANES:
        x = jnp.concatenate([x, jnp.zeros((LANES - x.shape[0], LANES), jnp.float32)], axis=0)
    return x.T


def loop(count, body, start=None, unroll=1):
    if start is None:

        def step(n, _):
            body(n)
            return 0

        lax.fori_loop(0, count, step, 0, unroll=unroll)
        return None
    return lax.fori_loop(0, count, body, start, unroll=unroll)


def fetch(sources, targets, sems):
    copies = [
        pltpu.make_async_copy(src, dst, sems.at[n])
        for n, (src, dst) in enumerate(zip(sources, targets))
    ]
    for copy in copies:
        copy.start()
    return copies


def tile_stage(planes, load, mets, shift_i, shift_j, hold, done):
    kv = viscosity * unit
    fk, ws, acc = hold

    def spread(k):
        for s in range(2):
            vax, vay, vbx, vby, niv, rw, cw, tw = mets[s]
            x = [load(c, s, k) for c in range(CH)]
            w, p, h = point(x)
            fi, fj = flux(x, w, p, h, vax, vay), flux(x, w, p, h, vbx, vby)
            for c in range(CH):
                val = niv * (slope(fi[c], shift_i(0, c, s, k)) + slope(fj[c], shift_j))
                if c > 0:
                    v = w[c - 1]
                    val = val + (
                        rw * curve(v, shift_i(1, c - 1, s, k)) + cw * curve(v, shift_j) - tw * v
                    )
                    ws[c - 1, s, k] = v
                acc[c, s, k] = x[c] + val
            for c, v in enumerate(flux_planes(x, w, p, h)):
                fk[c, s, k] = v

    def gather(k):
        at = {o: lax.rem(k + o + planes, planes) for o in (-2, -1, 0, 1, 2)}
        for s in range(2):
            for c in range(CH):
                val = acc[c, s, k] - unit * slope(0, lambda _, o: fk[c, s, at[o]])
                if c > 0:
                    val = val + kv * curve(0, lambda _, o: ws[c - 1, s, at[o]])
                done(c, s, k, val)

    loop(planes, spread)
    loop(planes, gather)


def cut_kernel(
    halves, dens, mom, en, met, vol, placed, face, orient, send, own, *rest
):
    edges, (packed, strips, *held, sems) = rest[:-8], rest[-8:]
    copies = fetch((dens, mom, en, met, vol), held, sems)
    planes, rows = dens.shape[1], dens.shape[2]
    block = placed[lax.axis_index("blk")]
    half = lax.axis_index("ij")
    row, lane = rows_of((64, LANES)), lanes_of((8, LANES))
    high_side = row % 8 < 4
    mirror = jnp.where(
        rows_of((LANES, LANES)) + lanes_of((LANES, LANES)) == rows - 1, 1.0, 0.0
    )
    flip = [jnp.where(orient[f, block] == 1, -1.0, 1.0) for f in range(2)]
    same = [jnp.where(face[f, block] == f, -1.0, 1.0) for f in range(2)]
    rising = [face[f, block] == 1 for f in range(2)]
    turned = jnp.where(high_side, flip[1], flip[0])
    facing = jnp.where(high_side, same[1], same[0])
    for copy in copies:
        copy.wait()
    if rows < LANES:
        packed[...] = jnp.zeros(packed.shape, jnp.float32)

    def pack(r):
        for c in range(CH):
            out = turn(metric_at(held, c, pl.ds(r, 8)), 8 * planes + 4, 1)
            for k in range(planes):
                x = turn(field_at(held, c, k, pl.ds(r, 8)), 8 * k + 4, 1)
                out = jnp.where(within(lane, 8 * k, 8), x, out)
            packed[c, pl.ds(r, 8)] = out

    chunks(rows // 8, pack)

    def orient_strip(c):
        strip = packed[c].T[0:64]
        own[c] = strip
        back = jnp.dot(
            strip,
            mirror,
            precision=lax.Precision.HIGHEST,
            preferred_element_type=jnp.float32,
        )
        moved = jnp.where(turned < 0.0, back, strip)
        sign = jnp.where(c < 2, turned, jnp.where(c < 4, facing, 1.0))
        moved = jnp.where(row >= planes * 8, moved * sign, moved)
        strips[pl.ds(pl.multiple_of(c * 64, 64), 64)] = moved

    loop(CH, orient_strip)

    def put(n):
        k, e = n >> 2, n & 3
        at = (FIRST + n) * SENT
        low = k * 8 + 4 + jnp.where(rising[0], e, 3 - e)
        high = k * 8 + jnp.where(rising[1], 3 - e, e)
        send[pl.ds(at, CH)] = strips[pl.ds(low, CH, stride=64)]
        send[pl.ds(at + CH, CH)] = strips[pl.ds(high, CH, stride=64)]

    loop(DEPTH * (planes + 1), put, unroll=4)

    def edge(c, at, low, high):
        if len(edges) == 1:
            edges[0][c, pl.ds(at, 4)] = jnp.where(half == 0, high, low)
        else:
            edges[0][c, pl.ds(at, 4)] = low
            edges[1][c, pl.ds(at, 4)] = high

    def cut_ends(k):
        for c in range(CH):
            low = field_at(held, c, k, slice(0, 4))
            edge(c, k * 4, low, field_at(held, c, k, slice(rows - 4, rows)))

    loop(planes, cut_ends)
    for c in range(CH):
        low = metric_at(held, c, slice(0, 4))
        edge(c, planes * 4, low, metric_at(held, c, slice(rows - 4, rows)))


def relay_kernel(
    halves, rows, planes, placed, neighbour, face, orient, got, part,
    send, below, above, signs, where_is,
):
    del part
    blocks = placed.shape[0]
    devices = blocks * halves
    me = lax.axis_index("blk") * halves + lax.axis_index("ij")
    is_field = (me >= FIRST) & (me < FIRST + DEPTH * planes)

    def note(slot, _):
        where_is[placed[slot]] = slot
        return 0

    lax.fori_loop(0, blocks, note, 0, unroll=True)

    def pass_on(slot, _):
        block = placed[slot]
        for f in range(2):
            partner = where_is[neighbour[f, block]]
            side, turned = face[f, block], orient[f, block]
            sign = jnp.where(turned == 1, -1.0, 1.0)

            def piece(h):
                h = jnp.where(turned == 1, halves - 1 - h, h)
                return got[pl.ds((partner * halves + h) * SENT + side * CH, CH)]

            pieces = [piece(h) for h in range(halves)]
            for half in range(halves):
                at = slot * halves + half
                send[pl.ds(at * PASSED + f * CH, CH)] = pieces[half]
                below[pl.ds((f * devices + at) * 8, CH)] = pieces[max(half - 1, 0)]
                above[pl.ds((f * devices + at) * 8, CH)] = pieces[min(half + 1, halves - 1)]
                signs[pl.ds(f * devices + at, 1)] = jnp.full((1, LANES), sign, jnp.float32)
        return 0

    lax.fori_loop(0, blocks, pass_on, 0, unroll=4)
    count = 2 * devices
    lane = lanes_of((count, LANES))
    half = rows_of((count, LANES)) % halves
    sign = signs[...]
    ends = jnp.zeros((count, LANES), jnp.float32)
    for c in range(CH):
        low, high = below[pl.ds(c, count, stride=8)], above[pl.ds(c, count, stride=8)]
        at = 4 * c
        low_wall = jnp.where(lane == at, turn(low, at - 1, 1), turn(low, at + 1, 1))
        high_wall = jnp.where(
            lane == at + 2, turn(high, at + 3 - rows, 1), turn(high, at + 5 - rows, 1)
        )
        if 1 <= c <= 3:
            low_wall = jnp.where(is_field, -sign * low_wall, low_wall)
            high_wall = jnp.where(is_field, sign * high_wall, high_wall)
        low = jnp.where(half == 0, low_wall, turn(low, at + 2 - rows, 1))
        high = jnp.where(half == halves - 1, high_wall, turn(high, at + 2, 1))
        ends = jnp.where(within(lane, at, 2), low, jnp.where(within(lane, at + 2, 2), high, ends))
    send[pl.ds(2 * CH, devices, stride=PASSED)] = ends[0:devices] + turn(
        ends[devices:], 4 * CH, 1
    )


def flux_chunk(get, mets, fi, w, fk, acc, r):
    rows = pl.ds(r, 8)
    vax, vay, vbx, vby, niv, rw, cw, tw = [mets[j, rows] for j in range(8)]
    at_j = along(1)
    for k in range(fi.shape[1]):
        f = [get(c, k, r) for c in range(CH)]
        wk, p, h = point(f)
        for c, x in enumerate(flux(f, wk, p, h, vax, vay)):
            fi[c, k, rows] = x
        for c in range(4):
            w[c, k, rows] = wk[c]
        fj = flux(f, wk, p, h, vbx, vby)
        for c in range(CH):
            val = niv * slope(fj[c], at_j)
            if c > 0:
                val = val + (cw * curve(wk[c - 1], at_j) - tw * wk[c - 1])
            acc[c, k, rows] = val
        for c, x in enumerate(flux_planes(f, wk, p, h)):
            fk[c, k, rows] = x


def sum_chunk(mets, fi, w, fk, acc, r, emit):
    planes = fi.shape[1]
    kv = viscosity * unit
    rows = pl.ds(r, 8)
    niv, rw = mets[4, rows], mets[5, rows]
    for c in range(CH):
        t = [fk[c, k, rows] for k in range(planes)]
        x = [w[c - 1, k, rows] for k in range(planes)] if c > 0 else None
        for k in range(planes):

            def near(v, o):
                return v[(k + o) % planes]

            def at_i(v, o):
                return v[pl.ds(r + o, 8)]

            val = acc[c, k, rows] + niv * slope(fi.at[c, k], at_i) - unit * slope(t, near)
            if c > 0:
                val = val + (rw * curve(w.at[c - 1, k], at_i) + kv * curve(x, near))
            emit(c, k, r, val)


def chunks(count, body):
    def step(n, _):
        body(pl.multiple_of(n * 8, 8))
        return 0

    lax.fori_loop(0, count, step, 0)


def first_kernel(
    dens, mom, en, met, vol, part, d, m, e, t, v, full, mets, fi, w, fk, acc, sems, out_sems
):
    held = (d, m, e, t, v)
    copies = fetch((dens, mom, en, met, vol), held, sems)
    planes, rows = dens.shape[1], dens.shape[2]
    for copy in copies:
        copy.wait()

    def get(c, k, r):
        return field_at(held, c, k, pl.ds(r - PAD, 8))

    def fluxes(r):
        terms = metric_terms([metric_at(held, c, pl.ds(r, 8)) for c in range(CH)])
        for j, x in enumerate(terms):
            mets[j, pl.ds(r + PAD, 8)] = x
        flux_chunk(get, mets, fi, w, fk, acc, r + PAD)

    def emit(c, k, r, val):
        full[c, k, pl.ds(r - PAD, 8)] = get(c, k, r) + val

    def leave(r):
        at = pl.ds(r, 8)
        return pltpu.make_async_copy(full.at[:, :, at], part.at[:, :, at], out_sems.at[r // 8])

    def sums(r):
        sum_chunk(mets, fi, w, fk, acc, r + PAD, emit)
        leave(r).start()

    chunks(rows // 8, fluxes)
    chunks(rows // 8, sums)
    chunks(rows // 8, lambda r: leave(r).wait())


def pack_ends(tall, scratch, planes, extra):
    sub, lane = rows_of((8, LANES)), lanes_of((8, LANES))
    count = planes + extra

    def first(k, packed):
        out = []
        for c in range(CH):
            x = roll_by(jnp.where(sub < 4, tall[0, c, k], tall[1, c, k]), 8 * k + 4)
            out.append(jnp.where(within(lane, 8 * k, 8), x, packed[c]))
        return tuple(out)

    empty = jnp.zeros((8, LANES), jnp.float32)
    packed = loop(count, first, (empty,) * CH)
    scratch[...] = across(jnp.concatenate(packed, axis=0))

    def second(k, packed):
        x = scratch[pl.ds(pl.multiple_of(8 * k, 8), 8)]
        return tuple(
            jnp.where(within(lane, 4 * k, 4), roll_by(x, 4 * k - (8 * c + 2)), packed[c])
            for c in range(CH)
        )

    return loop(count, second, (empty,) * CH)


def second_kernel(
    halves, dens, mom, en, met, vol, below, above, part,
    out, ends_base, ends_sec, inner,
    d, m, e, t, v, tall, packed, tile_fk, tile_w, tile_acc,
    sec, full, mets, fi, w, fk, acc, sems, out_sems,
):
    held = (d, m, e, t, v)
    planes, rows = dens.shape[1], dens.shape[2]
    copies = fetch((dens, mom, en, met, vol), held, sems)
    arrive = pltpu.make_async_copy(part, sec.at[:, :, PAD : PAD + rows], sems.at[5])
    arrive.start()
    half = lax.axis_index("ij")
    low_wall, high_wall = half == 0, half == halves - 1
    low_flag, high_flag = jnp.where(low_wall, 1, 0), jnp.where(high_wall, 1, 0)
    sub, lane = rows_of((8, LANES)), lanes_of((8, LANES))
    for copy in copies:
        copy.wait()

    def ends_of(c, k, low, high, others, sign):
        tall[0, c, k, 4:8] = low
        tall[1, c, k, 0:4] = high
        for n in range(4):
            near = jnp.where(low_wall, sign * low[3 - n : 4 - n], others[0][n : n + 1])
            far = jnp.where(high_wall, high[3 - n : 4 - n], others[1][n : n + 1])
            tall[0, c, k, n : n + 1] = near
            tall[1, c, k, 4 + n : 5 + n] = far

    def set_ends(k):
        for c in range(CH):
            low, high = (
                field_at(held, c, k, slice(0, 4)),
                field_at(held, c, k, slice(rows - 4, rows)),
            )
            others = (below[c, pl.ds(4 * k, 4)], above[c, pl.ds(4 * k, 4)])
            ends_of(c, k, low, high, others, -1.0 if 1 <= c <= 3 else 1.0)

    loop(planes, set_ends)
    for c in range(CH):
        low, high = metric_at(held, c, slice(0, 4)), metric_at(held, c, slice(rows - 4, rows))
        others = (below[c, 4 * planes : 4 * planes + 4], above[c, 4 * planes : 4 * planes + 4])
        ends_of(c, planes, low, high, others, 1.0)
    for c, x in enumerate(pack_ends(tall, packed.at[0], planes, 1)):
        ends_base[c] = x

    def terms(r):
        out = metric_terms([metric_at(held, c, pl.ds(r, 8)) for c in range(CH)])
        for j, x in enumerate(out):
            mets[j, pl.ds(r + PAD, 8)] = x

    chunks(rows // 8, terms)
    tall_mets = [metric_terms([tall[s, c, planes] for c in range(CH)]) for s in range(2)]
    for s, at in ((0, PAD - 4), (1, PAD + rows - 4)):
        for j, x in enumerate(tall_mets[s]):
            mets[j, at : at + 8] = x

    arrive.wait()

    def done(c, s, k, x):
        tall[s, c, k] = x
        if s == 0:
            sign = -1.0 if 1 <= c <= 3 else 1.0
            wall = sign * jnp.where(sub == 2, turn(x, -3, 0), turn(x, -1, 0))
            x = jnp.where((sub < 4) & (low_flag == 1), wall, x)
        else:
            wall = jnp.where(sub == 4, turn(x, 1, 0), turn(x, 3, 0))
            x = jnp.where((sub >= 4) & (high_flag == 1), wall, x)
        start = PAD - 2 if s == 0 else PAD + rows - 2
        sec[c, k, start : start + 4] = x[2:6]

    tile_stage(
        planes, lambda c, s, k: tall[s, c, k], tall_mets, lambda *_: along(0), along(1),
        (tile_fk, tile_w, tile_acc), done,
    )
    for c, x in enumerate(pack_ends(tall, packed.at[0], planes, 0)):
        ends_sec[c] = x

    if rows < LANES:
        packed[...] = jnp.zeros(packed.shape, jnp.float32)

    def pack(r):
        for c in range(CH):
            x = metric_at(held, c, pl.ds(r, 8))
            at = 8 * planes
            out = jnp.where(lane < at + 4, turn(x, at + 6, 1), turn(x, at + 2, 1))
            for k in range(planes):
                x = sec[c, k, pl.ds(r + PAD, 8)]
                at = 8 * k
                out = jnp.where(within(lane, at, 4), turn(x, at + 6, 1), out)
                out = jnp.where(within(lane, at + 4, 4), turn(x, at + 2, 1), out)
            packed[c, pl.ds(r, 8)] = out

    chunks(rows // 8, pack)

    def flip(c):
        inner[c] = packed[c].T[0:64]

    loop(CH, flip)

    def get(c, k, r):
        return sec[c, k, pl.ds(r, 8)]

    def emit(c, k, r, val):
        at = pl.ds(r - PAD, 8)
        full[c, k, at] = 0.5 * (field_at(held, c, k, at) + (get(c, k, r) + val))

    def leave(r):
        at = pl.ds(r, 8)
        return pltpu.make_async_copy(full.at[:, :, at], out.at[:, :, at], out_sems.at[r // 8])

    def sums(r):
        sum_chunk(mets, fi, w, fk, acc, r + PAD, emit)
        leave(r).start()

    chunks(rows // 8 + 2, lambda r: flux_chunk(get, mets, fi, w, fk, acc, r))
    chunks(rows // 8, sums)
    chunks(rows // 8, lambda r: leave(r).wait())


def beyond(packed, f, k, rows):
    base = 28 * f + 4 * k
    low = roll_by(packed, LANES - 2 - base)
    top = rows % LANES
    high = low if top == 0 else roll_by(packed, top - 2 - base)
    lane = lanes_of(packed.shape)

    def at(x, o):
        if o < 0:
            x = jnp.where(lane >= LANES + o, low, x)
        else:
            x = jnp.where(within(lane, top, o), high, x)
        return turn(x, -o, 1)

    return at


def last_kernel(
    halves, rows, planes, own, ends_base, ends_sec, inner, got, out,
    next_dens, next_mom, next_en,
    base, sec, fk, ws, acc, turned, back, full, sems,
):
    arrive = pltpu.make_async_copy(out, full, sems.at[CH])
    arrive.start()
    half = lax.axis_index("ij")
    low_wall, high_wall = half == 0, half == halves - 1
    sub, lane = rows_of((8, LANES)), lanes_of((8, LANES))

    def mix(f, mine, others):
        return jnp.where((sub < 4) == (f == 1), mine, others)

    def gather(k, others):
        start = DEPTH * k * PASSED

        def ghost(row, f):
            x = got[pl.ds(start + row, 8, stride=PASSED)]
            return x if f == 1 else turn(x, 4, 0)

        others = list(others)
        for f in range(2):
            arrived = ghost(2 * CH, f)
            to = 28 * f + 4 * k
            for c in range(CH):
                mine = own[c, pl.ds(pl.multiple_of(k * 8, 8), 8)]
                base[c, f, k] = mix(f, mine, ghost(f * CH + c, f))
                moved = roll_by(arrived, to - 4 * CH * f - 4 * c)
                others[c] = jnp.where(within(lane, to, 4), moved, others[c])
        return tuple(others)

    empty = jnp.zeros((8, LANES), jnp.float32)
    others = loop(planes + 1, gather, (empty,) * CH)
    low_lanes = lane < 28
    twice = [jnp.where(low_lanes, ends_base[c], turn(ends_base[c], 28, 1)) for c in range(CH)]
    ends = [jnp.where(low_lanes == (sub >= 4), twice[c], others[c]) for c in range(CH)]
    slot = jnp.where(low_lanes, lane, lane - 28)

    def spread(k, kept):
        shift, hit = 4 * (k - planes), within(slot, 4 * k, 4)
        return tuple((x, jnp.where(hit, roll_by(x, shift), y)) for x, y in kept)

    kept = metric_terms(ends)[0:5] + metric_terms(ends)[6:7] + metric_terms(twice)[2:4]
    kept = loop(planes, spread, tuple((x, x) for x in kept))
    vax, vay, vbx, vby, niv, cw, *wrapped = [y for _, y in kept]

    def keep(c, f, k, val):
        sec[c, f, k] = val

    def stage(held, ends, gx, gy):
        mets = [metric_terms([held[c, f, planes] for c in range(CH)]) for f in range(2)]
        w, p, h = point(ends)
        rims = (flux(ends, w, p, h, gx, gy), w)
        tile_stage(
            planes,
            lambda c, f, k: held[c, f, k],
            mets,
            lambda kind, c, f, k: beyond(rims[kind][c], f, k, rows),
            along(0),
            (fk, ws, acc),
            keep,
        )

    stage(base, ends, vax, vay)

    def move(k, source):
        for c in range(CH):
            mine = inner[c, pl.ds(pl.multiple_of(k * 8, 8), 8)]
            for f in range(2):
                sec[c, f, k] = mix(f, mine, turn(source[c, f, k], 2 if f == 1 else -2, 0))

    loop(planes, lambda k: move(k, sec))
    move(jnp.int32(planes), base)

    def shifted(x):
        return jnp.where(low_lanes, turn(x, -2, 0), turn(x, 2, 0))

    w1, p1, h1 = point(ends)
    w0, p0, h0 = point(twice)
    new, old = flux(ends, w1, p1, h1, vbx, vby), flux(twice, w0, p0, h0, *wrapped)
    at_j = along(0)
    touched = within(sub, jnp.where(low_lanes, 4, 2), 2)
    second = []
    for c in range(CH):
        add = niv * slope(new[c] - old[c], at_j)
        if c > 0:
            add = add + cw * curve(w1[c - 1] - w0[c - 1], at_j)
        x = jnp.where(low_lanes, ends_sec[c], turn(ends_sec[c], 28, 1))
        second.append(shifted(x + jnp.where(touched, add, 0.0)))
    walled = low_wall | high_wall

    def reflect(k, second):
        second = list(second)
        for f in range(2):
            to = 28 * f + 4 * k
            first = jnp.where(walled, jnp.where(low_wall, to, to + 2), -8)
            shift = jnp.where(low_wall, to - 1, to + 3 - rows)
            for c in range(CH):
                x = sec[c, f, k]
                one, two = roll_by(x, shift), roll_by(x, shift + 2)
                if 1 <= c <= 3:
                    sign = jnp.where(low_wall, -1.0, 1.0)
                    one, two = sign * one, sign * two
                x = jnp.where(lane == first, one, second[c])
                second[c] = jnp.where(lane == first + 1, two, x)
        return tuple(second)

    second = loop(planes, reflect, tuple(second))
    stage(sec, second, shifted(vax), shifted(vay))

    per = LANES // 8

    def finish(k):
        for c in range(CH):
            x = jnp.where(sub < 4, turn(sec[c, 1, k], -2, 0), turn(sec[c, 0, k], 2, 0))
            at = pl.multiple_of((c * planes + k) * 8, 8)
            mine = own[c, pl.ds(pl.multiple_of(k * 8, 8), 8)]
            turned[pl.ds(at, 8)] = 0.5 * (mine + x)

    loop(planes, finish)

    def flip(n):
        back[n] = turned[pl.ds(pl.multiple_of(n * LANES, LANES), LANES)].T

    loop(turned.shape[0] // LANES, flip)
    arrive.wait()
    inside = within(lane, 4, LANES - 8)
    copies = []
    for c in range(CH):

        def merge(k, c=c):
            index = c * planes + k
            which, place = index // per, lax.rem(index, per)
            for r in range(0, rows, 8):
                moved = roll_by(back[which, r : r + 8], LANES - 4 - 8 * place)
                full[c, k, r : r + 8] = jnp.where(inside, full[c, k, r : r + 8], moved)

        loop(planes, merge)
        dst = next_dens.at[0] if c == 0 else next_en.at[0] if c == 4 else next_mom.at[0, c - 1]
        copies.append(pltpu.make_async_copy(full.at[c], dst, sems.at[c]))
        copies[-1].start()
    for copy in copies:
        copy.wait()


def local(mesh_shape, density, momentum, energy, metrics, volume, placed, neighbour, face, orient):
    halves = mesh_shape["ij"]
    devices = mesh_shape["blk"] * halves
    planes, rows = density.shape[1], density.shape[2]
    every = planes + 1
    fields = (density, momentum, energy, metrics, volume)
    f32 = jnp.float32
    vmem = pl.BlockSpec(memory_space=pltpu.VMEM)
    smem = pl.BlockSpec(memory_space=pltpu.SMEM)
    hbm = pl.BlockSpec(memory_space=pltpu.HBM)

    def call(kernel, name, outs, ins, out_specs, scratch, cost=None):
        return pl.pallas_call(
            kernel,
            out_shape=outs,
            in_specs=ins,
            out_specs=out_specs,
            scratch_shapes=scratch,
            compiler_params=pltpu.CompilerParams(vmem_limit_bytes=VMEM_LIMIT),
            cost_estimate=cost,
            name=name,
        )

    def shape(*dims):
        return jax.ShapeDtypeStruct(dims, f32)

    neighbour, face, orient = neighbour.T, face.T, orient.T
    strip = pltpu.VMEM((CH, 2, every, 8, LANES), f32)
    held = [pltpu.VMEM(x.shape, f32) for x in fields]
    edge = shape(CH, 4 * every, LANES)
    edges = 1 if halves == 2 else 2
    sent, own, *halo = call(
        functools.partial(cut_kernel, halves),
        "cut",
        [shape(devices * SENT, LANES), shape(CH, 64, LANES)] + [edge] * edges,
        [hbm] * 5 + [smem] * 3,
        [vmem] * (2 + edges),
        [pltpu.VMEM((CH, LANES, LANES), f32), pltpu.VMEM((CH * 64, LANES), f32)]
        + held
        + [pltpu.SemaphoreType.DMA((5,))],
    )(*fields, placed, face, orient)

    def swap(x):
        x = x.reshape(devices, x.shape[0] // devices, 1, LANES)
        x = lax.all_to_all(x, ("blk", "ij"), 0, 0, tiled=True)
        return x.reshape(x.shape[0] * x.shape[1], LANES)

    got = swap(sent)
    if edges == 1:
        below = above = lax.ppermute(halo[0], "ij", [(0, 1), (1, 0)])
    else:
        below = lax.ppermute(halo[1], "ij", [(i, i + 1) for i in range(halves - 1)])
        above = lax.ppermute(halo[0], "ij", [(i + 1, i) for i in range(halves - 1)])

    tall = rows + 2 * PAD
    block = shape(CH, planes, rows, LANES)
    stage = [
        pltpu.VMEM((CH, planes, rows, LANES), f32),
        pltpu.VMEM((8, tall, LANES), f32),
        pltpu.VMEM((CH, planes, tall, LANES), f32),
        pltpu.VMEM((4, planes, tall, LANES), f32),
        pltpu.VMEM((CH, planes, tall, LANES), f32),
        pltpu.VMEM((CH, planes, tall, LANES), f32),
    ]
    work = planes * rows * LANES
    cost = pl.CostEstimate(flops=300 * work, bytes_accessed=150 * work, transcendentals=work)
    leaving = pltpu.SemaphoreType.DMA((rows // 8,))
    part = call(
        first_kernel,
        "first_section",
        block,
        [hbm] * 5,
        hbm,
        held + stage + [pltpu.SemaphoreType.DMA((5,)), leaving],
        cost,
    )(*fields)
    relayed = call(
        functools.partial(relay_kernel, halves, rows, planes),
        "relay",
        shape(devices * PASSED, LANES),
        [smem] * 4 + [vmem, hbm],
        vmem,
        [
            pltpu.VMEM((devices * 16, LANES), f32),
            pltpu.VMEM((devices * 16, LANES), f32),
            pltpu.VMEM((devices * 2, LANES), f32),
            pltpu.SMEM((placed.shape[0],), jnp.int32),
        ],
    )(placed, neighbour, face, orient, got, part)
    ghosts = swap(relayed)
    out, ends_base, ends_sec, inner = call(
        functools.partial(second_kernel, halves),
        "second_section",
        [block, shape(CH, 8, LANES), shape(CH, 8, LANES), shape(CH, 64, LANES)],
        [hbm] * 5 + [vmem] * 2 + [hbm],
        [hbm] + [vmem] * 3,
        held
        + [
            pltpu.VMEM((2, CH, every, 8, LANES), f32),
            pltpu.VMEM((CH, LANES, LANES), f32),
            strip,
            strip,
            strip,
            pltpu.VMEM((CH, planes, tall, LANES), f32),
        ]
        + stage
        + [pltpu.SemaphoreType.DMA((6,)), leaving],
        cost,
    )(*fields, below, above, part)
    flat = -(-CH * planes * 8 // LANES)
    return call(
        functools.partial(last_kernel, halves, rows, planes),
        "strips",
        [shape(*density.shape), shape(*momentum.shape), shape(*energy.shape)],
        [vmem] * 5 + [hbm],
        [hbm] * 3,
        [strip] * 5
        + [
            pltpu.VMEM((flat * LANES, LANES), f32),
            pltpu.VMEM((flat, LANES, LANES), f32),
            pltpu.VMEM((CH, planes, rows, LANES), f32),
            pltpu.SemaphoreType.DMA((CH + 1,)),
        ],
    )(own, ends_base, ends_sec, inner, ghosts, out)


def solution(mesh):
    return jax.shard_map(
        functools.partial(local, dict(mesh.shape)),
        mesh=mesh,
        in_specs=(
            P("blk", None, "ij", None),
            P("blk", None, None, "ij", None),
            P("blk", None, "ij", None),
            P("blk", None, "ij", None),
            P("blk", "ij", None),
            P(),
            P(),
            P(),
            P(),
        ),
        out_specs=(
            P("blk", None, "ij", None),
            P("blk", None, None, "ij", None),
            P("blk", None, "ij", None),
        ),
        check_vma=False,
    )
```

time: 89.2 us -> 66.6 us (0.75)
  local copies, waits for them, and re-layouts: 25.4 us -> 1.99 us
  Pallas kernels: 42.7 us -> 44.4 us
    unnamed x59 -> x8, local copies, waits for them, and re-layouts: 25.4 us -> 1.99 us
    pallas_call x1, Pallas kernels: 21.2 us -> 9.68 us  [local(): call(functools.partial(last_kernel, halves, rows, planes), 'strips', [sha...]
    pallas_call x1, Pallas kernels: 9.68 us -> 17.6 us  [local(): call(functools.partial(second_kernel, halves), 'second_section', [block,...]
    pallas_call x1, Pallas kernels: 6.41 us -> 8.81 us  [local(): call(first_kernel, 'first_section', block, [hbm] * 5, hbm, held + stage +...]
    pallas_call x1, Pallas kernels: 3.88 us -> 6.14 us  [local(): call(functools.partial(cut_kernel, halves), 'cut', [shape(devices * SENT,...]
  transfers between devices with their start and end apart: 3 -> 3, of which waited for: 1 -> 2; matrix products, arithmetic and copies ran while one was open for 2% -> 0% of each run, Pallas kernels for 18% -> 40%
where the time goes in v2:
time: 66.6 us; the launch traced here: 66.2 us
  Pallas kernels  44.4 us (67%)
  starting transfers between devices  14.7 us (22%)
  waiting for transfers between devices  4.4 us (7%)
  local copies, waits for them, and re-layouts  1.99 us (3%)
  between operations  0.71 us (1%)
    pallas_call x1, Pallas kernels, local(): call(functools.partial(second_kernel, halves), 'second_section', [block,...  17.6 us
    all_to_all x2, starting transfers between devices, swap(): x = lax.all_to_all(x, ('blk', 'ij'), 0, 0, tiled=True)  12.8 us
    pallas_call x1, Pallas kernels, local(): call(functools.partial(last_kernel, halves, rows, planes), 'strips', [sha...  9.68 us
    pallas_call x1, Pallas kernels, local(): call(first_kernel, 'first_section', block, [hbm] * 5, hbm, held + stage +...  8.81 us
    pallas_call x1, Pallas kernels, local(): call(functools.partial(cut_kernel, halves), 'cut', [shape(devices * SENT,...  6.14 us
    ppermute x1, waiting for transfers between devices, local(): below = above = lax.ppermute(halo[0], 'ij', [(0, 1), (1, 0)])  4.08 us
    pallas_call x1, Pallas kernels, local(): call(functools.partial(relay_kernel, halves, rows, planes), 'relay', shap...  2.25 us
    unnamed x8, local copies, waits for them, and re-layouts  1.99 us
  transfers between devices with their start and end apart: 3, of which 2 were waited for; matrix products, arithmetic and copies ran while one was open for 0% of the time, Pallas kernels for 40%

profile of v2, /device:TPU:0, one launch (start us, length us, event | category | flops | bytes accessed | tf_op | source)
XLA Modules:
  0.0 66.2 jit_solution(4383558135041175893)
XLA Ops:
  0.6 6.1 %cut.1 = (f32[320,128]{1,0:T(8,128)}, f32[5,64,128]{2,1,0:T(8,128)}, f32[5,28,128]{2,1,0:T(8,128)}) custom-call(f32[1,6,128,128]{3,2,1,0:T(8,128)} %dens.5, f32[1,3,6,128,128]{4,3,2,1,0:T(8,128)} %mom.5, f32[1,6,128,128]{3,2,1,0:T(8,128)} %en.5, f32[1,4,128,128]{3,2,1,0:T(8,128)} %met.5, f32[1,128,128]{2,1,0:T(8,128)} %vol.5, s32[16]{0:T(128)} %placed.3, ...), custom_call_target="tpu_custom_call" | custom-call | tf_op jit(solution)/shard_map/cut/pallas_call | solution.py:722
  6.8 7.3 %all-to-all-start = ((f32[32,10,1,128]{3,2,1,0:T(1,128)}), f32[32,10,1,128]{3,2,1,0:T(1,128)S(1)}, u32[]{:S(2)}, u32[]{:S(2)}) async-start(f32[32,10,1,128]{3,2,1,0:T(1,128)} %bitcast.10), calls=%async_computation | async-start | bytes 327680 | tf_op jit(solution)/shard_map/all_to_all | solution.py:735
  14.1 8.8 %first_section.1.part = f32[5,6,128,128]{3,2,1,0:T(8,128)} custom-call(f32[1,6,128,128]{3,2,1,0:T(8,128)} %dens.5, f32[1,3,6,128,128]{4,3,2,1,0:T(8,128)} %mom.5, f32[1,6,128,128]{3,2,1,0:T(8,128)} %en.5, f32[1,4,128,128]{3,2,1,0:T(8,128)} %met.5, f32[1,128,128]{2,1,0:T(8,128)} %vol.5), custom_call_target="tpu_custom_call" | custom-call | flops 29491200 | bytes 14745600 | tf_op jit(solution)/shard_map/first_section/pallas_call | solution.py:758
  22.9 0.0 copy-start.3
  22.9 0.3 all-to-all-done
  23.2 0.0 copy-start.1
  23.2 0.7 %copy-done.1 = f32[32,10,1,128]{3,2,1,0:T(1,128)} copy-done((f32[32,10,1,128]{3,2,1,0:T(1,128)}, f32[32,10,1,128]{3,2,1,0:T(1,128)S(1)}, u32[]{:S(2)}) %copy-start.1) | copy-done | bytes 163864
  23.9 2.2 %relay.1 = f32[352,128]{1,0:T(8,128)} custom-call(s32[16]{0:T(128)} %placed.3, s32[2,16]{1,0:T(2,128)} %bitcast.15, s32[2,16]{1,0:T(2,128)} %bitcast.12, s32[2,16]{1,0:T(2,128)} %bitcast.14, f32[320,128]{1,0:T(8,128)} %bitcast.9, f32[5,6,128,128]{3,2,1,0:T(8,128)} %first_section.1.part), custom_call_target="tpu_custom_call" | custom-call | tf_op jit(solution)/shard_map/relay/pallas_call | solution.py:767
  26.1 5.5 %all-to-all-start.1 = ((f32[32,11,1,128]{3,2,1,0:T(1,128)}), f32[32,11,1,128]{3,2,1,0:T(1,128)S(1)}, u32[]{:S(2)}, u32[]{:S(2)}) async-start(f32[32,11,1,128]{3,2,1,0:T(1,128)} %bitcast.8), calls=%async_computation.1 | async-start | bytes 360448 | tf_op jit(solution)/shard_map/all_to_all | solution.py:735
  31.7 0.0 copy-done.3
  31.7 1.8 %collective-permute-start = (f32[5,28,128]{2,1,0:T(8,128)S(1)}, f32[5,28,128]{2,1,0:T(8,128)S(1)}, u32[]{:S(2)}, u32[]{:S(2)}) collective-permute-start(f32[5,28,128]{2,1,0:T(8,128)S(1)} %copy-done.3), channel_id=1, source_target_pairs={{0,1},{1,0},{2,3},{3,2},{4,5},{5,4},{6,7},{7,6},{8,9},{9,8},{10,11... | collective-permute-start | bytes 215048 | tf_op jit(solution)/shard_map/ppermute | solution.py:740
  33.5 4.1 %collective-permute-done.below.above = f32[5,28,128]{2,1,0:T(8,128)S(1)} collective-permute-done((f32[5,28,128]{2,1,0:T(8,128)S(1)}, f32[5,28,128]{2,1,0:T(8,128)S(1)}, u32[]{:S(2)}, u32[]{:S(2)}) %collective-permute-start) | collective-permute-done | bytes 71712 | tf_op jit(solution)/shard_map/ppermute | solution.py:740
  37.6 0.0 copy-start.2
  37.6 0.6 copy-done.2
  38.2 17.6 %second_section.1 = (f32[5,6,128,128]{3,2,1,0:T(8,128)}, f32[5,8,128]{2,1,0:T(8,128)}, f32[5,8,128]{2,1,0:T(8,128)}, f32[5,64,128]{2,1,0:T(8,128)}) custom-call(f32[1,6,128,128]{3,2,1,0:T(8,128)} %dens.5, f32[1,3,6,128,128]{4,3,2,1,0:T(8,128)} %mom.5, f32[1,6,128,128]{3,2,1,0:T(8,128)} %en.5, f32[1,4,128,128]{3,2,1,0:T(8,128)} %met.5, f32[1,128,128]{2,1,0:T(8,128)} %vol.5, ...), custom_call_target="tpu_custom_call" | custom-call | flops 29491200 | bytes 14745600 | tf_op jit(solution)/shard_map/second_section/pallas_call | solution.py:781
  55.8 0.0 all-to-all-done.1
  55.8 0.0 copy-start
  55.8 0.7 %copy-done = f32[32,11,1,128]{3,2,1,0:T(1,128)} copy-done((f32[32,11,1,128]{3,2,1,0:T(1,128)}, f32[32,11,1,128]{3,2,1,0:T(1,128)S(1)}, u32[]{:S(2)}) %copy-start) | copy-done | bytes 180248
  56.5 9.7 %strips.1 = (f32[1,6,128,128]{3,2,1,0:T(8,128)}, f32[1,3,6,128,128]{4,3,2,1,0:T(8,128)}, f32[1,6,128,128]{3,2,1,0:T(8,128)}) custom-call(f32[5,64,128]{2,1,0:T(8,128)} %get-tuple-element.10.own, f32[5,8,128]{2,1,0:T(8,128)} %get-tuple-element.12.ends_base, f32[5,8,128]{2,1,0:T(8,128)} %get-tuple-element.13.ends_sec, f32[5,64,128]{2,1,0:T(8,128)} %get-tuple-element.14.inner, ...), custom_call_target="tpu_custom_call" | custom-call | tf_op jit(solution)/shard_map/strips/pallas_call | solution.py:801
Async XLA Ops:
  6.8 16.5 %all-to-all-start = ((f32[32,10,1,128]{3,2,1,0:T(1,128)}), f32[32,10,1,128]{3,2,1,0:T(1,128)S(1)}, u32[]{:S(2)}, u32[]{:S(2)}) async-start(f32[32,10,1,128]{3,2,1,0:T(1,128)} %bitcast.10), calls=%async_computation | async-start | bytes 327680 | tf_op jit(solution)/shard_map/all_to_all | solution.py:735
  22.9 8.8 %copy-start.3 = (f32[5,28,128]{2,1,0:T(8,128)S(1)}, f32[5,28,128]{2,1,0:T(8,128)}, u32[]{:S(2)}) copy-start(f32[5,28,128]{2,1,0:T(8,128)} %get-tuple-element.11) | copy-start | bytes 215044
  23.2 0.7 %copy-start.1 = (f32[32,10,1,128]{3,2,1,0:T(1,128)}, f32[32,10,1,128]{3,2,1,0:T(1,128)S(1)}, u32[]{:S(2)}) copy-start(f32[32,10,1,128]{3,2,1,0:T(1,128)S(1)} %all-to-all-done) | copy-start | bytes 491524
  26.1 29.7 %all-to-all-start.1 = ((f32[32,11,1,128]{3,2,1,0:T(1,128)}), f32[32,11,1,128]{3,2,1,0:T(1,128)S(1)}, u32[]{:S(2)}, u32[]{:S(2)}) async-start(f32[32,11,1,128]{3,2,1,0:T(1,128)} %bitcast.8), calls=%async_computation.1 | async-start | bytes 360448 | tf_op jit(solution)/shard_map/all_to_all | solution.py:735
  31.7 5.9 %collective-permute-start = (f32[5,28,128]{2,1,0:T(8,128)S(1)}, f32[5,28,128]{2,1,0:T(8,128)S(1)}, u32[]{:S(2)}, u32[]{:S(2)}) collective-permute-start(f32[5,28,128]{2,1,0:T(8,128)S(1)} %copy-done.3), channel_id=1, source_target_pairs={{0,1},{1,0},{2,3},{3,2},{4,5},{5,4},{6,7},{7,6},{8,9},{9,8},{10,11... | collective-permute-start | bytes 215048 | tf_op jit(solution)/shard_map/ppermute | solution.py:740
  37.6 0.6 copy-start.2
  55.8 0.7 %copy-start = (f32[32,11,1,128]{3,2,1,0:T(1,128)}, f32[32,11,1,128]{3,2,1,0:T(1,128)S(1)}, u32[]{:S(2)}) copy-start(f32[32,11,1,128]{3,2,1,0:T(1,128)S(1)} %all-to-all-done.1) | copy-start | bytes 540676

commit v3 on v2

v3 whole, which is shorter than its diff:
```python
import functools

import jax
import jax.numpy as jnp
from jax import lax
from jax.experimental import pallas as pl
from jax.experimental.pallas import tpu as pltpu
from jax.sharding import PartitionSpec as P

pressure_factor = 0.4
viscosity = 0.05
time_step = 0.03
unit = time_step / 12.0

LANES = 128
PAD = 16
DEPTH = 4
CH = 5
VMEM_LIMIT = 63 * 1024 * 1024
SENT = 2 * CH
PASSED = 2 * CH + 1
FIRST = 4


def turn(x, shift, axis):
    shift = shift % x.shape[axis]
    return x if shift == 0 else pltpu.roll(x, shift, axis)


def lanes_of(shape):
    return lax.broadcasted_iota(jnp.int32, shape, len(shape) - 1)


def rows_of(shape):
    return lax.broadcasted_iota(jnp.int32, shape, len(shape) - 2)


def point(f):
    rho, m1, m2, m3, e = f
    r = 1.0 / rho
    u1, u2, u3 = m1 * r, m2 * r, m3 * r
    kin = 0.5 * (m1 * u1 + m2 * u2 + m3 * u3)
    p = pressure_factor * (e - kin)
    return (u1, u2, u3, (kin + 2.0 * p) * r), p, e + p


def metric_terms(m):
    ax, ay, bx, by, v = m
    kv = viscosity * unit
    rw = kv * (ax * ax + ay * ay)
    cw = kv * (bx * bx + by * by)
    return v * ax, v * ay, v * bx, v * by, -unit / v, rw, cw, 30.0 * (rw + cw + kv)


def flux(f, w, p, h, gx, gy):
    rho, m1, m2, m3, _ = f
    u = gx * w[0] + gy * w[1]
    return (rho * u, m1 * u + gx * p, m2 * u + gy * p, m3 * u, h * u)


def flux_planes(f, w, p, h):
    u3 = w[2]
    return (f[3], f[1] * u3, f[2] * u3, f[3] * u3 + p, h * u3)


def slope(x, at):
    return 8.0 * (at(x, 1) - at(x, -1)) - (at(x, 2) - at(x, -2))


def curve(x, at):
    return 16.0 * (at(x, 1) + at(x, -1)) - (at(x, 2) + at(x, -2))


def along(axis):
    return lambda x, o: turn(x, -o, axis)


def within(lane, start, size):
    return (lane >= start) & (lane < start + size)


def roll_by(x, shift, axis=1):
    size = x.shape[axis]
    return pltpu.roll(x, lax.rem(shift + 4 * size, size), axis)


def across(x):
    if x.shape[0] < LANES:
        x = jnp.concatenate([x, jnp.zeros((LANES - x.shape[0], LANES), jnp.float32)], axis=0)
    return x.T


def loop(count, body, start=None, unroll=1):
    if start is None:

        def step(n, _):
            body(n)
            return 0

        lax.fori_loop(0, count, step, 0, unroll=unroll)
        return None
    return lax.fori_loop(0, count, body, start, unroll=unroll)


def copy_all(pairs, sems, first=0):
    copies = [
        pltpu.make_async_copy(src, dst, sems.at[first + n]) for n, (src, dst) in enumerate(pairs)
    ]
    for copy in copies:
        copy.start()
    return copies


def state_pairs(fields, state, planes, rows):
    dens, mom, en, met, vol = fields
    return [
        (dens.at[0], state.at[0, 0:planes, rows]),
        (mom.at[0], state.at[1:4, 0:planes, rows]),
        (en.at[0], state.at[4, 0:planes, rows]),
        (met.at[0], state.at[0:4, planes, rows]),
        (vol.at[0], state.at[4, planes, rows]),
    ]


def wait_all(copies):
    for copy in copies:
        copy.wait()


def tile_stage(planes, load, mets, shift_i, shift_j, hold, done):
    kv = viscosity * unit
    fk, ws, acc = hold

    def spread(k):
        for s in range(2):
            vax, vay, vbx, vby, niv, rw, cw, tw = mets[s]
            x = [load(c, s, k) for c in range(CH)]
            w, p, h = point(x)
            fi, fj = flux(x, w, p, h, vax, vay), flux(x, w, p, h, vbx, vby)
            for c in range(CH):
                val = niv * (slope(fi[c], shift_i(0, c, s, k)) + slope(fj[c], shift_j))
                if c > 0:
                    v = w[c - 1]
                    val = val + (
                        rw * curve(v, shift_i(1, c - 1, s, k)) + cw * curve(v, shift_j) - tw * v
                    )
                    ws[c - 1, s, k] = v
                acc[c, s, k] = x[c] + val
            for c, v in enumerate(flux_planes(x, w, p, h)):
                fk[c, s, k] = v

    def gather(k):
        at = {o: lax.rem(k + o + planes, planes) for o in (-2, -1, 0, 1, 2)}
        for s in range(2):
            for c in range(CH):
                val = acc[c, s, k] - unit * slope(0, lambda _, o: fk[c, s, at[o]])
                if c > 0:
                    val = val + kv * curve(0, lambda _, o: ws[c - 1, s, at[o]])
                done(c, s, k, val)

    loop(planes, spread)
    loop(planes, gather)


def cut_kernel(halves, dens, mom, en, met, vol, placed, face, orient, send, own, *rest):
    edges, rest = rest[: -7 - (1 if halves == 2 else 2)], rest[-7 - (1 if halves == 2 else 2) :]
    held_send, held_own, *held_edges = rest[: 2 + len(edges)]
    state, packed, strips, sems, out_sems = rest[2 + len(edges) :]
    planes, rows = dens.shape[1], dens.shape[2]
    copies = copy_all(
        state_pairs((dens, mom, en, met, vol), state, planes, slice(None)), sems
    )
    block = placed[lax.axis_index("blk")]
    half = lax.axis_index("ij")
    row, lane = rows_of((64, LANES)), lanes_of((8, LANES))
    high_side = row % 8 < 4
    mirror = jnp.where(
        rows_of((LANES, LANES)) + lanes_of((LANES, LANES)) == rows - 1, 1.0, 0.0
    )
    flip = [jnp.where(orient[f, block] == 1, -1.0, 1.0) for f in range(2)]
    same = [jnp.where(face[f, block] == f, -1.0, 1.0) for f in range(2)]
    rising = [face[f, block] == 1 for f in range(2)]
    turned = jnp.where(high_side, flip[1], flip[0])
    facing = jnp.where(high_side, same[1], same[0])
    if rows < LANES:
        packed[...] = jnp.zeros(packed.shape, jnp.float32)
    wait_all(copies)

    def cut_ends(k):
        for c in range(CH):
            low, high = state[c, k, 0:4], state[c, k, rows - 4 : rows]
            if len(edges) == 1:
                held_edges[0][c, pl.ds(k * 4, 4)] = jnp.where(half == 0, high, low)
            else:
                held_edges[0][c, pl.ds(k * 4, 4)] = low
                held_edges[1][c, pl.ds(k * 4, 4)] = high

    loop(planes + 1, cut_ends)
    out = copy_all(list(zip(held_edges, edges)), out_sems, 2)

    def pack(r):
        for c in range(CH):
            packs = jnp.zeros((8, LANES), jnp.float32)
            for k in range(planes + 1):
                x = turn(state[c, k, pl.ds(r, 8)], 8 * k + 4, 1)
                packs = jnp.where(within(lane, 8 * k, 8), x, packs)
            packed[c, pl.ds(r, 8)] = packs

    chunks(rows // 8, pack)

    def orient_strip(c):
        strip = packed[c].T[0:64]
        held_own[c] = strip
        back = jnp.dot(
            strip,
            mirror,
            precision=lax.Precision.HIGHEST,
            preferred_element_type=jnp.float32,
        )
        moved = jnp.where(turned < 0.0, back, strip)
        sign = jnp.where(c < 2, turned, jnp.where(c < 4, facing, 1.0))
        moved = jnp.where(row >= planes * 8, moved * sign, moved)
        strips[pl.ds(pl.multiple_of(c * 64, 64), 64)] = moved

    loop(CH, orient_strip)
    out += copy_all([(held_own, own)], out_sems, 1)

    def put(n):
        k, e = n >> 2, n & 3
        at = (FIRST + n) * SENT
        low = k * 8 + 4 + jnp.where(rising[0], e, 3 - e)
        high = k * 8 + jnp.where(rising[1], 3 - e, e)
        held_send[pl.ds(at, CH)] = strips[pl.ds(low, CH, stride=64)]
        held_send[pl.ds(at + CH, CH)] = strips[pl.ds(high, CH, stride=64)]

    loop(DEPTH * (planes + 1), put, unroll=4)
    wait_all(out + copy_all([(held_send, send)], out_sems, 0))


def relay_kernel(
    halves, rows, planes, devices, route, got, send,
    held_got, held_send, below, above, signs, sems,
):
    arrive = copy_all([(got, held_got)], sems)
    me = lax.axis_index("blk") * halves + lax.axis_index("ij")
    is_field = (me >= FIRST) & (me < FIRST + DEPTH * planes)
    arrive[0].wait()

    def pass_on(slot):
        for f in range(2):
            code = route[2 * slot + f]
            partner, side, turned = code >> 2, (code >> 1) & 1, code & 1
            sign = jnp.where(turned == 1, -1.0, 1.0)

            def piece(h):
                h = jnp.where(turned == 1, halves - 1 - h, h)
                return held_got[pl.ds((partner * halves + h) * SENT + side * CH, CH)]

            pieces = [piece(h) for h in range(halves)]
            for half in range(halves):
                at = slot * halves + half
                held_send[pl.ds(at * PASSED + f * CH, CH)] = pieces[half]
                below[pl.ds((f * devices + at) * 8, CH)] = pieces[max(half - 1, 0)]
                above[pl.ds((f * devices + at) * 8, CH)] = pieces[min(half + 1, halves - 1)]
                signs[pl.ds(f * devices + at, 1)] = jnp.full((1, LANES), sign, jnp.float32)

    loop(devices // halves, pass_on, unroll=4)
    count = 2 * devices
    lane = lanes_of((count, LANES))
    half = rows_of((count, LANES)) % halves
    sign = signs[...]
    ends = jnp.zeros((count, LANES), jnp.float32)
    for c in range(CH):
        low, high = below[pl.ds(c, count, stride=8)], above[pl.ds(c, count, stride=8)]
        at = 4 * c
        low_wall = jnp.where(lane == at, turn(low, at - 1, 1), turn(low, at + 1, 1))
        high_wall = jnp.where(
            lane == at + 2, turn(high, at + 3 - rows, 1), turn(high, at + 5 - rows, 1)
        )
        if 1 <= c <= 3:
            low_wall = jnp.where(is_field, -sign * low_wall, low_wall)
            high_wall = jnp.where(is_field, sign * high_wall, high_wall)
        low = jnp.where(half == 0, low_wall, turn(low, at + 2 - rows, 1))
        high = jnp.where(half == halves - 1, high_wall, turn(high, at + 2, 1))
        ends = jnp.where(within(lane, at, 2), low, jnp.where(within(lane, at + 2, 2), high, ends))
    held_send[pl.ds(2 * CH, devices, stride=PASSED)] = ends[0:devices] + turn(
        ends[devices:], 4 * CH, 1
    )
    wait_all(copy_all([(held_send, send)], sems, 1))


def flux_chunk(get, mets, fi, w, fk, acc, r):
    rows = pl.ds(r, 8)
    vax, vay, vbx, vby, niv, rw, cw, tw = [mets[j, rows] for j in range(8)]
    at_j = along(1)
    for k in range(fi.shape[1]):
        f = [get(c, k, r) for c in range(CH)]
        wk, p, h = point(f)
        for c, x in enumerate(flux(f, wk, p, h, vax, vay)):
            fi[c, k, rows] = x
        for c in range(4):
            w[c, k, rows] = wk[c]
        fj = flux(f, wk, p, h, vbx, vby)
        for c in range(CH):
            val = niv * slope(fj[c], at_j)
            if c > 0:
                val = val + (cw * curve(wk[c - 1], at_j) - tw * wk[c - 1])
            acc[c, k, rows] = val
        for c, x in enumerate(flux_planes(f, wk, p, h)):
            fk[c, k, rows] = x


def sum_chunk(mets, fi, w, fk, acc, r, emit):
    planes = fi.shape[1]
    kv = viscosity * unit
    rows = pl.ds(r, 8)
    niv, rw = mets[4, rows], mets[5, rows]
    for c in range(CH):
        t = [fk[c, k, rows] for k in range(planes)]
        x = [w[c - 1, k, rows] for k in range(planes)] if c > 0 else None
        for k in range(planes):

            def near(v, o):
                return v[(k + o) % planes]

            def at_i(v, o):
                return v[pl.ds(r + o, 8)]

            val = acc[c, k, rows] + niv * slope(fi.at[c, k], at_i) - unit * slope(t, near)
            if c > 0:
                val = val + (rw * curve(w.at[c - 1, k], at_i) + kv * curve(x, near))
            emit(c, k, r, val)


def chunks(count, body):
    def step(n, _):
        body(pl.multiple_of(n * 8, 8))
        return 0

    lax.fori_loop(0, count, step, 0)


def pack_ends(arr, rows, scratch, planes):
    sub, lane = rows_of((8, LANES)), lanes_of((8, LANES))

    def first(k, packed):
        out = []
        for c in range(CH):
            low, high = arr[c, k, PAD - 4 : PAD + 4], arr[c, k, PAD + rows - 4 : PAD + rows + 4]
            x = roll_by(jnp.where(sub < 4, low, high), 8 * k + 4)
            out.append(jnp.where(within(lane, 8 * k, 8), x, packed[c]))
        return tuple(out)

    empty = jnp.zeros((8, LANES), jnp.float32)
    packed = loop(planes, first, (empty,) * CH)
    scratch[...] = across(jnp.concatenate(packed, axis=0))

    def second(k, packed):
        x = scratch[pl.ds(pl.multiple_of(8 * k, 8), 8)]
        return tuple(
            jnp.where(within(lane, 4 * k, 4), roll_by(x, 4 * k - (8 * c + 2)), packed[c])
            for c in range(CH)
        )

    return loop(planes, second, (empty,) * CH)


def at_walls(halves, arr, rows, planes, fields):
    half = lax.axis_index("ij")

    @pl.when(half == 0)
    def _():
        def low(k):
            sign = jnp.where(k < fields, -1.0, 1.0)
            for c in range(CH):
                for n in range(2):
                    x = arr[c, k, PAD + n : PAD + n + 1]
                    arr[c, k, PAD - 1 - n : PAD - n] = sign * x if 1 <= c <= 3 else x

        loop(planes, low)

    @pl.when(half == halves - 1)
    def _():
        def high(k):
            for c in range(CH):
                for n in range(2):
                    at = PAD + rows + n
                    arr[c, k, at : at + 1] = arr[c, k, PAD + rows - 1 - n : PAD + rows - n]

        loop(planes, high)


def first_kernel(
    halves, dens, mom, en, met, vol, below, above, placed, neighbour, face, orient,
    part, terms_out, ends_base, route,
    state, low, high, sec, mets, fi, w, fk, acc, ends, scratch, where_is, sems, out_sems,
):
    planes, rows = dens.shape[1], dens.shape[2]
    inside = slice(PAD, PAD + rows)
    pairs = state_pairs((dens, mom, en, met, vol), state, planes, inside)
    copies = copy_all(pairs + [(below, low), (above, high)], sems)
    blocks = placed.shape[0]

    def note(slot):
        where_is[placed[slot]] = slot

    def direct(slot):
        block = placed[slot]
        for f in range(2):
            partner = where_is[neighbour[f, block]]
            route[2 * slot + f] = partner * 4 + face[f, block] * 2 + orient[f, block]

    loop(blocks, note)
    loop(blocks, direct)
    wait_all(copies)
    half = lax.axis_index("ij")

    @pl.when(half > 0)
    def _():
        def fill(k):
            for c in range(CH):
                state[c, k, PAD - 4 : PAD] = low[c, pl.ds(4 * k, 4)]

        loop(planes + 1, fill)

    @pl.when(half < halves - 1)
    def _():
        def fill(k):
            for c in range(CH):
                state[c, k, PAD + rows : PAD + rows + 4] = high[c, pl.ds(4 * k, 4)]

        loop(planes + 1, fill)

    at_walls(halves, state, rows, planes + 1, planes)
    for c, x in enumerate(pack_ends(state, rows, scratch, planes + 1)):
        ends[c] = x
    out = copy_all([(ends, ends_base)], out_sems, 0)

    def get(c, k, r):
        return state[c, k, pl.ds(r, 8)]

    def fluxes(n):
        r = n + PAD - 8
        at = pl.ds(r, 8)
        for j, x in enumerate(metric_terms([state[c, planes, at] for c in range(CH)])):
            mets[j, at] = x
        flux_chunk(get, mets, fi, w, fk, acc, r)

    chunks(rows // 8 + 2, fluxes)
    out += copy_all([(mets.at[:, PAD - 8 : PAD + rows + 8], terms_out)], out_sems, 1)

    def emit(c, k, r, val):
        sec[c, k, pl.ds(r, 8)] = get(c, k, r) + val

    chunks(rows // 8 + 2, lambda n: sum_chunk(mets, fi, w, fk, acc, n + PAD - 8, emit))
    at_walls(halves, sec, rows, planes, planes)
    wait_all(out + copy_all([(sec.at[:, :, PAD - 8 : PAD + rows + 8], part)], out_sems, 2))


def second_kernel(
    dens, mom, en, met, vol, part, terms, out, ends_sec, inner,
    state, sec, full, mets, fi, w, fk, acc, packed, scratch, ends, strips, sems, out_sems,
):
    planes, rows = dens.shape[1], dens.shape[2]
    tall = slice(PAD - 8, PAD + rows + 8)
    early = copy_all([(part, sec.at[:, :, tall]), (terms, mets.at[:, tall])], sems)
    pairs = state_pairs((dens, mom, en, met, vol), state, planes, slice(None))
    late = copy_all(pairs, sems, 2)
    lane = lanes_of((8, LANES))
    wait_all(early)

    def get(c, k, r):
        return sec[c, k, pl.ds(r, 8)]

    chunks(rows // 8 + 2, lambda n: flux_chunk(get, mets, fi, w, fk, acc, n + PAD - 8))
    wait_all(late)

    def emit(c, k, r, val):
        at = pl.ds(r - PAD, 8)
        full[c, k, at] = 0.5 * (state[c, k, at] + (get(c, k, r) + val))

    def leave(n):
        at = pl.ds(n, 8)
        return pltpu.make_async_copy(full.at[:, :, at], out.at[:, :, at], out_sems.at[n // 8])

    def sums(n):
        sum_chunk(mets, fi, w, fk, acc, n + PAD, emit)
        leave(n).start()

    chunks(rows // 8, sums)

    for c, x in enumerate(pack_ends(sec, rows, scratch, planes)):
        ends[c] = x
    if rows < LANES:
        packed[...] = jnp.zeros(packed.shape, jnp.float32)

    def pack(n):
        for c in range(CH):
            x = state[c, planes, pl.ds(n, 8)]
            at = 8 * planes
            packs = jnp.where(lane < at + 4, turn(x, at + 6, 1), turn(x, at + 2, 1))
            for k in range(planes):
                x = sec[c, k, pl.ds(n + PAD, 8)]
                at = 8 * k
                packs = jnp.where(within(lane, at, 4), turn(x, at + 6, 1), packs)
                packs = jnp.where(within(lane, at + 4, 4), turn(x, at + 2, 1), packs)
            packed[c, pl.ds(n, 8)] = packs

    chunks(rows // 8, pack)

    def flip(c):
        strips[c] = packed[c].T[0:64]

    loop(CH, flip)
    last = copy_all([(ends, ends_sec), (strips, inner)], out_sems, rows // 8)
    chunks(rows // 8, lambda n: leave(n).wait())
    wait_all(last)


def beyond(packed, f, k, rows):
    base = 28 * f + 4 * k
    low = roll_by(packed, LANES - 2 - base)
    top = rows % LANES
    high = low if top == 0 else roll_by(packed, top - 2 - base)
    lane = lanes_of(packed.shape)

    def at(x, o):
        if o < 0:
            x = jnp.where(lane >= LANES + o, low, x)
        else:
            x = jnp.where(within(lane, top, o), high, x)
        return turn(x, -o, 1)

    return at


def last_kernel(
    halves, rows, planes, own_at, ends_base_at, ends_sec_at, inner_at, got_at, out,
    next_dens, next_mom, next_en,
    own, ends_base, ends_sec, inner, got, base, sec, fk, ws, acc, turned, back, full, sems,
):
    late = copy_all([(inner_at, inner), (ends_sec_at, ends_sec), (out, full)], sems)
    early = copy_all([(got_at, got), (own_at, own), (ends_base_at, ends_base)], sems, 3)
    half = lax.axis_index("ij")
    low_wall, high_wall = half == 0, half == halves - 1
    sub, lane = rows_of((8, LANES)), lanes_of((8, LANES))

    def mix(f, mine, others):
        return jnp.where((sub < 4) == (f == 1), mine, others)

    wait_all(early)

    def gather(k, others):
        start = DEPTH * k * PASSED

        def ghost(row, f):
            x = got[pl.ds(start + row, 8, stride=PASSED)]
            return x if f == 1 else turn(x, 4, 0)

        others = list(others)
        for f in range(2):
            arrived = ghost(2 * CH, f)
            to = 28 * f + 4 * k
            for c in range(CH):
                mine = own[c, pl.ds(pl.multiple_of(k * 8, 8), 8)]
                base[c, f, k] = mix(f, mine, ghost(f * CH + c, f))
                moved = roll_by(arrived, to - 4 * CH * f - 4 * c)
                others[c] = jnp.where(within(lane, to, 4), moved, others[c])
        return tuple(others)

    empty = jnp.zeros((8, LANES), jnp.float32)
    others = loop(planes + 1, gather, (empty,) * CH)
    low_lanes = lane < 28
    twice = [jnp.where(low_lanes, ends_base[c], turn(ends_base[c], 28, 1)) for c in range(CH)]
    ends = [jnp.where(low_lanes == (sub >= 4), twice[c], others[c]) for c in range(CH)]
    slot = jnp.where(low_lanes, lane, lane - 28)

    def spread(k, kept):
        shift, hit = 4 * (k - planes), within(slot, 4 * k, 4)
        return tuple((x, jnp.where(hit, roll_by(x, shift), y)) for x, y in kept)

    kept = metric_terms(ends)[0:5] + metric_terms(ends)[6:7] + metric_terms(twice)[2:4]
    kept = loop(planes, spread, tuple((x, x) for x in kept))
    vax, vay, vbx, vby, niv, cw, *wrapped = [y for _, y in kept]

    def keep(c, f, k, val):
        sec[c, f, k] = val

    def stage(held, ends, gx, gy):
        mets = [metric_terms([held[c, f, planes] for c in range(CH)]) for f in range(2)]
        w, p, h = point(ends)
        rims = (flux(ends, w, p, h, gx, gy), w)
        tile_stage(
            planes,
            lambda c, f, k: held[c, f, k],
            mets,
            lambda kind, c, f, k: beyond(rims[kind][c], f, k, rows),
            along(0),
            (fk, ws, acc),
            keep,
        )

    stage(base, ends, vax, vay)
    wait_all(late[0:2])

    def move(k, source):
        for c in range(CH):
            mine = inner[c, pl.ds(pl.multiple_of(k * 8, 8), 8)]
            for f in range(2):
                sec[c, f, k] = mix(f, mine, turn(source[c, f, k], 2 if f == 1 else -2, 0))

    loop(planes, lambda k: move(k, sec))
    move(jnp.int32(planes), base)

    def shifted(x):
        return jnp.where(low_lanes, turn(x, -2, 0), turn(x, 2, 0))

    w1, p1, h1 = point(ends)
    w0, p0, h0 = point(twice)
    new, old = flux(ends, w1, p1, h1, vbx, vby), flux(twice, w0, p0, h0, *wrapped)
    at_j = along(0)
    touched = within(sub, jnp.where(low_lanes, 4, 2), 2)
    second = []
    for c in range(CH):
        add = niv * slope(new[c] - old[c], at_j)
        if c > 0:
            add = add + cw * curve(w1[c - 1] - w0[c - 1], at_j)
        x = jnp.where(low_lanes, ends_sec[c], turn(ends_sec[c], 28, 1))
        second.append(shifted(x + jnp.where(touched, add, 0.0)))
    walled = low_wall | high_wall

    def reflect(k, second):
        second = list(second)
        for f in range(2):
            to = 28 * f + 4 * k
            first = jnp.where(walled, jnp.where(low_wall, to, to + 2), -8)
            shift = jnp.where(low_wall, to - 1, to + 3 - rows)
            for c in range(CH):
                x = sec[c, f, k]
                one, two = roll_by(x, shift), roll_by(x, shift + 2)
                if 1 <= c <= 3:
                    sign = jnp.where(low_wall, -1.0, 1.0)
                    one, two = sign * one, sign * two
                x = jnp.where(lane == first, one, second[c])
                second[c] = jnp.where(lane == first + 1, two, x)
        return tuple(second)

    second = loop(planes, reflect, tuple(second))
    stage(sec, second, shifted(vax), shifted(vay))

    per = LANES // 8

    def finish(k):
        for c in range(CH):
            x = jnp.where(sub < 4, turn(sec[c, 1, k], -2, 0), turn(sec[c, 0, k], 2, 0))
            at = pl.multiple_of((c * planes + k) * 8, 8)
            mine = own[c, pl.ds(pl.multiple_of(k * 8, 8), 8)]
            turned[pl.ds(at, 8)] = 0.5 * (mine + x)

    loop(planes, finish)

    def flip(n):
        back[n] = turned[pl.ds(pl.multiple_of(n * LANES, LANES), LANES)].T

    loop(turned.shape[0] // LANES, flip)
    late[2].wait()
    inside = within(lane, 4, LANES - 8)
    copies = []
    for c in range(CH):

        def merge(k, c=c):
            index = c * planes + k
            which, place = index // per, lax.rem(index, per)
            for r in range(0, rows, 8):
                moved = roll_by(back[which, r : r + 8], LANES - 4 - 8 * place)
                full[c, k, r : r + 8] = jnp.where(inside, full[c, k, r : r + 8], moved)

        loop(planes, merge)
        dst = next_dens.at[0] if c == 0 else next_en.at[0] if c == 4 else next_mom.at[0, c - 1]
        copies.append(pltpu.make_async_copy(full.at[c], dst, sems.at[6 + c]))
        copies[-1].start()
    for copy in copies:
        copy.wait()


def local(mesh_shape, density, momentum, energy, metrics, volume, placed, neighbour, face, orient):
    halves = mesh_shape["ij"]
    blocks = mesh_shape["blk"]
    devices = blocks * halves
    planes, rows = density.shape[1], density.shape[2]
    every = planes + 1
    fields = (density, momentum, energy, metrics, volume)
    neighbour, face, orient = neighbour.T, face.T, orient.T
    smem = pl.BlockSpec(memory_space=pltpu.SMEM)
    hbm = pl.BlockSpec(memory_space=pltpu.HBM)

    def call(kernel, name, outs, ins, out_specs, scratch, cost=None):
        return pl.pallas_call(
            kernel,
            out_shape=outs,
            in_specs=ins,
            out_specs=out_specs,
            scratch_shapes=scratch,
            compiler_params=pltpu.CompilerParams(vmem_limit_bytes=VMEM_LIMIT),
            cost_estimate=cost,
            name=name,
        )

    def shape(*dims):
        return jax.ShapeDtypeStruct(dims, jnp.float32)

    def vmem(x):
        return pltpu.VMEM(x.shape, jnp.float32)

    def sems(count):
        return pltpu.SemaphoreType.DMA((count,))

    sent, passed = shape(devices * SENT, LANES), shape(devices * PASSED, LANES)
    strip, rim = shape(CH, 64, LANES), shape(CH, 8, LANES)
    edge = shape(CH, 4 * every, LANES)
    edges = 1 if halves == 2 else 2
    square = shape(LANES, LANES)
    state = shape(CH, every, rows, LANES)
    outs = [sent, strip] + [edge] * edges
    to_send, own, *halo = call(
        functools.partial(cut_kernel, halves),
        "cut",
        outs,
        [hbm] * 5 + [smem] * 3,
        [hbm] * (2 + edges),
        [vmem(x) for x in outs]
        + [
            vmem(state),
            pltpu.VMEM((CH, LANES, LANES), jnp.float32),
            pltpu.VMEM((CH * 64, LANES), jnp.float32),
            sems(5),
            sems(2 + edges),
        ],
    )(*fields, placed, face, orient)

    def swap(x):
        x = x.reshape(devices, x.shape[0] // devices, 1, LANES)
        x = lax.all_to_all(x, ("blk", "ij"), 0, 0, tiled=True)
        return x.reshape(x.shape[0] * x.shape[1], LANES)

    if edges == 1:
        below = above = lax.ppermute(halo[0], "ij", [(0, 1), (1, 0)])
    else:
        below = lax.ppermute(halo[1], "ij", [(i, i + 1) for i in range(halves - 1)])
        above = lax.ppermute(halo[0], "ij", [(i + 1, i) for i in range(halves - 1)])
    got = swap(to_send)

    tall = rows + 2 * PAD
    block = shape(CH, planes, rows, LANES)
    high = shape(CH, planes, rows + 16, LANES)
    terms = shape(8, rows + 16, LANES)
    padded = shape(CH, planes, tall, LANES)
    stage = [
        vmem(shape(8, tall, LANES)),
        vmem(padded),
        vmem(shape(4, planes, tall, LANES)),
        vmem(padded),
        vmem(padded),
    ]
    work = planes * rows * LANES
    cost = pl.CostEstimate(flops=300 * work, bytes_accessed=150 * work, transcendentals=work)
    part, kept, ends_base, route = call(
        functools.partial(first_kernel, halves),
        "first_section",
        [high, terms, rim, jax.ShapeDtypeStruct((2 * blocks,), jnp.int32)],
        [hbm] * 7 + [smem] * 4,
        [hbm] * 3 + [smem],
        [vmem(shape(CH, every, tall, LANES)), vmem(edge), vmem(edge), vmem(padded)]
        + stage
        + [vmem(rim), vmem(square), pltpu.SMEM((blocks,), jnp.int32), sems(7), sems(3)],
        cost,
    )(*fields, below, above, placed, neighbour, face, orient)
    relayed = call(
        functools.partial(relay_kernel, halves, rows, planes, devices),
        "relay",
        passed,
        [smem, hbm],
        hbm,
        [
            vmem(sent),
            vmem(passed),
            vmem(shape(devices * 16, LANES)),
            vmem(shape(devices * 16, LANES)),
            vmem(shape(devices * 2, LANES)),
            sems(2),
        ],
    )(route, got)
    ghosts = swap(relayed)
    out, ends_sec, inner = call(
        second_kernel,
        "second_section",
        [block, rim, strip],
        [hbm] * 7,
        [hbm] * 3,
        [vmem(state), vmem(padded), vmem(block)]
        + stage
        + [
            pltpu.VMEM((CH, LANES, LANES), jnp.float32),
            vmem(square),
            vmem(rim),
            vmem(strip),
            sems(7),
            sems(rows // 8 + 2),
        ],
        cost,
    )(*fields, part, kept)
    tiles = shape(CH, 2, every, 8, LANES)
    flat = -(-CH * planes * 8 // LANES)
    return call(
        functools.partial(last_kernel, halves, rows, planes),
        "strips",
        [shape(*density.shape), shape(*momentum.shape), shape(*energy.shape)],
        [hbm] * 6,
        [hbm] * 3,
        [vmem(x) for x in (strip, rim, rim, strip, passed)]
        + [vmem(tiles)] * 5
        + [
            vmem(shape(flat * LANES, LANES)),
            vmem(shape(flat, LANES, LANES)),
            vmem(block),
            sems(6 + CH),
        ],
    )(own, ends_base, ends_sec, inner, ghosts, out)


def solution(mesh):
    return jax.shard_map(
        functools.partial(local, dict(mesh.shape)),
        mesh=mesh,
        in_specs=(
            P("blk", None, "ij", None),
            P("blk", None, None, "ij", None),
            P("blk", None, "ij", None),
            P("blk", None, "ij", None),
            P("blk", "ij", None),
            P(),
            P(),
            P(),
            P(),
        ),
        out_specs=(
            P("blk", None, "ij", None),
            P("blk", None, None, "ij", None),
            P("blk", None, "ij", None),
        ),
        check_vma=False,
    )
```

time: 66.6 us -> 70.2 us (1.054)
  Pallas kernels: 44.4 us -> 48.6 us
    pallas_call x4, Pallas kernels: 34.8 us -> 38.3 us  [the longest x1 14.9 us: local(): call(second_kernel, 'second_section', [block, rim, strip], [hbm] * 7, [hb...]
    unnamed x8 -> x6, local copies, waits for them, and re-layouts: 1.99 us -> 1.96 us
  transfers between devices with their start and end apart: 3 -> 3, of which waited for: 2 -> 1; matrix products, arithmetic and copies ran while one was open for 0% -> 0% of each run, Pallas kernels for 40% -> 42%
where the time goes in v3:
time: 70.2 us; the launch traced here: 69.8 us
  Pallas kernels  48.6 us (69%)
  starting transfers between devices  14.5 us (21%)
  waiting for transfers between devices  4.06 us (6%)
  local copies, waits for them, and re-layouts  1.96 us (3%)
  between operations  0.71 us (1%)
    pallas_call x1, Pallas kernels, local(): call(second_kernel, 'second_section', [block, rim, strip], [hbm] * 7, [hb...  14.9 us
    pallas_call x1, Pallas kernels, local(): call(functools.partial(first_kernel, halves), 'first_section', [high, ter...  14.5 us
    all_to_all x2, starting transfers between devices, swap(): x = lax.all_to_all(x, ('blk', 'ij'), 0, 0, tiled=True)  12.6 us
    pallas_call x1, Pallas kernels, local(): call(functools.partial(last_kernel, halves, rows, planes), 'strips', [sha...  10.3 us
    pallas_call x1, Pallas kernels, local(): call(functools.partial(cut_kernel, halves), 'cut', outs, [hbm] * 5 + [sme...  6.08 us
    ppermute x1, waiting for transfers between devices, local(): below = above = lax.ppermute(halo[0], 'ij', [(0, 1), (1, 0)])  4.05 us
    pallas_call x1, Pallas kernels, local(): call(functools.partial(relay_kernel, halves, rows, planes, devices), 'rel...  2.83 us
    unnamed x6, local copies, waits for them, and re-layouts  1.96 us
  transfers between devices with their start and end apart: 3, of which 1 were waited for; matrix products, arithmetic and copies ran while one was open for 0% of the time, Pallas kernels for 42%

profile of v3, /device:TPU:0, one launch (start us, length us, event | category | flops | bytes accessed | tf_op | source)
XLA Modules:
  0.0 69.8 jit_solution(12100584336121894606)
XLA Ops:
  0.6 6.1 %cut.1 = (f32[320,128]{1,0:T(8,128)}, f32[5,64,128]{2,1,0:T(8,128)}, f32[5,28,128]{2,1,0:T(8,128)}) custom-call(f32[1,6,128,128]{3,2,1,0:T(8,128)} %dens.5, f32[1,3,6,128,128]{4,3,2,1,0:T(8,128)} %mom.5, f32[1,6,128,128]{3,2,1,0:T(8,128)} %en.5, f32[1,4,128,128]{3,2,1,0:T(8,128)} %met.5, f32[1,128,128]{2,1,0:T(8,128)} %vol.5, s32[16]{0:T(128)} %placed.3, ...), custom_call_target="tpu_custom_call" | custom-call | tf_op jit(solution)/shard_map/cut/pallas_call | solution.py:725
  6.7 7.3 %all-to-all-start = ((f32[32,10,1,128]{3,2,1,0:T(1,128)}), f32[32,10,1,128]{3,2,1,0:T(1,128)S(1)}, u32[]{:S(2)}, u32[]{:S(2)}) async-start(f32[32,10,1,128]{3,2,1,0:T(1,128)} %bitcast.10), calls=%async_computation | async-start | bytes 327680 | tf_op jit(solution)/shard_map/all_to_all | solution.py:743
  14.0 1.8 %collective-permute-start = (f32[5,28,128]{2,1,0:T(8,128)}, f32[5,28,128]{2,1,0:T(8,128)S(1)}, u32[]{:S(2)}, u32[]{:S(2)}) collective-permute-start(f32[5,28,128]{2,1,0:T(8,128)} %get-tuple-element.14), channel_id=1, source_target_pairs={{0,1},{1,0},{2,3},{3,2},{4,5},{5,4},{6,7},{7,6},{8,9},{9,8},{10,11... | collective-permute-start | bytes 215048 | tf_op jit(solution)/shard_map/ppermute | solution.py:747
  15.9 4.1 %collective-permute-done.below.above = f32[5,28,128]{2,1,0:T(8,128)S(1)} collective-permute-done((f32[5,28,128]{2,1,0:T(8,128)}, f32[5,28,128]{2,1,0:T(8,128)S(1)}, u32[]{:S(2)}, u32[]{:S(2)}) %collective-permute-start) | collective-permute-done | bytes 71712 | tf_op jit(solution)/shard_map/ppermute | solution.py:747
  19.9 0.0 copy-start.2
  19.9 0.6 copy-done.2
  20.5 14.5 %first_section.1 = (f32[5,6,144,128]{3,2,1,0:T(8,128)}, f32[8,144,128]{2,1,0:T(8,128)}, f32[5,8,128]{2,1,0:T(8,128)}, s32[32]{0:T(128)}) custom-call(f32[1,6,128,128]{3,2,1,0:T(8,128)} %dens.5, f32[1,3,6,128,128]{4,3,2,1,0:T(8,128)} %mom.5, f32[1,6,128,128]{3,2,1,0:T(8,128)} %en.5, f32[1,4,128,128]{3,2,1,0:T(8,128)} %met.5, f32[1,128,128]{2,1,0:T(8,128)} %vol.5, ...), custom_call_target="tpu_custom_call" | custom-call | flops 29491200 | bytes 14745600 | tf_op jit(solution)/shard_map/first_section/pallas_call | solution.py:767
  35.0 0.0 all-to-all-done
  35.0 0.0 copy-start.1
  35.0 0.7 copy-done.1
  35.7 2.8 %relay.1 = f32[352,128]{1,0:T(8,128)} custom-call(s32[32]{0:T(128)} %get-tuple-element.20.route, f32[320,128]{1,0:T(8,128)} %bitcast.9), custom_call_target="tpu_custom_call" | custom-call | tf_op jit(solution)/shard_map/relay/pallas_call | solution.py:778
  38.5 5.3 %all-to-all-start.1 = ((f32[32,11,1,128]{3,2,1,0:T(1,128)}), f32[32,11,1,128]{3,2,1,0:T(1,128)S(1)}, u32[]{:S(2)}, u32[]{:S(2)}) async-start(f32[32,11,1,128]{3,2,1,0:T(1,128)} %bitcast.8), calls=%async_computation.1 | async-start | bytes 360448 | tf_op jit(solution)/shard_map/all_to_all | solution.py:743
  43.9 14.9 %second_section.1 = (f32[5,6,128,128]{3,2,1,0:T(8,128)}, f32[5,8,128]{2,1,0:T(8,128)}, f32[5,64,128]{2,1,0:T(8,128)}) custom-call(f32[1,6,128,128]{3,2,1,0:T(8,128)} %dens.5, f32[1,3,6,128,128]{4,3,2,1,0:T(8,128)} %mom.5, f32[1,6,128,128]{3,2,1,0:T(8,128)} %en.5, f32[1,4,128,128]{3,2,1,0:T(8,128)} %met.5, f32[1,128,128]{2,1,0:T(8,128)} %vol.5, ...), custom_call_target="tpu_custom_call" | custom-call | flops 29491200 | bytes 14745600 | tf_op jit(solution)/shard_map/second_section/pallas_call | solution.py:794
  58.8 0.0 all-to-all-done.1
  58.8 0.0 copy-start
  58.8 0.7 copy-done
  59.5 10.3 %strips.1 = (f32[1,6,128,128]{3,2,1,0:T(8,128)}, f32[1,3,6,128,128]{4,3,2,1,0:T(8,128)}, f32[1,6,128,128]{3,2,1,0:T(8,128)}) custom-call(f32[5,64,128]{2,1,0:T(8,128)} %get-tuple-element.13.own_at, f32[5,8,128]{2,1,0:T(8,128)} %get-tuple-element.15.ends_base_at, f32[5,8,128]{2,1,0:T(8,128)} %get-tuple-element.18.ends_sec_at, ...), custom_call_target="tpu_custom_call" | custom-call | tf_op jit(solution)/shard_map/strips/pallas_call | solution.py:814
Async XLA Ops:
  6.7 28.3 %all-to-all-start = ((f32[32,10,1,128]{3,2,1,0:T(1,128)}), f32[32,10,1,128]{3,2,1,0:T(1,128)S(1)}, u32[]{:S(2)}, u32[]{:S(2)}) async-start(f32[32,10,1,128]{3,2,1,0:T(1,128)} %bitcast.10), calls=%async_computation | async-start | bytes 327680 | tf_op jit(solution)/shard_map/all_to_all | solution.py:743
  14.0 5.9 %collective-permute-start = (f32[5,28,128]{2,1,0:T(8,128)}, f32[5,28,128]{2,1,0:T(8,128)S(1)}, u32[]{:S(2)}, u32[]{:S(2)}) collective-permute-start(f32[5,28,128]{2,1,0:T(8,128)} %get-tuple-element.14), channel_id=1, source_target_pairs={{0,1},{1,0},{2,3},{3,2},{4,5},{5,4},{6,7},{7,6},{8,9},{9,8},{10,11... | collective-permute-start | bytes 215048 | tf_op jit(solution)/shard_map/ppermute | solution.py:747
  19.9 0.6 copy-start.2
  35.0 0.7 copy-start.1
  38.5 20.3 %all-to-all-start.1 = ((f32[32,11,1,128]{3,2,1,0:T(1,128)}), f32[32,11,1,128]{3,2,1,0:T(1,128)S(1)}, u32[]{:S(2)}, u32[]{:S(2)}) async-start(f32[32,11,1,128]{3,2,1,0:T(1,128)} %bitcast.8), calls=%async_computation.1 | async-start | bytes 360448 | tf_op jit(solution)/shard_map/all_to_all | solution.py:743
  58.8 0.7 copy-start

commit v4 on v3

--- a/solution.py
+++ b/solution.py
@@ -13,10 +13,11 @@
 unit = time_step / 12.0
 
 LANES = 128
-PAD = 16
+PAD = 8
+PIECES = 4
 DEPTH = 4
 CH = 5
-VMEM_LIMIT = 63 * 1024 * 1024
+VMEM_MIB = 63
 SENT = 2 * CH
 PASSED = 2 * CH + 1
 FIRST = 4
@@ -90,16 +91,12 @@
     return x.T
 
 
-def loop(count, body, start=None, unroll=1):
-    if start is None:
-
-        def step(n, _):
-            body(n)
-            return 0
-
-        lax.fori_loop(0, count, step, 0, unroll=unroll)
-        return None
-    return lax.fori_loop(0, count, body, start, unroll=unroll)
+def loop(count, body, unroll=1):
+    def step(n, _):
+        body(n)
+        return 0
+
+    lax.fori_loop(0, count, step, 0, unroll=unroll)
 
 
 def copy_all(pairs, sems, first=0):
@@ -111,15 +108,31 @@
     return copies
 
 
-def state_pairs(fields, state, planes, rows):
+def state_pairs(fields, state, planes, start, size):
     dens, mom, en, met, vol = fields
+    at = pl.ds(start, size)
     return [
-        (dens.at[0], state.at[0, 0:planes, rows]),
-        (mom.at[0], state.at[1:4, 0:planes, rows]),
-        (en.at[0], state.at[4, 0:planes, rows]),
-        (met.at[0], state.at[0:4, planes, rows]),
-        (vol.at[0], state.at[4, planes, rows]),
+        (dens.at[0, :, at], state.at[0, 0:planes, at]),
+        (mom.at[0, :, :, at], state.at[1:4, 0:planes, at]),
+        (en.at[0, :, at], state.at[4, 0:planes, at]),
+        (met.at[0, :, at], state.at[0:4, planes, at]),
+        (vol.at[0, at], state.at[4, planes, at]),
     ]
+
+
+def arrive_in_pieces(fields, state, sems):
+    planes, rows = fields[0].shape[1], fields[0].shape[2]
+    size = max(8, rows // PIECES)
+    for n in range(rows // size):
+        copy_all(state_pairs(fields, state, planes, n * size, size), sems, 5 * n)
+
+    def expect(start):
+        @pl.when(lax.rem(start, size) == 0)
+        def _():
+            for n, (src, dst) in enumerate(state_pairs(fields, state, planes, start, size)):
+                pltpu.make_async_copy(src, dst, sems.at[5 * (start // size) + n]).wait()
+
+    return expect
 
 
 def wait_all(copies):
@@ -158,8 +171,8 @@
                     val = val + kv * curve(0, lambda _, o: ws[c - 1, s, at[o]])
                 done(c, s, k, val)
 
-    loop(planes, spread)
-    loop(planes, gather)
+    loop(planes, spread, unroll=2)
+    loop(planes, gather, unroll=2)
 
 
 def cut_kernel(halves, dens, mom, en, met, vol, placed, face, orient, send, own, *rest):
@@ -167,9 +180,7 @@
     held_send, held_own, *held_edges = rest[: 2 + len(edges)]
     state, packed, strips, sems, out_sems = rest[2 + len(edges) :]
     planes, rows = dens.shape[1], dens.shape[2]
-    copies = copy_all(
-        state_pairs((dens, mom, en, met, vol), state, planes, slice(None)), sems
-    )
+    expect = arrive_in_pieces((dens, mom, en, met, vol), state, sems)
     block = placed[lax.axis_index("blk")]
     half = lax.axis_index("ij")
     row, lane = rows_of((64, LANES)), lanes_of((8, LANES))
@@ -184,21 +195,8 @@
     facing = jnp.where(high_side, same[1], same[0])
     if rows < LANES:
         packed[...] = jnp.zeros(packed.shape, jnp.float32)
-    wait_all(copies)
-
-    def cut_ends(k):
-        for c in range(CH):
-            low, high = state[c, k, 0:4], state[c, k, rows - 4 : rows]
-            if len(edges) == 1:
-                held_edges[0][c, pl.ds(k * 4, 4)] = jnp.where(half == 0, high, low)
-            else:
-                held_edges[0][c, pl.ds(k * 4, 4)] = low
-                held_edges[1][c, pl.ds(k * 4, 4)] = high
-
-    loop(planes + 1, cut_ends)
-    out = copy_all(list(zip(held_edges, edges)), out_sems, 2)
-
     def pack(r):
+        expect(r)
         for c in range(CH):
             packs = jnp.zeros((8, LANES), jnp.float32)
             for k in range(planes + 1):
@@ -207,6 +205,19 @@
             packed[c, pl.ds(r, 8)] = packs
 
     chunks(rows // 8, pack)
+
+    def cut_ends(k):
+        for c in range(CH):
+            low, high = state[c, k, 0:4], state[c, k, rows - 4 : rows]
+            if len(edges) == 1:
+                held_edges[0][c, k * 4 : k * 4 + 4] = jnp.where(half == 0, high, low)
+            else:
+                held_edges[0][c, k * 4 : k * 4 + 4] = low
+                held_edges[1][c, k * 4 : k * 4 + 4] = high
+
+    for k in range(planes + 1):
+        cut_ends(k)
+    out = copy_all(list(zip(held_edges, edges)), out_sems, 2)
 
     def orient_strip(c):
         strip = packed[c].T[0:64]
@@ -238,13 +249,12 @@
 
 
 def relay_kernel(
-    halves, rows, planes, devices, route, got, send,
-    held_got, held_send, below, above, signs, sems,
+    halves, rows, planes, devices, route, halo, held_got, send,
+    held_send, below, above, signs, sems,
 ):
-    arrive = copy_all([(got, held_got)], sems)
+    del halo
     me = lax.axis_index("blk") * halves + lax.axis_index("ij")
     is_field = (me >= FIRST) & (me < FIRST + DEPTH * planes)
-    arrive[0].wait()
 
     def pass_on(slot):
         for f in range(2):
@@ -286,7 +296,7 @@
     held_send[pl.ds(2 * CH, devices, stride=PASSED)] = ends[0:devices] + turn(
         ends[devices:], 4 * CH, 1
     )
-    wait_all(copy_all([(held_send, send)], sems, 1))
+    wait_all(copy_all([(held_send, send)], sems))
 
 
 def flux_chunk(get, mets, fi, w, fk, acc, r):
@@ -340,65 +350,12 @@
     lax.fori_loop(0, count, step, 0)
 
 
-def pack_ends(arr, rows, scratch, planes):
-    sub, lane = rows_of((8, LANES)), lanes_of((8, LANES))
-
-    def first(k, packed):
-        out = []
-        for c in range(CH):
-            low, high = arr[c, k, PAD - 4 : PAD + 4], arr[c, k, PAD + rows - 4 : PAD + rows + 4]
-            x = roll_by(jnp.where(sub < 4, low, high), 8 * k + 4)
-            out.append(jnp.where(within(lane, 8 * k, 8), x, packed[c]))
-        return tuple(out)
-
-    empty = jnp.zeros((8, LANES), jnp.float32)
-    packed = loop(planes, first, (empty,) * CH)
-    scratch[...] = across(jnp.concatenate(packed, axis=0))
-
-    def second(k, packed):
-        x = scratch[pl.ds(pl.multiple_of(8 * k, 8), 8)]
-        return tuple(
-            jnp.where(within(lane, 4 * k, 4), roll_by(x, 4 * k - (8 * c + 2)), packed[c])
-            for c in range(CH)
-        )
-
-    return loop(planes, second, (empty,) * CH)
-
-
-def at_walls(halves, arr, rows, planes, fields):
-    half = lax.axis_index("ij")
-
-    @pl.when(half == 0)
-    def _():
-        def low(k):
-            sign = jnp.where(k < fields, -1.0, 1.0)
-            for c in range(CH):
-                for n in range(2):
-                    x = arr[c, k, PAD + n : PAD + n + 1]
-                    arr[c, k, PAD - 1 - n : PAD - n] = sign * x if 1 <= c <= 3 else x
-
-        loop(planes, low)
-
-    @pl.when(half == halves - 1)
-    def _():
-        def high(k):
-            for c in range(CH):
-                for n in range(2):
-                    at = PAD + rows + n
-                    arr[c, k, at : at + 1] = arr[c, k, PAD + rows - 1 - n : PAD + rows - n]
-
-        loop(planes, high)
-
-
 def first_kernel(
-    halves, dens, mom, en, met, vol, below, above, placed, neighbour, face, orient,
-    part, terms_out, ends_base, route,
-    state, low, high, sec, mets, fi, w, fk, acc, ends, scratch, where_is, sems, out_sems,
+    dens, mom, en, met, vol, placed, neighbour, face, orient, part, route,
+    state, full, mets, fi, w, fk, acc, where_is, sems, out_sems,
 ):
     planes, rows = dens.shape[1], dens.shape[2]
-    inside = slice(PAD, PAD + rows)
-    pairs = state_pairs((dens, mom, en, met, vol), state, planes, inside)
-    copies = copy_all(pairs + [(below, low), (above, high)], sems)
+    expect = arrive_in_pieces((dens, mom, en, met, vol), state, sems)
     blocks = placed.shape[0]
 
     def note(slot):
@@ -410,87 +367,147 @@
             partner = where_is[neighbour[f, block]]
             route[2 * slot + f] = partner * 4 + face[f, block] * 2 + orient[f, block]
 
-    loop(blocks, note)
-    loop(blocks, direct)
-    wait_all(copies)
-    half = lax.axis_index("ij")
-
-    @pl.when(half > 0)
-    def _():
-        def fill(k):
-            for c in range(CH):
-                state[c, k, PAD - 4 : PAD] = low[c, pl.ds(4 * k, 4)]
-
-        loop(planes + 1, fill)
-
-    @pl.when(half < halves - 1)
-    def _():
-        def fill(k):
-            for c in range(CH):
-                state[c, k, PAD + rows : PAD + rows + 4] = high[c, pl.ds(4 * k, 4)]
-
-        loop(planes + 1, fill)
-
-    at_walls(halves, state, rows, planes + 1, planes)
-    for c, x in enumerate(pack_ends(state, rows, scratch, planes + 1)):
-        ends[c] = x
-    out = copy_all([(ends, ends_base)], out_sems, 0)
+    loop(blocks, note, unroll=8)
+    loop(blocks, direct, unroll=4)
 
     def get(c, k, r):
-        return state[c, k, pl.ds(r, 8)]
+        return state[c, k, pl.ds(r - PAD, 8)]
 
     def fluxes(n):
-        r = n + PAD - 8
-        at = pl.ds(r, 8)
-        for j, x in enumerate(metric_terms([state[c, planes, at] for c in range(CH)])):
-            mets[j, at] = x
-        flux_chunk(get, mets, fi, w, fk, acc, r)
-
-    chunks(rows // 8 + 2, fluxes)
-    out += copy_all([(mets.at[:, PAD - 8 : PAD + rows + 8], terms_out)], out_sems, 1)
+        expect(n)
+        m = [state[c, planes, pl.ds(n, 8)] for c in range(CH)]
+        for j, x in enumerate(metric_terms(m)):
+            mets[j, pl.ds(n + PAD, 8)] = x
+        flux_chunk(get, mets, fi, w, fk, acc, n + PAD)
 
     def emit(c, k, r, val):
-        sec[c, k, pl.ds(r, 8)] = get(c, k, r) + val
-
-    chunks(rows // 8 + 2, lambda n: sum_chunk(mets, fi, w, fk, acc, n + PAD - 8, emit))
-    at_walls(halves, sec, rows, planes, planes)
-    wait_all(out + copy_all([(sec.at[:, :, PAD - 8 : PAD + rows + 8], part)], out_sems, 2))
-
-
-def second_kernel(
-    dens, mom, en, met, vol, part, terms, out, ends_sec, inner,
-    state, sec, full, mets, fi, w, fk, acc, packed, scratch, ends, strips, sems, out_sems,
-):
-    planes, rows = dens.shape[1], dens.shape[2]
-    tall = slice(PAD - 8, PAD + rows + 8)
-    early = copy_all([(part, sec.at[:, :, tall]), (terms, mets.at[:, tall])], sems)
-    pairs = state_pairs((dens, mom, en, met, vol), state, planes, slice(None))
-    late = copy_all(pairs, sems, 2)
-    lane = lanes_of((8, LANES))
-    wait_all(early)
-
-    def get(c, k, r):
-        return sec[c, k, pl.ds(r, 8)]
-
-    chunks(rows // 8 + 2, lambda n: flux_chunk(get, mets, fi, w, fk, acc, n + PAD - 8))
-    wait_all(late)
-
-    def emit(c, k, r, val):
-        at = pl.ds(r - PAD, 8)
-        full[c, k, at] = 0.5 * (state[c, k, at] + (get(c, k, r) + val))
-
-    def leave(n):
-        at = pl.ds(n, 8)
-        return pltpu.make_async_copy(full.at[:, :, at], out.at[:, :, at], out_sems.at[n // 8])
+        full[c, k, pl.ds(r - PAD, 8)] = get(c, k, r) + val
+
+    leave = leaving(full, part, out_sems)
 
     def sums(n):
         sum_chunk(mets, fi, w, fk, acc, n + PAD, emit)
         leave(n).start()
 
+    chunks(rows // 8, fluxes)
     chunks(rows // 8, sums)
-
-    for c, x in enumerate(pack_ends(sec, rows, scratch, planes)):
-        ends[c] = x
+    chunks(rows // 8, lambda n: leave(n).wait())
+
+
+def leaving(full, out, sems):
+    def leave(n):
+        at = pl.ds(n, 8)
+        return pltpu.make_async_copy(full.at[:, :, at], out.at[:, :, at], sems.at[n // 8])
+
+    return leave
+
+
+def pack_ends(tall, planes):
+    sub, lane = rows_of((8, LANES)), lanes_of((8, LANES))
+    stacked = []
+    for c in range(CH):
+        packed = jnp.zeros((8, LANES), jnp.float32)
+        for k in range(planes):
+            x = turn(jnp.where(sub < 4, tall[0, c, k], tall[1, c, k]), 8 * k + 4, 1)
+            packed = jnp.where(within(lane, 8 * k, 8), x, packed)
+        stacked.append(packed)
+    ends = across(jnp.concatenate(stacked, axis=0))
+    out = []
+    for c in range(CH):
+        packed = jnp.zeros((8, LANES), jnp.float32)
+        for k in range(planes):
+            x = turn(ends[k * 8 : k * 8 + 8], 4 * k - (8 * c + 2), 1)
+            packed = jnp.where(within(lane, 4 * k, 4), x, packed)
+        out.append(packed)
+    return out
+
+
+def second_kernel(
+    halves, dens, mom, en, met, vol, below, above, part,
+    out, ends_base, ends_sec, inner,
+    state, low, high, tall, tile_fk, tile_w, tile_acc, packed, ends, strips,
+    sec, full, mets, fi, w, fk, acc, sems, out_sems,
+):
+    planes, rows = dens.shape[1], dens.shape[2]
+    every = planes + 1
+    halo = copy_all([(below, low), (above, high)], sems, 5 * PIECES)
+    expect = arrive_in_pieces((dens, mom, en, met, vol), state, sems)
+    arrive = copy_all([(part, sec.at[:, :, PAD : PAD + rows])], sems, 5 * PIECES + 2)
+    half = lax.axis_index("ij")
+    low_wall, high_wall = half == 0, half == halves - 1
+    low_flag, high_flag = jnp.where(low_wall, 1, 0), jnp.where(high_wall, 1, 0)
+    sub, lane = rows_of((8, LANES)), lanes_of((8, LANES))
+    wait_all(halo)
+    loop(min(PIECES, rows // 8), lambda n: expect(n * max(8, rows // PIECES)))
+
+    for c in range(CH):
+        for k in range(every):
+            tall[0, c, k, 4:8] = state[c, k, 0:4]
+            tall[1, c, k, 0:4] = state[c, k, rows - 4 : rows]
+
+    @pl.when(low_wall)
+    def _():
+        for c in range(CH):
+            for k in range(every):
+                for n in range(2):
+                    x = state[c, k, n : n + 1]
+                    tall[0, c, k, 3 - n : 4 - n] = -x if 1 <= c <= 3 and k < planes else x
+
+    @pl.when(jnp.logical_not(low_wall))
+    def _():
+        for c in range(CH):
+            for k in range(every):
+                tall[0, c, k, 0:4] = low[c, 4 * k : 4 * k + 4]
+
+    @pl.when(high_wall)
+    def _():
+        for c in range(CH):
+            for k in range(every):
+                for n in range(2):
+                    tall[1, c, k, 4 + n : 5 + n] = state[c, k, rows - 1 - n : rows - n]
+
+    @pl.when(jnp.logical_not(high_wall))
+    def _():
+        for c in range(CH):
+            for k in range(every):
+                tall[1, c, k, 4:8] = high[c, 4 * k : 4 * k + 4]
+
+    for c, x in enumerate(pack_ends(tall, every)):
+        ends[0, c] = x
+
+    def terms(n):
+        m = [state[c, planes, pl.ds(n, 8)] for c in range(CH)]
+        for j, x in enumerate(metric_terms(m)):
+            mets[j, pl.ds(n + PAD, 8)] = x
+
+    chunks(rows // 8, terms)
+    tall_mets = [metric_terms([tall[s, c, planes] for c in range(CH)]) for s in range(2)]
+    for s, at in ((0, PAD - 4), (1, PAD + rows - 4)):
+        for j, x in enumerate(tall_mets[s]):
+            mets[j, at : at + 8] = x
+
+    wait_all(arrive)
+
+    def done(c, s, k, x):
+        tall[s, c, k] = x
+        if s == 0:
+            sign = -1.0 if 1 <= c <= 3 else 1.0
+            wall = sign * jnp.where(sub == 2, turn(x, -3, 0), turn(x, -1, 0))
+            x = jnp.where((sub < 4) & (low_flag == 1), wall, x)
+        else:
+            wall = jnp.where(sub == 4, turn(x, 1, 0), turn(x, 3, 0))
+            x = jnp.where((sub >= 4) & (high_flag == 1), wall, x)
+        start = PAD - 2 if s == 0 else PAD + rows - 2
+        sec[c, k, start : start + 4] = x[2:6]
+
+    tile_stage(
+        planes, lambda c, s, k: tall[s, c, k], tall_mets, lambda *_: along(0), along(1),
+        (tile_fk, tile_w, tile_acc), done,
+    )
+    for c, x in enumerate(pack_ends(tall, planes)):
+        ends[1, c] = x
+    last = copy_all([(ends.at[0], ends_base), (ends.at[1], ends_sec)], out_sems, rows // 8)
+
     if rows < LANES:
         packed[...] = jnp.zeros(packed.shape, jnp.float32)
 
@@ -507,12 +524,25 @@
             packed[c, pl.ds(n, 8)] = packs
 
     chunks(rows // 8, pack)
-
-    def flip(c):
+    for c in range(CH):
         strips[c] = packed[c].T[0:64]
-
-    loop(CH, flip)
-    last = copy_all([(ends, ends_sec), (strips, inner)], out_sems, rows // 8)
+    last += copy_all([(strips, inner)], out_sems, rows // 8 + 2)
+
+    def get(c, k, r):
+        return sec[c, k, pl.ds(r, 8)]
+
+    def emit(c, k, r, val):
+        at = pl.ds(r - PAD, 8)
+        full[c, k, at] = 0.5 * (state[c, k, at] + (get(c, k, r) + val))
+
+    leave = leaving(full, out, out_sems)
+
+    def sums(n):
+        sum_chunk(mets, fi, w, fk, acc, n + PAD, emit)
+        leave(n).start()
+
+    chunks(rows // 8 + 2, lambda r: flux_chunk(get, mets, fi, w, fk, acc, r))
+    chunks(rows // 8, sums)
     chunks(rows // 8, lambda n: leave(n).wait())
     wait_all(last)
 
@@ -550,38 +580,35 @@
 
     wait_all(early)
 
-    def gather(k, others):
+    others = [jnp.zeros((8, LANES), jnp.float32)] * CH
+    for k in range(planes + 1):
         start = DEPTH * k * PASSED
-
-        def ghost(row, f):
-            x = got[pl.ds(start + row, 8, stride=PASSED)]
-            return x if f == 1 else turn(x, 4, 0)
-
-        others = list(others)
         for f in range(2):
-            arrived = ghost(2 * CH, f)
+
+            def ghost(row):
+                x = got[pl.ds(start + row, 8, stride=PASSED)]
+                return x if f == 1 else turn(x, 4, 0)
+
+            arrived = ghost(2 * CH)
             to = 28 * f + 4 * k
             for c in range(CH):
-                mine = own[c, pl.ds(pl.multiple_of(k * 8, 8), 8)]
-                base[c, f, k] = mix(f, mine, ghost(f * CH + c, f))
-                moved = roll_by(arrived, to - 4 * CH * f - 4 * c)
+                base[c, f, k] = mix(f, own[c, k * 8 : k * 8 + 8], ghost(f * CH + c))
+                moved = turn(arrived, to - 4 * CH * f - 4 * c, 1)
                 others[c] = jnp.where(within(lane, to, 4), moved, others[c])
-        return tuple(others)
-
-    empty = jnp.zeros((8, LANES), jnp.float32)
-    others = loop(planes + 1, gather, (empty,) * CH)
+
     low_lanes = lane < 28
     twice = [jnp.where(low_lanes, ends_base[c], turn(ends_base[c], 28, 1)) for c in range(CH)]
     ends = [jnp.where(low_lanes == (sub >= 4), twice[c], others[c]) for c in range(CH)]
     slot = jnp.where(low_lanes, lane, lane - 28)
 
-    def spread(k, kept):
-        shift, hit = 4 * (k - planes), within(slot, 4 * k, 4)
-        return tuple((x, jnp.where(hit, roll_by(x, shift), y)) for x, y in kept)
-
-    kept = metric_terms(ends)[0:5] + metric_terms(ends)[6:7] + metric_terms(twice)[2:4]
-    kept = loop(planes, spread, tuple((x, x) for x in kept))
-    vax, vay, vbx, vby, niv, cw, *wrapped = [y for _, y in kept]
+    def spread(x):
+        y = x
+        for k in range(planes):
+            y = jnp.where(within(slot, 4 * k, 4), turn(x, 4 * (k - planes), 1), y)
+        return y
+
+    vax, vay, vbx, vby, niv, _, cw, _ = [spread(x) for x in metric_terms(ends)]
+    wrapped = [spread(x) for x in metric_terms(twice)[2:4]]
 
     def keep(c, f, k, val):
         sec[c, f, k] = val
@@ -605,12 +632,13 @@
 
     def move(k, source):
         for c in range(CH):
-            mine = inner[c, pl.ds(pl.multiple_of(k * 8, 8), 8)]
+            mine = inner[c, k * 8 : k * 8 + 8]
             for f in range(2):
                 sec[c, f, k] = mix(f, mine, turn(source[c, f, k], 2 if f == 1 else -2, 0))
 
-    loop(planes, lambda k: move(k, sec))
-    move(jnp.int32(planes), base)
+    for k in range(planes):
+        move(k, sec)
+    move(planes, base)
 
     def shifted(x):
         return jnp.where(low_lanes, turn(x, -2, 0), turn(x, 2, 0))
@@ -629,58 +657,60 @@
         second.append(shifted(x + jnp.where(touched, add, 0.0)))
     walled = low_wall | high_wall
 
-    def reflect(k, second):
-        second = list(second)
+    for k in range(planes):
         for f in range(2):
             to = 28 * f + 4 * k
             first = jnp.where(walled, jnp.where(low_wall, to, to + 2), -8)
-            shift = jnp.where(low_wall, to - 1, to + 3 - rows)
+            shift = jnp.where(low_wall, (to - 1) % LANES, (to + 3 - rows) % LANES)
+            next_shift = jnp.where(low_wall, (to + 1) % LANES, (to + 5 - rows) % LANES)
             for c in range(CH):
                 x = sec[c, f, k]
-                one, two = roll_by(x, shift), roll_by(x, shift + 2)
+                one, two = pltpu.roll(x, shift, 1), pltpu.roll(x, next_shift, 1)
+                x = jnp.where(lane == first, one, two)
                 if 1 <= c <= 3:
-                    sign = jnp.where(low_wall, -1.0, 1.0)
-                    one, two = sign * one, sign * two
-                x = jnp.where(lane == first, one, second[c])
-                second[c] = jnp.where(lane == first + 1, two, x)
-        return tuple(second)
-
-    second = loop(planes, reflect, tuple(second))
+                    x = jnp.where(low_wall, -1.0, 1.0) * x
+                second[c] = jnp.where(within(lane, first, 2), x, second[c])
     stage(sec, second, shifted(vax), shifted(vay))
 
     per = LANES // 8
 
-    def finish(k):
+    for k in range(planes):
         for c in range(CH):
             x = jnp.where(sub < 4, turn(sec[c, 1, k], -2, 0), turn(sec[c, 0, k], 2, 0))
-            at = pl.multiple_of((c * planes + k) * 8, 8)
-            mine = own[c, pl.ds(pl.multiple_of(k * 8, 8), 8)]
-            turned[pl.ds(at, 8)] = 0.5 * (mine + x)
-
-    loop(planes, finish)
-
-    def flip(n):
-        back[n] = turned[pl.ds(pl.multiple_of(n * LANES, LANES), LANES)].T
-
-    loop(turned.shape[0] // LANES, flip)
-    late[2].wait()
+            at = (c * planes + k) * 8
+            turned[at : at + 8] = 0.5 * (own[c, k * 8 : k * 8 + 8] + x)
+    for n in range(turned.shape[0] // LANES):
+        back[n] = turned[n * LANES : (n + 1) * LANES].T
+    wait_all(late[2:])
     inside = within(lane, 4, LANES - 8)
-    copies = []
-    for c in range(CH):
-
-        def merge(k, c=c):
-            index = c * planes + k
-            which, place = index // per, lax.rem(index, per)
-            for r in range(0, rows, 8):
-                moved = roll_by(back[which, r : r + 8], LANES - 4 - 8 * place)
-                full[c, k, r : r + 8] = jnp.where(inside, full[c, k, r : r + 8], moved)
-
-        loop(planes, merge)
-        dst = next_dens.at[0] if c == 0 else next_en.at[0] if c == 4 else next_mom.at[0, c - 1]
-        copies.append(pltpu.make_async_copy(full.at[c], dst, sems.at[6 + c]))
-        copies[-1].start()
-    for copy in copies:
-        copy.wait()
+    size = max(8, rows // PIECES)
+
+    def leave(start):
+        at = pl.ds(start, size)
+        targets = [next_dens.at[0, :, at], next_en.at[0, :, at], next_mom.at[0, :, :, at]]
+        sources = [full.at[0, :, at], full.at[4, :, at], full.at[1:4, :, at]]
+        first = 6 + 3 * (start // size)
+        return [
+            pltpu.make_async_copy(src, dst, sems.at[first + n])
+            for n, (src, dst) in enumerate(zip(sources, targets))
+        ]
+
+    def merge(r):
+        at = pl.ds(r, 8)
+        for c in range(CH):
+            for k in range(planes):
+                index = c * planes + k
+                moved = turn(back[index // per, at], LANES - 4 - 8 * (index % per), 1)
+                full[c, k, at] = jnp.where(inside, full[c, k, at], moved)
+
+        @pl.when(lax.rem(r + 8, size) == 0)
+        def _():
+            for copy in leave(pl.multiple_of(r + 8 - size, 8)):
+                copy.start()
+
+    chunks(rows // 8, merge)
+    for n in range(rows // size):
+        wait_all(leave(n * size))
 
 
 def local(mesh_shape, density, momentum, energy, metrics, volume, placed, neighbour, face, orient):
@@ -694,14 +724,14 @@
     smem = pl.BlockSpec(memory_space=pltpu.SMEM)
     hbm = pl.BlockSpec(memory_space=pltpu.HBM)
 
-    def call(kernel, name, outs, ins, out_specs, scratch, cost=None):
+    def call(kernel, name, outs, ins, out_specs, scratch, cost=None, mib=VMEM_MIB):
         return pl.pallas_call(
             kernel,
             out_shape=outs,
             in_specs=ins,
             out_specs=out_specs,
             scratch_shapes=scratch,
-            compiler_params=pltpu.CompilerParams(vmem_limit_bytes=VMEM_LIMIT),
+            compiler_params=pltpu.CompilerParams(vmem_limit_bytes=mib * 1024 * 1024),
             cost_estimate=cost,
             name=name,
         )
@@ -733,7 +763,7 @@
             vmem(state),
             pltpu.VMEM((CH, LANES, LANES), jnp.float32),
             pltpu.VMEM((CH * 64, LANES), jnp.float32),
-            sems(5),
+            sems(5 * PIECES),
             sems(2 + edges),
         ],
     )(*fields, placed, face, orient)
@@ -752,8 +782,6 @@
 
     tall = rows + 2 * PAD
     block = shape(CH, planes, rows, LANES)
-    high = shape(CH, planes, rows + 16, LANES)
-    terms = shape(8, rows + 16, LANES)
     padded = shape(CH, planes, tall, LANES)
     stage = [
         vmem(shape(8, tall, LANES)),
@@ -764,53 +792,55 @@
     ]
     work = planes * rows * LANES
     cost = pl.CostEstimate(flops=300 * work, bytes_accessed=150 * work, transcendentals=work)
-    part, kept, ends_base, route = call(
-        functools.partial(first_kernel, halves),
+    leave = sems(rows // 8 + 3)
+    part, route = call(
+        first_kernel,
         "first_section",
-        [high, terms, rim, jax.ShapeDtypeStruct((2 * blocks,), jnp.int32)],
-        [hbm] * 7 + [smem] * 4,
-        [hbm] * 3 + [smem],
-        [vmem(shape(CH, every, tall, LANES)), vmem(edge), vmem(edge), vmem(padded)]
+        [block, jax.ShapeDtypeStruct((2 * blocks,), jnp.int32)],
+        [hbm] * 5 + [smem] * 4,
+        [hbm, smem],
+        [vmem(state), vmem(block)]
         + stage
-        + [vmem(rim), vmem(square), pltpu.SMEM((blocks,), jnp.int32), sems(7), sems(3)],
+        + [pltpu.SMEM((blocks,), jnp.int32), sems(5 * PIECES), leave],
         cost,
-    )(*fields, below, above, placed, neighbour, face, orient)
+    )(*fields, placed, neighbour, face, orient)
     relayed = call(
         functools.partial(relay_kernel, halves, rows, planes, devices),
         "relay",
         passed,
-        [smem, hbm],
+        [smem, hbm, pl.BlockSpec(memory_space=pltpu.VMEM)],
         hbm,
         [
-            vmem(sent),
             vmem(passed),
             vmem(shape(devices * 16, LANES)),
             vmem(shape(devices * 16, LANES)),
             vmem(shape(devices * 2, LANES)),
-            sems(2),
+            sems(1),
         ],
-    )(route, got)
+        mib=16,
+    )(route, below, got)
     ghosts = swap(relayed)
-    out, ends_sec, inner = call(
-        second_kernel,
+    tiles = shape(CH, 2, every, 8, LANES)
+    flat = -(-CH * planes * 8 // LANES)
+    out, ends_base, ends_sec, inner = call(
+        functools.partial(second_kernel, halves),
         "second_section",
-        [block, rim, strip],
-        [hbm] * 7,
-        [hbm] * 3,
-        [vmem(state), vmem(padded), vmem(block)]
-        + stage
+        [block, rim, rim, strip],
+        [hbm] * 8,
+        [hbm] * 4,
+        [vmem(state), vmem(edge), vmem(edge), vmem(shape(2, CH, every, 8, LANES))]
+        + [vmem(tiles)] * 3
         + [
             pltpu.VMEM((CH, LANES, LANES), jnp.float32),
-            vmem(square),
-            vmem(rim),
+            vmem(shape(2, CH, 8, LANES)),
             vmem(strip),
-            sems(7),
-            sems(rows // 8 + 2),
-        ],
+            vmem(padded),
+            vmem(block),
+        ]
+        + stage
+        + [sems(5 * PIECES + 3), leave],
         cost,
-    )(*fields, part, kept)
-    tiles = shape(CH, 2, every, 8, LANES)
-    flat = -(-CH * planes * 8 // LANES)
+    )(*fields, below, above, part)
     return call(
         functools.partial(last_kernel, halves, rows, planes),
         "strips",
@@ -823,7 +853,7 @@
             vmem(shape(flat * LANES, LANES)),
             vmem(shape(flat, LANES, LANES)),
             vmem(block),
-            sems(6 + CH),
+            sems(6 + 3 * PIECES),
         ],
     )(own, ends_base, ends_sec, inner, ghosts, out)
 

time: 70.2 us -> 58.2 us (0.83)
  Pallas kernels: 48.6 us -> 42 us
  waiting for transfers between devices: 4.06 us -> 0.01 us
    pallas_call x2, Pallas kernels: 29.4 us -> 24.2 us  [the longest x1 14.4 us: local(): call(functools.partial(second_kernel, halves), 'second_section', [block,...]
    ppermute x1, waiting for transfers between devices: 4.05 us -> 0.01 us  [local(): below = above = lax.ppermute(halo[0], 'ij', [(0, 1), (1, 0)])]
    pallas_call x1, Pallas kernels: 2.83 us -> 1.82 us  [local(): call(functools.partial(relay_kernel, halves, rows, planes, devices), 'rel...]
  transfers between devices with their start and end apart: 3 -> 3, of which waited for: 1 -> 0; matrix products, arithmetic and copies ran while one was open for 0% -> 0% of each run, Pallas kernels for 42% -> 42%
where the time goes in v4:
time: 58.2 us; the launch traced here: 57.9 us
  Pallas kernels  42 us (72%)
  starting transfers between devices  13.8 us (24%)
  local copies, waits for them, and re-layouts  1.36 us (2%)
  between operations  0.73 us (1%)
    pallas_call x1, Pallas kernels, local(): call(functools.partial(second_kernel, halves), 'second_section', [block,...  14.4 us
    all_to_all x2, starting transfers between devices, swap(): x = lax.all_to_all(x, ('blk', 'ij'), 0, 0, tiled=True)  11.9 us
    pallas_call x1, Pallas kernels, local(): call(functools.partial(last_kernel, halves, rows, planes), 'strips', [sha...  10.1 us
    pallas_call x1, Pallas kernels, local(): call(first_kernel, 'first_section', [block, jax.ShapeDtypeStruct((2 * blo...  9.87 us
    pallas_call x1, Pallas kernels, local(): call(functools.partial(cut_kernel, halves), 'cut', outs, [hbm] * 5 + [sme...  5.8 us
    ppermute x1, starting transfers between devices, local(): below = above = lax.ppermute(halo[0], 'ij', [(0, 1), (1, 0)])  1.83 us
    pallas_call x1, Pallas kernels, local(): call(functools.partial(relay_kernel, halves, rows, planes, devices), 'rel...  1.82 us
    unnamed x6, local copies, waits for them, and re-layouts  1.36 us
  transfers between devices with their start and end apart: 3, of which 0 were waited for; matrix products, arithmetic and copies ran while one was open for 0% of the time, Pallas kernels for 42%

profile of v4, /device:TPU:0, one launch (start us, length us, event | category | flops | bytes accessed | tf_op | source)
XLA Modules:
  0.0 57.9 jit_solution(5926612244225548161)
XLA Ops:
  0.6 5.8 %cut.1 = (f32[320,128]{1,0:T(8,128)}, f32[5,64,128]{2,1,0:T(8,128)}, f32[5,28,128]{2,1,0:T(8,128)}) custom-call(f32[1,6,128,128]{3,2,1,0:T(8,128)} %dens.5, f32[1,3,6,128,128]{4,3,2,1,0:T(8,128)} %mom.5, f32[1,6,128,128]{3,2,1,0:T(8,128)} %en.5, f32[1,4,128,128]{3,2,1,0:T(8,128)} %met.5, f32[1,128,128]{2,1,0:T(8,128)} %vol.5, s32[16]{0:T(128)} %placed.3, ...), custom_call_target="tpu_custom_call" | custom-call | tf_op jit(solution)/shard_map/cut/pallas_call | solution.py:755
  6.4 7.3 %all-to-all-start = ((f32[32,10,1,128]{3,2,1,0:T(1,128)}), f32[32,10,1,128]{3,2,1,0:T(1,128)S(1)}, u32[]{:S(2)}, u32[]{:S(2)}) async-start(f32[32,10,1,128]{3,2,1,0:T(1,128)} %bitcast.9), calls=%async_computation | async-start | bytes 327680 | tf_op jit(solution)/shard_map/all_to_all | solution.py:773
  13.7 1.8 %collective-permute-start = (f32[5,28,128]{2,1,0:T(8,128)}, f32[5,28,128]{2,1,0:T(8,128)S(1)}, u32[]{:S(2)}, u32[]{:S(2)}) collective-permute-start(f32[5,28,128]{2,1,0:T(8,128)} %get-tuple-element.13), channel_id=1, source_target_pairs={{0,1},{1,0},{2,3},{3,2},{4,5},{5,4},{6,7},{7,6},{8,9},{9,8},{10,11... | collective-permute-start | bytes 215048 | tf_op jit(solution)/shard_map/ppermute | solution.py:777
  15.6 9.9 %first_section.1 = (f32[5,6,128,128]{3,2,1,0:T(8,128)}, s32[32]{0:T(128)}) custom-call(f32[1,6,128,128]{3,2,1,0:T(8,128)} %dens.5, f32[1,3,6,128,128]{4,3,2,1,0:T(8,128)} %mom.5, f32[1,6,128,128]{3,2,1,0:T(8,128)} %en.5, f32[1,4,128,128]{3,2,1,0:T(8,128)} %met.5, f32[1,128,128]{2,1,0:T(8,128)} %vol.5, s32[16]{0:T(128)} %placed.3, s32[2,16]{1,0:T(2,128)} %bitcast.14, ...), custom_call_target="tpu_custom_call" | custom-call | flops 29491200 | bytes 14745600 | tf_op jit(solution)/shard_map/first_section/pallas_call | solution.py:796
  25.5 0.0 collective-permute-done.below.above.halo
  25.5 0.0 copy-start
  25.5 0.0 all-to-all-done
  25.5 0.0 copy-start.1
  25.5 0.7 %copy-done.1 = s32[32]{0:T(128)S(1)} copy-done((s32[32]{0:T(128)S(1)}, s32[32]{0:T(128)}, u32[]{:S(2)}) %copy-start.1) | copy-done | bytes 152
  26.2 1.8 %relay.1 = f32[352,128]{1,0:T(8,128)} custom-call(s32[32]{0:T(128)S(1)} %copy-done.1, f32[5,28,128]{2,1,0:T(8,128)S(1)} %collective-permute-done.below.above.halo, f32[320,128]{1,0:T(8,128)S(1)} %bitcast.7), custom_call_target="tpu_custom_call" | custom-call | tf_op jit(solution)/shard_map/relay/pallas_call | solution.py:807
  28.0 4.6 %all-to-all-start.1 = ((f32[32,11,1,128]{3,2,1,0:T(1,128)}), f32[32,11,1,128]{3,2,1,0:T(1,128)S(1)}, u32[]{:S(2)}, u32[]{:S(2)}) async-start(f32[32,11,1,128]{3,2,1,0:T(1,128)} %bitcast.5), calls=%async_computation.1 | async-start | bytes 360448 | tf_op jit(solution)/shard_map/all_to_all | solution.py:773
  32.6 0.0 copy-done
  32.7 14.4 %second_section.1 = (f32[5,6,128,128]{3,2,1,0:T(8,128)}, f32[5,8,128]{2,1,0:T(8,128)}, f32[5,8,128]{2,1,0:T(8,128)}, f32[5,64,128]{2,1,0:T(8,128)}) custom-call(f32[1,6,128,128]{3,2,1,0:T(8,128)} %dens.5, f32[1,3,6,128,128]{4,3,2,1,0:T(8,128)} %mom.5, f32[1,6,128,128]{3,2,1,0:T(8,128)} %en.5, f32[1,4,128,128]{3,2,1,0:T(8,128)} %met.5, f32[1,128,128]{2,1,0:T(8,128)} %vol.5, ...), custom_call_target="tpu_custom_call" | custom-call | flops 29491200 | bytes 14745600 | tf_op jit(solution)/shard_map/second_section/pallas_call | solution.py:825
  47.0 0.0 all-to-all-done.1
  47.0 0.0 copy-start.2
  47.1 0.7 %copy-done.2 = f32[32,11,1,128]{3,2,1,0:T(1,128)} copy-done((f32[32,11,1,128]{3,2,1,0:T(1,128)}, f32[32,11,1,128]{3,2,1,0:T(1,128)S(1)}, u32[]{:S(2)}) %copy-start.2) | copy-done | bytes 180248
  47.7 10.1 %strips.1 = (f32[1,6,128,128]{3,2,1,0:T(8,128)}, f32[1,3,6,128,128]{4,3,2,1,0:T(8,128)}, f32[1,6,128,128]{3,2,1,0:T(8,128)}) custom-call(f32[5,64,128]{2,1,0:T(8,128)} %get-tuple-element.12.own_at, f32[5,8,128]{2,1,0:T(8,128)} %get-tuple-element.15.ends_base_at, f32[5,8,128]{2,1,0:T(8,128)} %get-tuple-element.16.ends_sec_at, ...), custom_call_target="tpu_custom_call" | custom-call | tf_op jit(solution)/shard_map/strips/pallas_call | solution.py:844
Async XLA Ops:
  6.4 19.0 %all-to-all-start = ((f32[32,10,1,128]{3,2,1,0:T(1,128)}), f32[32,10,1,128]{3,2,1,0:T(1,128)S(1)}, u32[]{:S(2)}, u32[]{:S(2)}) async-start(f32[32,10,1,128]{3,2,1,0:T(1,128)} %bitcast.9), calls=%async_computation | async-start | bytes 327680 | tf_op jit(solution)/shard_map/all_to_all | solution.py:773
  13.7 11.7 %collective-permute-start = (f32[5,28,128]{2,1,0:T(8,128)}, f32[5,28,128]{2,1,0:T(8,128)S(1)}, u32[]{:S(2)}, u32[]{:S(2)}) collective-permute-start(f32[5,28,128]{2,1,0:T(8,128)} %get-tuple-element.13), channel_id=1, source_target_pairs={{0,1},{1,0},{2,3},{3,2},{4,5},{5,4},{6,7},{7,6},{8,9},{9,8},{10,11... | collective-permute-start | bytes 215048 | tf_op jit(solution)/shard_map/ppermute | solution.py:777
  25.5 7.2 %copy-start = (f32[5,28,128]{2,1,0:T(8,128)}, f32[5,28,128]{2,1,0:T(8,128)S(1)}, u32[]{:S(2)}) copy-start(f32[5,28,128]{2,1,0:T(8,128)S(1)} %collective-permute-done.below.above.halo) | copy-start | bytes 215044
  25.5 0.7 %copy-start.1 = (s32[32]{0:T(128)S(1)}, s32[32]{0:T(128)}, u32[]{:S(2)}) copy-start(s32[32]{0:T(128)} %get-tuple-element.18.route) | copy-start | bytes 388
  28.0 19.0 %all-to-all-start.1 = ((f32[32,11,1,128]{3,2,1,0:T(1,128)}), f32[32,11,1,128]{3,2,1,0:T(1,128)S(1)}, u32[]{:S(2)}, u32[]{:S(2)}) async-start(f32[32,11,1,128]{3,2,1,0:T(1,128)} %bitcast.5), calls=%async_computation.1 | async-start | bytes 360448 | tf_op jit(solution)/shard_map/all_to_all | solution.py:773
  47.0 0.7 %copy-start.2 = (f32[32,11,1,128]{3,2,1,0:T(1,128)}, f32[32,11,1,128]{3,2,1,0:T(1,128)S(1)}, u32[]{:S(2)}) copy-start(f32[32,11,1,128]{3,2,1,0:T(1,128)S(1)} %all-to-all-done.1) | copy-start | bytes 540676

commit v5 on v4

--- a/solution.py
+++ b/solution.py
@@ -17,7 +17,7 @@
 PIECES = 4
 DEPTH = 4
 CH = 5
-VMEM_MIB = 63
+VMEM_MIB = 32
 SENT = 2 * CH
 PASSED = 2 * CH + 1
 FIRST = 4
@@ -175,15 +175,46 @@
     loop(planes, gather, unroll=2)
 
 
-def cut_kernel(halves, dens, mom, en, met, vol, placed, face, orient, send, own, *rest):
-    edges, rest = rest[: -7 - (1 if halves == 2 else 2)], rest[-7 - (1 if halves == 2 else 2) :]
-    held_send, held_own, *held_edges = rest[: 2 + len(edges)]
-    state, packed, strips, sems, out_sems = rest[2 + len(edges) :]
+def cut_kernel(
+    halves, dens, mom, en, met, vol, placed_at, face_at, orient_at, send, own, state, *rest
+):
+    edges, rest = rest[: 1 if halves == 2 else 2], rest[1 if halves == 2 else 2 :]
+    held_send, packed, strips, placed, face, orient, sems, table_sems, out_sems = rest
+    tables = copy_all(
+        [(placed_at, placed), (face_at, face), (orient_at, orient)], table_sems
+    )
     planes, rows = dens.shape[1], dens.shape[2]
     expect = arrive_in_pieces((dens, mom, en, met, vol), state, sems)
+    half = lax.axis_index("ij")
+    lane = lanes_of((8, LANES))
+    if rows < LANES:
+        packed[...] = jnp.zeros(packed.shape, jnp.float32)
+    def pack(r):
+        expect(r)
+        for c in range(CH):
+            packs = jnp.zeros((8, LANES), jnp.float32)
+            for k in range(planes + 1):
+                x = turn(state[c, k, pl.ds(r, 8)], 8 * k + 4, 1)
+                packs = jnp.where(within(lane, 8 * k, 8), x, packs)
+            packed[c, pl.ds(r, 8)] = packs
+
+    chunks(rows // 8, pack)
+
+    def cut_ends(k):
+        for c in range(CH):
+            low, high = state[c, k, 0:4], state[c, k, rows - 4 : rows]
+            if len(edges) == 1:
+                edges[0][c, k * 4 : k * 4 + 4] = jnp.where(half == 0, high, low)
+            else:
+                edges[0][c, k * 4 : k * 4 + 4] = low
+                edges[1][c, k * 4 : k * 4 + 4] = high
+
+    for k in range(planes + 1):
+        cut_ends(k)
+
+    wait_all(tables)
     block = placed[lax.axis_index("blk")]
-    half = lax.axis_index("ij")
-    row, lane = rows_of((64, LANES)), lanes_of((8, LANES))
+    row = rows_of((64, LANES))
     high_side = row % 8 < 4
     mirror = jnp.where(
         rows_of((LANES, LANES)) + lanes_of((LANES, LANES)) == rows - 1, 1.0, 0.0
@@ -193,35 +224,10 @@
     rising = [face[f, block] == 1 for f in range(2)]
     turned = jnp.where(high_side, flip[1], flip[0])
     facing = jnp.where(high_side, same[1], same[0])
-    if rows < LANES:
-        packed[...] = jnp.zeros(packed.shape, jnp.float32)
-    def pack(r):
-        expect(r)
-        for c in range(CH):
-            packs = jnp.zeros((8, LANES), jnp.float32)
-            for k in range(planes + 1):
-                x = turn(state[c, k, pl.ds(r, 8)], 8 * k + 4, 1)
-                packs = jnp.where(within(lane, 8 * k, 8), x, packs)
-            packed[c, pl.ds(r, 8)] = packs
-
-    chunks(rows // 8, pack)
-
-    def cut_ends(k):
-        for c in range(CH):
-            low, high = state[c, k, 0:4], state[c, k, rows - 4 : rows]
-            if len(edges) == 1:
-                held_edges[0][c, k * 4 : k * 4 + 4] = jnp.where(half == 0, high, low)
-            else:
-                held_edges[0][c, k * 4 : k * 4 + 4] = low
-                held_edges[1][c, k * 4 : k * 4 + 4] = high
-
-    for k in range(planes + 1):
-        cut_ends(k)
-    out = copy_all(list(zip(held_edges, edges)), out_sems, 2)
 
     def orient_strip(c):
         strip = packed[c].T[0:64]
-        held_own[c] = strip
+        own[c] = strip
         back = jnp.dot(
             strip,
             mirror,
@@ -234,7 +240,6 @@
         strips[pl.ds(pl.multiple_of(c * 64, 64), 64)] = moved
 
     loop(CH, orient_strip)
-    out += copy_all([(held_own, own)], out_sems, 1)
 
     def put(n):
         k, e = n >> 2, n & 3
@@ -245,14 +250,15 @@
         held_send[pl.ds(at + CH, CH)] = strips[pl.ds(high, CH, stride=64)]
 
     loop(DEPTH * (planes + 1), put, unroll=4)
-    wait_all(out + copy_all([(held_send, send)], out_sems, 0))
+    wait_all(copy_all([(held_send, send)], out_sems))
 
 
 def relay_kernel(
-    halves, rows, planes, devices, route, halo, held_got, send,
-    held_send, below, above, signs, sems,
+    halves, rows, planes, devices, route_at, halo, held_got, send,
+    held_send, below, above, signs, route, sems,
 ):
     del halo
+    wait_all(copy_all([(route_at, route)], sems, 1))
     me = lax.axis_index("blk") * halves + lax.axis_index("ij")
     is_field = (me >= FIRST) & (me < FIRST + DEPTH * planes)
 
@@ -351,11 +357,28 @@
 
 
 def first_kernel(
-    dens, mom, en, met, vol, placed, neighbour, face, orient, part, route,
-    state, full, mets, fi, w, fk, acc, where_is, sems, out_sems,
+    state, placed_at, neighbour_at, face_at, orient_at, part, route,
+    mets, fi, w, fk, acc, placed, neighbour, face, orient, where_is, sems,
 ):
-    planes, rows = dens.shape[1], dens.shape[2]
-    expect = arrive_in_pieces((dens, mom, en, met, vol), state, sems)
+    planes, rows = part.shape[1], part.shape[2]
+    pairs = zip((placed_at, neighbour_at, face_at, orient_at), (placed, neighbour, face, orient))
+    tables = copy_all(list(pairs), sems)
+
+    def get(c, k, r):
+        return state[c, k, pl.ds(r - PAD, 8)]
+
+    def fluxes(n):
+        m = [state[c, planes, pl.ds(n, 8)] for c in range(CH)]
+        for j, x in enumerate(metric_terms(m)):
+            mets[j, pl.ds(n + PAD, 8)] = x
+        flux_chunk(get, mets, fi, w, fk, acc, n + PAD)
+
+    def emit(c, k, r, val):
+        part[c, k, pl.ds(r - PAD, 8)] = get(c, k, r) + val
+
+    chunks(rows // 8, fluxes)
+    chunks(rows // 8, lambda n: sum_chunk(mets, fi, w, fk, acc, n + PAD, emit))
+    wait_all(tables)
     blocks = placed.shape[0]
 
     def note(slot):
@@ -369,37 +392,6 @@
 
     loop(blocks, note, unroll=8)
     loop(blocks, direct, unroll=4)
-
-    def get(c, k, r):
-        return state[c, k, pl.ds(r - PAD, 8)]
-
-    def fluxes(n):
-        expect(n)
-        m = [state[c, planes, pl.ds(n, 8)] for c in range(CH)]
-        for j, x in enumerate(metric_terms(m)):
-            mets[j, pl.ds(n + PAD, 8)] = x
-        flux_chunk(get, mets, fi, w, fk, acc, n + PAD)
-
-    def emit(c, k, r, val):
-        full[c, k, pl.ds(r - PAD, 8)] = get(c, k, r) + val
-
-    leave = leaving(full, part, out_sems)
-
-    def sums(n):
-        sum_chunk(mets, fi, w, fk, acc, n + PAD, emit)
-        leave(n).start()
-
-    chunks(rows // 8, fluxes)
-    chunks(rows // 8, sums)
-    chunks(rows // 8, lambda n: leave(n).wait())
-
-
-def leaving(full, out, sems):
-    def leave(n):
-        at = pl.ds(n, 8)
-        return pltpu.make_async_copy(full.at[:, :, at], out.at[:, :, at], sems.at[n // 8])
-
-    return leave
 
 
 def pack_ends(tall, planes):
@@ -423,22 +415,16 @@
 
 
 def second_kernel(
-    halves, dens, mom, en, met, vol, below, above, part,
-    out, ends_base, ends_sec, inner,
-    state, low, high, tall, tile_fk, tile_w, tile_acc, packed, ends, strips,
-    sec, full, mets, fi, w, fk, acc, sems, out_sems,
+    halves, state, low, high, part, out, ends_base, ends_sec, strips,
+    tall, tile_fk, tile_w, tile_acc, packed, sec, mets, fi, w, fk, acc, sems,
 ):
-    planes, rows = dens.shape[1], dens.shape[2]
+    planes, rows = part.shape[1], part.shape[2]
     every = planes + 1
-    halo = copy_all([(below, low), (above, high)], sems, 5 * PIECES)
-    expect = arrive_in_pieces((dens, mom, en, met, vol), state, sems)
-    arrive = copy_all([(part, sec.at[:, :, PAD : PAD + rows])], sems, 5 * PIECES + 2)
+    arrive = copy_all([(part, sec.at[:, :, PAD : PAD + rows])], sems)
     half = lax.axis_index("ij")
     low_wall, high_wall = half == 0, half == halves - 1
     low_flag, high_flag = jnp.where(low_wall, 1, 0), jnp.where(high_wall, 1, 0)
     sub, lane = rows_of((8, LANES)), lanes_of((8, LANES))
-    wait_all(halo)
-    loop(min(PIECES, rows // 8), lambda n: expect(n * max(8, rows // PIECES)))
 
     for c in range(CH):
         for k in range(every):
@@ -473,7 +459,7 @@
                 tall[1, c, k, 4:8] = high[c, 4 * k : 4 * k + 4]
 
     for c, x in enumerate(pack_ends(tall, every)):
-        ends[0, c] = x
+        ends_base[c] = x
 
     def terms(n):
         m = [state[c, planes, pl.ds(n, 8)] for c in range(CH)]
@@ -505,8 +491,7 @@
         (tile_fk, tile_w, tile_acc), done,
     )
     for c, x in enumerate(pack_ends(tall, planes)):
-        ends[1, c] = x
-    last = copy_all([(ends.at[0], ends_base), (ends.at[1], ends_sec)], out_sems, rows // 8)
+        ends_sec[c] = x
 
     if rows < LANES:
         packed[...] = jnp.zeros(packed.shape, jnp.float32)
@@ -526,25 +511,16 @@
     chunks(rows // 8, pack)
     for c in range(CH):
         strips[c] = packed[c].T[0:64]
-    last += copy_all([(strips, inner)], out_sems, rows // 8 + 2)
 
     def get(c, k, r):
         return sec[c, k, pl.ds(r, 8)]
 
     def emit(c, k, r, val):
         at = pl.ds(r - PAD, 8)
-        full[c, k, at] = 0.5 * (state[c, k, at] + (get(c, k, r) + val))
-
-    leave = leaving(full, out, out_sems)
-
-    def sums(n):
-        sum_chunk(mets, fi, w, fk, acc, n + PAD, emit)
-        leave(n).start()
+        out[c, k, at] = 0.5 * (state[c, k, at] + (get(c, k, r) + val))
 
     chunks(rows // 8 + 2, lambda r: flux_chunk(get, mets, fi, w, fk, acc, r))
-    chunks(rows // 8, sums)
-    chunks(rows // 8, lambda n: leave(n).wait())
-    wait_all(last)
+    chunks(rows // 8, lambda n: sum_chunk(mets, fi, w, fk, acc, n + PAD, emit))
 
 
 def beyond(packed, f, k, rows):
@@ -565,20 +541,16 @@
 
 
 def last_kernel(
-    halves, rows, planes, own_at, ends_base_at, ends_sec_at, inner_at, got_at, out,
+    halves, rows, planes, own, ends_base, ends_sec, inner, got, out,
     next_dens, next_mom, next_en,
-    own, ends_base, ends_sec, inner, got, base, sec, fk, ws, acc, turned, back, full, sems,
+    base, sec, fk, ws, acc, turned, back, full, sems,
 ):
-    late = copy_all([(inner_at, inner), (ends_sec_at, ends_sec), (out, full)], sems)
-    early = copy_all([(got_at, got), (own_at, own), (ends_base_at, ends_base)], sems, 3)
     half = lax.axis_index("ij")
     low_wall, high_wall = half == 0, half == halves - 1
     sub, lane = rows_of((8, LANES)), lanes_of((8, LANES))
 
     def mix(f, mine, others):
         return jnp.where((sub < 4) == (f == 1), mine, others)
-
-    wait_all(early)
 
     others = [jnp.zeros((8, LANES), jnp.float32)] * CH
     for k in range(planes + 1):
@@ -628,7 +600,6 @@
         )
 
     stage(base, ends, vax, vay)
-    wait_all(late[0:2])
 
     def move(k, source):
         for c in range(CH):
@@ -681,7 +652,6 @@
             turned[at : at + 8] = 0.5 * (own[c, k * 8 : k * 8 + 8] + x)
     for n in range(turned.shape[0] // LANES):
         back[n] = turned[n * LANES : (n + 1) * LANES].T
-    wait_all(late[2:])
     inside = within(lane, 4, LANES - 8)
     size = max(8, rows // PIECES)
 
@@ -689,7 +659,7 @@
         at = pl.ds(start, size)
         targets = [next_dens.at[0, :, at], next_en.at[0, :, at], next_mom.at[0, :, :, at]]
         sources = [full.at[0, :, at], full.at[4, :, at], full.at[1:4, :, at]]
-        first = 6 + 3 * (start // size)
+        first = 3 * (start // size)
         return [
             pltpu.make_async_copy(src, dst, sems.at[first + n])
             for n, (src, dst) in enumerate(zip(sources, targets))
@@ -701,7 +671,7 @@
             for k in range(planes):
                 index = c * planes + k
                 moved = turn(back[index // per, at], LANES - 4 - 8 * (index % per), 1)
-                full[c, k, at] = jnp.where(inside, full[c, k, at], moved)
+                full[c, k, at] = jnp.where(inside, out[c, k, at], moved)
 
         @pl.when(lax.rem(r + 8, size) == 0)
         def _():
@@ -721,26 +691,49 @@
     every = planes + 1
     fields = (density, momentum, energy, metrics, volume)
     neighbour, face, orient = neighbour.T, face.T, orient.T
+    vmem = pl.BlockSpec(memory_space=pltpu.VMEM)
     smem = pl.BlockSpec(memory_space=pltpu.SMEM)
     hbm = pl.BlockSpec(memory_space=pltpu.HBM)
-
-    def call(kernel, name, outs, ins, out_specs, scratch, cost=None, mib=VMEM_MIB):
-        return pl.pallas_call(
+    anywhere = pl.BlockSpec(memory_space=pl.ANY)
+
+    def call(kernel, name, outs, ins, out_specs, scratch, cost=None):
+        run = pl.pallas_call(
             kernel,
-            out_shape=outs,
+            out_shape=[
+                held(x) if spec is vmem else far(x) if spec is hbm else x
+                for x, spec in zip(outs, out_specs)
+            ],
             in_specs=ins,
             out_specs=out_specs,
             scratch_shapes=scratch,
-            compiler_params=pltpu.CompilerParams(vmem_limit_bytes=mib * 1024 * 1024),
+            compiler_params=pltpu.CompilerParams(vmem_limit_bytes=VMEM_MIB * 1024 * 1024),
             cost_estimate=cost,
             name=name,
         )
 
+        def keep(*operands):
+            return run(
+                *[
+                    x
+                    if spec not in (vmem, hbm)
+                    else pltpu.with_memory_space_constraint(x, spec.memory_space)
+                    for x, spec in zip(operands, ins)
+                ]
+            )
+
+        return keep
+
     def shape(*dims):
         return jax.ShapeDtypeStruct(dims, jnp.float32)
 
-    def vmem(x):
-        return pltpu.VMEM(x.shape, jnp.float32)
+    def held(x):
+        return pltpu.VMEM(x.shape, x.dtype)
+
+    def far(x):
+        return pltpu.HBM(x.shape, x.dtype)
+
+    def table(x):
+        return pltpu.SMEM(x.shape, jnp.int32)
 
     def sems(count):
         return pltpu.SemaphoreType.DMA((count,))
@@ -749,22 +742,23 @@
     strip, rim = shape(CH, 64, LANES), shape(CH, 8, LANES)
     edge = shape(CH, 4 * every, LANES)
     edges = 1 if halves == 2 else 2
-    square = shape(LANES, LANES)
-    state = shape(CH, every, rows, LANES)
-    outs = [sent, strip] + [edge] * edges
-    to_send, own, *halo = call(
+    square = shape(CH, LANES, LANES)
+    to_send, own, state, *halo = call(
         functools.partial(cut_kernel, halves),
         "cut",
-        outs,
-        [hbm] * 5 + [smem] * 3,
-        [hbm] * (2 + edges),
-        [vmem(x) for x in outs]
-        + [
-            vmem(state),
-            pltpu.VMEM((CH, LANES, LANES), jnp.float32),
-            pltpu.VMEM((CH * 64, LANES), jnp.float32),
+        [sent, strip, shape(CH, every, rows, LANES)] + [edge] * edges,
+        [hbm] * 8,
+        [hbm] + [vmem] * (2 + edges),
+        [
+            held(sent),
+            held(square),
+            held(shape(CH * 64, LANES)),
+            table(placed),
+            table(face),
+            table(orient),
             sems(5 * PIECES),
-            sems(2 + edges),
+            sems(3),
+            sems(1),
         ],
     )(*fields, placed, face, orient)
 
@@ -782,78 +776,69 @@
 
     tall = rows + 2 * PAD
     block = shape(CH, planes, rows, LANES)
-    padded = shape(CH, planes, tall, LANES)
+    padded = held(shape(CH, planes, tall, LANES))
     stage = [
-        vmem(shape(8, tall, LANES)),
-        vmem(padded),
-        vmem(shape(4, planes, tall, LANES)),
-        vmem(padded),
-        vmem(padded),
+        held(shape(8, tall, LANES)),
+        padded,
+        held(shape(4, planes, tall, LANES)),
+        padded,
+        padded,
     ]
     work = planes * rows * LANES
     cost = pl.CostEstimate(flops=300 * work, bytes_accessed=150 * work, transcendentals=work)
-    leave = sems(rows // 8 + 3)
-    part, route = call(
+    route = jax.ShapeDtypeStruct((2 * blocks,), jnp.int32)
+    part, route_out = call(
         first_kernel,
         "first_section",
-        [block, jax.ShapeDtypeStruct((2 * blocks,), jnp.int32)],
-        [hbm] * 5 + [smem] * 4,
-        [hbm, smem],
-        [vmem(state), vmem(block)]
-        + stage
-        + [pltpu.SMEM((blocks,), jnp.int32), sems(5 * PIECES), leave],
+        [block, route],
+        [vmem] + [hbm] * 4,
+        [vmem, smem],
+        stage + [table(x) for x in (placed, neighbour, face, orient, placed)] + [sems(4)],
         cost,
-    )(*fields, placed, neighbour, face, orient)
-    relayed = call(
+    )(state, placed, neighbour, face, orient)
+    (relayed,) = call(
         functools.partial(relay_kernel, halves, rows, planes, devices),
         "relay",
-        passed,
-        [smem, hbm, pl.BlockSpec(memory_space=pltpu.VMEM)],
-        hbm,
+        [passed],
+        [anywhere, anywhere, vmem],
+        [hbm],
         [
-            vmem(passed),
-            vmem(shape(devices * 16, LANES)),
-            vmem(shape(devices * 16, LANES)),
-            vmem(shape(devices * 2, LANES)),
-            sems(1),
+            held(passed),
+            held(shape(devices * 16, LANES)),
+            held(shape(devices * 16, LANES)),
+            held(shape(devices * 2, LANES)),
+            table(route),
+            sems(2),
         ],
-        mib=16,
-    )(route, below, got)
+    )(route_out, below, got)
     ghosts = swap(relayed)
-    tiles = shape(CH, 2, every, 8, LANES)
+    tiles = held(shape(CH, 2, every, 8, LANES))
     flat = -(-CH * planes * 8 // LANES)
     out, ends_base, ends_sec, inner = call(
         functools.partial(second_kernel, halves),
         "second_section",
         [block, rim, rim, strip],
-        [hbm] * 8,
-        [hbm] * 4,
-        [vmem(state), vmem(edge), vmem(edge), vmem(shape(2, CH, every, 8, LANES))]
-        + [vmem(tiles)] * 3
-        + [
-            pltpu.VMEM((CH, LANES, LANES), jnp.float32),
-            vmem(shape(2, CH, 8, LANES)),
-            vmem(strip),
-            vmem(padded),
-            vmem(block),
-        ]
+        [vmem] * 4,
+        [vmem] * 4,
+        [held(shape(2, CH, every, 8, LANES))]
+        + [tiles] * 3
+        + [held(square), padded]
         + stage
-        + [sems(5 * PIECES + 3), leave],
+        + [sems(1)],
         cost,
-    )(*fields, below, above, part)
+    )(state, below, above, part)
     return call(
         functools.partial(last_kernel, halves, rows, planes),
         "strips",
         [shape(*density.shape), shape(*momentum.shape), shape(*energy.shape)],
-        [hbm] * 6,
+        [vmem] * 6,
         [hbm] * 3,
-        [vmem(x) for x in (strip, rim, rim, strip, passed)]
-        + [vmem(tiles)] * 5
+        [tiles] * 5
         + [
-            vmem(shape(flat * LANES, LANES)),
-            vmem(shape(flat, LANES, LANES)),
-            vmem(block),
-            sems(6 + 3 * PIECES),
+            held(shape(flat * LANES, LANES)),
+            held(shape(flat, LANES, LANES)),
+            held(block),
+            sems(3 * PIECES),
         ],
     )(own, ends_base, ends_sec, inner, ghosts, out)
 

time: 58.2 us -> 54.4 us (0.935)
  Pallas kernels: 42 us -> 34 us
  local copies, waits for them, and re-layouts: 1.36 us -> 5.66 us
    pallas_call x5, Pallas kernels: 42 us -> 34 us  [keep(): run(*[x if spec not in (vmem, hbm) else pltpu.with_memory_space_constrain...]
    unnamed x6 -> x8, local copies, waits for them, and re-layouts: 1.36 us -> 5.66 us
  transfers between devices with their start and end apart: 3 -> 3, of which waited for: 0 -> 0; matrix products, arithmetic and copies ran while one was open for 0% -> 0% of each run, Pallas kernels for 42% -> 34%
where the time goes in v5:
time: 54.4 us; the launch traced here: 54.1 us
  Pallas kernels  34 us (62%)
  starting transfers between devices  13.8 us (25%)
  local copies, waits for them, and re-layouts  5.66 us (10%)
  between operations  0.71 us (1%)
    pallas_call x5, Pallas kernels, keep(): run(*[x if spec not in (vmem, hbm) else pltpu.with_memory_space_constrain...  34 us
    all_to_all x2, starting transfers between devices, swap(): x = lax.all_to_all(x, ('blk', 'ij'), 0, 0, tiled=True)  11.9 us
    unnamed x8, local copies, waits for them, and re-layouts  5.66 us
    ppermute x1, starting transfers between devices, local(): below = above = lax.ppermute(halo[0], 'ij', [(0, 1), (1, 0)])  1.83 us
  transfers between devices with their start and end apart: 3, of which 0 were waited for; matrix products, arithmetic and copies ran while one was open for 0% of the time, Pallas kernels for 34%

profile of v5, /device:TPU:0, one launch (start us, length us, event | category | flops | bytes accessed | tf_op | source)
XLA Modules:
  0.0 54.1 jit_solution(17942964643526081817)
XLA Ops:
  0.6 5.1 %cut.1 = (f32[320,128]{1,0:T(8,128)}, f32[5,64,128]{2,1,0:T(8,128)S(1)}, f32[5,7,128,128]{3,2,1,0:T(8,128)S(1)}, f32[5,28,128]{2,1,0:T(8,128)S(1)}) custom-call(f32[1,6,128,128]{3,2,1,0:T(8,128)} %dens.1, f32[1,3,6,128,128]{4,3,2,1,0:T(8,128)} %mom.1, f32[1,6,128,128]{3,2,1,0:T(8,128)} %en.1, f32[1,4,128,128]{3,2,1,0:T(8,128)} %met.1, f32[1,128,128]{2,1,0:T(8,128)} %vol.1, ...), custom_call_target="tpu_custom_call" | custom-call | tf_op jit(solution)/shard_map/cut/pallas_call | solution.py:715
  5.8 7.3 %all-to-all-start = ((f32[32,10,1,128]{3,2,1,0:T(1,128)}), f32[32,10,1,128]{3,2,1,0:T(1,128)S(1)}, u32[]{:S(2)}, u32[]{:S(2)}) async-start(f32[32,10,1,128]{3,2,1,0:T(1,128)} %bitcast.10), calls=%async_computation | async-start | bytes 327680 | tf_op jit(solution)/shard_map/all_to_all | solution.py:767
  13.1 1.8 %collective-permute-start = (f32[5,28,128]{2,1,0:T(8,128)S(1)}, f32[5,28,128]{2,1,0:T(8,128)S(1)}, u32[]{:S(2)}, u32[]{:S(2)}) collective-permute-start(f32[5,28,128]{2,1,0:T(8,128)S(1)} %get-tuple-element.15), channel_id=1, source_target_pairs={{0,1},{1,0},{2,3},{3,2},{4,5},{5,4},{6,7},{7,6},{8,9},{9,8},{10,11... | collective-permute-start | bytes 215048 | tf_op jit(solution)/shard_map/ppermute | solution.py:771
  14.9 7.2 %first_section.1 = (f32[5,6,128,128]{3,2,1,0:T(8,128)S(1)}, s32[32]{0:T(128)S(1)}) custom-call(f32[5,7,128,128]{3,2,1,0:T(8,128)S(1)} %get-tuple-element.14.state, s32[16]{0:T(128)} %placed_at.3, s32[2,16]{1,0:T(2,128)} %bitcast.15, s32[2,16]{1,0:T(2,128)} %bitcast.12, s32[2,16]{1,0:T(2,128)} %bitcast.14), custom_call_target="tpu_custom_call" | custom-call | flops 29491200 | bytes 14745600 | tf_op jit(solution)/shard_map/first_section/pallas_call | solution.py:715
  22.1 0.0 copy-start.2
  22.1 1.3 %copy-done.2 = f32[5,6,128,128]{3,2,1,0:T(8,128)} copy-done((f32[5,6,128,128]{3,2,1,0:T(8,128)}, f32[5,6,128,128]{3,2,1,0:T(8,128)S(1)}, u32[]{:S(2)}) %copy-start.2) | copy-done | bytes 1966104
  23.4 0.0 collective-permute-done.low.high.halo
  23.4 0.0 all-to-all-done
  23.4 1.8 %relay.1 = f32[352,128]{1,0:T(8,128)} custom-call(s32[32]{0:T(128)S(1)} %get-tuple-element.20.route_at, f32[5,28,128]{2,1,0:T(8,128)S(1)} %collective-permute-done.low.high.halo, f32[320,128]{1,0:T(8,128)S(1)} %bitcast.8), custom_call_target="tpu_custom_call" | custom-call | tf_op jit(solution)/shard_map/relay/pallas_call | solution.py:715
  25.3 4.6 %all-to-all-start.1 = ((f32[32,11,1,128]{3,2,1,0:T(1,128)}), f32[32,11,1,128]{3,2,1,0:T(1,128)S(1)}, u32[]{:S(2)}, u32[]{:S(2)}) async-start(f32[32,11,1,128]{3,2,1,0:T(1,128)} %bitcast.9), calls=%async_computation.1 | async-start | bytes 360448 | tf_op jit(solution)/shard_map/all_to_all | solution.py:767
  29.9 0.0 copy-start.3
  29.9 1.5 %copy-done.3 = f32[5,6,128,128]{3,2,1,0:T(8,128)S(1)} copy-done((f32[5,6,128,128]{3,2,1,0:T(8,128)S(1)}, f32[5,6,128,128]{3,2,1,0:T(8,128)}, u32[]{:S(2)}) %copy-start.3) | copy-done | bytes 1966104
  31.5 11.4 %second_section.1 = (f32[5,6,128,128]{3,2,1,0:T(8,128)S(1)}, f32[5,8,128]{2,1,0:T(8,128)S(1)}, f32[5,8,128]{2,1,0:T(8,128)S(1)}, f32[5,64,128]{2,1,0:T(8,128)S(1)}) custom-call(f32[5,7,128,128]{3,2,1,0:T(8,128)S(1)} %get-tuple-element.14.state, f32[5,28,128]{2,1,0:T(8,128)S(1)} %collective-permute-done.low.high.halo, ...), custom_call_target="tpu_custom_call" | custom-call | flops 29491200 | bytes 14745600 | tf_op jit(solution)/shard_map/second_section/pallas_call | solution.py:715
  42.9 0.0 copy-start
  42.9 1.3 %copy-done = f32[5,6,128,128]{3,2,1,0:T(8,128)} copy-done((f32[5,6,128,128]{3,2,1,0:T(8,128)}, f32[5,6,128,128]{3,2,1,0:T(8,128)S(1)}, u32[]{:S(2)}) %copy-start) | copy-done | bytes 1966104
  44.2 0.0 all-to-all-done.1
  44.2 0.0 copy-start.1
  44.2 1.5 %copy-done.1 = f32[5,6,128,128]{3,2,1,0:T(8,128)S(1)} copy-done((f32[5,6,128,128]{3,2,1,0:T(8,128)S(1)}, f32[5,6,128,128]{3,2,1,0:T(8,128)}, u32[]{:S(2)}) %copy-start.1) | copy-done | bytes 1966104
  45.7 8.4 %strips.1 = (f32[1,6,128,128]{3,2,1,0:T(8,128)}, f32[1,3,6,128,128]{4,3,2,1,0:T(8,128)}, f32[1,6,128,128]{3,2,1,0:T(8,128)}) custom-call(f32[5,64,128]{2,1,0:T(8,128)S(1)} %get-tuple-element.13.own, f32[5,8,128]{2,1,0:T(8,128)S(1)} %get-tuple-element.17.ends_base, f32[5,8,128]{2,1,0:T(8,128)S(1)} %get-tuple-element.18.ends_sec, ...), custom_call_target="tpu_custom_call" | custom-call | tf_op jit(solution)/shard_map/strips/pallas_call | solution.py:715
Async XLA Ops:
  5.8 17.7 %all-to-all-start = ((f32[32,10,1,128]{3,2,1,0:T(1,128)}), f32[32,10,1,128]{3,2,1,0:T(1,128)S(1)}, u32[]{:S(2)}, u32[]{:S(2)}) async-start(f32[32,10,1,128]{3,2,1,0:T(1,128)} %bitcast.10), calls=%async_computation | async-start | bytes 327680 | tf_op jit(solution)/shard_map/all_to_all | solution.py:767
  13.1 10.3 %collective-permute-start = (f32[5,28,128]{2,1,0:T(8,128)S(1)}, f32[5,28,128]{2,1,0:T(8,128)S(1)}, u32[]{:S(2)}, u32[]{:S(2)}) collective-permute-start(f32[5,28,128]{2,1,0:T(8,128)S(1)} %get-tuple-element.15), channel_id=1, source_target_pairs={{0,1},{1,0},{2,3},{3,2},{4,5},{5,4},{6,7},{7,6},{8,9},{9,8},{10,11... | collective-permute-start | bytes 215048 | tf_op jit(solution)/shard_map/ppermute | solution.py:771
  22.1 1.3 %copy-start.2 = (f32[5,6,128,128]{3,2,1,0:T(8,128)}, f32[5,6,128,128]{3,2,1,0:T(8,128)S(1)}, u32[]{:S(2)}) copy-start(f32[5,6,128,128]{3,2,1,0:T(8,128)S(1)} %get-tuple-element.16.part) | copy-start | bytes 5898244
  25.3 18.9 %all-to-all-start.1 = ((f32[32,11,1,128]{3,2,1,0:T(1,128)}), f32[32,11,1,128]{3,2,1,0:T(1,128)S(1)}, u32[]{:S(2)}, u32[]{:S(2)}) async-start(f32[32,11,1,128]{3,2,1,0:T(1,128)} %bitcast.9), calls=%async_computation.1 | async-start | bytes 360448 | tf_op jit(solution)/shard_map/all_to_all | solution.py:767
  29.9 1.5 %copy-start.3 = (f32[5,6,128,128]{3,2,1,0:T(8,128)S(1)}, f32[5,6,128,128]{3,2,1,0:T(8,128)}, u32[]{:S(2)}) copy-start(f32[5,6,128,128]{3,2,1,0:T(8,128)} %copy-done.2) | copy-start | bytes 5898244
  42.9 1.3 %copy-start = (f32[5,6,128,128]{3,2,1,0:T(8,128)}, f32[5,6,128,128]{3,2,1,0:T(8,128)S(1)}, u32[]{:S(2)}) copy-start(f32[5,6,128,128]{3,2,1,0:T(8,128)S(1)} %get-tuple-element.22.out) | copy-start | bytes 5898244
  44.2 1.5 %copy-start.1 = (f32[5,6,128,128]{3,2,1,0:T(8,128)S(1)}, f32[5,6,128,128]{3,2,1,0:T(8,128)}, u32[]{:S(2)}) copy-start(f32[5,6,128,128]{3,2,1,0:T(8,128)} %copy-done) | copy-start | bytes 5898244

commit v6 on v5

--- a/solution.py
+++ b/solution.py
@@ -198,7 +198,7 @@
                 packs = jnp.where(within(lane, 8 * k, 8), x, packs)
             packed[c, pl.ds(r, 8)] = packs
 
-    chunks(rows // 8, pack)
+    chunks(rows // 8, pack, unroll=2)
 
     def cut_ends(k):
         for c in range(CH):
@@ -254,10 +254,10 @@
 
 
 def relay_kernel(
-    halves, rows, planes, devices, route_at, halo, held_got, send,
+    halves, rows, planes, devices, route_at, halo, part, held_got, send,
     held_send, below, above, signs, route, sems,
 ):
-    del halo
+    del halo, part
     wait_all(copy_all([(route_at, route)], sems, 1))
     me = lax.axis_index("blk") * halves + lax.axis_index("ij")
     is_field = (me >= FIRST) & (me < FIRST + DEPTH * planes)
@@ -348,12 +348,12 @@
             emit(c, k, r, val)
 
 
-def chunks(count, body):
+def chunks(count, body, unroll=1):
     def step(n, _):
         body(pl.multiple_of(n * 8, 8))
         return 0
 
-    lax.fori_loop(0, count, step, 0)
+    lax.fori_loop(0, count, step, 0, unroll=unroll)
 
 
 def first_kernel(
@@ -362,12 +362,20 @@
 ):
     planes, rows = part.shape[1], part.shape[2]
     pairs = zip((placed_at, neighbour_at, face_at, orient_at), (placed, neighbour, face, orient))
-    tables = copy_all(list(pairs), sems)
+    wait_all(copy_all(list(pairs), sems))
+    count = rows // 8
+    blocks = placed.shape[0]
+    share = -(-blocks // count)
+
+    def slots(n):
+        return [jnp.minimum((n // 8) * share + i, blocks - 1) for i in range(share)]
 
     def get(c, k, r):
         return state[c, k, pl.ds(r - PAD, 8)]
 
     def fluxes(n):
+        for slot in slots(n):
+            where_is[placed[slot]] = slot
         m = [state[c, planes, pl.ds(n, 8)] for c in range(CH)]
         for j, x in enumerate(metric_terms(m)):
             mets[j, pl.ds(n + PAD, 8)] = x
@@ -376,22 +384,16 @@
     def emit(c, k, r, val):
         part[c, k, pl.ds(r - PAD, 8)] = get(c, k, r) + val
 
-    chunks(rows // 8, fluxes)
-    chunks(rows // 8, lambda n: sum_chunk(mets, fi, w, fk, acc, n + PAD, emit))
-    wait_all(tables)
-    blocks = placed.shape[0]
-
-    def note(slot):
-        where_is[placed[slot]] = slot
-
-    def direct(slot):
-        block = placed[slot]
-        for f in range(2):
-            partner = where_is[neighbour[f, block]]
-            route[2 * slot + f] = partner * 4 + face[f, block] * 2 + orient[f, block]
-
-    loop(blocks, note, unroll=8)
-    loop(blocks, direct, unroll=4)
+    def sums(n):
+        for slot in slots(n):
+            block = placed[slot]
+            for f in range(2):
+                partner = where_is[neighbour[f, block]]
+                route[2 * slot + f] = partner * 4 + face[f, block] * 2 + orient[f, block]
+        sum_chunk(mets, fi, w, fk, acc, n + PAD, emit)
+
+    chunks(count, fluxes, unroll=2)
+    chunks(count, sums, unroll=2)
 
 
 def pack_ends(tall, planes):
@@ -415,7 +417,7 @@
 
 
 def second_kernel(
-    halves, state, low, high, part, out, ends_base, ends_sec, strips,
+    halves, state, low, high, part, out, ends_base, ends_sec, inner,
     tall, tile_fk, tile_w, tile_acc, packed, sec, mets, fi, w, fk, acc, sems,
 ):
     planes, rows = part.shape[1], part.shape[2]
@@ -498,19 +500,15 @@
 
     def pack(n):
         for c in range(CH):
-            x = state[c, planes, pl.ds(n, 8)]
-            at = 8 * planes
-            packs = jnp.where(lane < at + 4, turn(x, at + 6, 1), turn(x, at + 2, 1))
+            packs = turn(state[c, planes, pl.ds(n, 8)], 12 * planes + 6, 1)
             for k in range(planes):
-                x = sec[c, k, pl.ds(n + PAD, 8)]
-                at = 8 * k
-                packs = jnp.where(within(lane, at, 4), turn(x, at + 6, 1), packs)
-                packs = jnp.where(within(lane, at + 4, 4), turn(x, at + 2, 1), packs)
+                x = turn(sec[c, k, pl.ds(n + PAD, 8)], 12 * k + 6, 1)
+                packs = jnp.where(within(lane, 12 * k, 12), x, packs)
             packed[c, pl.ds(n, 8)] = packs
 
-    chunks(rows // 8, pack)
+    chunks(rows // 8, pack, unroll=2)
     for c in range(CH):
-        strips[c] = packed[c].T[0:64]
+        inner[c] = packed[c].T[0 : inner.shape[1]]
 
     def get(c, k, r):
         return sec[c, k, pl.ds(r, 8)]
@@ -519,8 +517,8 @@
         at = pl.ds(r - PAD, 8)
         out[c, k, at] = 0.5 * (state[c, k, at] + (get(c, k, r) + val))
 
-    chunks(rows // 8 + 2, lambda r: flux_chunk(get, mets, fi, w, fk, acc, r))
-    chunks(rows // 8, lambda n: sum_chunk(mets, fi, w, fk, acc, n + PAD, emit))
+    chunks(rows // 8 + 2, lambda r: flux_chunk(get, mets, fi, w, fk, acc, r), unroll=2)
+    chunks(rows // 8, lambda n: sum_chunk(mets, fi, w, fk, acc, n + PAD, emit), unroll=2)
 
 
 def beyond(packed, f, k, rows):
@@ -603,7 +601,8 @@
 
     def move(k, source):
         for c in range(CH):
-            mine = inner[c, k * 8 : k * 8 + 8]
+            at = 12 * k
+            mine = jnp.where(sub < 4, inner[c, at : at + 8], inner[c, at + 4 : at + 12])
             for f in range(2):
                 sec[c, f, k] = mix(f, mine, turn(source[c, f, k], 2 if f == 1 else -2, 0))
 
@@ -696,7 +695,7 @@
     hbm = pl.BlockSpec(memory_space=pltpu.HBM)
     anywhere = pl.BlockSpec(memory_space=pl.ANY)
 
-    def call(kernel, name, outs, ins, out_specs, scratch, cost=None):
+    def call(kernel, name, outs, ins, out_specs, scratch, cost=None, alias=None):
         run = pl.pallas_call(
             kernel,
             out_shape=[
@@ -708,6 +707,7 @@
             scratch_shapes=scratch,
             compiler_params=pltpu.CompilerParams(vmem_limit_bytes=VMEM_MIB * 1024 * 1024),
             cost_estimate=cost,
+            input_output_aliases=alias or {},
             name=name,
         )
 
@@ -743,10 +743,11 @@
     edge = shape(CH, 4 * every, LANES)
     edges = 1 if halves == 2 else 2
     square = shape(CH, LANES, LANES)
+    whole = shape(CH, every, rows, LANES)
     to_send, own, state, *halo = call(
         functools.partial(cut_kernel, halves),
         "cut",
-        [sent, strip, shape(CH, every, rows, LANES)] + [edge] * edges,
+        [sent, strip, whole] + [edge] * edges,
         [hbm] * 8,
         [hbm] + [vmem] * (2 + edges),
         [
@@ -800,7 +801,7 @@
         functools.partial(relay_kernel, halves, rows, planes, devices),
         "relay",
         [passed],
-        [anywhere, anywhere, vmem],
+        [anywhere, anywhere, anywhere, vmem],
         [hbm],
         [
             held(passed),
@@ -810,14 +811,14 @@
             table(route),
             sems(2),
         ],
-    )(route_out, below, got)
+    )(route_out, below, part, got)
     ghosts = swap(relayed)
     tiles = held(shape(CH, 2, every, 8, LANES))
     flat = -(-CH * planes * 8 // LANES)
     out, ends_base, ends_sec, inner = call(
         functools.partial(second_kernel, halves),
         "second_section",
-        [block, rim, rim, strip],
+        [whole, rim, rim, shape(CH, 12 * every + 4, LANES)],
         [vmem] * 4,
         [vmem] * 4,
         [held(shape(2, CH, every, 8, LANES))]
@@ -826,6 +827,7 @@
         + stage
         + [sems(1)],
         cost,
+        {0: 0},
     )(state, below, above, part)
     return call(
         functools.partial(last_kernel, halves, rows, planes),

time: 54.4 us -> 52.4 us (0.963)
  local copies, waits for them, and re-layouts: 5.66 us -> 4.37 us
  Pallas kernels: 34 us -> 33.3 us
    unnamed x8 -> x6, local copies, waits for them, and re-layouts: 5.66 us -> 4.37 us
    pallas_call x5, Pallas kernels: 34 us -> 33.3 us  [keep(): run(*[x if spec not in (vmem, hbm) else pltpu.with_memory_space_constrain...]
where the time goes in v6:
time: 52.4 us; the launch traced here: 52.1 us
  Pallas kernels  33.3 us (64%)
  starting transfers between devices  13.8 us (26%)
  local copies, waits for them, and re-layouts  4.37 us (8%)
  between operations  0.71 us (1%)
    pallas_call x5, Pallas kernels, keep(): run(*[x if spec not in (vmem, hbm) else pltpu.with_memory_space_constrain...  33.3 us
    all_to_all x2, starting transfers between devices, swap(): x = lax.all_to_all(x, ('blk', 'ij'), 0, 0, tiled=True)  11.9 us
    unnamed x6, local copies, waits for them, and re-layouts  4.37 us
    ppermute x1, starting transfers between devices, local(): below = above = lax.ppermute(halo[0], 'ij', [(0, 1), (1, 0)])  1.83 us
  transfers between devices with their start and end apart: 3, of which 0 were waited for; matrix products, arithmetic and copies ran while one was open for 0% of the time, Pallas kernels for 34%

profile of v6, /device:TPU:0, one launch (start us, length us, event | category | flops | bytes accessed | tf_op | source)
XLA Modules:
  0.0 52.1 jit_solution(9504637524509654645)
XLA Ops:
  0.6 5.1 %cut.1 = (f32[320,128]{1,0:T(8,128)}, f32[5,64,128]{2,1,0:T(8,128)S(1)}, f32[5,7,128,128]{3,2,1,0:T(8,128)S(1)}, f32[5,28,128]{2,1,0:T(8,128)S(1)}) custom-call(f32[1,6,128,128]{3,2,1,0:T(8,128)} %dens.1, f32[1,3,6,128,128]{4,3,2,1,0:T(8,128)} %mom.1, f32[1,6,128,128]{3,2,1,0:T(8,128)} %en.1, f32[1,4,128,128]{3,2,1,0:T(8,128)} %met.1, f32[1,128,128]{2,1,0:T(8,128)} %vol.1, ...), custom_call_target="tpu_custom_call" | custom-call | tf_op jit(solution)/shard_map/cut/pallas_call | solution.py:715
  5.7 7.3 %all-to-all-start = ((f32[32,10,1,128]{3,2,1,0:T(1,128)}), f32[32,10,1,128]{3,2,1,0:T(1,128)S(1)}, u32[]{:S(2)}, u32[]{:S(2)}) async-start(f32[32,10,1,128]{3,2,1,0:T(1,128)} %bitcast.10), calls=%async_computation | async-start | bytes 327680 | tf_op jit(solution)/shard_map/all_to_all | solution.py:768
  13.0 1.8 %collective-permute-start = (f32[5,28,128]{2,1,0:T(8,128)S(1)}, f32[5,28,128]{2,1,0:T(8,128)S(1)}, u32[]{:S(2)}, u32[]{:S(2)}) collective-permute-start(f32[5,28,128]{2,1,0:T(8,128)S(1)} %get-tuple-element.15), channel_id=1, source_target_pairs={{0,1},{1,0},{2,3},{3,2},{4,5},{5,4},{6,7},{7,6},{8,9},{9,8},{10,11... | collective-permute-start | bytes 215048 | tf_op jit(solution)/shard_map/ppermute | solution.py:772
  14.9 7.1 %first_section.1 = (f32[5,6,128,128]{3,2,1,0:T(8,128)S(1)}, s32[32]{0:T(128)S(1)}) custom-call(f32[5,7,128,128]{3,2,1,0:T(8,128)S(1)} %get-tuple-element.14.state, s32[16]{0:T(128)} %placed_at.3, s32[2,16]{1,0:T(2,128)} %bitcast.15, s32[2,16]{1,0:T(2,128)} %bitcast.12, s32[2,16]{1,0:T(2,128)} %bitcast.14), custom_call_target="tpu_custom_call" | custom-call | flops 29491200 | bytes 14745600 | tf_op jit(solution)/shard_map/first_section/pallas_call | solution.py:715
  21.9 0.0 copy-start
  21.9 1.3 %copy-done = f32[5,6,128,128]{3,2,1,0:T(8,128)} copy-done((f32[5,6,128,128]{3,2,1,0:T(8,128)}, f32[5,6,128,128]{3,2,1,0:T(8,128)S(1)}, u32[]{:S(2)}) %copy-start) | copy-done | bytes 1966104
  23.2 0.0 collective-permute-done.low.high.halo
  23.2 0.0 all-to-all-done
  23.2 0.0 copy-start.1
  23.2 1.5 %copy-done.1 = f32[5,6,128,128]{3,2,1,0:T(8,128)S(1)} copy-done((f32[5,6,128,128]{3,2,1,0:T(8,128)S(1)}, f32[5,6,128,128]{3,2,1,0:T(8,128)}, u32[]{:S(2)}) %copy-start.1) | copy-done | bytes 1966104
  24.8 1.8 %relay.1 = f32[352,128]{1,0:T(8,128)} custom-call(s32[32]{0:T(128)S(1)} %get-tuple-element.20.route_at, f32[5,28,128]{2,1,0:T(8,128)S(1)} %collective-permute-done.low.high.halo, f32[5,6,128,128]{3,2,1,0:T(8,128)S(1)} %copy-done.1, f32[320,128]{1,0:T(8,128)S(1)} %bitcast.8), custom_call_target="tpu_custom_call" | custom-call | tf_op jit(solution)/shard_map/relay/pallas_call | solution.py:715
  26.6 4.6 %all-to-all-start.1 = ((f32[32,11,1,128]{3,2,1,0:T(1,128)}), f32[32,11,1,128]{3,2,1,0:T(1,128)S(1)}, u32[]{:S(2)}, u32[]{:S(2)}) async-start(f32[32,11,1,128]{3,2,1,0:T(1,128)} %bitcast.9), calls=%async_computation.1 | async-start | bytes 360448 | tf_op jit(solution)/shard_map/all_to_all | solution.py:768
  31.3 0.0 copy-start.2
  31.3 1.5 %copy-done.2 = f32[5,6,128,128]{3,2,1,0:T(8,128)S(1)} copy-done((f32[5,6,128,128]{3,2,1,0:T(8,128)S(1)}, f32[5,6,128,128]{3,2,1,0:T(8,128)}, u32[]{:S(2)}) %copy-start.2) | copy-done | bytes 1966104
  32.8 10.9 %second_section.1 = (f32[5,7,128,128]{3,2,1,0:T(8,128)S(1)}, f32[5,8,128]{2,1,0:T(8,128)S(1)}, f32[5,8,128]{2,1,0:T(8,128)S(1)}, f32[5,88,128]{2,1,0:T(8,128)S(1)}) custom-call(f32[5,7,128,128]{3,2,1,0:T(8,128)S(1)} %get-tuple-element.14.state, f32[5,28,128]{2,1,0:T(8,128)S(1)} %collective-permute-done.low.high.halo, ...), custom_call_target="tpu_custom_call", output_to_operand_aliasing={{0}: (0, {})} | custom-call | flops 29491200 | bytes 14745600 | tf_op jit(solution)/shard_map/second_section/pallas_call | solution.py:715
  43.7 0.0 all-to-all-done.1
  43.7 8.4 %strips.1 = (f32[1,6,128,128]{3,2,1,0:T(8,128)}, f32[1,3,6,128,128]{4,3,2,1,0:T(8,128)}, f32[1,6,128,128]{3,2,1,0:T(8,128)}) custom-call(f32[5,64,128]{2,1,0:T(8,128)S(1)} %get-tuple-element.13.own, f32[5,8,128]{2,1,0:T(8,128)S(1)} %get-tuple-element.17.ends_base, f32[5,8,128]{2,1,0:T(8,128)S(1)} %get-tuple-element.18.ends_sec, ...), custom_call_target="tpu_custom_call" | custom-call | tf_op jit(solution)/shard_map/strips/pallas_call | solution.py:715
Async XLA Ops:
  5.7 17.5 %all-to-all-start = ((f32[32,10,1,128]{3,2,1,0:T(1,128)}), f32[32,10,1,128]{3,2,1,0:T(1,128)S(1)}, u32[]{:S(2)}, u32[]{:S(2)}) async-start(f32[32,10,1,128]{3,2,1,0:T(1,128)} %bitcast.10), calls=%async_computation | async-start | bytes 327680 | tf_op jit(solution)/shard_map/all_to_all | solution.py:768
  13.0 10.2 %collective-permute-start = (f32[5,28,128]{2,1,0:T(8,128)S(1)}, f32[5,28,128]{2,1,0:T(8,128)S(1)}, u32[]{:S(2)}, u32[]{:S(2)}) collective-permute-start(f32[5,28,128]{2,1,0:T(8,128)S(1)} %get-tuple-element.15), channel_id=1, source_target_pairs={{0,1},{1,0},{2,3},{3,2},{4,5},{5,4},{6,7},{7,6},{8,9},{9,8},{10,11... | collective-permute-start | bytes 215048 | tf_op jit(solution)/shard_map/ppermute | solution.py:772
  21.9 1.3 %copy-start = (f32[5,6,128,128]{3,2,1,0:T(8,128)}, f32[5,6,128,128]{3,2,1,0:T(8,128)S(1)}, u32[]{:S(2)}) copy-start(f32[5,6,128,128]{3,2,1,0:T(8,128)S(1)} %get-tuple-element.16.part) | copy-start | bytes 5898244
  23.2 1.5 %copy-start.1 = (f32[5,6,128,128]{3,2,1,0:T(8,128)S(1)}, f32[5,6,128,128]{3,2,1,0:T(8,128)}, u32[]{:S(2)}) copy-start(f32[5,6,128,128]{3,2,1,0:T(8,128)} %copy-done) | copy-start | bytes 5898244
  26.6 17.1 %all-to-all-start.1 = ((f32[32,11,1,128]{3,2,1,0:T(1,128)}), f32[32,11,1,128]{3,2,1,0:T(1,128)S(1)}, u32[]{:S(2)}, u32[]{:S(2)}) async-start(f32[32,11,1,128]{3,2,1,0:T(1,128)} %bitcast.9), calls=%async_computation.1 | async-start | bytes 360448 | tf_op jit(solution)/shard_map/all_to_all | solution.py:768
  31.3 1.5 %copy-start.2 = (f32[5,6,128,128]{3,2,1,0:T(8,128)S(1)}, f32[5,6,128,128]{3,2,1,0:T(8,128)}, u32[]{:S(2)}) copy-start(f32[5,6,128,128]{3,2,1,0:T(8,128)} %copy-done) | copy-start | bytes 5898244

commit v7 on v6

--- a/solution.py
+++ b/solution.py
@@ -110,13 +110,13 @@
 
 def state_pairs(fields, state, planes, start, size):
     dens, mom, en, met, vol = fields
-    at = pl.ds(start, size)
+    at, to = pl.ds(start, size), pl.ds(start + PAD, size)
     return [
-        (dens.at[0, :, at], state.at[0, 0:planes, at]),
-        (mom.at[0, :, :, at], state.at[1:4, 0:planes, at]),
-        (en.at[0, :, at], state.at[4, 0:planes, at]),
-        (met.at[0, :, at], state.at[0:4, planes, at]),
-        (vol.at[0, at], state.at[4, planes, at]),
+        (dens.at[0, :, at], state.at[0, 0:planes, to]),
+        (mom.at[0, :, :, at], state.at[1:4, 0:planes, to]),
+        (en.at[0, :, at], state.at[4, 0:planes, to]),
+        (met.at[0, :, at], state.at[0:4, planes, to]),
+        (vol.at[0, at], state.at[4, planes, to]),
     ]
 
 
@@ -194,7 +194,7 @@
         for c in range(CH):
             packs = jnp.zeros((8, LANES), jnp.float32)
             for k in range(planes + 1):
-                x = turn(state[c, k, pl.ds(r, 8)], 8 * k + 4, 1)
+                x = turn(state[c, k, pl.ds(r + PAD, 8)], 8 * k + 4, 1)
                 packs = jnp.where(within(lane, 8 * k, 8), x, packs)
             packed[c, pl.ds(r, 8)] = packs
 
@@ -202,7 +202,7 @@
 
     def cut_ends(k):
         for c in range(CH):
-            low, high = state[c, k, 0:4], state[c, k, rows - 4 : rows]
+            low, high = state[c, k, PAD : PAD + 4], state[c, k, PAD + rows - 4 : PAD + rows]
             if len(edges) == 1:
                 edges[0][c, k * 4 : k * 4 + 4] = jnp.where(half == 0, high, low)
             else:
@@ -239,7 +239,7 @@
         moved = jnp.where(row >= planes * 8, moved * sign, moved)
         strips[pl.ds(pl.multiple_of(c * 64, 64), 64)] = moved
 
-    loop(CH, orient_strip)
+    loop(CH, orient_strip, unroll=CH)
 
     def put(n):
         k, e = n >> 2, n & 3
@@ -254,37 +254,47 @@
 
 
 def relay_kernel(
-    halves, rows, planes, devices, route_at, halo, part, held_got, send,
-    held_send, below, above, signs, route, sems,
+    halves, rows, planes, slots, route_at, after, *rest,
 ):
-    del halo, part
+    del after
+    sources, (send, held_send, below, above, signs, route, sems) = rest[:-7], rest[-7:]
     wait_all(copy_all([(route_at, route)], sems, 1))
-    me = lax.axis_index("blk") * halves + lax.axis_index("ij")
-    is_field = (me >= FIRST) & (me < FIRST + DEPTH * planes)
+    blocks = route.shape[0] // 2
+    per = slots // blocks
+    half = lax.axis_index("ij")
+    first = lax.axis_index("blk") * per - FIRST
 
     def pass_on(slot):
         for f in range(2):
             code = route[2 * slot + f]
             partner, side, turned = code >> 2, (code >> 1) & 1, code & 1
             sign = jnp.where(turned == 1, -1.0, 1.0)
-
-            def piece(h):
-                h = jnp.where(turned == 1, halves - 1 - h, h)
-                return held_got[pl.ds((partner * halves + h) * SENT + side * CH, CH)]
-
-            pieces = [piece(h) for h in range(halves)]
-            for half in range(halves):
-                at = slot * halves + half
-                held_send[pl.ds(at * PASSED + f * CH, CH)] = pieces[half]
-                below[pl.ds((f * devices + at) * 8, CH)] = pieces[max(half - 1, 0)]
-                above[pl.ds((f * devices + at) * 8, CH)] = pieces[min(half + 1, halves - 1)]
-                signs[pl.ds(f * devices + at, 1)] = jnp.full((1, LANES), sign, jnp.float32)
-
-    loop(devices // halves, pass_on, unroll=4)
-    count = 2 * devices
+            for i in range(per):
+
+                def piece(offset):
+                    part = jnp.clip(half + offset, 0, halves - 1)
+                    part = jnp.where(turned == 1, halves - 1 - part, part)
+                    at = (partner * per + i) * SENT + side * CH
+                    if len(sources) == 1:
+                        return sources[0][pl.ds(part * (slots * SENT) + at, CH)]
+                    mine, others = (x[pl.ds(at, CH)] for x in sources)
+                    return jnp.where(part == half, mine, others)
+
+                at = slot * per + i
+                held_send[pl.ds(at * PASSED + f * CH, CH)] = piece(0)
+                below[pl.ds((f * slots + at) * 8, CH)] = piece(-1)
+                above[pl.ds((f * slots + at) * 8, CH)] = piece(1)
+                signs[pl.ds(f * slots + at, 1)] = jnp.full((1, LANES), sign, jnp.float32)
+
+    loop(blocks, pass_on, unroll=4)
+    count = 2 * slots
     lane = lanes_of((count, LANES))
-    half = rows_of((count, LANES)) % halves
+    piece_at = first + lax.rem(rows_of((count, LANES)), per)
+    is_field = (piece_at >= 0) & (piece_at < DEPTH * planes)
     sign = signs[...]
+    low_end, high_end = half == 0, half == halves - 1
+    low_sign = jnp.where(is_field, -sign, 1.0)
+    high_sign = jnp.where(is_field, sign, 1.0)
     ends = jnp.zeros((count, LANES), jnp.float32)
     for c in range(CH):
         low, high = below[pl.ds(c, count, stride=8)], above[pl.ds(c, count, stride=8)]
@@ -294,13 +304,12 @@
             lane == at + 2, turn(high, at + 3 - rows, 1), turn(high, at + 5 - rows, 1)
         )
         if 1 <= c <= 3:
-            low_wall = jnp.where(is_field, -sign * low_wall, low_wall)
-            high_wall = jnp.where(is_field, sign * high_wall, high_wall)
-        low = jnp.where(half == 0, low_wall, turn(low, at + 2 - rows, 1))
-        high = jnp.where(half == halves - 1, high_wall, turn(high, at + 2, 1))
+            low_wall, high_wall = low_sign * low_wall, high_sign * high_wall
+        low = jnp.where(low_end, low_wall, turn(low, at + 2 - rows, 1))
+        high = jnp.where(high_end, high_wall, turn(high, at + 2, 1))
         ends = jnp.where(within(lane, at, 2), low, jnp.where(within(lane, at + 2, 2), high, ends))
-    held_send[pl.ds(2 * CH, devices, stride=PASSED)] = ends[0:devices] + turn(
-        ends[devices:], 4 * CH, 1
+    held_send[pl.ds(2 * CH, slots, stride=PASSED)] = ends[0:slots] + turn(
+        ends[slots:], 4 * CH, 1
     )
     wait_all(copy_all([(held_send, send)], sems))
 
@@ -357,10 +366,11 @@
 
 
 def first_kernel(
-    state, placed_at, neighbour_at, face_at, orient_at, part, route,
+    state_in, placed_at, neighbour_at, face_at, orient_at, state, route,
     mets, fi, w, fk, acc, placed, neighbour, face, orient, where_is, sems,
 ):
-    planes, rows = part.shape[1], part.shape[2]
+    del state_in
+    planes, rows = fi.shape[1], fi.shape[2] - 2 * PAD
     pairs = zip((placed_at, neighbour_at, face_at, orient_at), (placed, neighbour, face, orient))
     wait_all(copy_all(list(pairs), sems))
     count = rows // 8
@@ -371,18 +381,18 @@
         return [jnp.minimum((n // 8) * share + i, blocks - 1) for i in range(share)]
 
     def get(c, k, r):
-        return state[c, k, pl.ds(r - PAD, 8)]
+        return state[c, k, pl.ds(r, 8)]
 
     def fluxes(n):
         for slot in slots(n):
             where_is[placed[slot]] = slot
-        m = [state[c, planes, pl.ds(n, 8)] for c in range(CH)]
-        for j, x in enumerate(metric_terms(m)):
-            mets[j, pl.ds(n + PAD, 8)] = x
+        at = pl.ds(n + PAD, 8)
+        for j, x in enumerate(metric_terms([state[c, planes, at] for c in range(CH)])):
+            mets[j, at] = x
         flux_chunk(get, mets, fi, w, fk, acc, n + PAD)
 
     def emit(c, k, r, val):
-        part[c, k, pl.ds(r - PAD, 8)] = get(c, k, r) + val
+        state[c, planes + 1 + k, pl.ds(r, 8)] = get(c, k, r) + val
 
     def sums(n):
         for slot in slots(n):
@@ -392,8 +402,8 @@
                 route[2 * slot + f] = partner * 4 + face[f, block] * 2 + orient[f, block]
         sum_chunk(mets, fi, w, fk, acc, n + PAD, emit)
 
-    chunks(count, fluxes, unroll=2)
-    chunks(count, sums, unroll=2)
+    chunks(count, fluxes)
+    chunks(count, sums)
 
 
 def pack_ends(tall, planes):
@@ -416,29 +426,30 @@
     return out
 
 
-def second_kernel(
-    halves, state, low, high, part, out, ends_base, ends_sec, inner,
-    tall, tile_fk, tile_w, tile_acc, packed, sec, mets, fi, w, fk, acc, sems,
+def ends_kernel(
+    halves, state_in, low, high, state, ends_base, ends_sec, inner,
+    tall, tile_fk, tile_w, tile_acc, packed,
 ):
-    planes, rows = part.shape[1], part.shape[2]
+    del state_in
+    planes, rows = tall.shape[2] - 1, state.shape[2] - 2 * PAD
     every = planes + 1
-    arrive = copy_all([(part, sec.at[:, :, PAD : PAD + rows])], sems)
     half = lax.axis_index("ij")
     low_wall, high_wall = half == 0, half == halves - 1
     low_flag, high_flag = jnp.where(low_wall, 1, 0), jnp.where(high_wall, 1, 0)
     sub, lane = rows_of((8, LANES)), lanes_of((8, LANES))
+    top = PAD + rows
 
     for c in range(CH):
         for k in range(every):
-            tall[0, c, k, 4:8] = state[c, k, 0:4]
-            tall[1, c, k, 0:4] = state[c, k, rows - 4 : rows]
+            tall[0, c, k, 4:8] = state[c, k, PAD : PAD + 4]
+            tall[1, c, k, 0:4] = state[c, k, top - 4 : top]
 
     @pl.when(low_wall)
     def _():
         for c in range(CH):
             for k in range(every):
                 for n in range(2):
-                    x = state[c, k, n : n + 1]
+                    x = state[c, k, PAD + n : PAD + n + 1]
                     tall[0, c, k, 3 - n : 4 - n] = -x if 1 <= c <= 3 and k < planes else x
 
     @pl.when(jnp.logical_not(low_wall))
@@ -452,7 +463,7 @@
         for c in range(CH):
             for k in range(every):
                 for n in range(2):
-                    tall[1, c, k, 4 + n : 5 + n] = state[c, k, rows - 1 - n : rows - n]
+                    tall[1, c, k, 4 + n : 5 + n] = state[c, k, top - 1 - n : top - n]
 
     @pl.when(jnp.logical_not(high_wall))
     def _():
@@ -462,19 +473,10 @@
 
     for c, x in enumerate(pack_ends(tall, every)):
         ends_base[c] = x
-
-    def terms(n):
-        m = [state[c, planes, pl.ds(n, 8)] for c in range(CH)]
-        for j, x in enumerate(metric_terms(m)):
-            mets[j, pl.ds(n + PAD, 8)] = x
-
-    chunks(rows // 8, terms)
-    tall_mets = [metric_terms([tall[s, c, planes] for c in range(CH)]) for s in range(2)]
-    for s, at in ((0, PAD - 4), (1, PAD + rows - 4)):
-        for j, x in enumerate(tall_mets[s]):
-            mets[j, at : at + 8] = x
-
-    wait_all(arrive)
+    for c in range(CH):
+        state[c, planes, PAD - 4 : PAD] = tall[0, c, planes, 0:4]
+        state[c, planes, top : top + 4] = tall[1, c, planes, 4:8]
+    mets = [metric_terms([tall[s, c, planes] for c in range(CH)]) for s in range(2)]
 
     def done(c, s, k, x):
         tall[s, c, k] = x
@@ -485,11 +487,11 @@
         else:
             wall = jnp.where(sub == 4, turn(x, 1, 0), turn(x, 3, 0))
             x = jnp.where((sub >= 4) & (high_flag == 1), wall, x)
-        start = PAD - 2 if s == 0 else PAD + rows - 2
-        sec[c, k, start : start + 4] = x[2:6]
+        start = PAD - 2 if s == 0 else top - 2
+        state[c, every + k, start : start + 4] = x[2:6]
 
     tile_stage(
-        planes, lambda c, s, k: tall[s, c, k], tall_mets, lambda *_: along(0), along(1),
+        planes, lambda c, s, k: tall[s, c, k], mets, lambda *_: along(0), along(1),
         (tile_fk, tile_w, tile_acc), done,
     )
     for c, x in enumerate(pack_ends(tall, planes)):
@@ -499,10 +501,11 @@
         packed[...] = jnp.zeros(packed.shape, jnp.float32)
 
     def pack(n):
-        for c in range(CH):
-            packs = turn(state[c, planes, pl.ds(n, 8)], 12 * planes + 6, 1)
+        at = pl.ds(n + PAD, 8)
+        for c in range(CH):
+            packs = turn(state[c, planes, at], 12 * planes + 6, 1)
             for k in range(planes):
-                x = turn(sec[c, k, pl.ds(n + PAD, 8)], 12 * k + 6, 1)
+                x = turn(state[c, every + k, at], 12 * k + 6, 1)
                 packs = jnp.where(within(lane, 12 * k, 12), x, packs)
             packed[c, pl.ds(n, 8)] = packs
 
@@ -510,15 +513,26 @@
     for c in range(CH):
         inner[c] = packed[c].T[0 : inner.shape[1]]
 
+
+def second_kernel(state_in, after, state, mets, fi, w, fk, acc):
+    del state_in, after
+    planes, rows = fi.shape[1], fi.shape[2] - 2 * PAD
+
     def get(c, k, r):
-        return sec[c, k, pl.ds(r, 8)]
+        return state[c, planes + 1 + k, pl.ds(r, 8)]
+
+    def fluxes(n):
+        at = pl.ds(n, 8)
+        for j, x in enumerate(metric_terms([state[c, planes, at] for c in range(CH)])):
+            mets[j, at] = x
+        flux_chunk(get, mets, fi, w, fk, acc, n)
 
     def emit(c, k, r, val):
-        at = pl.ds(r - PAD, 8)
-        out[c, k, at] = 0.5 * (state[c, k, at] + (get(c, k, r) + val))
-
-    chunks(rows // 8 + 2, lambda r: flux_chunk(get, mets, fi, w, fk, acc, r), unroll=2)
-    chunks(rows // 8, lambda n: sum_chunk(mets, fi, w, fk, acc, n + PAD, emit), unroll=2)
+        at = pl.ds(r, 8)
+        state[c, k, at] = 0.5 * (state[c, k, at] + (get(c, k, r) + val))
+
+    chunks(rows // 8 + 2, fluxes)
+    chunks(rows // 8, lambda n: sum_chunk(mets, fi, w, fk, acc, n + PAD, emit))
 
 
 def beyond(packed, f, k, rows):
@@ -670,14 +684,14 @@
             for k in range(planes):
                 index = c * planes + k
                 moved = turn(back[index // per, at], LANES - 4 - 8 * (index % per), 1)
-                full[c, k, at] = jnp.where(inside, out[c, k, at], moved)
+                full[c, k, at] = jnp.where(inside, out[c, k, pl.ds(r + PAD, 8)], moved)
 
         @pl.when(lax.rem(r + 8, size) == 0)
         def _():
             for copy in leave(pl.multiple_of(r + 8 - size, 8)):
                 copy.start()
 
-    chunks(rows // 8, merge)
+    chunks(rows // 8, merge, unroll=2)
     for n in range(rows // size):
         wait_all(leave(n * size))
 
@@ -685,7 +699,6 @@
 def local(mesh_shape, density, momentum, energy, metrics, volume, placed, neighbour, face, orient):
     halves = mesh_shape["ij"]
     blocks = mesh_shape["blk"]
-    devices = blocks * halves
     planes, rows = density.shape[1], density.shape[2]
     every = planes + 1
     fields = (density, momentum, energy, metrics, volume)
@@ -738,12 +751,15 @@
     def sems(count):
         return pltpu.SemaphoreType.DMA((count,))
 
-    sent, passed = shape(devices * SENT, LANES), shape(devices * PASSED, LANES)
+    slots = max(FIRST + DEPTH * every, blocks)
+    slots = -(-slots // blocks) * blocks
+    sent, passed = shape(slots * SENT, LANES), shape(slots * PASSED, LANES)
     strip, rim = shape(CH, 64, LANES), shape(CH, 8, LANES)
     edge = shape(CH, 4 * every, LANES)
     edges = 1 if halves == 2 else 2
-    square = shape(CH, LANES, LANES)
-    whole = shape(CH, every, rows, LANES)
+    square = held(shape(CH, LANES, LANES))
+    tall = rows + 2 * PAD
+    whole = shape(CH, every + planes, tall, LANES)
     to_send, own, state, *halo = call(
         functools.partial(cut_kernel, halves),
         "cut",
@@ -752,7 +768,7 @@
         [hbm] + [vmem] * (2 + edges),
         [
             held(sent),
-            held(square),
+            square,
             held(shape(CH * 64, LANES)),
             table(placed),
             table(face),
@@ -764,8 +780,8 @@
     )(*fields, placed, face, orient)
 
     def swap(x):
-        x = x.reshape(devices, x.shape[0] // devices, 1, LANES)
-        x = lax.all_to_all(x, ("blk", "ij"), 0, 0, tiled=True)
+        x = x.reshape(blocks, x.shape[0] // blocks, 1, LANES)
+        x = lax.all_to_all(x, "blk", 0, 0, tiled=True)
         return x.reshape(x.shape[0] * x.shape[1], LANES)
 
     if edges == 1:
@@ -775,8 +791,6 @@
         above = lax.ppermute(halo[0], "ij", [(i + 1, i) for i in range(halves - 1)])
     got = swap(to_send)
 
-    tall = rows + 2 * PAD
-    block = shape(CH, planes, rows, LANES)
     padded = held(shape(CH, planes, tall, LANES))
     stage = [
         held(shape(8, tall, LANES)),
@@ -788,47 +802,58 @@
     work = planes * rows * LANES
     cost = pl.CostEstimate(flops=300 * work, bytes_accessed=150 * work, transcendentals=work)
     route = jax.ShapeDtypeStruct((2 * blocks,), jnp.int32)
-    part, route_out = call(
+    state, route_out = call(
         first_kernel,
         "first_section",
-        [block, route],
+        [whole, route],
         [vmem] + [hbm] * 4,
         [vmem, smem],
         stage + [table(x) for x in (placed, neighbour, face, orient, placed)] + [sems(4)],
         cost,
+        {0: 0},
     )(state, placed, neighbour, face, orient)
+    if halves == 2:
+        sources = [got, lax.ppermute(got, "ij", [(0, 1), (1, 0)])]
+    else:
+        sources = [lax.all_gather(got, "ij", axis=0, tiled=True)]
+    tiles = held(shape(CH, 2, every, 8, LANES))
+    state, ends_base, ends_sec, inner = call(
+        functools.partial(ends_kernel, halves),
+        "ends",
+        [whole, rim, rim, shape(CH, 12 * every + 4, LANES)],
+        [vmem] * 3,
+        [vmem] * 4,
+        [held(shape(2, CH, every, 8, LANES))] + [tiles] * 3 + [square],
+        cost,
+        {0: 0},
+    )(state, below, above)
     (relayed,) = call(
-        functools.partial(relay_kernel, halves, rows, planes, devices),
+        functools.partial(relay_kernel, halves, rows, planes, slots),
         "relay",
         [passed],
-        [anywhere, anywhere, anywhere, vmem],
+        [anywhere] * 2 + [vmem] * len(sources),
         [hbm],
         [
             held(passed),
-            held(shape(devices * 16, LANES)),
-            held(shape(devices * 16, LANES)),
-            held(shape(devices * 2, LANES)),
+            held(shape(slots * 16, LANES)),
+            held(shape(slots * 16, LANES)),
+            held(shape(slots * 2, LANES)),
             table(route),
             sems(2),
         ],
-    )(route_out, below, part, got)
+    )(route_out, ends_sec, *sources)
     ghosts = swap(relayed)
-    tiles = held(shape(CH, 2, every, 8, LANES))
-    flat = -(-CH * planes * 8 // LANES)
-    out, ends_base, ends_sec, inner = call(
-        functools.partial(second_kernel, halves),
+    (state,) = call(
+        second_kernel,
         "second_section",
-        [whole, rim, rim, shape(CH, 12 * every + 4, LANES)],
-        [vmem] * 4,
-        [vmem] * 4,
-        [held(shape(2, CH, every, 8, LANES))]
-        + [tiles] * 3
-        + [held(square), padded]
-        + stage
-        + [sems(1)],
+        [whole],
+        [vmem, hbm],
+        [vmem],
+        stage,
         cost,
         {0: 0},
-    )(state, below, above, part)
+    )(state, relayed)
+    flat = -(-CH * planes * 8 // LANES)
     return call(
         functools.partial(last_kernel, halves, rows, planes),
         "strips",
@@ -839,10 +864,10 @@
         + [
             held(shape(flat * LANES, LANES)),
             held(shape(flat, LANES, LANES)),
-            held(block),
+            held(shape(CH, planes, rows, LANES)),
             sems(3 * PIECES),
         ],
-    )(own, ends_base, ends_sec, inner, ghosts, out)
+    )(own, ends_base, ends_sec, inner, ghosts, state)
 
 
 def solution(mesh):

time: 52.4 us -> 63.4 us (1.21)
  blocking collectives: 0 us -> 15.9 us
  starting transfers between devices: 13.8 us -> 5.56 us
  local copies, waits for them, and re-layouts: 4.37 us -> 9 us
  Pallas kernels: 33.3 us -> 31.9 us
    all_to_all x0 -> x1, blocking collectives: none -> 15.9 us  [swap(): x = lax.all_to_all(x, 'blk', 0, 0, tiled=True)]
    all_to_all x2 -> x1, starting transfers between devices: 11.9 us -> 3.53 us  [swap(): x = lax.all_to_all(x, 'blk', 0, 0, tiled=True)]
    unnamed x6 -> x8, local copies, waits for them, and re-layouts: 4.37 us -> 9 us
    ppermute x0 -> x1, starting transfers between devices: none -> 1.49 us  [local(): sources = [got, lax.ppermute(got, 'ij', [(0, 1), (1, 0)])]]
    pallas_call x5 -> x6, Pallas kernels: 33.3 us -> 31.9 us  [keep(): run(*[x if spec not in (vmem, hbm) else pltpu.with_memory_space_constrain...]
    ppermute x1, starting transfers between devices: 1.83 us -> 0.53 us  [local(): below = above = lax.ppermute(halo[0], 'ij', [(0, 1), (1, 0)])]
  transfers between devices with their start and end apart: 3 -> 3, of which waited for: 0 -> 0; matrix products, arithmetic and copies ran while one was open for 0% -> 0% of each run, Pallas kernels for 34% -> 28%
where the time goes in v7:
time: 63.4 us; the launch traced here: 63 us
  Pallas kernels  31.9 us (50%)
  blocking collectives  15.9 us (25%)
  local copies, waits for them, and re-layouts  9 us (14%)
  starting transfers between devices  5.56 us (9%)
  between operations  0.71 us (1%)
    pallas_call x6, Pallas kernels, keep(): run(*[x if spec not in (vmem, hbm) else pltpu.with_memory_space_constrain...  31.9 us
    all_to_all x1, blocking collectives, swap(): x = lax.all_to_all(x, 'blk', 0, 0, tiled=True)  15.9 us
    unnamed x8, local copies, waits for them, and re-layouts  9 us
    all_to_all x1, starting transfers between devices, swap(): x = lax.all_to_all(x, 'blk', 0, 0, tiled=True)  3.53 us
    ppermute x1, starting transfers between devices, local(): sources = [got, lax.ppermute(got, 'ij', [(0, 1), (1, 0)])]  1.49 us
  transfers between devices with their start and end apart: 3, of which 0 were waited for; matrix products, arithmetic and copies ran while one was open for 0% of the time, Pallas kernels for 28%

profile of v7, /device:TPU:0, one launch (start us, length us, event | category | flops | bytes accessed | tf_op | source)
XLA Modules:
  0.0 63.0 jit_solution(4999547405455824405)
XLA Ops:
  0.6 4.3 %cut.1 = (f32[320,128]{1,0:T(8,128)}, f32[5,64,128]{2,1,0:T(8,128)S(1)}, f32[5,13,144,128]{3,2,1,0:T(8,128)S(1)}, f32[5,28,128]{2,1,0:T(8,128)S(1)}) custom-call(f32[1,6,128,128]{3,2,1,0:T(8,128)} %dens.1, f32[1,3,6,128,128]{4,3,2,1,0:T(8,128)} %mom.1, f32[1,6,128,128]{3,2,1,0:T(8,128)} %en.1, f32[1,4,128,128]{3,2,1,0:T(8,128)} %met.1, f32[1,128,128]{2,1,0:T(8,128)} %vol.1, ...), custom_call_target="tpu_custom_call" | custom-call | tf_op jit(solution)/shard_map/cut/pallas_call | solution.py:728
  4.9 15.9 %all_to_all.10 = f32[16,20,1,128]{3,2,1,0:T(1,128)S(1)} all-to-all(f32[16,20,1,128]{3,2,1,0:T(1,128)} %bitcast.11), channel_id=1, replica_groups=mesh['blk'=16,'ij'=2] {'blk'}, dimensions={0} | all-to-all | bytes 327680 | tf_op jit(solution)/shard_map/all_to_all | solution.py:784
  20.8 1.5 %collective-permute-start.1 = (f32[320,128]{1,0:T(8,128)S(1)}, f32[320,128]{1,0:T(8,128)S(1)}, u32[]{:S(2)}, u32[]{:S(2)}) collective-permute-start(f32[320,128]{1,0:T(8,128)S(1)} %bitcast.8), channel_id=1, source_target_pairs={{0,1},{1,0},{2,3},{3,2},{4,5},{5,4},{6,7},{7,6},{8,9},{9,8},{10,11... | collective-permute-start | bytes 491528 | tf_op jit(solution)/shard_map/ppermute | solution.py:816
  22.3 0.5 collective-permute-start
  22.8 7.8 %first_section.1 = (f32[5,13,144,128]{3,2,1,0:T(8,128)S(1)}, s32[32]{0:T(128)S(1)}) custom-call(f32[5,13,144,128]{3,2,1,0:T(8,128)S(1)} %get-tuple-element.14.state_in, s32[16]{0:T(128)} %placed_at.3, s32[2,16]{1,0:T(2,128)} %bitcast.16, s32[2,16]{1,0:T(2,128)} %bitcast.13, s32[2,16]{1,0:T(2,128)} %bitcast.15), custom_call_target="tpu_custom_call", output_to_operand_aliasing={{0}: (0, {})} | custom-call | flops 29491200 | bytes 14745600 | tf_op jit(solution)/shard_map/first_section/pallas_call | solution.py:728
  30.7 0.0 collective-permute-done.low.high
  30.7 2.8 %ends.1 = (f32[5,13,144,128]{3,2,1,0:T(8,128)S(1)}, f32[5,8,128]{2,1,0:T(8,128)S(1)}, f32[5,8,128]{2,1,0:T(8,128)S(1)}, f32[5,88,128]{2,1,0:T(8,128)S(1)}) custom-call(f32[5,13,144,128]{3,2,1,0:T(8,128)S(1)} %get-tuple-element.15.state_in, f32[5,28,128]{2,1,0:T(8,128)S(1)} %collective-permute-done.low.high, ...), custom_call_target="tpu_custom_call", output_to_operand_aliasing={{0}: (0, {})} | custom-call | flops 29491200 | bytes 14745600 | tf_op jit(solution)/shard_map/ends/pallas_call | solution.py:728
  33.5 0.0 copy-start
  33.5 2.1 %copy-done = f32[5,13,144,128]{3,2,1,0:T(8,128)} copy-done((f32[5,13,144,128]{3,2,1,0:T(8,128)}, f32[5,13,144,128]{3,2,1,0:T(8,128)S(1)}, u32[]{:S(2)}) %copy-start) | copy-done | bytes 4792344
  35.7 0.0 collective-permute-done.1.rest_1_
  35.7 1.9 %relay.1.after = f32[352,128]{1,0:T(8,128)} custom-call(s32[32]{0:T(128)S(1)} %get-tuple-element.20.route_at, f32[5,8,128]{2,1,0:T(8,128)S(1)} %get-tuple-element.18.after.ends_sec, f32[320,128]{1,0:T(8,128)S(1)} %bitcast.9, f32[320,128]{1,0:T(8,128)S(1)} %collective-permute-done.1.rest_1_), custom_call_target="tpu_custom_call" | custom-call | tf_op jit(solution)/shard_map/relay/pallas_call | solution.py:728
  37.5 3.5 %all-to-all-start.1 = ((f32[16,22,1,128]{3,2,1,0:T(1,128)}), f32[16,22,1,128]{3,2,1,0:T(1,128)S(1)}, u32[]{:S(2)}, u32[]{:S(2)}) async-start(f32[16,22,1,128]{3,2,1,0:T(1,128)} %bitcast.10), calls=%async_computation.1 | async-start | bytes 360448 | tf_op jit(solution)/shard_map/all_to_all | solution.py:784
  41.1 0.0 copy-start.1
  41.1 2.3 %copy-done.1 = f32[5,13,144,128]{3,2,1,0:T(8,128)S(1)} copy-done((f32[5,13,144,128]{3,2,1,0:T(8,128)S(1)}, f32[5,13,144,128]{3,2,1,0:T(8,128)}, u32[]{:S(2)}) %copy-start.1) | copy-done | bytes 4792344
  43.4 7.2 %second_section.1.out = f32[5,13,144,128]{3,2,1,0:T(8,128)S(1)} custom-call(f32[5,13,144,128]{3,2,1,0:T(8,128)S(1)} %copy-done.1, f32[352,128]{1,0:T(8,128)} %relay.1.after), custom_call_target="tpu_custom_call", output_to_operand_aliasing={{}: (0, {})} | custom-call | flops 29491200 | bytes 14745600 | tf_op jit(solution)/shard_map/second_section/pallas_call | solution.py:728
  50.6 0.0 copy-start.2
  50.7 2.1 %copy-done.2 = f32[5,13,144,128]{3,2,1,0:T(8,128)} copy-done((f32[5,13,144,128]{3,2,1,0:T(8,128)}, f32[5,13,144,128]{3,2,1,0:T(8,128)S(1)}, u32[]{:S(2)}) %copy-start.2) | copy-done | bytes 4792344
  52.8 0.0 all-to-all-done.1
  52.8 0.0 copy-start.3
  52.8 2.4 %copy-done.3 = f32[5,13,144,128]{3,2,1,0:T(8,128)S(1)} copy-done((f32[5,13,144,128]{3,2,1,0:T(8,128)S(1)}, f32[5,13,144,128]{3,2,1,0:T(8,128)}, u32[]{:S(2)}) %copy-start.3) | copy-done | bytes 4792344
  55.2 7.9 %strips.1 = (f32[1,6,128,128]{3,2,1,0:T(8,128)}, f32[1,3,6,128,128]{4,3,2,1,0:T(8,128)}, f32[1,6,128,128]{3,2,1,0:T(8,128)}) custom-call(f32[5,64,128]{2,1,0:T(8,128)S(1)} %get-tuple-element.13.own, f32[5,8,128]{2,1,0:T(8,128)S(1)} %get-tuple-element.17.ends_base, f32[5,8,128]{2,1,0:T(8,128)S(1)} %get-tuple-element.18.after.ends_sec, ...), custom_call_target="tpu_custom_call" | custom-call | tf_op jit(solution)/shard_map/strips/pallas_call | solution.py:728
Async XLA Ops:
  20.8 14.9 %collective-permute-start.1 = (f32[320,128]{1,0:T(8,128)S(1)}, f32[320,128]{1,0:T(8,128)S(1)}, u32[]{:S(2)}, u32[]{:S(2)}) collective-permute-start(f32[320,128]{1,0:T(8,128)S(1)} %bitcast.8), channel_id=1, source_target_pairs={{0,1},{1,0},{2,3},{3,2},{4,5},{5,4},{6,7},{7,6},{8,9},{9,8},{10,11... | collective-permute-start | bytes 491528 | tf_op jit(solution)/shard_map/ppermute | solution.py:816
  22.3 8.4 %collective-permute-start = (f32[5,28,128]{2,1,0:T(8,128)S(1)}, f32[5,28,128]{2,1,0:T(8,128)S(1)}, u32[]{:S(2)}, u32[]{:S(2)}) collective-permute-start(f32[5,28,128]{2,1,0:T(8,128)S(1)} %get-tuple-element.16), channel_id=1, source_target_pairs={{0,1},{1,0},{2,3},{3,2},{4,5},{5,4},{6,7},{7,6},{8,9},{9,8},{10,11... | collective-permute-start | bytes 215048 | tf_op jit(solution)/shard_map/ppermute | solution.py:788
  33.5 2.2 %copy-start = (f32[5,13,144,128]{3,2,1,0:T(8,128)}, f32[5,13,144,128]{3,2,1,0:T(8,128)S(1)}, u32[]{:S(2)}) copy-start(f32[5,13,144,128]{3,2,1,0:T(8,128)S(1)} %get-tuple-element.22.state_in) | copy-start | bytes 14376964
  37.5 15.3 %all-to-all-start.1 = ((f32[16,22,1,128]{3,2,1,0:T(1,128)}), f32[16,22,1,128]{3,2,1,0:T(1,128)S(1)}, u32[]{:S(2)}, u32[]{:S(2)}) async-start(f32[16,22,1,128]{3,2,1,0:T(1,128)} %bitcast.10), calls=%async_computation.1 | async-start | bytes 360448 | tf_op jit(solution)/shard_map/all_to_all | solution.py:784
  41.1 2.4 %copy-start.1 = (f32[5,13,144,128]{3,2,1,0:T(8,128)S(1)}, f32[5,13,144,128]{3,2,1,0:T(8,128)}, u32[]{:S(2)}) copy-start(f32[5,13,144,128]{3,2,1,0:T(8,128)} %copy-done) | copy-start | bytes 14376964
  50.6 2.1 %copy-start.2 = (f32[5,13,144,128]{3,2,1,0:T(8,128)}, f32[5,13,144,128]{3,2,1,0:T(8,128)S(1)}, u32[]{:S(2)}) copy-start(f32[5,13,144,128]{3,2,1,0:T(8,128)S(1)} %second_section.1.out) | copy-start | bytes 14376964
  52.8 2.4 %copy-start.3 = (f32[5,13,144,128]{3,2,1,0:T(8,128)S(1)}, f32[5,13,144,128]{3,2,1,0:T(8,128)}, u32[]{:S(2)}) copy-start(f32[5,13,144,128]{3,2,1,0:T(8,128)} %copy-done.2) | copy-start | bytes 14376964

commit v8 on v7

--- a/solution.py
+++ b/solution.py
@@ -176,7 +176,7 @@
 
 
 def cut_kernel(
-    halves, dens, mom, en, met, vol, placed_at, face_at, orient_at, send, own, state, *rest
+    halves, dens, mom, en, met, vol, placed_at, face_at, orient_at, send, own, tall, state, *rest
 ):
     edges, rest = rest[: 1 if halves == 2 else 2], rest[1 if halves == 2 else 2 :]
     held_send, packed, strips, placed, face, orient, sems, table_sems, out_sems = rest
@@ -203,6 +203,8 @@
     def cut_ends(k):
         for c in range(CH):
             low, high = state[c, k, PAD : PAD + 4], state[c, k, PAD + rows - 4 : PAD + rows]
+            tall[0, c, k, 4:8] = low
+            tall[1, c, k, 0:4] = high
             if len(edges) == 1:
                 edges[0][c, k * 4 : k * 4 + 4] = jnp.where(half == 0, high, low)
             else:
@@ -372,7 +374,7 @@
     del state_in
     planes, rows = fi.shape[1], fi.shape[2] - 2 * PAD
     pairs = zip((placed_at, neighbour_at, face_at, orient_at), (placed, neighbour, face, orient))
-    wait_all(copy_all(list(pairs), sems))
+    tables = copy_all(list(pairs), sems)
     count = rows // 8
     blocks = placed.shape[0]
     share = -(-blocks // count)
@@ -384,15 +386,13 @@
         return state[c, k, pl.ds(r, 8)]
 
     def fluxes(n):
-        for slot in slots(n):
-            where_is[placed[slot]] = slot
         at = pl.ds(n + PAD, 8)
         for j, x in enumerate(metric_terms([state[c, planes, at] for c in range(CH)])):
             mets[j, at] = x
         flux_chunk(get, mets, fi, w, fk, acc, n + PAD)
 
     def emit(c, k, r, val):
-        state[c, planes + 1 + k, pl.ds(r, 8)] = get(c, k, r) + val
+        state[c, k, pl.ds(r, 8)] = get(c, k, r) + val
 
     def sums(n):
         for slot in slots(n):
@@ -402,8 +402,13 @@
                 route[2 * slot + f] = partner * 4 + face[f, block] * 2 + orient[f, block]
         sum_chunk(mets, fi, w, fk, acc, n + PAD, emit)
 
-    chunks(count, fluxes)
-    chunks(count, sums)
+    def note(slot):
+        where_is[placed[slot]] = slot
+
+    chunks(count, fluxes, unroll=2)
+    wait_all(tables)
+    loop(blocks, note, unroll=8)
+    chunks(count, sums, unroll=2)
 
 
 def pack_ends(tall, planes):
@@ -427,10 +432,10 @@
 
 
 def ends_kernel(
-    halves, state_in, low, high, state, ends_base, ends_sec, inner,
-    tall, tile_fk, tile_w, tile_acc, packed,
+    halves, state_in, tall_in, low, high, state, tall, ends_base, ends_sec, inner,
+    tile_fk, tile_w, tile_acc, packed,
 ):
-    del state_in
+    del state_in, tall_in
     planes, rows = tall.shape[2] - 1, state.shape[2] - 2 * PAD
     every = planes + 1
     half = lax.axis_index("ij")
@@ -439,17 +444,12 @@
     sub, lane = rows_of((8, LANES)), lanes_of((8, LANES))
     top = PAD + rows
 
-    for c in range(CH):
-        for k in range(every):
-            tall[0, c, k, 4:8] = state[c, k, PAD : PAD + 4]
-            tall[1, c, k, 0:4] = state[c, k, top - 4 : top]
-
     @pl.when(low_wall)
     def _():
         for c in range(CH):
             for k in range(every):
                 for n in range(2):
-                    x = state[c, k, PAD + n : PAD + n + 1]
+                    x = tall[0, c, k, 4 + n : 5 + n]
                     tall[0, c, k, 3 - n : 4 - n] = -x if 1 <= c <= 3 and k < planes else x
 
     @pl.when(jnp.logical_not(low_wall))
@@ -463,7 +463,7 @@
         for c in range(CH):
             for k in range(every):
                 for n in range(2):
-                    tall[1, c, k, 4 + n : 5 + n] = state[c, k, top - 1 - n : top - n]
+                    tall[1, c, k, 4 + n : 5 + n] = tall[1, c, k, 3 - n : 4 - n]
 
     @pl.when(jnp.logical_not(high_wall))
     def _():
@@ -488,7 +488,7 @@
             wall = jnp.where(sub == 4, turn(x, 1, 0), turn(x, 3, 0))
             x = jnp.where((sub >= 4) & (high_flag == 1), wall, x)
         start = PAD - 2 if s == 0 else top - 2
-        state[c, every + k, start : start + 4] = x[2:6]
+        state[c, k, start : start + 4] = x[2:6]
 
     tile_stage(
         planes, lambda c, s, k: tall[s, c, k], mets, lambda *_: along(0), along(1),
@@ -505,7 +505,7 @@
         for c in range(CH):
             packs = turn(state[c, planes, at], 12 * planes + 6, 1)
             for k in range(planes):
-                x = turn(state[c, every + k, at], 12 * k + 6, 1)
+                x = turn(state[c, k, at], 12 * k + 6, 1)
                 packs = jnp.where(within(lane, 12 * k, 12), x, packs)
             packed[c, pl.ds(n, 8)] = packs
 
@@ -514,12 +514,16 @@
         inner[c] = packed[c].T[0 : inner.shape[1]]
 
 
-def second_kernel(state_in, after, state, mets, fi, w, fk, acc):
+def second_kernel(
+    state_in, after, dens, mom, en, state, fields, mets, fi, w, fk, acc, sems
+):
     del state_in, after
-    planes, rows = fi.shape[1], fi.shape[2] - 2 * PAD
+    planes, rows = fields.shape[1:3]
+    pairs = [(dens.at[0], fields.at[0]), (mom.at[0], fields.at[1:4]), (en.at[0], fields.at[4])]
+    copies = copy_all(pairs, sems)
 
     def get(c, k, r):
-        return state[c, planes + 1 + k, pl.ds(r, 8)]
+        return state[c, k, pl.ds(r, 8)]
 
     def fluxes(n):
         at = pl.ds(n, 8)
@@ -528,11 +532,12 @@
         flux_chunk(get, mets, fi, w, fk, acc, n)
 
     def emit(c, k, r, val):
-        at = pl.ds(r, 8)
-        state[c, k, at] = 0.5 * (state[c, k, at] + (get(c, k, r) + val))
-
-    chunks(rows // 8 + 2, fluxes)
-    chunks(rows // 8, lambda n: sum_chunk(mets, fi, w, fk, acc, n + PAD, emit))
+        x = 0.5 * (fields[c, k, pl.ds(r - PAD, 8)] + (get(c, k, r) + val))
+        state[c, k, pl.ds(r, 8)] = x
+
+    chunks(rows // 8 + 2, fluxes, unroll=2)
+    wait_all(copies)
+    chunks(rows // 8, lambda n: sum_chunk(mets, fi, w, fk, acc, n + PAD, emit), unroll=2)
 
 
 def beyond(packed, f, k, rows):
@@ -759,13 +764,14 @@
     edges = 1 if halves == 2 else 2
     square = held(shape(CH, LANES, LANES))
     tall = rows + 2 * PAD
-    whole = shape(CH, every + planes, tall, LANES)
-    to_send, own, state, *halo = call(
+    whole = shape(CH, every, tall, LANES)
+    rows_about = shape(2, CH, every, 8, LANES)
+    to_send, own, about, state, *halo = call(
         functools.partial(cut_kernel, halves),
         "cut",
-        [sent, strip, whole] + [edge] * edges,
+        [sent, strip, rows_about, whole] + [edge] * edges,
         [hbm] * 8,
-        [hbm] + [vmem] * (2 + edges),
+        [hbm] + [vmem] * (3 + edges),
         [
             held(sent),
             square,
@@ -812,21 +818,22 @@
         cost,
         {0: 0},
     )(state, placed, neighbour, face, orient)
+    got, route_out, below, above = lax.optimization_barrier((got, route_out, below, above))
     if halves == 2:
         sources = [got, lax.ppermute(got, "ij", [(0, 1), (1, 0)])]
     else:
         sources = [lax.all_gather(got, "ij", axis=0, tiled=True)]
     tiles = held(shape(CH, 2, every, 8, LANES))
-    state, ends_base, ends_sec, inner = call(
+    state, _, ends_base, ends_sec, inner = call(
         functools.partial(ends_kernel, halves),
         "ends",
-        [whole, rim, rim, shape(CH, 12 * every + 4, LANES)],
-        [vmem] * 3,
+        [whole, rows_about, rim, rim, shape(CH, 12 * every + 4, LANES)],
         [vmem] * 4,
-        [held(shape(2, CH, every, 8, LANES))] + [tiles] * 3 + [square],
+        [vmem] * 5,
+        [tiles] * 3 + [square],
         cost,
-        {0: 0},
-    )(state, below, above)
+        {0: 0, 1: 1},
+    )(state, about, below, above)
     (relayed,) = call(
         functools.partial(relay_kernel, halves, rows, planes, slots),
         "relay",
@@ -847,12 +854,12 @@
         second_kernel,
         "second_section",
         [whole],
-        [vmem, hbm],
+        [vmem] + [hbm] * 4,
         [vmem],
-        stage,
+        [held(shape(CH, planes, rows, LANES))] + stage + [sems(3)],
         cost,
         {0: 0},
-    )(state, relayed)
+    )(state, relayed, density, momentum, energy)
     flat = -(-CH * planes * 8 // LANES)
     return call(
         functools.partial(last_kernel, halves, rows, planes),

time: 63.4 us -> 51.4 us (0.81)
  blocking collectives: 15.9 us -> 0 us
  starting transfers between devices: 5.56 us -> 16.2 us
  local copies, waits for them, and re-layouts: 9 us -> 0 us
  waiting for transfers between devices: 0.01 us -> 4.03 us
  Pallas kernels: 31.9 us -> 30.1 us
    all_to_all x1 -> x0, blocking collectives: 15.9 us -> none  [swap(): x = lax.all_to_all(x, 'blk', 0, 0, tiled=True)]
    all_to_all x1 -> x2, starting transfers between devices: 3.53 us -> 13.2 us  [swap(): x = lax.all_to_all(x, 'blk', 0, 0, tiled=True)]
    unnamed x8 -> x0, local copies, waits for them, and re-layouts: 9 us -> none
    all_to_all x1 -> x2, waiting for transfers between devices: 0.01 us -> 2.35 us  [swap(): x = lax.all_to_all(x, 'blk', 0, 0, tiled=True)]
    pallas_call x6, Pallas kernels: 31.9 us -> 30.1 us  [keep(): run(*[x if spec not in (vmem, hbm) else pltpu.with_memory_space_constrain...]
    ppermute x1, waiting for transfers between devices: 0.01 us -> 1.68 us  [local(): sources = [got, lax.ppermute(got, 'ij', [(0, 1), (1, 0)])]]
    ppermute x1, starting transfers between devices: 0.53 us -> 1.56 us  [local(): below = above = lax.ppermute(halo[0], 'ij', [(0, 1), (1, 0)])]
  transfers between devices with their start and end apart: 3 -> 4, of which waited for: 0 -> 3; matrix products, arithmetic and copies ran while one was open for 0% -> 0% of each run, Pallas kernels for 28% -> 31%
where the time goes in v8:
time: 51.4 us; the launch traced here: 51.1 us
  Pallas kernels  30.1 us (59%)
  starting transfers between devices  16.2 us (32%)
  waiting for transfers between devices  4.03 us (8%)
  between operations  0.69 us (1%)
    pallas_call x6, Pallas kernels, keep(): run(*[x if spec not in (vmem, hbm) else pltpu.with_memory_space_constrain...  30.1 us
    all_to_all x2, starting transfers between devices, swap(): x = lax.all_to_all(x, 'blk', 0, 0, tiled=True)  13.2 us
    all_to_all x2, waiting for transfers between devices, swap(): x = lax.all_to_all(x, 'blk', 0, 0, tiled=True)  2.35 us
    ppermute x1, waiting for transfers between devices, local(): sources = [got, lax.ppermute(got, 'ij', [(0, 1), (1, 0)])]  1.68 us
    ppermute x1, starting transfers between devices, local(): below = above = lax.ppermute(halo[0], 'ij', [(0, 1), (1, 0)])  1.56 us
    ppermute x1, starting transfers between devices, local(): sources = [got, lax.ppermute(got, 'ij', [(0, 1), (1, 0)])]  1.49 us
  transfers between devices with their start and end apart: 4, of which 3 were waited for; matrix products, arithmetic and copies ran while one was open for 0% of the time, Pallas kernels for 31%

profile of v8, /device:TPU:0, one launch (start us, length us, event | category | flops | bytes accessed | tf_op | source)
XLA Modules:
  0.0 51.1 jit_solution(13218714368065108770)
XLA Ops:
  0.6 4.3 %cut.1 = (f32[320,128]{1,0:T(8,128)}, f32[5,64,128]{2,1,0:T(8,128)S(1)}, f32[2,5,7,8,128]{4,3,2,1,0:T(8,128)S(1)}, f32[5,7,144,128]{3,2,1,0:T(8,128)S(1)}, f32[5,28,128]{2,1,0:T(8,128)S(1)}) custom-call(f32[1,6,128,128]{3,2,1,0:T(8,128)} %dens.3, f32[1,3,6,128,128]{4,3,2,1,0:T(8,128)} %mom.3, f32[1,6,128,128]{3,2,1,0:T(8,128)} %en.3, ...), custom_call_target="tpu_custom_call" | custom-call | tf_op jit(solution)/shard_map/cut/pallas_call | solution.py:733
  5.0 7.4 %all-to-all-start = ((f32[16,20,1,128]{3,2,1,0:T(1,128)}), f32[16,20,1,128]{3,2,1,0:T(1,128)S(1)}, u32[]{:S(2)}, u32[]{:S(2)}) async-start(f32[16,20,1,128]{3,2,1,0:T(1,128)} %bitcast.11), calls=%async_computation | async-start | bytes 327680 | tf_op jit(solution)/shard_map/all_to_all | solution.py:790
  12.4 1.6 %collective-permute-start = (f32[5,28,128]{2,1,0:T(8,128)S(1)}, f32[5,28,128]{2,1,0:T(8,128)S(1)}, u32[]{:S(2)}, u32[]{:S(2)}) collective-permute-start(f32[5,28,128]{2,1,0:T(8,128)S(1)} %get-tuple-element.24), channel_id=1, source_target_pairs={{0,1},{1,0},{2,3},{3,2},{4,5},{5,4},{6,7},{7,6},{8,9},{9,8},{10,11... | collective-permute-start | bytes 215048 | tf_op jit(solution)/shard_map/ppermute | solution.py:794
  13.9 6.6 %first_section.1 = (f32[5,7,144,128]{3,2,1,0:T(8,128)S(1)}, s32[32]{0:T(128)S(1)}) custom-call(f32[5,7,144,128]{3,2,1,0:T(8,128)S(1)} %get-tuple-element.19.state_in, s32[16]{0:T(128)} %placed_at.3, s32[2,16]{1,0:T(2,128)} %bitcast.16, s32[2,16]{1,0:T(2,128)} %bitcast.13, s32[2,16]{1,0:T(2,128)} %bitcast.15), custom_call_target="tpu_custom_call", output_to_operand_aliasing={{0}: (0, {})} | custom-call | flops 29491200 | bytes 14745600 | tf_op jit(solution)/shard_map/first_section/pallas_call | solution.py:733
  20.5 0.0 collective-permute-done.low.high
  20.5 0.3 all-to-all-done
  20.8 1.5 %collective-permute-start.1 = (f32[320,128]{1,0:T(8,128)S(1)}, f32[320,128]{1,0:T(8,128)S(1)}, u32[]{:S(2)}, u32[]{:S(2)}) collective-permute-start(f32[320,128]{1,0:T(8,128)S(1)} %bitcast.8), channel_id=1, source_target_pairs={{0,1},{1,0},{2,3},{3,2},{4,5},{5,4},{6,7},{7,6},{8,9},{9,8},{10,11... | collective-permute-start | bytes 491528 | tf_op jit(solution)/shard_map/ppermute | solution.py:823
  22.3 2.8 %ends.1 = (f32[5,7,144,128]{3,2,1,0:T(8,128)S(1)}, f32[2,5,7,8,128]{4,3,2,1,0:T(8,128)S(1)}, f32[5,8,128]{2,1,0:T(8,128)S(1)}, f32[5,8,128]{2,1,0:T(8,128)S(1)}, f32[5,88,128]{2,1,0:T(8,128)S(1)}) custom-call(f32[5,7,144,128]{3,2,1,0:T(8,128)S(1)} %get-tuple-element.20.state_in, ...), custom_call_target="tpu_custom_call", output_to_operand_aliasing={{0}: (0, {}), {1}: (1, {})} | custom-call | flops 29491200 | bytes 14745600 | tf_op jit(solution)/shard_map/ends/pallas_call | solution.py:733
  25.1 1.7 %collective-permute-done.1.rest_1_ = f32[320,128]{1,0:T(8,128)S(1)} collective-permute-done((f32[320,128]{1,0:T(8,128)S(1)}, f32[320,128]{1,0:T(8,128)S(1)}, u32[]{:S(2)}, u32[]{:S(2)}) %collective-permute-start.1) | collective-permute-done | bytes 163872 | tf_op jit(solution)/shard_map/ppermute | solution.py:823
  26.8 1.9 %relay.1.after = f32[352,128]{1,0:T(8,128)} custom-call(s32[32]{0:T(128)S(1)} %get-tuple-element.30.route_at, f32[5,8,128]{2,1,0:T(8,128)S(1)} %get-tuple-element.28.after.ends_sec, f32[320,128]{1,0:T(8,128)S(1)} %bitcast.9, f32[320,128]{1,0:T(8,128)S(1)} %collective-permute-done.1.rest_1_), custom_call_target="tpu_custom_call" | custom-call | tf_op jit(solution)/shard_map/relay/pallas_call | solution.py:733
  28.7 5.8 %all-to-all-start.1 = ((f32[16,22,1,128]{3,2,1,0:T(1,128)}), f32[16,22,1,128]{3,2,1,0:T(1,128)S(1)}, u32[]{:S(2)}, u32[]{:S(2)}) async-start(f32[16,22,1,128]{3,2,1,0:T(1,128)} %bitcast.10), calls=%async_computation.1 | async-start | bytes 360448 | tf_op jit(solution)/shard_map/all_to_all | solution.py:790
  34.4 6.7 %second_section.1.out = f32[5,7,144,128]{3,2,1,0:T(8,128)S(1)} custom-call(f32[5,7,144,128]{3,2,1,0:T(8,128)S(1)} %get-tuple-element.32.state_in, f32[352,128]{1,0:T(8,128)} %relay.1.after, f32[1,6,128,128]{3,2,1,0:T(8,128)} %dens.3, f32[1,3,6,128,128]{4,3,2,1,0:T(8,128)} %mom.3, f32[1,6,128,128]{3,2,1,0:T(8,128)} %en.3), custom_call_target="tpu_custom_call", output_to_operand_aliasing={{}: (0, {})} | custom-call | flops 29491200 | bytes 14745600 | tf_op jit(solution)/shard_map/second_section/pallas_call | solution.py:733
  41.1 2.1 %all-to-all-done.1 = f32[16,22,1,128]{3,2,1,0:T(1,128)S(1)} async-done(((f32[16,22,1,128]{3,2,1,0:T(1,128)}), f32[16,22,1,128]{3,2,1,0:T(1,128)S(1)}, u32[]{:S(2)}, u32[]{:S(2)}) %all-to-all-start.1) | async-done | bytes 180256 | tf_op jit(solution)/shard_map/all_to_all | solution.py:790
  43.2 7.9 %strips.1 = (f32[1,6,128,128]{3,2,1,0:T(8,128)}, f32[1,3,6,128,128]{4,3,2,1,0:T(8,128)}, f32[1,6,128,128]{3,2,1,0:T(8,128)}) custom-call(f32[5,64,128]{2,1,0:T(8,128)S(1)} %get-tuple-element.18.own, f32[5,8,128]{2,1,0:T(8,128)S(1)} %get-tuple-element.27.ends_base, f32[5,8,128]{2,1,0:T(8,128)S(1)} %get-tuple-element.28.after.ends_sec, ...), custom_call_target="tpu_custom_call" | custom-call | tf_op jit(solution)/shard_map/strips/pallas_call | solution.py:733
Async XLA Ops:
  5.0 15.9 %all-to-all-start = ((f32[16,20,1,128]{3,2,1,0:T(1,128)}), f32[16,20,1,128]{3,2,1,0:T(1,128)S(1)}, u32[]{:S(2)}, u32[]{:S(2)}) async-start(f32[16,20,1,128]{3,2,1,0:T(1,128)} %bitcast.11), calls=%async_computation | async-start | bytes 327680 | tf_op jit(solution)/shard_map/all_to_all | solution.py:790
  12.4 8.2 %collective-permute-start = (f32[5,28,128]{2,1,0:T(8,128)S(1)}, f32[5,28,128]{2,1,0:T(8,128)S(1)}, u32[]{:S(2)}, u32[]{:S(2)}) collective-permute-start(f32[5,28,128]{2,1,0:T(8,128)S(1)} %get-tuple-element.24), channel_id=1, source_target_pairs={{0,1},{1,0},{2,3},{3,2},{4,5},{5,4},{6,7},{7,6},{8,9},{9,8},{10,11... | collective-permute-start | bytes 215048 | tf_op jit(solution)/shard_map/ppermute | solution.py:794
  20.8 6.0 %collective-permute-start.1 = (f32[320,128]{1,0:T(8,128)S(1)}, f32[320,128]{1,0:T(8,128)S(1)}, u32[]{:S(2)}, u32[]{:S(2)}) collective-permute-start(f32[320,128]{1,0:T(8,128)S(1)} %bitcast.8), channel_id=1, source_target_pairs={{0,1},{1,0},{2,3},{3,2},{4,5},{5,4},{6,7},{7,6},{8,9},{9,8},{10,11... | collective-permute-start | bytes 491528 | tf_op jit(solution)/shard_map/ppermute | solution.py:823
  28.7 14.5 %all-to-all-start.1 = ((f32[16,22,1,128]{3,2,1,0:T(1,128)}), f32[16,22,1,128]{3,2,1,0:T(1,128)S(1)}, u32[]{:S(2)}, u32[]{:S(2)}) async-start(f32[16,22,1,128]{3,2,1,0:T(1,128)} %bitcast.10), calls=%async_computation.1 | async-start | bytes 360448 | tf_op jit(solution)/shard_map/all_to_all | solution.py:790

commit v9 on v8

--- a/solution.py
+++ b/solution.py
@@ -256,47 +256,37 @@
 
 
 def relay_kernel(
-    halves, rows, planes, slots, route_at, after, *rest,
+    halves, rows, planes, devices, route_at, halo, held_got, send,
+    held_send, below, above, signs, route, sems,
 ):
-    del after
-    sources, (send, held_send, below, above, signs, route, sems) = rest[:-7], rest[-7:]
+    del halo
     wait_all(copy_all([(route_at, route)], sems, 1))
-    blocks = route.shape[0] // 2
-    per = slots // blocks
-    half = lax.axis_index("ij")
-    first = lax.axis_index("blk") * per - FIRST
+    me = lax.axis_index("blk") * halves + lax.axis_index("ij")
+    is_field = (me >= FIRST) & (me < FIRST + DEPTH * planes)
 
     def pass_on(slot):
         for f in range(2):
             code = route[2 * slot + f]
             partner, side, turned = code >> 2, (code >> 1) & 1, code & 1
             sign = jnp.where(turned == 1, -1.0, 1.0)
-            for i in range(per):
-
-                def piece(offset):
-                    part = jnp.clip(half + offset, 0, halves - 1)
-                    part = jnp.where(turned == 1, halves - 1 - part, part)
-                    at = (partner * per + i) * SENT + side * CH
-                    if len(sources) == 1:
-                        return sources[0][pl.ds(part * (slots * SENT) + at, CH)]
-                    mine, others = (x[pl.ds(at, CH)] for x in sources)
-                    return jnp.where(part == half, mine, others)
-
-                at = slot * per + i
-                held_send[pl.ds(at * PASSED + f * CH, CH)] = piece(0)
-                below[pl.ds((f * slots + at) * 8, CH)] = piece(-1)
-                above[pl.ds((f * slots + at) * 8, CH)] = piece(1)
-                signs[pl.ds(f * slots + at, 1)] = jnp.full((1, LANES), sign, jnp.float32)
-
-    loop(blocks, pass_on, unroll=4)
-    count = 2 * slots
+
+            def piece(h):
+                h = jnp.where(turned == 1, halves - 1 - h, h)
+                return held_got[pl.ds((partner * halves + h) * SENT + side * CH, CH)]
+
+            pieces = [piece(h) for h in range(halves)]
+            for half in range(halves):
+                at = slot * halves + half
+                held_send[pl.ds(at * PASSED + f * CH, CH)] = pieces[half]
+                below[pl.ds((f * devices + at) * 8, CH)] = pieces[max(half - 1, 0)]
+                above[pl.ds((f * devices + at) * 8, CH)] = pieces[min(half + 1, halves - 1)]
+                signs[pl.ds(f * devices + at, 1)] = jnp.full((1, LANES), sign, jnp.float32)
+
+    loop(devices // halves, pass_on, unroll=4)
+    count = 2 * devices
     lane = lanes_of((count, LANES))
-    piece_at = first + lax.rem(rows_of((count, LANES)), per)
-    is_field = (piece_at >= 0) & (piece_at < DEPTH * planes)
+    half = rows_of((count, LANES)) % halves
     sign = signs[...]
-    low_end, high_end = half == 0, half == halves - 1
-    low_sign = jnp.where(is_field, -sign, 1.0)
-    high_sign = jnp.where(is_field, sign, 1.0)
     ends = jnp.zeros((count, LANES), jnp.float32)
     for c in range(CH):
         low, high = below[pl.ds(c, count, stride=8)], above[pl.ds(c, count, stride=8)]
@@ -306,12 +296,13 @@
             lane == at + 2, turn(high, at + 3 - rows, 1), turn(high, at + 5 - rows, 1)
         )
         if 1 <= c <= 3:
-            low_wall, high_wall = low_sign * low_wall, high_sign * high_wall
-        low = jnp.where(low_end, low_wall, turn(low, at + 2 - rows, 1))
-        high = jnp.where(high_end, high_wall, turn(high, at + 2, 1))
+            low_wall = jnp.where(is_field, -sign * low_wall, low_wall)
+            high_wall = jnp.where(is_field, sign * high_wall, high_wall)
+        low = jnp.where(half == 0, low_wall, turn(low, at + 2 - rows, 1))
+        high = jnp.where(half == halves - 1, high_wall, turn(high, at + 2, 1))
         ends = jnp.where(within(lane, at, 2), low, jnp.where(within(lane, at + 2, 2), high, ends))
-    held_send[pl.ds(2 * CH, slots, stride=PASSED)] = ends[0:slots] + turn(
-        ends[slots:], 4 * CH, 1
+    held_send[pl.ds(2 * CH, devices, stride=PASSED)] = ends[0:devices] + turn(
+        ends[devices:], 4 * CH, 1
     )
     wait_all(copy_all([(held_send, send)], sems))
 
@@ -432,10 +423,10 @@
 
 
 def ends_kernel(
-    halves, state_in, tall_in, low, high, state, tall, ends_base, ends_sec, inner,
+    halves, state_in, tall_in, low, high, after, state, tall, ends_base, ends_sec, inner,
     tile_fk, tile_w, tile_acc, packed,
 ):
-    del state_in, tall_in
+    del state_in, tall_in, after
     planes, rows = tall.shape[2] - 1, state.shape[2] - 2 * PAD
     every = planes + 1
     half = lax.axis_index("ij")
@@ -515,9 +506,9 @@
 
 
 def second_kernel(
-    state_in, after, dens, mom, en, state, fields, mets, fi, w, fk, acc, sems
+    state_in, dens, mom, en, state, fields, mets, fi, w, fk, acc, sems
 ):
-    del state_in, after
+    del state_in
     planes, rows = fields.shape[1:3]
     pairs = [(dens.at[0], fields.at[0]), (mom.at[0], fields.at[1:4]), (en.at[0], fields.at[4])]
     copies = copy_all(pairs, sems)
@@ -756,9 +747,8 @@
     def sems(count):
         return pltpu.SemaphoreType.DMA((count,))
 
-    slots = max(FIRST + DEPTH * every, blocks)
-    slots = -(-slots // blocks) * blocks
-    sent, passed = shape(slots * SENT, LANES), shape(slots * PASSED, LANES)
+    devices = blocks * halves
+    sent, passed = shape(devices * SENT, LANES), shape(devices * PASSED, LANES)
     strip, rim = shape(CH, 64, LANES), shape(CH, 8, LANES)
     edge = shape(CH, 4 * every, LANES)
     edges = 1 if halves == 2 else 2
@@ -786,8 +776,8 @@
     )(*fields, placed, face, orient)
 
     def swap(x):
-        x = x.reshape(blocks, x.shape[0] // blocks, 1, LANES)
-        x = lax.all_to_all(x, "blk", 0, 0, tiled=True)
+        x = x.reshape(devices, x.shape[0] // devices, 1, LANES)
+        x = lax.all_to_all(x, ("blk", "ij"), 0, 0, tiled=True)
         return x.reshape(x.shape[0] * x.shape[1], LANES)
 
     if edges == 1:
@@ -818,48 +808,43 @@
         cost,
         {0: 0},
     )(state, placed, neighbour, face, orient)
-    got, route_out, below, above = lax.optimization_barrier((got, route_out, below, above))
-    if halves == 2:
-        sources = [got, lax.ppermute(got, "ij", [(0, 1), (1, 0)])]
-    else:
-        sources = [lax.all_gather(got, "ij", axis=0, tiled=True)]
+    (relayed,) = call(
+        functools.partial(relay_kernel, halves, rows, planes, devices),
+        "relay",
+        [passed],
+        [anywhere, anywhere, vmem],
+        [hbm],
+        [
+            held(passed),
+            held(shape(devices * 16, LANES)),
+            held(shape(devices * 16, LANES)),
+            held(shape(devices * 2, LANES)),
+            table(route),
+            sems(2),
+        ],
+    )(route_out, below, got)
+    ghosts = swap(relayed)
     tiles = held(shape(CH, 2, every, 8, LANES))
     state, _, ends_base, ends_sec, inner = call(
         functools.partial(ends_kernel, halves),
         "ends",
         [whole, rows_about, rim, rim, shape(CH, 12 * every + 4, LANES)],
-        [vmem] * 4,
+        [vmem] * 4 + [hbm],
         [vmem] * 5,
         [tiles] * 3 + [square],
         cost,
         {0: 0, 1: 1},
-    )(state, about, below, above)
-    (relayed,) = call(
-        functools.partial(relay_kernel, halves, rows, planes, slots),
-        "relay",
-        [passed],
-        [anywhere] * 2 + [vmem] * len(sources),
-        [hbm],
-        [
-            held(passed),
-            held(shape(slots * 16, LANES)),
-            held(shape(slots * 16, LANES)),
-            held(shape(slots * 2, LANES)),
-            table(route),
-            sems(2),
-        ],
-    )(route_out, ends_sec, *sources)
-    ghosts = swap(relayed)
+    )(state, about, below, above, relayed)
     (state,) = call(
         second_kernel,
         "second_section",
         [whole],
-        [vmem] + [hbm] * 4,
+        [vmem] + [hbm] * 3,
         [vmem],
         [held(shape(CH, planes, rows, LANES))] + stage + [sems(3)],
         cost,
         {0: 0},
-    )(state, relayed, density, momentum, energy)
+    )(state, density, momentum, energy)
     flat = -(-CH * planes * 8 // LANES)
     return call(
         functools.partial(last_kernel, halves, rows, planes),

time: 51.4 us -> 45.1 us (0.88)
  starting transfers between devices: 16.2 us -> 12.9 us
  waiting for transfers between devices: 4.03 us -> 0.85 us
  local copies, waits for them, and re-layouts: 0 us -> 0.61 us
    all_to_all x2, starting transfers between devices: 13.2 us -> 11.1 us  [swap(): x = lax.all_to_all(x, ('blk', 'ij'), 0, 0, tiled=True)]
    ppermute x1 -> x0, waiting for transfers between devices: 1.68 us -> none  [local(): sources = [got, lax.ppermute(got, 'ij', [(0, 1), (1, 0)])]]
    all_to_all x2, waiting for transfers between devices: 2.35 us -> 0.85 us  [swap(): x = lax.all_to_all(x, ('blk', 'ij'), 0, 0, tiled=True)]
    ppermute x1 -> x0, starting transfers between devices: 1.49 us -> none  [local(): sources = [got, lax.ppermute(got, 'ij', [(0, 1), (1, 0)])]]
    unnamed x0 -> x4, local copies, waits for them, and re-layouts: none -> 0.61 us
  transfers between devices with their start and end apart: 4 -> 3, of which waited for: 3 -> 1; matrix products, arithmetic and copies ran while one was open for 0% -> 0% of each run, Pallas kernels for 31% -> 35%
where the time goes in v9:
time: 45.1 us; the launch traced here: 44.8 us
  Pallas kernels  29.7 us (66%)
  starting transfers between devices  12.9 us (29%)
  waiting for transfers between devices  0.85 us (2%)
  between operations  0.71 us (2%)
  local copies, waits for them, and re-layouts  0.61 us (1%)
    pallas_call x6, Pallas kernels, keep(): run(*[x if spec not in (vmem, hbm) else pltpu.with_memory_space_constrain...  29.7 us
    all_to_all x2, starting transfers between devices, swap(): x = lax.all_to_all(x, ('blk', 'ij'), 0, 0, tiled=True)  11.1 us
    ppermute x1, starting transfers between devices, local(): below = above = lax.ppermute(halo[0], 'ij', [(0, 1), (1, 0)])  1.83 us
  transfers between devices with their start and end apart: 3, of which 1 were waited for; matrix products, arithmetic and copies ran while one was open for 0% of the time, Pallas kernels for 35%

profile of v9, /device:TPU:0, one launch (start us, length us, event | category | flops | bytes accessed | tf_op | source)
XLA Modules:
  0.0 44.8 jit_solution(8799032954258916889)
XLA Ops:
  0.6 4.3 %cut.1 = (f32[320,128]{1,0:T(8,128)}, f32[5,64,128]{2,1,0:T(8,128)S(1)}, f32[2,5,7,8,128]{4,3,2,1,0:T(8,128)S(1)}, f32[5,7,144,128]{3,2,1,0:T(8,128)S(1)}, f32[5,28,128]{2,1,0:T(8,128)S(1)}) custom-call(f32[1,6,128,128]{3,2,1,0:T(8,128)} %dens.3, f32[1,3,6,128,128]{4,3,2,1,0:T(8,128)} %mom.3, f32[1,6,128,128]{3,2,1,0:T(8,128)} %en.3, ...), custom_call_target="tpu_custom_call" | custom-call | tf_op jit(solution)/shard_map/cut/pallas_call | solution.py:724
  5.0 7.3 %all-to-all-start = ((f32[32,10,1,128]{3,2,1,0:T(1,128)}), f32[32,10,1,128]{3,2,1,0:T(1,128)S(1)}, u32[]{:S(2)}, u32[]{:S(2)}) async-start(f32[32,10,1,128]{3,2,1,0:T(1,128)} %bitcast.10), calls=%async_computation | async-start | bytes 327680 | tf_op jit(solution)/shard_map/all_to_all | solution.py:780
  12.3 1.8 %collective-permute-start = (f32[5,28,128]{2,1,0:T(8,128)S(1)}, f32[5,28,128]{2,1,0:T(8,128)S(1)}, u32[]{:S(2)}, u32[]{:S(2)}) collective-permute-start(f32[5,28,128]{2,1,0:T(8,128)S(1)} %get-tuple-element.18), channel_id=1, source_target_pairs={{0,1},{1,0},{2,3},{3,2},{4,5},{5,4},{6,7},{7,6},{8,9},{9,8},{10,11... | collective-permute-start | bytes 215048 | tf_op jit(solution)/shard_map/ppermute | solution.py:784
  14.1 6.4 %first_section.1 = (f32[5,7,144,128]{3,2,1,0:T(8,128)S(1)}, s32[32]{0:T(128)S(1)}) custom-call(f32[5,7,144,128]{3,2,1,0:T(8,128)S(1)} %get-tuple-element.15.state_in, s32[16]{0:T(128)} %placed_at.3, s32[2,16]{1,0:T(2,128)} %bitcast.15, s32[2,16]{1,0:T(2,128)} %bitcast.12, s32[2,16]{1,0:T(2,128)} %bitcast.14), custom_call_target="tpu_custom_call", output_to_operand_aliasing={{0}: (0, {})} | custom-call | flops 29491200 | bytes 14745600 | tf_op jit(solution)/shard_map/first_section/pallas_call | solution.py:724
  20.5 0.0 collective-permute-done.halo.low.high
  20.6 0.8 %all-to-all-done = f32[32,10,1,128]{3,2,1,0:T(1,128)S(1)} async-done(((f32[32,10,1,128]{3,2,1,0:T(1,128)}), f32[32,10,1,128]{3,2,1,0:T(1,128)S(1)}, u32[]{:S(2)}, u32[]{:S(2)}) %all-to-all-start) | async-done | bytes 163872 | tf_op jit(solution)/shard_map/all_to_all | solution.py:780
  21.4 1.8 %relay.1.after = f32[352,128]{1,0:T(8,128)} custom-call(s32[32]{0:T(128)S(1)} %get-tuple-element.19.route_at, f32[5,28,128]{2,1,0:T(8,128)S(1)} %collective-permute-done.halo.low.high, f32[320,128]{1,0:T(8,128)S(1)} %bitcast.8), custom_call_target="tpu_custom_call" | custom-call | tf_op jit(solution)/shard_map/relay/pallas_call | solution.py:724
  23.2 3.8 %all-to-all-start.1 = ((f32[32,11,1,128]{3,2,1,0:T(1,128)}), f32[32,11,1,128]{3,2,1,0:T(1,128)S(1)}, u32[]{:S(2)}, u32[]{:S(2)}) async-start(f32[32,11,1,128]{3,2,1,0:T(1,128)} %bitcast.9), calls=%async_computation.1 | async-start | bytes 360448 | tf_op jit(solution)/shard_map/all_to_all | solution.py:780
  27.0 2.8 %ends.1 = (f32[5,7,144,128]{3,2,1,0:T(8,128)S(1)}, f32[2,5,7,8,128]{4,3,2,1,0:T(8,128)S(1)}, f32[5,8,128]{2,1,0:T(8,128)S(1)}, f32[5,8,128]{2,1,0:T(8,128)S(1)}, f32[5,88,128]{2,1,0:T(8,128)S(1)}) custom-call(f32[5,7,144,128]{3,2,1,0:T(8,128)S(1)} %get-tuple-element.16.state_in, ...), custom_call_target="tpu_custom_call", output_to_operand_aliasing={{0}: (0, {}), {1}: (1, {})} | custom-call | flops 29491200 | bytes 14745600 | tf_op jit(solution)/shard_map/ends/pallas_call | solution.py:724
  29.9 0.0 copy-start
  29.9 0.6 %copy-done = f32[5,8,128]{2,1,0:T(8,128)} copy-done((f32[5,8,128]{2,1,0:T(8,128)}, f32[5,8,128]{2,1,0:T(8,128)S(1)}, u32[]{:S(2)}) %copy-start) | copy-done | bytes 20504
  30.5 0.0 copy-start.1
  30.5 6.4 %second_section.1.out = f32[5,7,144,128]{3,2,1,0:T(8,128)S(1)} custom-call(f32[5,7,144,128]{3,2,1,0:T(8,128)S(1)} %get-tuple-element.24.state_in, f32[1,6,128,128]{3,2,1,0:T(8,128)} %dens.3, f32[1,3,6,128,128]{4,3,2,1,0:T(8,128)} %mom.3, f32[1,6,128,128]{3,2,1,0:T(8,128)} %en.3), custom_call_target="tpu_custom_call", output_to_operand_aliasing={{}: (0, {})} | custom-call | flops 29491200 | bytes 14745600 | tf_op jit(solution)/shard_map/second_section/pallas_call | solution.py:724
  36.9 0.0 all-to-all-done.1
  36.9 0.0 copy-done.1
  36.9 7.9 %strips.1 = (f32[1,6,128,128]{3,2,1,0:T(8,128)}, f32[1,3,6,128,128]{4,3,2,1,0:T(8,128)}, f32[1,6,128,128]{3,2,1,0:T(8,128)}) custom-call(f32[5,64,128]{2,1,0:T(8,128)S(1)} %get-tuple-element.14.own, f32[5,8,128]{2,1,0:T(8,128)S(1)} %get-tuple-element.21.ends_base, f32[5,8,128]{2,1,0:T(8,128)S(1)} %copy-done.1, f32[5,88,128]{2,1,0:T(8,128)S(1)} %get-tuple-element.23.inner, ...), custom_call_target="tpu_custom_call" | custom-call | tf_op jit(solution)/shard_map/strips/pallas_call | solution.py:724
Async XLA Ops:
  5.0 16.5 %all-to-all-start = ((f32[32,10,1,128]{3,2,1,0:T(1,128)}), f32[32,10,1,128]{3,2,1,0:T(1,128)S(1)}, u32[]{:S(2)}, u32[]{:S(2)}) async-start(f32[32,10,1,128]{3,2,1,0:T(1,128)} %bitcast.10), calls=%async_computation | async-start | bytes 327680 | tf_op jit(solution)/shard_map/all_to_all | solution.py:780
  12.3 8.3 %collective-permute-start = (f32[5,28,128]{2,1,0:T(8,128)S(1)}, f32[5,28,128]{2,1,0:T(8,128)S(1)}, u32[]{:S(2)}, u32[]{:S(2)}) collective-permute-start(f32[5,28,128]{2,1,0:T(8,128)S(1)} %get-tuple-element.18), channel_id=1, source_target_pairs={{0,1},{1,0},{2,3},{3,2},{4,5},{5,4},{6,7},{7,6},{8,9},{9,8},{10,11... | collective-permute-start | bytes 215048 | tf_op jit(solution)/shard_map/ppermute | solution.py:784
  23.2 13.7 %all-to-all-start.1 = ((f32[32,11,1,128]{3,2,1,0:T(1,128)}), f32[32,11,1,128]{3,2,1,0:T(1,128)S(1)}, u32[]{:S(2)}, u32[]{:S(2)}) async-start(f32[32,11,1,128]{3,2,1,0:T(1,128)} %bitcast.9), calls=%async_computation.1 | async-start | bytes 360448 | tf_op jit(solution)/shard_map/all_to_all | solution.py:780
  29.9 0.6 %copy-start = (f32[5,8,128]{2,1,0:T(8,128)}, f32[5,8,128]{2,1,0:T(8,128)S(1)}, u32[]{:S(2)}) copy-start(f32[5,8,128]{2,1,0:T(8,128)S(1)} %get-tuple-element.22.ends_sec) | copy-start | bytes 61444
  30.5 6.4 %copy-start.1 = (f32[5,8,128]{2,1,0:T(8,128)S(1)}, f32[5,8,128]{2,1,0:T(8,128)}, u32[]{:S(2)}) copy-start(f32[5,8,128]{2,1,0:T(8,128)} %copy-done) | copy-start | bytes 61444

commit v10 on v9

--- a/solution.py
+++ b/solution.py
@@ -171,15 +171,15 @@
                     val = val + kv * curve(0, lambda _, o: ws[c - 1, s, at[o]])
                 done(c, s, k, val)
 
-    loop(planes, spread, unroll=2)
-    loop(planes, gather, unroll=2)
+    loop(planes, spread, unroll=3)
+    loop(planes, gather, unroll=3)
 
 
 def cut_kernel(
     halves, dens, mom, en, met, vol, placed_at, face_at, orient_at, send, own, tall, state, *rest
 ):
     edges, rest = rest[: 1 if halves == 2 else 2], rest[1 if halves == 2 else 2 :]
-    held_send, packed, strips, placed, face, orient, sems, table_sems, out_sems = rest
+    packed, strips, placed, face, orient, sems, table_sems = rest
     tables = copy_all(
         [(placed_at, placed), (face_at, face), (orient_at, orient)], table_sems
     )
@@ -248,19 +248,18 @@
         at = (FIRST + n) * SENT
         low = k * 8 + 4 + jnp.where(rising[0], e, 3 - e)
         high = k * 8 + jnp.where(rising[1], 3 - e, e)
-        held_send[pl.ds(at, CH)] = strips[pl.ds(low, CH, stride=64)]
-        held_send[pl.ds(at + CH, CH)] = strips[pl.ds(high, CH, stride=64)]
+        send[pl.ds(at, CH)] = strips[pl.ds(low, CH, stride=64)]
+        send[pl.ds(at + CH, CH)] = strips[pl.ds(high, CH, stride=64)]
 
     loop(DEPTH * (planes + 1), put, unroll=4)
-    wait_all(copy_all([(held_send, send)], out_sems))
 
 
 def relay_kernel(
     halves, rows, planes, devices, route_at, halo, held_got, send,
-    held_send, below, above, signs, route, sems,
+    below, above, signs, route, sems,
 ):
     del halo
-    wait_all(copy_all([(route_at, route)], sems, 1))
+    wait_all(copy_all([(route_at, route)], sems))
     me = lax.axis_index("blk") * halves + lax.axis_index("ij")
     is_field = (me >= FIRST) & (me < FIRST + DEPTH * planes)
 
@@ -277,7 +276,7 @@
             pieces = [piece(h) for h in range(halves)]
             for half in range(halves):
                 at = slot * halves + half
-                held_send[pl.ds(at * PASSED + f * CH, CH)] = pieces[half]
+                send[pl.ds(at * PASSED + f * CH, CH)] = pieces[half]
                 below[pl.ds((f * devices + at) * 8, CH)] = pieces[max(half - 1, 0)]
                 above[pl.ds((f * devices + at) * 8, CH)] = pieces[min(half + 1, halves - 1)]
                 signs[pl.ds(f * devices + at, 1)] = jnp.full((1, LANES), sign, jnp.float32)
@@ -301,10 +300,9 @@
         low = jnp.where(half == 0, low_wall, turn(low, at + 2 - rows, 1))
         high = jnp.where(half == halves - 1, high_wall, turn(high, at + 2, 1))
         ends = jnp.where(within(lane, at, 2), low, jnp.where(within(lane, at + 2, 2), high, ends))
-    held_send[pl.ds(2 * CH, devices, stride=PASSED)] = ends[0:devices] + turn(
+    send[pl.ds(2 * CH, devices, stride=PASSED)] = ends[0:devices] + turn(
         ends[devices:], 4 * CH, 1
     )
-    wait_all(copy_all([(held_send, send)], sems))
 
 
 def flux_chunk(get, mets, fi, w, fk, acc, r):
@@ -422,11 +420,14 @@
     return out
 
 
-def ends_kernel(
-    halves, state_in, tall_in, low, high, after, state, tall, ends_base, ends_sec, inner,
-    tile_fk, tile_w, tile_acc, packed,
+def second_kernel(
+    halves, state_in, tall_in, low, high, dens, mom, en, after,
+    state, tall, ends_base, ends_sec, inner,
+    tile_fk, tile_w, tile_acc, packed, base, mets, fi, w, fk, acc, sems,
 ):
     del state_in, tall_in, after
+    pairs = [(dens.at[0], base.at[0]), (mom.at[0], base.at[1:4]), (en.at[0], base.at[4])]
+    copies = copy_all(pairs, sems)
     planes, rows = tall.shape[2] - 1, state.shape[2] - 2 * PAD
     every = planes + 1
     half = lax.axis_index("ij")
@@ -467,7 +468,7 @@
     for c in range(CH):
         state[c, planes, PAD - 4 : PAD] = tall[0, c, planes, 0:4]
         state[c, planes, top : top + 4] = tall[1, c, planes, 4:8]
-    mets = [metric_terms([tall[s, c, planes] for c in range(CH)]) for s in range(2)]
+    tall_mets = [metric_terms([tall[s, c, planes] for c in range(CH)]) for s in range(2)]
 
     def done(c, s, k, x):
         tall[s, c, k] = x
@@ -482,7 +483,7 @@
         state[c, k, start : start + 4] = x[2:6]
 
     tile_stage(
-        planes, lambda c, s, k: tall[s, c, k], mets, lambda *_: along(0), along(1),
+        planes, lambda c, s, k: tall[s, c, k], tall_mets, lambda *_: along(0), along(1),
         (tile_fk, tile_w, tile_acc), done,
     )
     for c, x in enumerate(pack_ends(tall, planes)):
@@ -504,15 +505,6 @@
     for c in range(CH):
         inner[c] = packed[c].T[0 : inner.shape[1]]
 
-
-def second_kernel(
-    state_in, dens, mom, en, state, fields, mets, fi, w, fk, acc, sems
-):
-    del state_in
-    planes, rows = fields.shape[1:3]
-    pairs = [(dens.at[0], fields.at[0]), (mom.at[0], fields.at[1:4]), (en.at[0], fields.at[4])]
-    copies = copy_all(pairs, sems)
-
     def get(c, k, r):
         return state[c, k, pl.ds(r, 8)]
 
@@ -523,7 +515,7 @@
         flux_chunk(get, mets, fi, w, fk, acc, n)
 
     def emit(c, k, r, val):
-        x = 0.5 * (fields[c, k, pl.ds(r - PAD, 8)] + (get(c, k, r) + val))
+        x = 0.5 * (base[c, k, pl.ds(r - PAD, 8)] + (get(c, k, r) + val))
         state[c, k, pl.ds(r, 8)] = x
 
     chunks(rows // 8 + 2, fluxes, unroll=2)
@@ -761,9 +753,8 @@
         "cut",
         [sent, strip, rows_about, whole] + [edge] * edges,
         [hbm] * 8,
-        [hbm] + [vmem] * (3 + edges),
+        [vmem] * (4 + edges),
         [
-            held(sent),
             square,
             held(shape(CH * 64, LANES)),
             table(placed),
@@ -771,14 +762,14 @@
             table(orient),
             sems(5 * PIECES),
             sems(3),
-            sems(1),
         ],
     )(*fields, placed, face, orient)
 
     def swap(x):
-        x = x.reshape(devices, x.shape[0] // devices, 1, LANES)
+        shape = x.shape
+        x = x.reshape(devices, 1, x.shape[0] * LANES // devices)
         x = lax.all_to_all(x, ("blk", "ij"), 0, 0, tiled=True)
-        return x.reshape(x.shape[0] * x.shape[1], LANES)
+        return x.reshape(shape)
 
     if edges == 1:
         below = above = lax.ppermute(halo[0], "ij", [(0, 1), (1, 0)])
@@ -813,38 +804,27 @@
         "relay",
         [passed],
         [anywhere, anywhere, vmem],
-        [hbm],
+        [vmem],
         [
-            held(passed),
             held(shape(devices * 16, LANES)),
             held(shape(devices * 16, LANES)),
             held(shape(devices * 2, LANES)),
             table(route),
-            sems(2),
+            sems(1),
         ],
     )(route_out, below, got)
     ghosts = swap(relayed)
     tiles = held(shape(CH, 2, every, 8, LANES))
     state, _, ends_base, ends_sec, inner = call(
-        functools.partial(ends_kernel, halves),
-        "ends",
+        functools.partial(second_kernel, halves),
+        "second_section",
         [whole, rows_about, rim, rim, shape(CH, 12 * every + 4, LANES)],
-        [vmem] * 4 + [hbm],
+        [vmem] * 4 + [hbm] * 3 + [anywhere],
         [vmem] * 5,
-        [tiles] * 3 + [square],
+        [tiles] * 3 + [square, held(shape(CH, planes, rows, LANES))] + stage + [sems(3)],
         cost,
         {0: 0, 1: 1},
-    )(state, about, below, above, relayed)
-    (state,) = call(
-        second_kernel,
-        "second_section",
-        [whole],
-        [vmem] + [hbm] * 3,
-        [vmem],
-        [held(shape(CH, planes, rows, LANES))] + stage + [sems(3)],
-        cost,
-        {0: 0},
-    )(state, density, momentum, energy)
+    )(state, about, below, above, density, momentum, energy, relayed)
     flat = -(-CH * planes * 8 // LANES)
     return call(
         functools.partial(last_kernel, halves, rows, planes),

time: 45.1 us -> 49.4 us (1.095)
  Pallas kernels: 29.7 us -> 33.3 us
  local copies, waits for them, and re-layouts: 0.61 us -> 1.33 us
    pallas_call x6 -> x5, Pallas kernels: 29.7 us -> 33.3 us  [keep(): run(*[x if spec not in (vmem, hbm) else pltpu.with_memory_space_constrain...]
    unnamed x4, local copies, waits for them, and re-layouts: 0.61 us -> 1.33 us
  transfers between devices with their start and end apart: 3 -> 3, of which waited for: 1 -> 1; matrix products, arithmetic and copies ran while one was open for 0% -> 0% of each run, Pallas kernels for 35% -> 32%
where the time goes in v10:
time: 49.4 us; the launch traced here: 49.1 us
  Pallas kernels  33.3 us (67%)
  starting transfers between devices  12.9 us (26%)
  local copies, waits for them, and re-layouts  1.33 us (3%)
  waiting for transfers between devices  0.85 us (2%)
  between operations  0.7 us (1%)
    pallas_call x5, Pallas kernels, keep(): run(*[x if spec not in (vmem, hbm) else pltpu.with_memory_space_constrain...  33.3 us
    all_to_all x2, starting transfers between devices, swap(): x = lax.all_to_all(x, ('blk', 'ij'), 0, 0, tiled=True)  11.1 us
    ppermute x1, starting transfers between devices, local(): below = above = lax.ppermute(halo[0], 'ij', [(0, 1), (1, 0)])  1.83 us
    unnamed x4, local copies, waits for them, and re-layouts  1.33 us
  transfers between devices with their start and end apart: 3, of which 1 were waited for; matrix products, arithmetic and copies ran while one was open for 0% of the time, Pallas kernels for 32%

profile of v10, /device:TPU:0, one launch (start us, length us, event | category | flops | bytes accessed | tf_op | source)
XLA Modules:
  0.0 49.1 jit_solution(9960195721097006474)
XLA Ops:
  0.6 4.3 %cut.1 = (f32[320,128]{1,0:T(8,128)}, f32[5,64,128]{2,1,0:T(8,128)S(1)}, f32[2,5,7,8,128]{4,3,2,1,0:T(8,128)S(1)}, f32[5,7,144,128]{3,2,1,0:T(8,128)S(1)}, f32[5,28,128]{2,1,0:T(8,128)S(1)}) custom-call(f32[1,6,128,128]{3,2,1,0:T(8,128)} %dens.3, f32[1,3,6,128,128]{4,3,2,1,0:T(8,128)} %mom.3, f32[1,6,128,128]{3,2,1,0:T(8,128)} %en.3, ...), custom_call_target="tpu_custom_call" | custom-call | tf_op jit(solution)/shard_map/cut/pallas_call | solution.py:716
  4.9 7.3 %all-to-all-start = ((f32[32,1,1280]{2,1,0:T(1,128)}), f32[32,1,1280]{2,1,0:T(1,128)S(1)}, u32[]{:S(2)}, u32[]{:S(2)}) async-start(f32[32,1,1280]{2,1,0:T(1,128)} %bitcast.3), calls=%async_computation | async-start | bytes 327680 | tf_op jit(solution)/shard_map/all_to_all | solution.py:771
  12.3 1.8 %collective-permute-start = (f32[5,28,128]{2,1,0:T(8,128)S(1)}, f32[5,28,128]{2,1,0:T(8,128)S(1)}, u32[]{:S(2)}, u32[]{:S(2)}) collective-permute-start(f32[5,28,128]{2,1,0:T(8,128)S(1)} %get-tuple-element.18), channel_id=1, source_target_pairs={{0,1},{1,0},{2,3},{3,2},{4,5},{5,4},{6,7},{7,6},{8,9},{9,8},{10,11... | collective-permute-start | bytes 215048 | tf_op jit(solution)/shard_map/ppermute | solution.py:775
  14.1 6.4 %first_section.1 = (f32[5,7,144,128]{3,2,1,0:T(8,128)S(1)}, s32[32]{0:T(128)S(1)}) custom-call(f32[5,7,144,128]{3,2,1,0:T(8,128)S(1)} %get-tuple-element.15.state_in, s32[16]{0:T(128)} %placed_at.3, s32[2,16]{1,0:T(2,128)} %bitcast.13, s32[2,16]{1,0:T(2,128)} %bitcast.10, s32[2,16]{1,0:T(2,128)} %bitcast.12), custom_call_target="tpu_custom_call", output_to_operand_aliasing={{0}: (0, {})} | custom-call | flops 29491200 | bytes 14745600 | tf_op jit(solution)/shard_map/first_section/pallas_call | solution.py:716
  20.5 0.0 collective-permute-done.halo.low.high
  20.5 0.8 %all-to-all-done = f32[32,1,1280]{2,1,0:T(1,128)S(1)} async-done(((f32[32,1,1280]{2,1,0:T(1,128)}), f32[32,1,1280]{2,1,0:T(1,128)S(1)}, u32[]{:S(2)}, u32[]{:S(2)}) %all-to-all-start) | async-done | bytes 163872 | tf_op jit(solution)/shard_map/all_to_all | solution.py:771
  21.4 1.8 %relay.1.after = f32[352,128]{1,0:T(8,128)} custom-call(s32[32]{0:T(128)S(1)} %get-tuple-element.19.route_at, f32[5,28,128]{2,1,0:T(8,128)S(1)} %collective-permute-done.halo.low.high, f32[320,128]{1,0:T(8,128)S(1)} %bitcast.8), custom_call_target="tpu_custom_call" | custom-call | tf_op jit(solution)/shard_map/relay/pallas_call | solution.py:716
  23.2 3.8 %all-to-all-start.1 = ((f32[32,1,1408]{2,1,0:T(1,128)}), f32[32,1,1408]{2,1,0:T(1,128)S(1)}, u32[]{:S(2)}, u32[]{:S(2)}) async-start(f32[32,1,1408]{2,1,0:T(1,128)} %bitcast.5), calls=%async_computation.1 | async-start | bytes 360448 | tf_op jit(solution)/shard_map/all_to_all | solution.py:771
  27.0 9.4 %second_section.1 = (f32[5,7,144,128]{3,2,1,0:T(8,128)S(1)}, f32[2,5,7,8,128]{4,3,2,1,0:T(8,128)S(1)}, f32[5,8,128]{2,1,0:T(8,128)S(1)}, f32[5,8,128]{2,1,0:T(8,128)S(1)}, f32[5,88,128]{2,1,0:T(8,128)S(1)}) custom-call(f32[5,7,144,128]{3,2,1,0:T(8,128)S(1)} %get-tuple-element.16.state_in, ...), custom_call_target="tpu_custom_call", output_to_operand_aliasing={{0}: (0, {}), {1}: (1, {})} | custom-call | flops 29491200 | bytes 14745600 | tf_op jit(solution)/shard_map/second_section/pallas_call | solution.py:716
  36.4 0.0 copy-start
  36.4 0.6 %copy-done = f32[5,8,128]{2,1,0:T(8,128)} copy-done((f32[5,8,128]{2,1,0:T(8,128)}, f32[5,8,128]{2,1,0:T(8,128)S(1)}, u32[]{:S(2)}) %copy-start) | copy-done | bytes 20504
  37.0 0.0 all-to-all-done.1
  37.0 0.0 copy-start.1
  37.0 0.7 %copy-done.1 = f32[5,8,128]{2,1,0:T(8,128)S(1)} copy-done((f32[5,8,128]{2,1,0:T(8,128)S(1)}, f32[5,8,128]{2,1,0:T(8,128)}, u32[]{:S(2)}) %copy-start.1) | copy-done | bytes 20504
  37.8 11.4 %strips.1 = (f32[1,6,128,128]{3,2,1,0:T(8,128)}, f32[1,3,6,128,128]{4,3,2,1,0:T(8,128)}, f32[1,6,128,128]{3,2,1,0:T(8,128)}) custom-call(f32[5,64,128]{2,1,0:T(8,128)S(1)} %get-tuple-element.14.own, f32[5,8,128]{2,1,0:T(8,128)S(1)} %get-tuple-element.21.ends_base, f32[5,8,128]{2,1,0:T(8,128)S(1)} %copy-done.1, f32[5,88,128]{2,1,0:T(8,128)S(1)} %get-tuple-element.23.inner, ...), custom_call_target="tpu_custom_call" | custom-call | tf_op jit(solution)/shard_map/strips/pallas_call | solution.py:716
Async XLA Ops:
  4.9 16.5 %all-to-all-start = ((f32[32,1,1280]{2,1,0:T(1,128)}), f32[32,1,1280]{2,1,0:T(1,128)S(1)}, u32[]{:S(2)}, u32[]{:S(2)}) async-start(f32[32,1,1280]{2,1,0:T(1,128)} %bitcast.3), calls=%async_computation | async-start | bytes 327680 | tf_op jit(solution)/shard_map/all_to_all | solution.py:771
  12.3 8.3 %collective-permute-start = (f32[5,28,128]{2,1,0:T(8,128)S(1)}, f32[5,28,128]{2,1,0:T(8,128)S(1)}, u32[]{:S(2)}, u32[]{:S(2)}) collective-permute-start(f32[5,28,128]{2,1,0:T(8,128)S(1)} %get-tuple-element.18), channel_id=1, source_target_pairs={{0,1},{1,0},{2,3},{3,2},{4,5},{5,4},{6,7},{7,6},{8,9},{9,8},{10,11... | collective-permute-start | bytes 215048 | tf_op jit(solution)/shard_map/ppermute | solution.py:775
  23.2 13.8 %all-to-all-start.1 = ((f32[32,1,1408]{2,1,0:T(1,128)}), f32[32,1,1408]{2,1,0:T(1,128)S(1)}, u32[]{:S(2)}, u32[]{:S(2)}) async-start(f32[32,1,1408]{2,1,0:T(1,128)} %bitcast.5), calls=%async_computation.1 | async-start | bytes 360448 | tf_op jit(solution)/shard_map/all_to_all | solution.py:771
  36.4 0.6 %copy-start = (f32[5,8,128]{2,1,0:T(8,128)}, f32[5,8,128]{2,1,0:T(8,128)S(1)}, u32[]{:S(2)}) copy-start(f32[5,8,128]{2,1,0:T(8,128)S(1)} %get-tuple-element.22.ends_sec) | copy-start | bytes 61444
  37.0 0.7 %copy-start.1 = (f32[5,8,128]{2,1,0:T(8,128)S(1)}, f32[5,8,128]{2,1,0:T(8,128)}, u32[]{:S(2)}) copy-start(f32[5,8,128]{2,1,0:T(8,128)} %copy-done) | copy-start | bytes 61444

commit v11 on v9

--- a/solution.py
+++ b/solution.py
@@ -171,8 +171,8 @@
                     val = val + kv * curve(0, lambda _, o: ws[c - 1, s, at[o]])
                 done(c, s, k, val)
 
-    loop(planes, spread, unroll=2)
-    loop(planes, gather, unroll=2)
+    loop(planes, spread)
+    loop(planes, gather)
 
 
 def cut_kernel(
@@ -424,7 +424,7 @@
 
 def ends_kernel(
     halves, state_in, tall_in, low, high, after, state, tall, ends_base, ends_sec, inner,
-    tile_fk, tile_w, tile_acc, packed,
+    tile_fk, tile_w, tile_acc, packed, rims, sems,
 ):
     del state_in, tall_in, after
     planes, rows = tall.shape[2] - 1, state.shape[2] - 2 * PAD
@@ -486,7 +486,8 @@
         (tile_fk, tile_w, tile_acc), done,
     )
     for c, x in enumerate(pack_ends(tall, planes)):
-        ends_sec[c] = x
+        rims[c] = x
+    leaving = copy_all([(rims, ends_sec)], sems)
 
     if rows < LANES:
         packed[...] = jnp.zeros(packed.shape, jnp.float32)
@@ -503,6 +504,7 @@
     chunks(rows // 8, pack, unroll=2)
     for c in range(CH):
         inner[c] = packed[c].T[0 : inner.shape[1]]
+    wait_all(leaving)
 
 
 def second_kernel(
@@ -549,10 +551,11 @@
 
 
 def last_kernel(
-    halves, rows, planes, own, ends_base, ends_sec, inner, got, out,
+    halves, rows, planes, own, ends_base, ends_sec_at, inner, got, out,
     next_dens, next_mom, next_en,
-    base, sec, fk, ws, acc, turned, back, full, sems,
+    base, sec, fk, ws, acc, turned, back, full, ends_sec, sems,
 ):
+    late = copy_all([(ends_sec_at, ends_sec)], sems, 3 * PIECES)
     half = lax.axis_index("ij")
     low_wall, high_wall = half == 0, half == halves - 1
     sub, lane = rows_of((8, LANES)), lanes_of((8, LANES))
@@ -608,6 +611,7 @@
         )
 
     stage(base, ends, vax, vay)
+    wait_all(late)
 
     def move(k, source):
         for c in range(CH):
@@ -830,8 +834,8 @@
         "ends",
         [whole, rows_about, rim, rim, shape(CH, 12 * every + 4, LANES)],
         [vmem] * 4 + [hbm],
-        [vmem] * 5,
-        [tiles] * 3 + [square],
+        [vmem] * 3 + [hbm, vmem],
+        [tiles] * 3 + [square, held(rim), sems(1)],
         cost,
         {0: 0, 1: 1},
     )(state, about, below, above, relayed)
@@ -850,14 +854,15 @@
         functools.partial(last_kernel, halves, rows, planes),
         "strips",
         [shape(*density.shape), shape(*momentum.shape), shape(*energy.shape)],
-        [vmem] * 6,
+        [vmem] * 2 + [hbm] + [vmem] * 3,
         [hbm] * 3,
         [tiles] * 5
         + [
             held(shape(flat * LANES, LANES)),
             held(shape(flat, LANES, LANES)),
             held(shape(CH, planes, rows, LANES)),
-            sems(3 * PIECES),
+            held(rim),
+            sems(3 * PIECES + 1),
         ],
     )(own, ends_base, ends_sec, inner, ghosts, state)
 

time: 45.1 us -> 42.5 us (0.942)
  Pallas kernels: 29.7 us -> 27.7 us
  local copies, waits for them, and re-layouts: 0.61 us -> 0 us
    pallas_call x6, Pallas kernels: 29.7 us -> 27.7 us  [keep(): run(*[x if spec not in (vmem, hbm) else pltpu.with_memory_space_constrain...]
    unnamed x4 -> x0, local copies, waits for them, and re-layouts: 0.61 us -> none
  transfers between devices with their start and end apart: 3 -> 3, of which waited for: 1 -> 1; matrix products, arithmetic and copies ran while one was open for 0% -> 0% of each run, Pallas kernels for 35% -> 38%
where the time goes in v11:
time: 42.5 us; the launch traced here: 42.2 us
  Pallas kernels  27.7 us (65%)
  starting transfers between devices  12.9 us (30%)
  waiting for transfers between devices  0.85 us (2%)
  between operations  0.7 us (2%)
    pallas_call x6, Pallas kernels, keep(): run(*[x if spec not in (vmem, hbm) else pltpu.with_memory_space_constrain...  27.7 us
    all_to_all x2, starting transfers between devices, swap(): x = lax.all_to_all(x, ('blk', 'ij'), 0, 0, tiled=True)  11.1 us
    ppermute x1, starting transfers between devices, local(): below = above = lax.ppermute(halo[0], 'ij', [(0, 1), (1, 0)])  1.83 us
    all_to_all x2, waiting for transfers between devices, swap(): x = lax.all_to_all(x, ('blk', 'ij'), 0, 0, tiled=True)  0.85 us
  transfers between devices with their start and end apart: 3, of which 1 were waited for; matrix products, arithmetic and copies ran while one was open for 0% of the time, Pallas kernels for 38%

profile of v11, /device:TPU:0, one launch (start us, length us, event | category | flops | bytes accessed | tf_op | source)
XLA Modules:
  0.0 42.2 jit_solution(12439555626903762072)
XLA Ops:
  0.6 4.3 %cut.1 = (f32[320,128]{1,0:T(8,128)}, f32[5,64,128]{2,1,0:T(8,128)S(1)}, f32[2,5,7,8,128]{4,3,2,1,0:T(8,128)S(1)}, f32[5,7,144,128]{3,2,1,0:T(8,128)S(1)}, f32[5,28,128]{2,1,0:T(8,128)S(1)}) custom-call(f32[1,6,128,128]{3,2,1,0:T(8,128)} %dens.3, f32[1,3,6,128,128]{4,3,2,1,0:T(8,128)} %mom.3, f32[1,6,128,128]{3,2,1,0:T(8,128)} %en.3, ...), custom_call_target="tpu_custom_call" | custom-call | tf_op jit(solution)/shard_map/cut/pallas_call | solution.py:728
  5.0 7.3 %all-to-all-start = ((f32[32,10,1,128]{3,2,1,0:T(1,128)}), f32[32,10,1,128]{3,2,1,0:T(1,128)S(1)}, u32[]{:S(2)}, u32[]{:S(2)}) async-start(f32[32,10,1,128]{3,2,1,0:T(1,128)} %bitcast.10), calls=%async_computation | async-start | bytes 327680 | tf_op jit(solution)/shard_map/all_to_all | solution.py:784
  12.3 1.8 %collective-permute-start = (f32[5,28,128]{2,1,0:T(8,128)S(1)}, f32[5,28,128]{2,1,0:T(8,128)S(1)}, u32[]{:S(2)}, u32[]{:S(2)}) collective-permute-start(f32[5,28,128]{2,1,0:T(8,128)S(1)} %get-tuple-element.18), channel_id=1, source_target_pairs={{0,1},{1,0},{2,3},{3,2},{4,5},{5,4},{6,7},{7,6},{8,9},{9,8},{10,11... | collective-permute-start | bytes 215048 | tf_op jit(solution)/shard_map/ppermute | solution.py:788
  14.1 6.4 %first_section.1 = (f32[5,7,144,128]{3,2,1,0:T(8,128)S(1)}, s32[32]{0:T(128)S(1)}) custom-call(f32[5,7,144,128]{3,2,1,0:T(8,128)S(1)} %get-tuple-element.15.state_in, s32[16]{0:T(128)} %placed_at.3, s32[2,16]{1,0:T(2,128)} %bitcast.15, s32[2,16]{1,0:T(2,128)} %bitcast.12, s32[2,16]{1,0:T(2,128)} %bitcast.14), custom_call_target="tpu_custom_call", output_to_operand_aliasing={{0}: (0, {})} | custom-call | flops 29491200 | bytes 14745600 | tf_op jit(solution)/shard_map/first_section/pallas_call | solution.py:728
  20.5 0.0 collective-permute-done.halo.low.high
  20.6 0.8 %all-to-all-done = f32[32,10,1,128]{3,2,1,0:T(1,128)S(1)} async-done(((f32[32,10,1,128]{3,2,1,0:T(1,128)}), f32[32,10,1,128]{3,2,1,0:T(1,128)S(1)}, u32[]{:S(2)}, u32[]{:S(2)}) %all-to-all-start) | async-done | bytes 163872 | tf_op jit(solution)/shard_map/all_to_all | solution.py:784
  21.4 1.8 %relay.1.after = f32[352,128]{1,0:T(8,128)} custom-call(s32[32]{0:T(128)S(1)} %get-tuple-element.19.route_at, f32[5,28,128]{2,1,0:T(8,128)S(1)} %collective-permute-done.halo.low.high, f32[320,128]{1,0:T(8,128)S(1)} %bitcast.8), custom_call_target="tpu_custom_call" | custom-call | tf_op jit(solution)/shard_map/relay/pallas_call | solution.py:728
  23.2 3.8 %all-to-all-start.1 = ((f32[32,11,1,128]{3,2,1,0:T(1,128)}), f32[32,11,1,128]{3,2,1,0:T(1,128)S(1)}, u32[]{:S(2)}, u32[]{:S(2)}) async-start(f32[32,11,1,128]{3,2,1,0:T(1,128)} %bitcast.9), calls=%async_computation.1 | async-start | bytes 360448 | tf_op jit(solution)/shard_map/all_to_all | solution.py:784
  27.0 3.1 %ends.1 = (f32[5,7,144,128]{3,2,1,0:T(8,128)S(1)}, f32[2,5,7,8,128]{4,3,2,1,0:T(8,128)S(1)}, f32[5,8,128]{2,1,0:T(8,128)S(1)}, f32[5,8,128]{2,1,0:T(8,128)}, f32[5,88,128]{2,1,0:T(8,128)S(1)}) custom-call(f32[5,7,144,128]{3,2,1,0:T(8,128)S(1)} %get-tuple-element.16.state_in, ...), custom_call_target="tpu_custom_call", output_to_operand_aliasing={{0}: (0, {}), {1}: (1, {})} | custom-call | flops 29491200 | bytes 14745600 | tf_op jit(solution)/shard_map/ends/pallas_call | solution.py:728
  30.2 6.4 %second_section.1.out = f32[5,7,144,128]{3,2,1,0:T(8,128)S(1)} custom-call(f32[5,7,144,128]{3,2,1,0:T(8,128)S(1)} %get-tuple-element.24.state_in, f32[1,6,128,128]{3,2,1,0:T(8,128)} %dens.3, f32[1,3,6,128,128]{4,3,2,1,0:T(8,128)} %mom.3, f32[1,6,128,128]{3,2,1,0:T(8,128)} %en.3), custom_call_target="tpu_custom_call", output_to_operand_aliasing={{}: (0, {})} | custom-call | flops 29491200 | bytes 14745600 | tf_op jit(solution)/shard_map/second_section/pallas_call | solution.py:728
  36.6 0.0 all-to-all-done.1
  36.6 5.6 %strips.1 = (f32[1,6,128,128]{3,2,1,0:T(8,128)}, f32[1,3,6,128,128]{4,3,2,1,0:T(8,128)}, f32[1,6,128,128]{3,2,1,0:T(8,128)}) custom-call(f32[5,64,128]{2,1,0:T(8,128)S(1)} %get-tuple-element.14.own, f32[5,8,128]{2,1,0:T(8,128)S(1)} %get-tuple-element.21.ends_base, f32[5,8,128]{2,1,0:T(8,128)} %get-tuple-element.22.ends_sec_at, ...), custom_call_target="tpu_custom_call" | custom-call | tf_op jit(solution)/shard_map/strips/pallas_call | solution.py:728
Async XLA Ops:
  5.0 16.5 %all-to-all-start = ((f32[32,10,1,128]{3,2,1,0:T(1,128)}), f32[32,10,1,128]{3,2,1,0:T(1,128)S(1)}, u32[]{:S(2)}, u32[]{:S(2)}) async-start(f32[32,10,1,128]{3,2,1,0:T(1,128)} %bitcast.10), calls=%async_computation | async-start | bytes 327680 | tf_op jit(solution)/shard_map/all_to_all | solution.py:784
  12.3 8.3 %collective-permute-start = (f32[5,28,128]{2,1,0:T(8,128)S(1)}, f32[5,28,128]{2,1,0:T(8,128)S(1)}, u32[]{:S(2)}, u32[]{:S(2)}) collective-permute-start(f32[5,28,128]{2,1,0:T(8,128)S(1)} %get-tuple-element.18), channel_id=1, source_target_pairs={{0,1},{1,0},{2,3},{3,2},{4,5},{5,4},{6,7},{7,6},{8,9},{9,8},{10,11... | collective-permute-start | bytes 215048 | tf_op jit(solution)/shard_map/ppermute | solution.py:788
  23.2 13.4 %all-to-all-start.1 = ((f32[32,11,1,128]{3,2,1,0:T(1,128)}), f32[32,11,1,128]{3,2,1,0:T(1,128)S(1)}, u32[]{:S(2)}, u32[]{:S(2)}) async-start(f32[32,11,1,128]{3,2,1,0:T(1,128)} %bitcast.9), calls=%async_computation.1 | async-start | bytes 360448 | tf_op jit(solution)/shard_map/all_to_all | solution.py:784

commit v12 on v11

--- a/solution.py
+++ b/solution.py
@@ -533,12 +533,10 @@
     chunks(rows // 8, lambda n: sum_chunk(mets, fi, w, fk, acc, n + PAD, emit), unroll=2)
 
 
-def beyond(packed, f, k, rows):
-    base = 28 * f + 4 * k
-    low = roll_by(packed, LANES - 2 - base)
+def beyond(low, rows):
     top = rows % LANES
-    high = low if top == 0 else roll_by(packed, top - 2 - base)
-    lane = lanes_of(packed.shape)
+    high = low if top == 0 else turn(low, top, 1)
+    lane = lanes_of(low.shape)
 
     def at(x, o):
         if o < 0:
@@ -553,7 +551,7 @@
 def last_kernel(
     halves, rows, planes, own, ends_base, ends_sec_at, inner, got, out,
     next_dens, next_mom, next_en,
-    base, sec, fk, ws, acc, turned, back, full, ends_sec, sems,
+    base, sec, fk, ws, acc, rims, turned, back, full, ends_sec, sems,
 ):
     late = copy_all([(ends_sec_at, ends_sec)], sems, 3 * PIECES)
     half = lax.axis_index("ij")
@@ -599,12 +597,15 @@
     def stage(held, ends, gx, gy):
         mets = [metric_terms([held[c, f, planes] for c in range(CH)]) for f in range(2)]
         w, p, h = point(ends)
-        rims = (flux(ends, w, p, h, gx, gy), w)
+        for n, x in enumerate((*flux(ends, w, p, h, gx, gy), *w)):
+            for f in range(2):
+                for k in range(planes):
+                    rims[n, f, k] = turn(x, LANES - 2 - (28 * f + 4 * k), 1)
         tile_stage(
             planes,
             lambda c, f, k: held[c, f, k],
             mets,
-            lambda kind, c, f, k: beyond(rims[kind][c], f, k, rows),
+            lambda kind, c, f, k: beyond(rims[CH * kind + c, f, k], rows),
             along(0),
             (fk, ws, acc),
             keep,
@@ -639,21 +640,29 @@
             add = add + cw * curve(w1[c - 1] - w0[c - 1], at_j)
         x = jnp.where(low_lanes, ends_sec[c], turn(ends_sec[c], 28, 1))
         second.append(shifted(x + jnp.where(touched, add, 0.0)))
-    walled = low_wall | high_wall
-
-    for k in range(planes):
-        for f in range(2):
-            to = 28 * f + 4 * k
-            first = jnp.where(walled, jnp.where(low_wall, to, to + 2), -8)
-            shift = jnp.where(low_wall, (to - 1) % LANES, (to + 3 - rows) % LANES)
-            next_shift = jnp.where(low_wall, (to + 1) % LANES, (to + 5 - rows) % LANES)
-            for c in range(CH):
-                x = sec[c, f, k]
-                one, two = pltpu.roll(x, shift, 1), pltpu.roll(x, next_shift, 1)
-                x = jnp.where(lane == first, one, two)
-                if 1 <= c <= 3:
-                    x = jnp.where(low_wall, -1.0, 1.0) * x
-                second[c] = jnp.where(within(lane, first, 2), x, second[c])
+
+    def mirror(at_low):
+        def reflect(*second):
+            second = list(second)
+            for k in range(planes):
+                for f in range(2):
+                    to = 28 * f + 4 * k + (0 if at_low else 2)
+                    shift = to - 1 if at_low else to + 1 - rows
+                    for c in range(CH):
+                        x = sec[c, f, k]
+                        x = jnp.where(lane == to, turn(x, shift, 1), turn(x, shift + 2, 1))
+                        if at_low and 1 <= c <= 3:
+                            x = -x
+                        second[c] = jnp.where(within(lane, to, 2), x, second[c])
+            return tuple(second)
+
+        return reflect
+
+    def leave(*second):
+        return second
+
+    second = lax.cond(low_wall, mirror(True), leave, *second)
+    second = lax.cond(high_wall, mirror(False), leave, *second)
     stage(sec, second, shifted(vax), shifted(vay))
 
     per = LANES // 8
@@ -858,6 +867,7 @@
         [hbm] * 3,
         [tiles] * 5
         + [
+            held(shape(CH + 4, 2, planes, 8, LANES)),
             held(shape(flat * LANES, LANES)),
             held(shape(flat, LANES, LANES)),
             held(shape(CH, planes, rows, LANES)),

time: 42.5 us -> 42.1 us (level)
  no operation moved by 1% of the time
where the time goes in v12:
time: 42.1 us; the launch traced here: 41.8 us
  Pallas kernels  27.4 us (65%)
  starting transfers between devices  12.9 us (31%)
  waiting for transfers between devices  0.85 us (2%)
  between operations  0.7 us (2%)
    pallas_call x6, Pallas kernels, keep(): run(*[x if spec not in (vmem, hbm) else pltpu.with_memory_space_constrain...  27.4 us
    all_to_all x2, starting transfers between devices, swap(): x = lax.all_to_all(x, ('blk', 'ij'), 0, 0, tiled=True)  11.1 us
    ppermute x1, starting transfers between devices, local(): below = above = lax.ppermute(halo[0], 'ij', [(0, 1), (1, 0)])  1.83 us
    all_to_all x2, waiting for transfers between devices, swap(): x = lax.all_to_all(x, ('blk', 'ij'), 0, 0, tiled=True)  0.85 us
  transfers between devices with their start and end apart: 3, of which 1 were waited for; matrix products, arithmetic and copies ran while one was open for 0% of the time, Pallas kernels for 38%

profile of v12, /device:TPU:0, one launch (start us, length us, event | category | flops | bytes accessed | tf_op | source)
XLA Modules:
  0.0 41.8 jit_solution(9383877976005979426)
XLA Ops:
  0.6 4.3 %cut.1 = (f32[320,128]{1,0:T(8,128)}, f32[5,64,128]{2,1,0:T(8,128)S(1)}, f32[2,5,7,8,128]{4,3,2,1,0:T(8,128)S(1)}, f32[5,7,144,128]{3,2,1,0:T(8,128)S(1)}, f32[5,28,128]{2,1,0:T(8,128)S(1)}) custom-call(f32[1,6,128,128]{3,2,1,0:T(8,128)} %dens.3, f32[1,3,6,128,128]{4,3,2,1,0:T(8,128)} %mom.3, f32[1,6,128,128]{3,2,1,0:T(8,128)} %en.3, ...), custom_call_target="tpu_custom_call" | custom-call | tf_op jit(solution)/shard_map/cut/pallas_call | solution.py:737
  5.0 7.3 %all-to-all-start = ((f32[32,10,1,128]{3,2,1,0:T(1,128)}), f32[32,10,1,128]{3,2,1,0:T(1,128)S(1)}, u32[]{:S(2)}, u32[]{:S(2)}) async-start(f32[32,10,1,128]{3,2,1,0:T(1,128)} %bitcast.10), calls=%async_computation | async-start | bytes 327680 | tf_op jit(solution)/shard_map/all_to_all | solution.py:793
  12.3 1.8 %collective-permute-start = (f32[5,28,128]{2,1,0:T(8,128)S(1)}, f32[5,28,128]{2,1,0:T(8,128)S(1)}, u32[]{:S(2)}, u32[]{:S(2)}) collective-permute-start(f32[5,28,128]{2,1,0:T(8,128)S(1)} %get-tuple-element.18), channel_id=1, source_target_pairs={{0,1},{1,0},{2,3},{3,2},{4,5},{5,4},{6,7},{7,6},{8,9},{9,8},{10,11... | collective-permute-start | bytes 215048 | tf_op jit(solution)/shard_map/ppermute | solution.py:797
  14.1 6.4 %first_section.1 = (f32[5,7,144,128]{3,2,1,0:T(8,128)S(1)}, s32[32]{0:T(128)S(1)}) custom-call(f32[5,7,144,128]{3,2,1,0:T(8,128)S(1)} %get-tuple-element.15.state_in, s32[16]{0:T(128)} %placed_at.3, s32[2,16]{1,0:T(2,128)} %bitcast.15, s32[2,16]{1,0:T(2,128)} %bitcast.12, s32[2,16]{1,0:T(2,128)} %bitcast.14), custom_call_target="tpu_custom_call", output_to_operand_aliasing={{0}: (0, {})} | custom-call | flops 29491200 | bytes 14745600 | tf_op jit(solution)/shard_map/first_section/pallas_call | solution.py:737
  20.5 0.0 collective-permute-done.halo.low.high
  20.6 0.8 %all-to-all-done = f32[32,10,1,128]{3,2,1,0:T(1,128)S(1)} async-done(((f32[32,10,1,128]{3,2,1,0:T(1,128)}), f32[32,10,1,128]{3,2,1,0:T(1,128)S(1)}, u32[]{:S(2)}, u32[]{:S(2)}) %all-to-all-start) | async-done | bytes 163872 | tf_op jit(solution)/shard_map/all_to_all | solution.py:793
  21.4 1.8 %relay.1.after = f32[352,128]{1,0:T(8,128)} custom-call(s32[32]{0:T(128)S(1)} %get-tuple-element.19.route_at, f32[5,28,128]{2,1,0:T(8,128)S(1)} %collective-permute-done.halo.low.high, f32[320,128]{1,0:T(8,128)S(1)} %bitcast.8), custom_call_target="tpu_custom_call" | custom-call | tf_op jit(solution)/shard_map/relay/pallas_call | solution.py:737
  23.2 3.8 %all-to-all-start.1 = ((f32[32,11,1,128]{3,2,1,0:T(1,128)}), f32[32,11,1,128]{3,2,1,0:T(1,128)S(1)}, u32[]{:S(2)}, u32[]{:S(2)}) async-start(f32[32,11,1,128]{3,2,1,0:T(1,128)} %bitcast.9), calls=%async_computation.1 | async-start | bytes 360448 | tf_op jit(solution)/shard_map/all_to_all | solution.py:793
  27.0 3.1 %ends.1 = (f32[5,7,144,128]{3,2,1,0:T(8,128)S(1)}, f32[2,5,7,8,128]{4,3,2,1,0:T(8,128)S(1)}, f32[5,8,128]{2,1,0:T(8,128)S(1)}, f32[5,8,128]{2,1,0:T(8,128)}, f32[5,88,128]{2,1,0:T(8,128)S(1)}) custom-call(f32[5,7,144,128]{3,2,1,0:T(8,128)S(1)} %get-tuple-element.16.state_in, ...), custom_call_target="tpu_custom_call", output_to_operand_aliasing={{0}: (0, {}), {1}: (1, {})} | custom-call | flops 29491200 | bytes 14745600 | tf_op jit(solution)/shard_map/ends/pallas_call | solution.py:737
  30.2 6.4 %second_section.1.out = f32[5,7,144,128]{3,2,1,0:T(8,128)S(1)} custom-call(f32[5,7,144,128]{3,2,1,0:T(8,128)S(1)} %get-tuple-element.24.state_in, f32[1,6,128,128]{3,2,1,0:T(8,128)} %dens.3, f32[1,3,6,128,128]{4,3,2,1,0:T(8,128)} %mom.3, f32[1,6,128,128]{3,2,1,0:T(8,128)} %en.3), custom_call_target="tpu_custom_call", output_to_operand_aliasing={{}: (0, {})} | custom-call | flops 29491200 | bytes 14745600 | tf_op jit(solution)/shard_map/second_section/pallas_call | solution.py:737
  36.6 0.0 all-to-all-done.1
  36.6 5.2 %strips.1 = (f32[1,6,128,128]{3,2,1,0:T(8,128)}, f32[1,3,6,128,128]{4,3,2,1,0:T(8,128)}, f32[1,6,128,128]{3,2,1,0:T(8,128)}) custom-call(f32[5,64,128]{2,1,0:T(8,128)S(1)} %get-tuple-element.14.own, f32[5,8,128]{2,1,0:T(8,128)S(1)} %get-tuple-element.21.ends_base, f32[5,8,128]{2,1,0:T(8,128)} %get-tuple-element.22.ends_sec_at, ...), custom_call_target="tpu_custom_call" | custom-call | tf_op jit(solution)/shard_map/strips/pallas_call | solution.py:737
Async XLA Ops:
  5.0 16.5 %all-to-all-start = ((f32[32,10,1,128]{3,2,1,0:T(1,128)}), f32[32,10,1,128]{3,2,1,0:T(1,128)S(1)}, u32[]{:S(2)}, u32[]{:S(2)}) async-start(f32[32,10,1,128]{3,2,1,0:T(1,128)} %bitcast.10), calls=%async_computation | async-start | bytes 327680 | tf_op jit(solution)/shard_map/all_to_all | solution.py:793
  12.3 8.3 %collective-permute-start = (f32[5,28,128]{2,1,0:T(8,128)S(1)}, f32[5,28,128]{2,1,0:T(8,128)S(1)}, u32[]{:S(2)}, u32[]{:S(2)}) collective-permute-start(f32[5,28,128]{2,1,0:T(8,128)S(1)} %get-tuple-element.18), channel_id=1, source_target_pairs={{0,1},{1,0},{2,3},{3,2},{4,5},{5,4},{6,7},{7,6},{8,9},{9,8},{10,11... | collective-permute-start | bytes 215048 | tf_op jit(solution)/shard_map/ppermute | solution.py:797
  23.2 13.4 %all-to-all-start.1 = ((f32[32,11,1,128]{3,2,1,0:T(1,128)}), f32[32,11,1,128]{3,2,1,0:T(1,128)S(1)}, u32[]{:S(2)}, u32[]{:S(2)}) async-start(f32[32,11,1,128]{3,2,1,0:T(1,128)} %bitcast.9), calls=%async_computation.1 | async-start | bytes 360448 | tf_op jit(solution)/shard_map/all_to_all | solution.py:793

commit v13 on v12

--- a/solution.py
+++ b/solution.py
@@ -50,7 +50,7 @@
     kv = viscosity * unit
     rw = kv * (ax * ax + ay * ay)
     cw = kv * (bx * bx + by * by)
-    return v * ax, v * ay, v * bx, v * by, -unit / v, rw, cw, 30.0 * (rw + cw + kv)
+    return v * ax, v * ay, v * bx, v * by, -unit / v, rw, cw, 30.0 * (rw + kv) + 28.0 * cw
 
 
 def flux(f, w, p, h, gx, gy):
@@ -70,6 +70,16 @@
 
 def curve(x, at):
     return 16.0 * (at(x, 1) + at(x, -1)) - (at(x, 2) + at(x, -2))
+
+
+def turned_slope(x, axis):
+    ahead = turn(x, -2, axis) - x
+    return 8.0 * turn(ahead, 1, axis) - (ahead + turn(ahead, 2, axis))
+
+
+def turned_curve(x, axis):
+    ahead = turn(x, -2, axis) + x
+    return 16.0 * turn(ahead, 1, axis) - (ahead + turn(ahead, 2, axis))
 
 
 def along(axis):
@@ -140,7 +150,7 @@
         copy.wait()
 
 
-def tile_stage(planes, load, mets, shift_i, shift_j, hold, done):
+def tile_stage(planes, load, mets, shift_i, axis_j, hold, done):
     kv = viscosity * unit
     fk, ws, acc = hold
 
@@ -151,11 +161,11 @@
             w, p, h = point(x)
             fi, fj = flux(x, w, p, h, vax, vay), flux(x, w, p, h, vbx, vby)
             for c in range(CH):
-                val = niv * (slope(fi[c], shift_i(0, c, s, k)) + slope(fj[c], shift_j))
+                val = niv * (slope(fi[c], shift_i(0, c, s, k)) + turned_slope(fj[c], axis_j))
                 if c > 0:
                     v = w[c - 1]
                     val = val + (
-                        rw * curve(v, shift_i(1, c - 1, s, k)) + cw * curve(v, shift_j) - tw * v
+                        rw * curve(v, shift_i(1, c - 1, s, k)) + cw * turned_curve(v, axis_j) - tw * v
                     )
                     ws[c - 1, s, k] = v
                 acc[c, s, k] = x[c] + val
@@ -220,7 +230,7 @@
     high_side = row % 8 < 4
     mirror = jnp.where(
         rows_of((LANES, LANES)) + lanes_of((LANES, LANES)) == rows - 1, 1.0, 0.0
-    )
+    ).astype(jnp.bfloat16)
     flip = [jnp.where(orient[f, block] == 1, -1.0, 1.0) for f in range(2)]
     same = [jnp.where(face[f, block] == f, -1.0, 1.0) for f in range(2)]
     rising = [face[f, block] == 1 for f in range(2)]
@@ -230,12 +240,14 @@
     def orient_strip(c):
         strip = packed[c].T[0:64]
         own[c] = strip
+        rest, parts = strip, []
+        for _ in range(3):
+            parts.append(rest.astype(jnp.bfloat16))
+            rest = rest - parts[-1].astype(jnp.float32)
         back = jnp.dot(
-            strip,
-            mirror,
-            precision=lax.Precision.HIGHEST,
-            preferred_element_type=jnp.float32,
+            jnp.concatenate(parts, axis=0), mirror, preferred_element_type=jnp.float32
         )
+        back = back[0:64] + (back[64:128] + back[128:192])
         moved = jnp.where(turned < 0.0, back, strip)
         sign = jnp.where(c < 2, turned, jnp.where(c < 4, facing, 1.0))
         moved = jnp.where(row >= planes * 8, moved * sign, moved)
@@ -310,7 +322,6 @@
 def flux_chunk(get, mets, fi, w, fk, acc, r):
     rows = pl.ds(r, 8)
     vax, vay, vbx, vby, niv, rw, cw, tw = [mets[j, rows] for j in range(8)]
-    at_j = along(1)
     for k in range(fi.shape[1]):
         f = [get(c, k, r) for c in range(CH)]
         wk, p, h = point(f)
@@ -320,9 +331,9 @@
             w[c, k, rows] = wk[c]
         fj = flux(f, wk, p, h, vbx, vby)
         for c in range(CH):
-            val = niv * slope(fj[c], at_j)
+            val = niv * turned_slope(fj[c], 1)
             if c > 0:
-                val = val + (cw * curve(wk[c - 1], at_j) - tw * wk[c - 1])
+                val = val + (cw * turned_curve(wk[c - 1], 1) - tw * wk[c - 1])
             acc[c, k, rows] = val
         for c, x in enumerate(flux_planes(f, wk, p, h)):
             fk[c, k, rows] = x
@@ -482,7 +493,7 @@
         state[c, k, start : start + 4] = x[2:6]
 
     tile_stage(
-        planes, lambda c, s, k: tall[s, c, k], mets, lambda *_: along(0), along(1),
+        planes, lambda c, s, k: tall[s, c, k], mets, lambda *_: along(0), 1,
         (tile_fk, tile_w, tile_acc), done,
     )
     for c, x in enumerate(pack_ends(tall, planes)):
@@ -606,7 +617,7 @@
             lambda c, f, k: held[c, f, k],
             mets,
             lambda kind, c, f, k: beyond(rims[CH * kind + c, f, k], rows),
-            along(0),
+            0,
             (fk, ws, acc),
             keep,
         )

time: 42.1 us -> 106 us (2.52)
  Pallas kernels: 27.4 us -> 91.3 us
    pallas_call x6, Pallas kernels: 27.4 us -> 91.3 us  [keep(): run(*[x if spec not in (vmem, hbm) else pltpu.with_memory_space_constrain...]
  transfers between devices with their start and end apart: 3 -> 3, of which waited for: 1 -> 0; matrix products, arithmetic and copies ran while one was open for 0% -> 0% of each run, Pallas kernels for 38% -> 76%
where the time goes in v13:
time: 106 us
  Pallas kernels  91.3 us (86%)
  starting transfers between devices  13.8 us (13%)
    pallas_call x6, Pallas kernels, keep(): run(*[x if spec not in (vmem, hbm) else pltpu.with_memory_space_constrain...  91.3 us
    all_to_all x2, starting transfers between devices, swap(): x = lax.all_to_all(x, ('blk', 'ij'), 0, 0, tiled=True)  11.9 us
  transfers between devices with their start and end apart: 3, of which 0 were waited for; matrix products, arithmetic and copies ran while one was open for 0% of the time, Pallas kernels for 76%

profile of v13, /device:TPU:0, one launch (start us, length us, event | category | flops | bytes accessed | tf_op | source)
XLA Modules:
  0.0 105.7 jit_solution(3968370629686476021)
XLA Ops:
  0.6 4.2 %cut.1 = (f32[320,128]{1,0:T(8,128)}, f32[5,64,128]{2,1,0:T(8,128)S(1)}, f32[2,5,7,8,128]{4,3,2,1,0:T(8,128)S(1)}, f32[5,7,144,128]{3,2,1,0:T(8,128)S(1)}, f32[5,28,128]{2,1,0:T(8,128)S(1)}) custom-call(f32[1,6,128,128]{3,2,1,0:T(8,128)} %dens.3, f32[1,3,6,128,128]{4,3,2,1,0:T(8,128)} %mom.3, f32[1,6,128,128]{3,2,1,0:T(8,128)} %en.3, ...), custom_call_target="tpu_custom_call" | custom-call | tf_op jit(solution)/shard_map/cut/pallas_call | solution.py:748
  4.8 7.3 %all-to-all-start = ((f32[32,10,1,128]{3,2,1,0:T(1,128)}), f32[32,10,1,128]{3,2,1,0:T(1,128)S(1)}, u32[]{:S(2)}, u32[]{:S(2)}) async-start(f32[32,10,1,128]{3,2,1,0:T(1,128)} %bitcast.10), calls=%async_computation | async-start | bytes 327680 | tf_op jit(solution)/shard_map/all_to_all | solution.py:804
  12.1 1.8 %collective-permute-start = (f32[5,28,128]{2,1,0:T(8,128)S(1)}, f32[5,28,128]{2,1,0:T(8,128)S(1)}, u32[]{:S(2)}, u32[]{:S(2)}) collective-permute-start(f32[5,28,128]{2,1,0:T(8,128)S(1)} %get-tuple-element.18), channel_id=1, source_target_pairs={{0,1},{1,0},{2,3},{3,2},{4,5},{5,4},{6,7},{7,6},{8,9},{9,8},{10,11... | collective-permute-start | bytes 215048 | tf_op jit(solution)/shard_map/ppermute | solution.py:808
  13.9 36.5 %first_section.1 = (f32[5,7,144,128]{3,2,1,0:T(8,128)S(1)}, s32[32]{0:T(128)S(1)}) custom-call(f32[5,7,144,128]{3,2,1,0:T(8,128)S(1)} %get-tuple-element.15.state_in, s32[16]{0:T(128)} %placed_at.3, s32[2,16]{1,0:T(2,128)} %bitcast.15, s32[2,16]{1,0:T(2,128)} %bitcast.12, s32[2,16]{1,0:T(2,128)} %bitcast.14), custom_call_target="tpu_custom_call", output_to_operand_aliasing={{0}: (0, {})} | custom-call | flops 29491200 | bytes 14745600 | tf_op jit(solution)/shard_map/first_section/pallas_call | solution.py:748
  50.5 0.0 collective-permute-done.halo.low.high
  50.5 0.0 all-to-all-done
  50.5 1.8 %relay.1.after = f32[352,128]{1,0:T(8,128)} custom-call(s32[32]{0:T(128)S(1)} %get-tuple-element.19.route_at, f32[5,28,128]{2,1,0:T(8,128)S(1)} %collective-permute-done.halo.low.high, f32[320,128]{1,0:T(8,128)S(1)} %bitcast.8), custom_call_target="tpu_custom_call" | custom-call | tf_op jit(solution)/shard_map/relay/pallas_call | solution.py:748
  52.3 4.6 %all-to-all-start.1 = ((f32[32,11,1,128]{3,2,1,0:T(1,128)}), f32[32,11,1,128]{3,2,1,0:T(1,128)S(1)}, u32[]{:S(2)}, u32[]{:S(2)}) async-start(f32[32,11,1,128]{3,2,1,0:T(1,128)} %bitcast.9), calls=%async_computation.1 | async-start | bytes 360448 | tf_op jit(solution)/shard_map/all_to_all | solution.py:804
  57.0 3.3 %ends.1 = (f32[5,7,144,128]{3,2,1,0:T(8,128)S(1)}, f32[2,5,7,8,128]{4,3,2,1,0:T(8,128)S(1)}, f32[5,8,128]{2,1,0:T(8,128)S(1)}, f32[5,8,128]{2,1,0:T(8,128)}, f32[5,88,128]{2,1,0:T(8,128)S(1)}) custom-call(f32[5,7,144,128]{3,2,1,0:T(8,128)S(1)} %get-tuple-element.16.state_in, ...), custom_call_target="tpu_custom_call", output_to_operand_aliasing={{0}: (0, {}), {1}: (1, {})} | custom-call | flops 29491200 | bytes 14745600 | tf_op jit(solution)/shard_map/ends/pallas_call | solution.py:748
  60.3 40.2 %second_section.1.out = f32[5,7,144,128]{3,2,1,0:T(8,128)S(1)} custom-call(f32[5,7,144,128]{3,2,1,0:T(8,128)S(1)} %get-tuple-element.24.state_in, f32[1,6,128,128]{3,2,1,0:T(8,128)} %dens.3, f32[1,3,6,128,128]{4,3,2,1,0:T(8,128)} %mom.3, f32[1,6,128,128]{3,2,1,0:T(8,128)} %en.3), custom_call_target="tpu_custom_call", output_to_operand_aliasing={{}: (0, {})} | custom-call | flops 29491200 | bytes 14745600 | tf_op jit(solution)/shard_map/second_section/pallas_call | solution.py:748
  100.5 0.0 all-to-all-done.1
  100.5 5.2 %strips.1 = (f32[1,6,128,128]{3,2,1,0:T(8,128)}, f32[1,3,6,128,128]{4,3,2,1,0:T(8,128)}, f32[1,6,128,128]{3,2,1,0:T(8,128)}) custom-call(f32[5,64,128]{2,1,0:T(8,128)S(1)} %get-tuple-element.14.own, f32[5,8,128]{2,1,0:T(8,128)S(1)} %get-tuple-element.21.ends_base, f32[5,8,128]{2,1,0:T(8,128)} %get-tuple-element.22.ends_sec_at, ...), custom_call_target="tpu_custom_call" | custom-call | tf_op jit(solution)/shard_map/strips/pallas_call | solution.py:748
Async XLA Ops:
  4.8 45.7 %all-to-all-start = ((f32[32,10,1,128]{3,2,1,0:T(1,128)}), f32[32,10,1,128]{3,2,1,0:T(1,128)S(1)}, u32[]{:S(2)}, u32[]{:S(2)}) async-start(f32[32,10,1,128]{3,2,1,0:T(1,128)} %bitcast.10), calls=%async_computation | async-start | bytes 327680 | tf_op jit(solution)/shard_map/all_to_all | solution.py:804
  12.1 38.3 %collective-permute-start = (f32[5,28,128]{2,1,0:T(8,128)S(1)}, f32[5,28,128]{2,1,0:T(8,128)S(1)}, u32[]{:S(2)}, u32[]{:S(2)}) collective-permute-start(f32[5,28,128]{2,1,0:T(8,128)S(1)} %get-tuple-element.18), channel_id=1, source_target_pairs={{0,1},{1,0},{2,3},{3,2},{4,5},{5,4},{6,7},{7,6},{8,9},{9,8},{10,11... | collective-permute-start | bytes 215048 | tf_op jit(solution)/shard_map/ppermute | solution.py:808
  52.3 48.2 %all-to-all-start.1 = ((f32[32,11,1,128]{3,2,1,0:T(1,128)}), f32[32,11,1,128]{3,2,1,0:T(1,128)S(1)}, u32[]{:S(2)}, u32[]{:S(2)}) async-start(f32[32,11,1,128]{3,2,1,0:T(1,128)} %bitcast.9), calls=%async_computation.1 | async-start | bytes 360448 | tf_op jit(solution)/shard_map/all_to_all | solution.py:804

commit v14 on v12

--- a/solution.py
+++ b/solution.py
@@ -14,7 +14,7 @@
 
 LANES = 128
 PAD = 8
-PIECES = 4
+PIECES = 8
 DEPTH = 4
 CH = 5
 VMEM_MIB = 32
@@ -220,7 +220,7 @@
     high_side = row % 8 < 4
     mirror = jnp.where(
         rows_of((LANES, LANES)) + lanes_of((LANES, LANES)) == rows - 1, 1.0, 0.0
-    )
+    ).astype(jnp.bfloat16)
     flip = [jnp.where(orient[f, block] == 1, -1.0, 1.0) for f in range(2)]
     same = [jnp.where(face[f, block] == f, -1.0, 1.0) for f in range(2)]
     rising = [face[f, block] == 1 for f in range(2)]
@@ -230,12 +230,14 @@
     def orient_strip(c):
         strip = packed[c].T[0:64]
         own[c] = strip
+        rest, parts = strip, []
+        for _ in range(3):
+            parts.append(rest.astype(jnp.bfloat16))
+            rest = rest - parts[-1].astype(jnp.float32)
         back = jnp.dot(
-            strip,
-            mirror,
-            precision=lax.Precision.HIGHEST,
-            preferred_element_type=jnp.float32,
+            jnp.concatenate(parts, axis=0), mirror, preferred_element_type=jnp.float32
         )
+        back = back[0:64] + (back[64:128] + back[128:192])
         moved = jnp.where(turned < 0.0, back, strip)
         sign = jnp.where(c < 2, turned, jnp.where(c < 4, facing, 1.0))
         moved = jnp.where(row >= planes * 8, moved * sign, moved)
@@ -399,7 +401,7 @@
     chunks(count, fluxes, unroll=2)
     wait_all(tables)
     loop(blocks, note, unroll=8)
-    chunks(count, sums, unroll=2)
+    chunks(count, sums)
 
 
 def pack_ends(tall, planes):
@@ -530,7 +532,7 @@
 
     chunks(rows // 8 + 2, fluxes, unroll=2)
     wait_all(copies)
-    chunks(rows // 8, lambda n: sum_chunk(mets, fi, w, fk, acc, n + PAD, emit), unroll=2)
+    chunks(rows // 8, lambda n: sum_chunk(mets, fi, w, fk, acc, n + PAD, emit))
 
 
 def beyond(low, rows):

time: 42.1 us -> 42.3 us (level)
  transfers between devices with their start and end apart: 3 -> 3, of which waited for: 1 -> 1; matrix products, arithmetic and copies ran while one was open for 0% -> 0% of each run, Pallas kernels for 38% -> 39%
where the time goes in v14:
time: 42.3 us; the launch traced here: 42 us
  Pallas kernels  27.5 us (65%)
  starting transfers between devices  13 us (31%)
  waiting for transfers between devices  0.74 us (2%)
  between operations  0.7 us (2%)
    pallas_call x6, Pallas kernels, keep(): run(*[x if spec not in (vmem, hbm) else pltpu.with_memory_space_constrain...  27.5 us
    all_to_all x2, starting transfers between devices, swap(): x = lax.all_to_all(x, ('blk', 'ij'), 0, 0, tiled=True)  11.2 us
    ppermute x1, starting transfers between devices, local(): below = above = lax.ppermute(halo[0], 'ij', [(0, 1), (1, 0)])  1.83 us
  transfers between devices with their start and end apart: 3, of which 1 were waited for; matrix products, arithmetic and copies ran while one was open for 0% of the time, Pallas kernels for 39%

profile of v14, /device:TPU:0, one launch (start us, length us, event | category | flops | bytes accessed | tf_op | source)
XLA Modules:
  0.0 42.0 jit_solution(11025842421541471209)
XLA Ops:
  0.6 4.3 %cut.1 = (f32[320,128]{1,0:T(8,128)}, f32[5,64,128]{2,1,0:T(8,128)S(1)}, f32[2,5,7,8,128]{4,3,2,1,0:T(8,128)S(1)}, f32[5,7,144,128]{3,2,1,0:T(8,128)S(1)}, f32[5,28,128]{2,1,0:T(8,128)S(1)}) custom-call(f32[1,6,128,128]{3,2,1,0:T(8,128)} %dens.3, f32[1,3,6,128,128]{4,3,2,1,0:T(8,128)} %mom.3, f32[1,6,128,128]{3,2,1,0:T(8,128)} %en.3, ...), custom_call_target="tpu_custom_call" | custom-call | tf_op jit(solution)/shard_map/cut/pallas_call | solution.py:739
  4.9 7.3 %all-to-all-start = ((f32[32,10,1,128]{3,2,1,0:T(1,128)}), f32[32,10,1,128]{3,2,1,0:T(1,128)S(1)}, u32[]{:S(2)}, u32[]{:S(2)}) async-start(f32[32,10,1,128]{3,2,1,0:T(1,128)} %bitcast.10), calls=%async_computation | async-start | bytes 327680 | tf_op jit(solution)/shard_map/all_to_all | solution.py:795
  12.2 1.8 %collective-permute-start = (f32[5,28,128]{2,1,0:T(8,128)S(1)}, f32[5,28,128]{2,1,0:T(8,128)S(1)}, u32[]{:S(2)}, u32[]{:S(2)}) collective-permute-start(f32[5,28,128]{2,1,0:T(8,128)S(1)} %get-tuple-element.18), channel_id=1, source_target_pairs={{0,1},{1,0},{2,3},{3,2},{4,5},{5,4},{6,7},{7,6},{8,9},{9,8},{10,11... | collective-permute-start | bytes 215048 | tf_op jit(solution)/shard_map/ppermute | solution.py:799
  14.0 6.6 %first_section.1 = (f32[5,7,144,128]{3,2,1,0:T(8,128)S(1)}, s32[32]{0:T(128)S(1)}) custom-call(f32[5,7,144,128]{3,2,1,0:T(8,128)S(1)} %get-tuple-element.15.state_in, s32[16]{0:T(128)} %placed_at.3, s32[2,16]{1,0:T(2,128)} %bitcast.15, s32[2,16]{1,0:T(2,128)} %bitcast.12, s32[2,16]{1,0:T(2,128)} %bitcast.14), custom_call_target="tpu_custom_call", output_to_operand_aliasing={{0}: (0, {})} | custom-call | flops 29491200 | bytes 14745600 | tf_op jit(solution)/shard_map/first_section/pallas_call | solution.py:739
  20.6 0.0 collective-permute-done.halo.low.high
  20.6 0.7 %all-to-all-done = f32[32,10,1,128]{3,2,1,0:T(1,128)S(1)} async-done(((f32[32,10,1,128]{3,2,1,0:T(1,128)}), f32[32,10,1,128]{3,2,1,0:T(1,128)S(1)}, u32[]{:S(2)}, u32[]{:S(2)}) %all-to-all-start) | async-done | bytes 163872 | tf_op jit(solution)/shard_map/all_to_all | solution.py:795
  21.4 1.8 %relay.1.after = f32[352,128]{1,0:T(8,128)} custom-call(s32[32]{0:T(128)S(1)} %get-tuple-element.19.route_at, f32[5,28,128]{2,1,0:T(8,128)S(1)} %collective-permute-done.halo.low.high, f32[320,128]{1,0:T(8,128)S(1)} %bitcast.8), custom_call_target="tpu_custom_call" | custom-call | tf_op jit(solution)/shard_map/relay/pallas_call | solution.py:739
  23.2 3.9 %all-to-all-start.1 = ((f32[32,11,1,128]{3,2,1,0:T(1,128)}), f32[32,11,1,128]{3,2,1,0:T(1,128)S(1)}, u32[]{:S(2)}, u32[]{:S(2)}) async-start(f32[32,11,1,128]{3,2,1,0:T(1,128)} %bitcast.9), calls=%async_computation.1 | async-start | bytes 360448 | tf_op jit(solution)/shard_map/all_to_all | solution.py:795
  27.1 3.1 %ends.1 = (f32[5,7,144,128]{3,2,1,0:T(8,128)S(1)}, f32[2,5,7,8,128]{4,3,2,1,0:T(8,128)S(1)}, f32[5,8,128]{2,1,0:T(8,128)S(1)}, f32[5,8,128]{2,1,0:T(8,128)}, f32[5,88,128]{2,1,0:T(8,128)S(1)}) custom-call(f32[5,7,144,128]{3,2,1,0:T(8,128)S(1)} %get-tuple-element.16.state_in, ...), custom_call_target="tpu_custom_call", output_to_operand_aliasing={{0}: (0, {}), {1}: (1, {})} | custom-call | flops 29491200 | bytes 14745600 | tf_op jit(solution)/shard_map/ends/pallas_call | solution.py:739
  30.2 6.5 %second_section.1.out = f32[5,7,144,128]{3,2,1,0:T(8,128)S(1)} custom-call(f32[5,7,144,128]{3,2,1,0:T(8,128)S(1)} %get-tuple-element.24.state_in, f32[1,6,128,128]{3,2,1,0:T(8,128)} %dens.3, f32[1,3,6,128,128]{4,3,2,1,0:T(8,128)} %mom.3, f32[1,6,128,128]{3,2,1,0:T(8,128)} %en.3), custom_call_target="tpu_custom_call", output_to_operand_aliasing={{}: (0, {})} | custom-call | flops 29491200 | bytes 14745600 | tf_op jit(solution)/shard_map/second_section/pallas_call | solution.py:739
  36.7 0.0 all-to-all-done.1
  36.8 5.3 %strips.1 = (f32[1,6,128,128]{3,2,1,0:T(8,128)}, f32[1,3,6,128,128]{4,3,2,1,0:T(8,128)}, f32[1,6,128,128]{3,2,1,0:T(8,128)}) custom-call(f32[5,64,128]{2,1,0:T(8,128)S(1)} %get-tuple-element.14.own, f32[5,8,128]{2,1,0:T(8,128)S(1)} %get-tuple-element.21.ends_base, f32[5,8,128]{2,1,0:T(8,128)} %get-tuple-element.22.ends_sec_at, ...), custom_call_target="tpu_custom_call" | custom-call | tf_op jit(solution)/shard_map/strips/pallas_call | solution.py:739
Async XLA Ops:
  4.9 16.5 %all-to-all-start = ((f32[32,10,1,128]{3,2,1,0:T(1,128)}), f32[32,10,1,128]{3,2,1,0:T(1,128)S(1)}, u32[]{:S(2)}, u32[]{:S(2)}) async-start(f32[32,10,1,128]{3,2,1,0:T(1,128)} %bitcast.10), calls=%async_computation | async-start | bytes 327680 | tf_op jit(solution)/shard_map/all_to_all | solution.py:795
  12.2 8.4 %collective-permute-start = (f32[5,28,128]{2,1,0:T(8,128)S(1)}, f32[5,28,128]{2,1,0:T(8,128)S(1)}, u32[]{:S(2)}, u32[]{:S(2)}) collective-permute-start(f32[5,28,128]{2,1,0:T(8,128)S(1)} %get-tuple-element.18), channel_id=1, source_target_pairs={{0,1},{1,0},{2,3},{3,2},{4,5},{5,4},{6,7},{7,6},{8,9},{9,8},{10,11... | collective-permute-start | bytes 215048 | tf_op jit(solution)/shard_map/ppermute | solution.py:799
  23.2 13.6 %all-to-all-start.1 = ((f32[32,11,1,128]{3,2,1,0:T(1,128)}), f32[32,11,1,128]{3,2,1,0:T(1,128)S(1)}, u32[]{:S(2)}, u32[]{:S(2)}) async-start(f32[32,11,1,128]{3,2,1,0:T(1,128)} %bitcast.9), calls=%async_computation.1 | async-start | bytes 360448 | tf_op jit(solution)/shard_map/all_to_all | solution.py:795

commit v15 on v14

--- a/solution.py
+++ b/solution.py
@@ -14,7 +14,7 @@
 
 LANES = 128
 PAD = 8
-PIECES = 8
+PIECES = 4
 DEPTH = 4
 CH = 5
 VMEM_MIB = 32
@@ -325,18 +325,19 @@
             val = niv * slope(fj[c], at_j)
             if c > 0:
                 val = val + (cw * curve(wk[c - 1], at_j) - tw * wk[c - 1])
-            acc[c, k, rows] = val
+            acc[c, k, rows] = f[c] + val
         for c, x in enumerate(flux_planes(f, wk, p, h)):
-            fk[c, k, rows] = x
-
-
-def sum_chunk(mets, fi, w, fk, acc, r, emit):
+            if c > 0:
+                fk[c - 1, k, rows] = x
+
+
+def sum_chunk(get, mets, fi, w, fk, acc, r, emit):
     planes = fi.shape[1]
     kv = viscosity * unit
     rows = pl.ds(r, 8)
     niv, rw = mets[4, rows], mets[5, rows]
     for c in range(CH):
-        t = [fk[c, k, rows] for k in range(planes)]
+        t = [fk[c - 1, k, rows] if c > 0 else get(3, k, r) for k in range(planes)]
         x = [w[c - 1, k, rows] for k in range(planes)] if c > 0 else None
         for k in range(planes):
 
@@ -385,7 +386,7 @@
         flux_chunk(get, mets, fi, w, fk, acc, n + PAD)
 
     def emit(c, k, r, val):
-        state[c, k, pl.ds(r, 8)] = get(c, k, r) + val
+        state[c, k, pl.ds(r, 8)] = val
 
     def sums(n):
         for slot in slots(n):
@@ -393,7 +394,7 @@
             for f in range(2):
                 partner = where_is[neighbour[f, block]]
                 route[2 * slot + f] = partner * 4 + face[f, block] * 2 + orient[f, block]
-        sum_chunk(mets, fi, w, fk, acc, n + PAD, emit)
+        sum_chunk(get, mets, fi, w, fk, acc, n + PAD, emit)
 
     def note(slot):
         where_is[placed[slot]] = slot
@@ -401,7 +402,7 @@
     chunks(count, fluxes, unroll=2)
     wait_all(tables)
     loop(blocks, note, unroll=8)
-    chunks(count, sums)
+    chunks(count, sums, unroll=2)
 
 
 def pack_ends(tall, planes):
@@ -527,12 +528,12 @@
         flux_chunk(get, mets, fi, w, fk, acc, n)
 
     def emit(c, k, r, val):
-        x = 0.5 * (fields[c, k, pl.ds(r - PAD, 8)] + (get(c, k, r) + val))
+        x = 0.5 * (fields[c, k, pl.ds(r - PAD, 8)] + val)
         state[c, k, pl.ds(r, 8)] = x
 
     chunks(rows // 8 + 2, fluxes, unroll=2)
     wait_all(copies)
-    chunks(rows // 8, lambda n: sum_chunk(mets, fi, w, fk, acc, n + PAD, emit))
+    chunks(rows // 8, lambda n: sum_chunk(get, mets, fi, w, fk, acc, n + PAD, emit), unroll=2)
 
 
 def beyond(low, rows):
@@ -807,7 +808,7 @@
         held(shape(8, tall, LANES)),
         padded,
         held(shape(4, planes, tall, LANES)),
-        padded,
+        held(shape(4, planes, tall, LANES)),
         padded,
     ]
     work = planes * rows * LANES

time: 42.3 us -> 41.8 us (0.988)
  Pallas kernels: 27.5 us -> 27 us
    pallas_call x6, Pallas kernels: 27.5 us -> 27 us  [keep(): run(*[x if spec not in (vmem, hbm) else pltpu.with_memory_space_constrain...]
  transfers between devices with their start and end apart: 3 -> 3, of which waited for: 1 -> 1; matrix products, arithmetic and copies ran while one was open for 0% -> 0% of each run, Pallas kernels for 39% -> 38%
where the time goes in v15:
time: 41.8 us; the launch traced here: 41.5 us
  Pallas kernels  27 us (65%)
  starting transfers between devices  12.8 us (31%)
  waiting for transfers between devices  0.94 us (2%)
  between operations  0.7 us (2%)
    pallas_call x6, Pallas kernels, keep(): run(*[x if spec not in (vmem, hbm) else pltpu.with_memory_space_constrain...  27 us
    all_to_all x2, starting transfers between devices, swap(): x = lax.all_to_all(x, ('blk', 'ij'), 0, 0, tiled=True)  11 us
    ppermute x1, starting transfers between devices, local(): below = above = lax.ppermute(halo[0], 'ij', [(0, 1), (1, 0)])  1.83 us
    all_to_all x2, waiting for transfers between devices, swap(): x = lax.all_to_all(x, ('blk', 'ij'), 0, 0, tiled=True)  0.94 us
  transfers between devices with their start and end apart: 3, of which 1 were waited for; matrix products, arithmetic and copies ran while one was open for 0% of the time, Pallas kernels for 38%

profile of v15, /device:TPU:0, one launch (start us, length us, event | category | flops | bytes accessed | tf_op | source)
XLA Modules:
  0.0 41.5 jit_solution(15746437370260429346)
XLA Ops:
  0.6 4.2 %cut.1 = (f32[320,128]{1,0:T(8,128)}, f32[5,64,128]{2,1,0:T(8,128)S(1)}, f32[2,5,7,8,128]{4,3,2,1,0:T(8,128)S(1)}, f32[5,7,144,128]{3,2,1,0:T(8,128)S(1)}, f32[5,28,128]{2,1,0:T(8,128)S(1)}) custom-call(f32[1,6,128,128]{3,2,1,0:T(8,128)} %dens.3, f32[1,3,6,128,128]{4,3,2,1,0:T(8,128)} %mom.3, f32[1,6,128,128]{3,2,1,0:T(8,128)} %en.3, ...), custom_call_target="tpu_custom_call" | custom-call | tf_op jit(solution)/shard_map/cut/pallas_call | solution.py:740
  4.8 7.3 %all-to-all-start = ((f32[32,10,1,128]{3,2,1,0:T(1,128)}), f32[32,10,1,128]{3,2,1,0:T(1,128)S(1)}, u32[]{:S(2)}, u32[]{:S(2)}) async-start(f32[32,10,1,128]{3,2,1,0:T(1,128)} %bitcast.10), calls=%async_computation | async-start | bytes 327680 | tf_op jit(solution)/shard_map/all_to_all | solution.py:796
  12.1 1.8 %collective-permute-start = (f32[5,28,128]{2,1,0:T(8,128)S(1)}, f32[5,28,128]{2,1,0:T(8,128)S(1)}, u32[]{:S(2)}, u32[]{:S(2)}) collective-permute-start(f32[5,28,128]{2,1,0:T(8,128)S(1)} %get-tuple-element.18), channel_id=1, source_target_pairs={{0,1},{1,0},{2,3},{3,2},{4,5},{5,4},{6,7},{7,6},{8,9},{9,8},{10,11... | collective-permute-start | bytes 215048 | tf_op jit(solution)/shard_map/ppermute | solution.py:800
  13.9 6.3 %first_section.1 = (f32[5,7,144,128]{3,2,1,0:T(8,128)S(1)}, s32[32]{0:T(128)S(1)}) custom-call(f32[5,7,144,128]{3,2,1,0:T(8,128)S(1)} %get-tuple-element.15.state_in, s32[16]{0:T(128)} %placed_at.3, s32[2,16]{1,0:T(2,128)} %bitcast.15, s32[2,16]{1,0:T(2,128)} %bitcast.12, s32[2,16]{1,0:T(2,128)} %bitcast.14), custom_call_target="tpu_custom_call", output_to_operand_aliasing={{0}: (0, {})} | custom-call | flops 29491200 | bytes 14745600 | tf_op jit(solution)/shard_map/first_section/pallas_call | solution.py:740
  20.3 0.0 collective-permute-done.halo.low.high
  20.3 0.9 %all-to-all-done = f32[32,10,1,128]{3,2,1,0:T(1,128)S(1)} async-done(((f32[32,10,1,128]{3,2,1,0:T(1,128)}), f32[32,10,1,128]{3,2,1,0:T(1,128)S(1)}, u32[]{:S(2)}, u32[]{:S(2)}) %all-to-all-start) | async-done | bytes 163872 | tf_op jit(solution)/shard_map/all_to_all | solution.py:796
  21.3 1.8 %relay.1.after = f32[352,128]{1,0:T(8,128)} custom-call(s32[32]{0:T(128)S(1)} %get-tuple-element.19.route_at, f32[5,28,128]{2,1,0:T(8,128)S(1)} %collective-permute-done.halo.low.high, f32[320,128]{1,0:T(8,128)S(1)} %bitcast.8), custom_call_target="tpu_custom_call" | custom-call | tf_op jit(solution)/shard_map/relay/pallas_call | solution.py:740
  23.1 3.7 %all-to-all-start.1 = ((f32[32,11,1,128]{3,2,1,0:T(1,128)}), f32[32,11,1,128]{3,2,1,0:T(1,128)S(1)}, u32[]{:S(2)}, u32[]{:S(2)}) async-start(f32[32,11,1,128]{3,2,1,0:T(1,128)} %bitcast.9), calls=%async_computation.1 | async-start | bytes 360448 | tf_op jit(solution)/shard_map/all_to_all | solution.py:796
  26.8 3.1 %ends.1 = (f32[5,7,144,128]{3,2,1,0:T(8,128)S(1)}, f32[2,5,7,8,128]{4,3,2,1,0:T(8,128)S(1)}, f32[5,8,128]{2,1,0:T(8,128)S(1)}, f32[5,8,128]{2,1,0:T(8,128)}, f32[5,88,128]{2,1,0:T(8,128)S(1)}) custom-call(f32[5,7,144,128]{3,2,1,0:T(8,128)S(1)} %get-tuple-element.16.state_in, ...), custom_call_target="tpu_custom_call", output_to_operand_aliasing={{0}: (0, {}), {1}: (1, {})} | custom-call | flops 29491200 | bytes 14745600 | tf_op jit(solution)/shard_map/ends/pallas_call | solution.py:740
  29.9 6.3 %second_section.1.out = f32[5,7,144,128]{3,2,1,0:T(8,128)S(1)} custom-call(f32[5,7,144,128]{3,2,1,0:T(8,128)S(1)} %get-tuple-element.24.state_in, f32[1,6,128,128]{3,2,1,0:T(8,128)} %dens.3, f32[1,3,6,128,128]{4,3,2,1,0:T(8,128)} %mom.3, f32[1,6,128,128]{3,2,1,0:T(8,128)} %en.3), custom_call_target="tpu_custom_call", output_to_operand_aliasing={{}: (0, {})} | custom-call | flops 29491200 | bytes 14745600 | tf_op jit(solution)/shard_map/second_section/pallas_call | solution.py:740
  36.3 0.0 all-to-all-done.1
  36.3 5.2 %strips.1 = (f32[1,6,128,128]{3,2,1,0:T(8,128)}, f32[1,3,6,128,128]{4,3,2,1,0:T(8,128)}, f32[1,6,128,128]{3,2,1,0:T(8,128)}) custom-call(f32[5,64,128]{2,1,0:T(8,128)S(1)} %get-tuple-element.14.own, f32[5,8,128]{2,1,0:T(8,128)S(1)} %get-tuple-element.21.ends_base, f32[5,8,128]{2,1,0:T(8,128)} %get-tuple-element.22.ends_sec_at, ...), custom_call_target="tpu_custom_call" | custom-call | tf_op jit(solution)/shard_map/strips/pallas_call | solution.py:740
Async XLA Ops:
  4.8 16.5 %all-to-all-start = ((f32[32,10,1,128]{3,2,1,0:T(1,128)}), f32[32,10,1,128]{3,2,1,0:T(1,128)S(1)}, u32[]{:S(2)}, u32[]{:S(2)}) async-start(f32[32,10,1,128]{3,2,1,0:T(1,128)} %bitcast.10), calls=%async_computation | async-start | bytes 327680 | tf_op jit(solution)/shard_map/all_to_all | solution.py:796
  12.1 8.2 %collective-permute-start = (f32[5,28,128]{2,1,0:T(8,128)S(1)}, f32[5,28,128]{2,1,0:T(8,128)S(1)}, u32[]{:S(2)}, u32[]{:S(2)}) collective-permute-start(f32[5,28,128]{2,1,0:T(8,128)S(1)} %get-tuple-element.18), channel_id=1, source_target_pairs={{0,1},{1,0},{2,3},{3,2},{4,5},{5,4},{6,7},{7,6},{8,9},{9,8},{10,11... | collective-permute-start | bytes 215048 | tf_op jit(solution)/shard_map/ppermute | solution.py:800
  23.1 13.2 %all-to-all-start.1 = ((f32[32,11,1,128]{3,2,1,0:T(1,128)}), f32[32,11,1,128]{3,2,1,0:T(1,128)S(1)}, u32[]{:S(2)}, u32[]{:S(2)}) async-start(f32[32,11,1,128]{3,2,1,0:T(1,128)} %bitcast.9), calls=%async_computation.1 | async-start | bytes 360448 | tf_op jit(solution)/shard_map/all_to_all | solution.py:796
